TPU v7x, 32 devices: a whole 2x2x4 slice. The times are simulated.
32 devices in a mesh: batch: 4 (over y, x), proto: 8 (over z, core).
Axes of the slice: x: 2, y: 2, z: 4, core: 2. Of those that a mesh axis runs over, the one named last changes fastest.
Arguments:
- embeddings: bfloat16 [8192, 1024], P('batch'), may hold values from -0.5 to 0.5
- prototypes: bfloat16 [8192, 1024], P('proto'), may hold values from -6 to 6
- partners: int32 [8192, 2], P('batch'), may hold values from 0 to 8191
Outputs:
- loss: float32 [], replicated
- grad_proto: float32 [8192, 1024], P('proto', 'batch')
- grad_embed: float32 [8192, 1024], P(('batch', 'proto'))
Inputs may be any that keep to these rules, and one draw needn't show every extreme that they name: `partners`: row indices over the whole batch.
All inputs are finite; a program needn't handle non-finite values.
Results may differ from a plain program's by a relative error of at most 0.0016.
Values may be sent and summed in bfloat16 or wider, within the bound.
No kernel may reach another device: no remote copies, remote signals or barrier semaphores. Data moves between devices by JAX's collectives and lax.ppermute only.
A program may use at most 128 MiB of HBM per device.

v0:
```python
import jax
import jax.numpy as jnp
from jax import lax
from jax.sharding import PartitionSpec as P

ITERS = 3


BALANCE_SMOOTHING = 0.05
SOFTMAX_HEAT = 0.1
NORM_EPSILON = 1e-06


def on_device(embeddings, prototypes, partners):
    row_count = embeddings.shape[0]
    proto_count = prototypes.shape[0]
    batch_size = lax.axis_size("batch")
    proto_size = lax.axis_size("proto")
    total_rows = row_count * batch_size
    centroid_number_value = proto_count * proto_size
    hidden_f = embeddings.astype(jnp.float32)
    inverse = 1.0 / jnp.sqrt(jnp.sum(hidden_f * hidden_f, axis=1, keepdims=True) + NORM_EPSILON)
    unit = (hidden_f * inverse).astype(jnp.bfloat16)
    proto_f = prototypes.astype(jnp.float32)
    wnorm = (
        proto_f / jnp.sqrt(jnp.sum(proto_f * proto_f, axis=1, keepdims=True) + NORM_EPSILON)
    ).astype(jnp.bfloat16)
    cosine_affinities = lax.dot_general(
        unit, wnorm, (((1,), (1,)), ((), ())), preferred_element_type=jnp.float32
    )
    exponent_matrix = jnp.exp(cosine_affinities / BALANCE_SMOOTHING)
    row_scale = jnp.ones((row_count,), jnp.float32)
    col_scale = jnp.ones((proto_count,), jnp.float32)
    for iteration in range(ITERS):
        col_part = jnp.sum(exponent_matrix * row_scale[:, None], axis=0)
        col_total = lax.psum(col_part, "batch")
        col_scale = 1.0 / (centroid_number_value * col_total)
        row_part = jnp.sum(exponent_matrix * col_scale[None, :], axis=1)
        row_total = lax.psum(row_part, "proto")
        row_scale = 1.0 / (total_rows * row_total)
    assign = (total_rows * row_scale[:, None] * exponent_matrix * col_scale[None, :]).astype(
        jnp.bfloat16
    )
    gathered = lax.all_gather(assign, "batch", axis=0, tiled=True)
    first_rows = jnp.take(gathered, partners[:, 0], axis=0).astype(jnp.float32)
    second_rows = jnp.take(gathered, partners[:, 1], axis=0).astype(jnp.float32)
    cluster_codes = 0.5 * (first_rows + second_rows)
    raw_activation_table = cosine_affinities / SOFTMAX_HEAT
    exponentiated_guesses = jnp.exp(raw_activation_table)
    normalizer_value, code_accumulated = lax.psum(
        (jnp.sum(exponentiated_guesses, axis=1), jnp.sum(cluster_codes, axis=1)), "proto"
    )
    local_loss = jnp.sum(
        jnp.sum(cluster_codes, axis=1) * jnp.log(normalizer_value)
        - jnp.sum(cluster_codes * raw_activation_table, axis=1)
    )
    loss = lax.psum(local_loss, ("batch", "proto")) / total_rows
    affinity_derivative = (
        exponentiated_guesses / normalizer_value[:, None] * code_accumulated[:, None]
        - cluster_codes
    ) * (centroid_number_value / (32.0 * SOFTMAX_HEAT))
    affinity_derivative = affinity_derivative.astype(jnp.bfloat16)
    proto_term = lax.dot_general(
        affinity_derivative, unit, (((0,), (0,)), ((), ())), preferred_element_type=jnp.float32
    )
    grad_proto = lax.psum_scatter(proto_term, "batch", scatter_dimension=1, tiled=True)
    share_rows = row_count // proto_size
    first_row = lax.axis_index("proto") * share_rows
    gunit = lax.psum_scatter(
        jnp.dot(affinity_derivative, wnorm, preferred_element_type=jnp.float32),
        "proto",
        scatter_dimension=0,
        tiled=True,
    )
    own_hidden = lax.dynamic_slice_in_dim(hidden_f, first_row, share_rows, 0)
    own_inverse = lax.dynamic_slice_in_dim(inverse, first_row, share_rows, 0)
    along = jnp.sum(own_hidden * gunit, axis=1, keepdims=True)
    grad_embed = own_inverse * gunit - own_hidden * own_inverse * own_inverse * own_inverse * along
    return (loss, grad_proto, grad_embed)


def solution(mesh):
    return jax.shard_map(
        on_device,
        mesh=mesh,
        in_specs=(P("batch", None), P("proto", None), P("batch", None)),
        out_specs=(P(), P("proto", "batch"), P(("batch", "proto"), None)),
        check_vma=False,
    )
```

profile of v0, /device:TPU:0, one launch (start us, length us, event | category | flops | bytes accessed | tf_op | source)
XLA Modules:
  0.0 554.4 jit_solution(18252838795014451785)
XLA Ops:
  7.2 3.1 multiply_reduce_fusion.6
  10.3 2.1 fusion.1
  12.4 10.8 %fusion.3 = (f32[1024]{0:T(1024)S(1)}, f32[2048,1024]{0,1:T(8,128)}) fusion(bf16[1024,1024]{1,0:T(8,128)(2,1)} %param.6, f32[1024]{0:T(1024)S(1)} %add_sqrt_fusion, f32[2048]{0:T(1024)S(1)} %add_rsqrt_fusion, bf16[2048,1024]{1,0:T(8,128)(2,1)} %param.5), kind=kOutput, calls=%fused_computation.22 | convolution fusion | flops 4308597760 | bytes 14696448 | tf_op jit(solution)/shard_map/dot_general | solution.py:28
  23.2 11.3 %psum.63 = f32[1024]{0:T(1024)S(1)} all-reduce(f32[1024]{0:T(1024)S(1)} %get-tuple-element.11), channel_id=1, replica_groups=mesh['batch'=4,'proto'=8] {'batch'}, use_global_device_ids=true, to_apply=%region_3.0 | all-reduce | flops 1024 | bytes 8192 | tf_op jit(solution)/shard_map/psum | solution.py:36
  34.5 4.3 multiply_reduce_fusion.5
  38.8 15.0 %psum.64 = f32[2048]{0:T(1024)S(1)} all-reduce(f32[2048]{0:T(1024)S(1)} %multiply_reduce_fusion.5), channel_id=1, replica_groups=mesh['batch'=4,'proto'=8] {'proto'}, use_global_device_ids=true, to_apply=%region_5.0 | all-reduce | flops 2048 | bytes 16384 | tf_op jit(solution)/shard_map/psum | solution.py:39
  53.9 4.8 multiply_reduce_fusion.4
  58.7 8.1 %psum.65 = f32[1024]{0:T(1024)S(1)} all-reduce(f32[1024]{0:T(1024)S(1)} %multiply_reduce_fusion.4), channel_id=1, replica_groups=mesh['batch'=4,'proto'=8] {'batch'}, use_global_device_ids=true, to_apply=%region_7.0 | all-reduce | flops 1024 | bytes 8192 | tf_op jit(solution)/shard_map/psum | solution.py:36
  66.8 4.3 multiply_reduce_fusion.3
  71.1 13.9 %psum.66 = f32[2048]{0:T(1024)S(1)} all-reduce(f32[2048]{0:T(1024)S(1)} %multiply_reduce_fusion.3), channel_id=1, replica_groups=mesh['batch'=4,'proto'=8] {'proto'}, use_global_device_ids=true, to_apply=%region_9.0 | all-reduce | flops 2048 | bytes 16384 | tf_op jit(solution)/shard_map/psum | solution.py:39
  85.0 4.8 multiply_reduce_fusion.2
  89.9 8.9 %psum.67 = f32[1024]{0:T(1024)S(1)} all-reduce(f32[1024]{0:T(1024)S(1)} %multiply_reduce_fusion.2), channel_id=1, replica_groups=mesh['batch'=4,'proto'=8] {'batch'}, use_global_device_ids=true, to_apply=%region_11.0 | all-reduce | flops 1024 | bytes 8192 | tf_op jit(solution)/shard_map/psum | solution.py:36
  98.8 4.3 multiply_reduce_fusion.1
  103.1 14.1 %psum.68 = f32[2048]{0:T(1024)S(1)} all-reduce(f32[2048]{0:T(1024)S(1)} %multiply_reduce_fusion.1), channel_id=1, replica_groups=mesh['batch'=4,'proto'=8] {'proto'}, use_global_device_ids=true, to_apply=%region_13.0 | all-reduce | flops 2048 | bytes 16384 | tf_op jit(solution)/shard_map/psum | solution.py:39
  117.2 5.7 %multiply_convert_fusion.1 = bf16[2048,1024]{0,1:T(8,128)(2,1)} fusion(f32[2048]{0:T(1024)S(1)} %divide_multiply_fusion, f32[1024]{0:T(1024)S(1)} %multiply_divide_fusion.2, f32[2048,1024]{0,1:T(8,128)} %get-tuple-element.12), kind=kLoop, calls=%fused_computation.5 | loop fusion | flops 8388608 | bytes 12595200 | tf_op jit(solution)/shard_map/convert_element_type | solution.py:41
  123.0 154.6 %all-gather.2.cloned.1.call-done = bf16[8192,1024]{0,1:T(8,128)(2,1)} async-done(((bf16[2048,1024]{0,1:T(8,128)(2,1)}), bf16[8192,1024]{0,1:T(8,128)(2,1)}) %all-gather.2.cloned.1.call-update) | async-done | bytes 16777232 | tf_op jit(solution)/shard_map/all_gather | solution.py:44
  277.6 22.4 %copy.6 = bf16[8192,1024]{1,0:T(8,128)(2,1)} copy(bf16[8192,1024]{0,1:T(8,128)(2,1)} %all-gather.2.cloned.1.call-done) | data formatting | bytes 33554432 | tf_op jit(solution)/shard_map/all_gather | solution.py:44
  300.1 18.9 %gather_fusion = bf16[2048,1024]{1,0:T(8,128)(2,1)} fusion(bf16[8192,1024]{1,0:T(8,128)(2,1)} %copy.6, s32[2048]{0:T(1024)S(1)} %fusion.6), kind=kCustom, calls=%fused_computation.clone | custom fusion | bytes 8396800 | tf_op jit(solution)/shard_map/jit(_take)/gather | solution.py:45
  319.0 6.5 %copy.7 = bf16[2048,1024]{0,1:T(8,128)(2,1)} copy(bf16[2048,1024]{1,0:T(8,128)(2,1)} %gather_fusion) | data formatting | bytes 8388608 | tf_op jit(solution)/shard_map/jit(_take)/gather | solution.py:45
  325.4 18.9 %gather_fusion.1 = bf16[2048,1024]{1,0:T(8,128)(2,1)} fusion(bf16[8192,1024]{1,0:T(8,128)(2,1)} %copy.6, s32[2048]{0:T(1024)S(1)} %fusion.7), kind=kCustom, calls=%fused_computation.1.clone | custom fusion | bytes 8396800 | tf_op jit(solution)/shard_map/jit(_take)/gather | solution.py:46
  344.4 6.5 %copy.9 = bf16[2048,1024]{0,1:T(8,128)(2,1)} copy(bf16[2048,1024]{1,0:T(8,128)(2,1)} %gather_fusion.1) | data formatting | bytes 8388608 | tf_op jit(solution)/shard_map/jit(_take)/gather | solution.py:46
  350.9 7.7 %fusion = (f32[2048]{0:T(1024)S(1)}, f32[2048]{0:T(1024)S(1)}, f32[2048]{0:T(1024)S(1)}) fusion(bf16[2048,1024]{0,1:T(8,128)(2,1)} %copy.7, pred[2048]{0:T(1024)(128)(4,1)S(1)} %get-tuple-element.14, bf16[2048,1024]{0,1:T(8,128)(2,1)} %copy.9, pred[2048]{0:T(1024)(128)(4,1)S(1)} %get-tuple-element.13, f32[2048,1024]{0,1:T(8,128)} %get-tuple-element.12), kind=kLoop, calls=%fused_computation.15 | loop fusion | flops 23062528 | bytes 16805888 | tf_op jit(solution)/shard_map/reduce_sum | solution.py:54
  358.6 28.5 %all-reduce = (f32[2048]{0:T(1024)S(1)}, f32[2048]{0:T(1024)S(1)}) all-reduce(f32[2048]{0:T(1024)S(1)} %get-tuple-element.6, f32[2048]{0:T(1024)S(1)} %get-tuple-element.4), channel_id=1, replica_groups=mesh['batch'=4,'proto'=8] {'proto'}, use_global_device_ids=true, to_apply=%region_16.18 | all-reduce | flops 4096 | bytes 32768 | tf_op jit(solution)/shard_map/psum | solution.py:50
  387.1 7.8 %multiply_convert_fusion = bf16[2048,1024]{0,1:T(8,128)(2,1)S(1)} fusion(f32[2048,1024]{0,1:T(8,128)} %get-tuple-element.12, f32[2048]{0:T(1024)S(1)} %get-tuple-element.8, f32[2048]{0:T(1024)S(1)} %get-tuple-element.7, bf16[2048,1024]{0,1:T(8,128)(2,1)} %copy.7, pred[2048]{0:T(1024)(128)(4,1)S(1)} %get-tuple-element.14, bf16[2048,1024]{0,1:T(8,128)(2,1)} %copy.9, ...), kind=kLoop, calls=%fused_computation.2 | loop fusion | flops 25165824 | bytes 20992000 | tf_op jit(solution)/shard_map/convert_element_type | solution.py:62
  395.0 2.0 copy-done
  397.0 7.1 %fusion.8 = f32[2048,1024]{1,0:T(8,128)} fusion(bf16[2048,1024]{0,1:T(8,128)(2,1)S(1)} %multiply_convert_fusion, bf16[1024,1024]{1,0:T(8,128)(2,1)S(1)} %copy-done.1, f32[1024]{0:T(1024)S(1)} %add_sqrt_fusion), kind=kOutput, calls=%fused_computation.42 | convolution fusion | flops 4298113024 | bytes 14684160 | tf_op jit(solution)/shard_map/dot_general | solution.py:70
  404.1 10.1 %fusion.4 = f32[1024,1024]{1,0:T(8,128)} fusion(bf16[2048,1024]{0,1:T(8,128)(2,1)} %copy-done, f32[2048]{0:T(1024)S(1)} %add_rsqrt_fusion, bf16[2048,1024]{1,0:T(8,128)(2,1)} %param.5), kind=kOutput, calls=%fused_computation.23 | convolution fusion | flops 4301258752 | bytes 12591104 | tf_op jit(solution)/shard_map/dot_general | solution.py:63
  414.3 6.5 %convert_element_type.24 = f32[2048,1024]{1,0:T(8,128)} convert(bf16[2048,1024]{1,0:T(8,128)(2,1)} %param.5) | non-fusion elementwise | flops 2097152 | bytes 12582912 | tf_op jit(solution)/shard_map/convert_element_type | solution.py:21
  421.5 38.8 %psum.70 = f32[]{:T(128)} all-reduce(f32[]{:T(128)} %subtract_reduce_fusion), channel_id=1, replica_groups=mesh['batch'=4,'proto'=8] {'batch','proto'}, use_global_device_ids=true, to_apply=%region_19.21 | all-reduce | flops 1 | bytes 8 | tf_op jit(solution)/shard_map/psum | solution.py:57
  461.0 31.2 %reduce-scatter.5.cloned.1.call-done = f32[256,1024]{1,0:T(8,128)} async-done(((f32[2048,1024]{1,0:T(8,128)}), f32[256,1024]{1,0:T(8,128)}) %reduce-scatter.5.cloned.1.call-update) | async-done | bytes 1048592 | tf_op jit(solution)/shard_map/reduce_scatter | solution.py:69
  493.9 2.8 multiply_subtract_fusion
  496.7 50.1 %reduce-scatter.3.cloned.1.call-done = f32[1024,256]{1,0:T(8,128)} async-done(((f32[1024,1024]{1,0:T(8,128)}), f32[1024,256]{1,0:T(8,128)}) %reduce-scatter.3.cloned.1.call-update) | async-done | bytes 1048592 | tf_op jit(solution)/shard_map/reduce_scatter | solution.py:66
  (26 shorter events, 2.7 us)
Async XLA Ops:
  7.2 270.5 %all-gather.2.cloned.1.call-start = ((), (), s32[]{:S(2)}) async-start(), calls=%async_computation.2 | async-start | bytes 20971520 | tf_op jit(solution)/shard_map/all_gather | solution.py:44
  117.2 5.7 %copy-start.2 = (s32[2048,2]{0,1:T(2,128)S(1)}, s32[2048,2]{0,1:T(2,128)}, u32[]{:S(2)}) copy-start(s32[2048,2]{0,1:T(2,128)} %param.7) | copy-start | bytes 49156
  122.9 369.3 %reduce-scatter.5.cloned.1.call-start = ((), (), s32[]{:S(2)}) async-start(), calls=%async_computation.4 | async-start | bytes 9437184 | tf_op jit(solution)/shard_map/reduce_scatter | solution.py:69
  387.1 9.8 %copy-start.1 = (bf16[1024,1024]{1,0:T(8,128)(2,1)S(1)}, bf16[1024,1024]{1,0:T(8,128)(2,1)}, u32[]{:S(2)}) copy-start(bf16[1024,1024]{1,0:T(8,128)(2,1)} %param.6) | copy-start | bytes 6291460
  395.0 2.0 copy-start
  404.1 142.7 %reduce-scatter.3.cloned.1.call-start = ((), (), s32[]{:S(2)}) async-start(), calls=%async_computation.3 | async-start | bytes 5242880 | tf_op jit(solution)/shard_map/reduce_scatter | solution.py:66
Sparse Core Ops, SparseCore 0:
  123.0 154.5 all-gather.1
  404.2 87.8 reduce-scatter.4
  495.7 51.0 reduce-scatter.2
where the time goes:
time: 556 us; the launch traced here: 554 us
  waiting for transfers between devices  236 us (42%)
  blocking collectives  139 us (25%)
  local copies, waits for them, and re-layouts  75.3 us (14%)
  other arithmetic  60.6 us (11%)
  matrix products  28 us (5%)
  between operations  15.7 us (3%)
    all_gather x1, waiting for transfers between devices, on_device(): gathered = lax.all_gather(assign, 'batch', axis=0, tiled=True)  155 us
    reduce_scatter x1, waiting for transfers between devices, on_device(): lax.psum_scatter(proto_term, 'batch', scatter_dimension=1, tiled=True)  50.1 us
    psum x3, blocking collectives, on_device(): row_total = lax.psum(row_part, 'proto')  43.1 us
    psum x1, blocking collectives, on_device(): loss = lax.psum(local_loss, ('batch', 'proto')) / total_rows  38.8 us
    reduce_scatter x1, waiting for transfers between devices, on_device(): lax.psum_scatter(jnp.dot(affinity_derivative, wnorm, preferred_element_ty...  31.2 us
    psum x1, blocking collectives, on_device(): lax.psum((jnp.sum(exponentiated_guesses, axis=1), jnp.sum(cluster_codes,...  28.5 us
    psum x3, blocking collectives, on_device(): col_total = lax.psum(col_part, 'batch')  28.3 us
    gather x2, local copies, waits for them, and re-layouts, on_device(): second_rows = jnp.take(gathered, partners[:, 1], axis=0).astype(jnp.float32)  25.5 us
  transfers between devices with their start and end apart: 3, of which 3 were waited for; matrix products, arithmetic and copies ran while one was open for 4% of the time, Pallas kernels for 0%

commit v1 on v0

v1 whole, which is shorter than its diff:
```python
import functools

import jax
import jax.numpy as jnp
from jax import lax
from jax.experimental import pallas as pl
from jax.experimental.pallas import tpu as pltpu
from jax.sharding import PartitionSpec as P

ITERS = 3
BALANCE_SMOOTHING = 0.05
SOFTMAX_HEAT = 0.1
NORM_EPSILON = 1e-06
BLOCK = 256
LANES = 128
MIB = 1 << 20
F32 = jnp.float32
BF16 = jnp.bfloat16


def params(mib):
    return pltpu.CompilerParams(vmem_limit_bytes=mib * MIB)


def cost(flops, moved, exps=0):
    return pl.CostEstimate(flops=flops, bytes_accessed=moved, transcendentals=exps)


def normalized(block):
    wide = block.astype(F32)
    inverse = 1.0 / jnp.sqrt(jnp.sum(wide * wide, axis=1, keepdims=True) + NORM_EPSILON)
    return wide * inverse


def lane_row_sums(values):
    columns = values.shape[1]
    part = values[:, 0:LANES]
    for start in range(LANES, columns, LANES):
        part = part + values[:, start : start + LANES]
    return jnp.sum(part.T, axis=0, keepdims=True)


def split_rows(row):
    high = row.astype(BF16).astype(F32)
    middle = (row - high).astype(BF16).astype(F32)
    low = row - high - middle
    place = lax.broadcasted_iota(jnp.int32, (16, row.shape[1]), 0)
    stacked = jnp.where(place == 0, high, jnp.where(place == 1, middle, jnp.where(place == 2, low, 0.0)))
    return stacked.astype(BF16)


def own_rows_kernel(index_ref, embeddings_ref, table_ref, stage_ref):
    del index_ref
    rows, columns = embeddings_ref.shape
    unit = normalized(embeddings_ref[...]).astype(BF16).astype(F32)
    groups = columns // LANES
    for k in range(groups):
        stage_ref[pl.ds(k, rows, stride=groups), :] = unit[:, k * LANES : (k + 1) * LANES]
    table_ref[...] = stage_ref[...].reshape(rows, groups, LANES).astype(BF16)


def own_rows(embeddings, index, share):
    columns = embeddings.shape[1]
    groups = columns // LANES
    return pl.pallas_call(
        own_rows_kernel,
        grid_spec=pltpu.PrefetchScalarGridSpec(
            num_scalar_prefetch=1,
            grid=(1,),
            in_specs=[pl.BlockSpec((share, columns), lambda i, index: (index[0], 0))],
            out_specs=pl.BlockSpec((share, groups, LANES), lambda i, index: (0, 0, 0)),
            scratch_shapes=[pltpu.VMEM((share * groups, LANES), F32)],
        ),
        out_shape=jax.ShapeDtypeStruct((share, groups, LANES), BF16),
        compiler_params=params(16),
        name="own_rows",
    )(index, embeddings)


def scores_kernel(embeddings_ref, prototypes_ref, unit_ref, wnorm_ref, scores_ref, expo_ref, zsum_ref, column_ref):
    step = pl.program_id(0)

    @pl.when(step == 0)
    def _():
        wnorm_ref[...] = normalized(prototypes_ref[...]).astype(BF16)

    unit = normalized(embeddings_ref[...]).astype(BF16)
    unit_ref[...] = unit
    scores = lax.dot_general(unit, wnorm_ref[...], (((1,), (1,)), ((), ())), preferred_element_type=F32)
    scores_ref[...] = scores
    soft = jnp.exp(scores * (1.0 / SOFTMAX_HEAT))
    zsum_ref[...] = lane_row_sums(soft)
    expo = soft * soft
    expo_ref[...] = expo.astype(BF16)
    sums = jnp.sum(expo, axis=0, keepdims=True)

    @pl.when(step == 0)
    def _():
        column_ref[...] = sums

    @pl.when(step > 0)
    def _():
        column_ref[...] += sums


def scores_of(embeddings, prototypes):
    rows, columns = embeddings.shape
    protos = prototypes.shape[0]
    return pl.pallas_call(
        scores_kernel,
        grid=(rows // BLOCK,),
        in_specs=[
            pl.BlockSpec((BLOCK, columns), lambda i: (i, 0)),
            pl.BlockSpec((protos, columns), lambda i: (0, 0), pipeline_mode=pl.Buffered(1)),
        ],
        out_specs=[
            pl.BlockSpec((BLOCK, columns), lambda i: (i, 0)),
            pl.BlockSpec((protos, columns), lambda i: (0, 0)),
            pl.BlockSpec((BLOCK, protos), lambda i: (i, 0)),
            pl.BlockSpec((BLOCK, protos), lambda i: (i, 0)),
            pl.BlockSpec((1, BLOCK), lambda i: (0, i)),
            pl.BlockSpec((1, protos), lambda i: (0, 0)),
        ],
        out_shape=[
            jax.ShapeDtypeStruct((rows, columns), BF16),
            jax.ShapeDtypeStruct((protos, columns), BF16),
            jax.ShapeDtypeStruct((rows, protos), F32),
            jax.ShapeDtypeStruct((rows, protos), BF16),
            jax.ShapeDtypeStruct((1, rows), F32),
            jax.ShapeDtypeStruct((1, protos), F32),
        ],
        compiler_params=params(40),
        cost_estimate=cost(2 * rows * columns * protos, 22 * MIB, rows * protos),
        name="scores",
    )(embeddings, prototypes)


def row_kernel(count, column_ref, expo_ref, row_ref):
    scale = 1.0 / (count * jnp.sum(column_ref[...], axis=0, keepdims=True))
    sums = lax.dot_general(
        split_rows(scale), expo_ref[...], (((1,), (1,)), ((), ())), preferred_element_type=F32
    )
    row_ref[...] = jnp.sum(sums, axis=0, keepdims=True)


def row_pass(columns, expo, count):
    rows, protos = expo.shape
    block = 2 * BLOCK
    return pl.pallas_call(
        functools.partial(row_kernel, count),
        grid=(rows // block,),
        in_specs=[
            pl.BlockSpec(columns.shape, lambda i: (0, 0)),
            pl.BlockSpec((block, protos), lambda i: (i, 0)),
        ],
        out_specs=pl.BlockSpec((1, block), lambda i: (0, i)),
        out_shape=jax.ShapeDtypeStruct((1, rows), F32),
        compiler_params=params(16),
        cost_estimate=cost(2 * rows * protos, 4 * MIB),
        name="row_pass",
    )(columns, expo)


def column_kernel(count, row_ref, expo_ref, column_ref):
    step = pl.program_id(0)
    scale = 1.0 / (count * jnp.sum(row_ref[...], axis=0, keepdims=True))
    sums = lax.dot_general(
        split_rows(scale), expo_ref[...], (((1,), (0,)), ((), ())), preferred_element_type=F32
    )
    sums = jnp.sum(sums, axis=0, keepdims=True)

    @pl.when(step == 0)
    def _():
        column_ref[...] = sums

    @pl.when(step > 0)
    def _():
        column_ref[...] += sums


def column_pass(row_totals, expo, count):
    rows, protos = expo.shape
    block = 2 * BLOCK
    return pl.pallas_call(
        functools.partial(column_kernel, count),
        grid=(rows // block,),
        in_specs=[
            pl.BlockSpec((row_totals.shape[0], block), lambda i: (0, i)),
            pl.BlockSpec((block, protos), lambda i: (i, 0)),
        ],
        out_specs=pl.BlockSpec((1, protos), lambda i: (0, 0)),
        out_shape=jax.ShapeDtypeStruct((1, protos), F32),
        compiler_params=params(16),
        cost_estimate=cost(2 * rows * protos, 4 * MIB),
        name="column_pass",
    )(row_totals, expo)


def partner_kernel(first_ref, second_ref, table_ref, wnorm_ref, first_expo_ref, second_expo_ref, stage_ref):
    step = pl.program_id(0)
    groups = table_ref.shape[1]
    wnorm = wnorm_ref[...]
    for which_ref, out_ref in ((first_ref, first_expo_ref), (second_ref, second_expo_ref)):

        @pl.loop(0, BLOCK // 16)
        def _(i):
            for j in range(16):
                row = i * 16 + j
                place = which_ref[step * BLOCK + row]
                stage_ref[pl.ds(pl.multiple_of(row * groups, groups), groups), :] = table_ref[place].astype(F32)

        unit = jnp.concatenate(
            [stage_ref[pl.ds(k, BLOCK, stride=groups), :].astype(BF16) for k in range(groups)], axis=1
        )
        scores = lax.dot_general(unit, wnorm, (((1,), (1,)), ((), ())), preferred_element_type=F32)
        soft = jnp.exp(scores * (1.0 / SOFTMAX_HEAT))
        out_ref[...] = soft * soft


def partner_pass(first, second, table, wnorm):
    rows = first.shape[0]
    protos, columns = wnorm.shape
    groups = columns // LANES
    return pl.pallas_call(
        partner_kernel,
        grid_spec=pltpu.PrefetchScalarGridSpec(
            num_scalar_prefetch=2,
            grid=(rows // BLOCK,),
            in_specs=[
                pl.BlockSpec(table.shape, lambda i, *_: (0, 0, 0), pipeline_mode=pl.Buffered(1)),
                pl.BlockSpec((protos, columns), lambda i, *_: (0, 0), pipeline_mode=pl.Buffered(1)),
            ],
            out_specs=[
                pl.BlockSpec((BLOCK, protos), lambda i, *_: (i, 0)),
                pl.BlockSpec((BLOCK, protos), lambda i, *_: (i, 0)),
            ],
            scratch_shapes=[pltpu.VMEM((BLOCK * groups, LANES), F32)],
        ),
        out_shape=[jax.ShapeDtypeStruct((rows, protos), F32)] * 2,
        compiler_params=params(52),
        cost_estimate=cost(4 * rows * columns * protos, 36 * MIB, 2 * rows * protos),
        name="partner_scores",
    )(first, second, table, wnorm)


def partner_row_kernel(count, column_ref, first_ref, second_ref, row_ref):
    scale = 1.0 / (count * jnp.sum(column_ref[...], axis=0, keepdims=True))
    row_ref[...] = jnp.concatenate(
        [lane_row_sums(first_ref[...] * scale), lane_row_sums(second_ref[...] * scale)], axis=0
    )


def partner_row_pass(columns, first, second, count):
    rows, protos = first.shape
    return pl.pallas_call(
        functools.partial(partner_row_kernel, count),
        grid=(rows // BLOCK,),
        in_specs=[
            pl.BlockSpec(columns.shape, lambda i: (0, 0)),
            pl.BlockSpec((BLOCK, protos), lambda i: (i, 0)),
            pl.BlockSpec((BLOCK, protos), lambda i: (i, 0)),
        ],
        out_specs=pl.BlockSpec((2, BLOCK), lambda i: (0, i)),
        out_shape=jax.ShapeDtypeStruct((2, rows), F32),
        compiler_params=params(16),
        cost_estimate=cost(4 * rows * protos, 16 * MIB),
        name="partner_row_pass",
    )(columns, first, second)


def gradient_kernel(
    count, total, heat_scale, proto_size,
    column_ref, row_ref, zsum_ref, first_ref, second_ref, scores_ref, unit_ref, wnorm_ref,
    gunit_ref, gproto_ref, loss_ref,
):
    step = pl.program_id(0)
    scale = 1.0 / (count * jnp.sum(column_ref[...], axis=0, keepdims=True))
    row_totals = row_ref[...]
    row_scales = 1.0 / (total * row_totals)
    weights = total * row_scales
    code_totals = 0.5 * jnp.sum(weights * row_totals, axis=0, keepdims=True)
    zsum = jnp.sum(zsum_ref[...], axis=0, keepdims=True)
    soft_scale = code_totals / zsum
    log_part = jnp.sum(code_totals * jnp.log(zsum)) * (1.0 / proto_size)
    place = lax.broadcasted_iota(jnp.int32, (8, BLOCK), 0)
    stacked = jnp.where(
        place == 0, weights[0:1], jnp.where(place == 1, weights[1:2], jnp.where(place == 2, soft_scale, 0.0))
    )
    stacked = stacked.T
    first = (stacked[:, 0:1] * first_ref[...] * scale).astype(BF16).astype(F32)
    second = (stacked[:, 1:2] * second_ref[...] * scale).astype(BF16).astype(F32)
    targets = 0.5 * (first + second)
    heated = scores_ref[...] * (1.0 / SOFTMAX_HEAT)
    loss = log_part - jnp.sum(targets * heated)
    dscore = ((jnp.exp(heated) * stacked[:, 2:3] - targets) * heat_scale).astype(BF16)
    gunit_ref[...] = jnp.dot(dscore, wnorm_ref[...], preferred_element_type=F32)
    gproto = lax.dot_general(dscore, unit_ref[...], (((0,), (0,)), ((), ())), preferred_element_type=F32)

    @pl.when(step == 0)
    def _():
        gproto_ref[...] = gproto
        loss_ref[...] = jnp.full(loss_ref.shape, loss, F32)

    @pl.when(step > 0)
    def _():
        gproto_ref[...] += gproto
        loss_ref[...] += loss


def gradients(columns, row_totals, zsum, first, second, scores, unit, wnorm, count, total, proto_size):
    rows, protos = first.shape
    width = wnorm.shape[1]
    heat_scale = count / (32.0 * SOFTMAX_HEAT)
    return pl.pallas_call(
        functools.partial(gradient_kernel, count, total, heat_scale, proto_size),
        grid=(rows // BLOCK,),
        in_specs=[
            pl.BlockSpec(columns.shape, lambda i: (0, 0)),
            pl.BlockSpec((2, BLOCK), lambda i: (0, i)),
            pl.BlockSpec((zsum.shape[0], BLOCK), lambda i: (0, i)),
            pl.BlockSpec((BLOCK, protos), lambda i: (i, 0)),
            pl.BlockSpec((BLOCK, protos), lambda i: (i, 0)),
            pl.BlockSpec((BLOCK, protos), lambda i: (i, 0)),
            pl.BlockSpec((BLOCK, width), lambda i: (i, 0)),
            pl.BlockSpec((protos, width), lambda i: (0, 0), pipeline_mode=pl.Buffered(1)),
        ],
        out_specs=[
            pl.BlockSpec((BLOCK, width), lambda i: (i, 0)),
            pl.BlockSpec((protos, width), lambda i: (0, 0)),
            pl.BlockSpec((8, LANES), lambda i: (0, 0)),
        ],
        out_shape=[
            jax.ShapeDtypeStruct((rows, width), F32),
            jax.ShapeDtypeStruct((protos, width), F32),
            jax.ShapeDtypeStruct((8, LANES), F32),
        ],
        compiler_params=params(52),
        cost_estimate=cost(4 * rows * width * protos, 42 * MIB, rows * protos),
        name="gradients",
    )(columns, row_totals, zsum, first, second, scores, unit, wnorm)


def swap(value, axis, distance):
    size = lax.axis_size(axis)
    return lax.ppermute(value, axis, [(i, i ^ distance) for i in range(size)])


def on_device(embeddings, prototypes, partners):
    row_count, width = embeddings.shape
    proto_count = prototypes.shape[0]
    batch_size = lax.axis_size("batch")
    proto_size = lax.axis_size("proto")
    total_rows = row_count * batch_size
    centroids = proto_count * proto_size
    share = row_count // proto_size
    batch_index = lax.axis_index("batch")
    proto_index = lax.axis_index("proto")

    own = own_rows(embeddings, jnp.full((1,), proto_index, jnp.int32), share)
    table = lax.all_gather(own, ("batch", "proto"), axis=0, tiled=True)

    unit, wnorm, scores, expo, zsum, columns = scores_of(embeddings, prototypes)
    columns = lax.psum(columns, "batch")
    for iteration in range(ITERS - 1):
        row_part = row_pass(columns, expo, centroids)
        if iteration == 0:
            row_totals, zsum = lax.psum((row_part, zsum), "proto")
        else:
            row_totals = lax.psum(row_part, "proto")
        columns = lax.psum(column_pass(row_totals, expo, total_rows), "batch")

    first, second = partner_pass(partners[:, 0], partners[:, 1], table, wnorm)
    row_totals = lax.psum(partner_row_pass(columns, first, second, centroids), "proto")
    gunit, gproto, loss = gradients(
        columns, row_totals, zsum, first, second, scores, unit, wnorm, centroids, total_rows, proto_size
    )
    loss = lax.psum(loss[0, 0], ("batch", "proto")) / total_rows

    pairs = gunit.reshape(proto_size // 2, 2, share, width)
    core = proto_index % 2
    kept = lax.dynamic_index_in_dim(pairs, core, 1, keepdims=False)
    sent = lax.dynamic_index_in_dim(pairs, 1 - core, 1, keepdims=False)
    halves = kept + swap(sent, "proto", 1)
    own_place = proto_index // 2
    gunit = lax.dynamic_index_in_dim(halves, own_place, 0, keepdims=False)
    for distance in range(1, proto_size // 2):
        block = lax.dynamic_index_in_dim(halves, own_place ^ distance, 0, keepdims=False).astype(BF16)
        gunit = gunit + swap(block, "proto", 2 * distance).astype(F32)

    part = width // batch_size
    grad_proto = lax.dynamic_slice_in_dim(gproto, batch_index * part, part, 1)
    for distance in range(1, batch_size):
        block = lax.dynamic_slice_in_dim(gproto, (batch_index ^ distance) * part, part, 1).astype(BF16)
        grad_proto = grad_proto + swap(block, "batch", distance).astype(F32)

    hidden = lax.dynamic_slice_in_dim(embeddings, proto_index * share, share, 0).astype(F32)
    inverse = 1.0 / jnp.sqrt(jnp.sum(hidden * hidden, axis=1, keepdims=True) + NORM_EPSILON)
    along = jnp.sum(hidden * gunit, axis=1, keepdims=True)
    grad_embed = inverse * gunit - hidden * inverse * inverse * inverse * along
    return (loss, grad_proto, grad_embed)


def solution(mesh):
    return jax.shard_map(
        on_device,
        mesh=mesh,
        in_specs=(P("batch", None), P("proto", None), P("batch", None)),
        out_specs=(P(), P("proto", "batch"), P(("batch", "proto"), None)),
        check_vma=False,
    )
```

time: 556 us -> 324 us (0.58)
  waiting for transfers between devices: 236 us -> 31 us
  Pallas kernels: 0 us -> 74.5 us
  other arithmetic: 60.6 us -> 12 us
  local copies, waits for them, and re-layouts: 75.3 us -> 34.7 us
  matrix products: 28 us -> 0 us
  blocking collectives: 139 us -> 149 us
  starting transfers between devices: 0.12 us -> 6.28 us
    all_gather x1, waiting for transfers between devices: 155 us -> 27.3 us  [on_device(): table = lax.all_gather(own, ('batch', 'proto'), axis=0, tiled=True)]
    reduce_scatter x2 -> x0, waiting for transfers between devices: 81.2 us -> none  [the longest x1 50.1 us: on_device(): lax.psum_scatter(proto_term, 'batch', scatter_dimension=1, tiled=True)]
    pallas_call x0 -> x9, Pallas kernels: none -> 74.5 us  [the longest x1 28.5 us: partner_pass(): pl.pallas_call(partner_kernel, grid_spec=pltpu.PrefetchScalarGridSpec(num...]
    gather x4 -> x0, local copies, waits for them, and re-layouts: 50.8 us -> none  [the longest x2 25.5 us: on_device(): second_rows = jnp.take(gathered, partners[:, 1], axis=0).astype(jnp.float32)]
    reduce_sum x10 -> x1, other arithmetic: 37.7 us -> 1.9 us  [on_device(): jnp.sum(hidden * hidden, axis=1, keepdims=True) + NORM_EPSILON]
    dot_general x3 -> x0, matrix products: 28 us -> none  [the longest x1 10.8 us: on_device(): lax.dot_general(unit, wnorm, (((1,), (1,)), ((), ())), preferred_element_...]
    unnamed x6 -> x28, local copies, waits for them, and re-layouts: 1.98 us -> 26.2 us
    all_gather x1 -> x0, local copies, waits for them, and re-layouts: 22.4 us -> none  [on_device(): gathered = lax.all_gather(assign, 'batch', axis=0, tiled=True)]
  transfers between devices with their start and end apart: 3 -> 8, of which waited for: 3 -> 3; matrix products, arithmetic and copies ran while one was open for 4% -> 3% of each run, Pallas kernels for 0% -> 6%
where the time goes in v1:
time: 324 us; the launch traced here: 323 us
  blocking collectives  149 us (46%)
  Pallas kernels  74.5 us (23%)
  local copies, waits for them, and re-layouts  34.7 us (11%)
  waiting for transfers between devices  31 us (10%)
  between operations  16 us (5%)
  other arithmetic  12 us (4%)
  starting transfers between devices  6.28 us (2%)
    psum x1, blocking collectives, on_device(): loss = lax.psum(loss[0, 0], ('batch', 'proto')) / total_rows  62.5 us
    pallas_call x1, Pallas kernels, partner_pass(): pl.pallas_call(partner_kernel, grid_spec=pltpu.PrefetchScalarGridSpec(num...  28.5 us
    all_gather x1, waiting for transfers between devices, on_device(): table = lax.all_gather(own, ('batch', 'proto'), axis=0, tiled=True)  27.3 us
    psum x1, blocking collectives, on_device(): lax.psum(partner_row_pass(columns, first, second, centroids), 'proto')  27.1 us
    unnamed x28, local copies, waits for them, and re-layouts  26.2 us
    pallas_call x1, Pallas kernels, gradients(): pl.pallas_call(functools.partial(gradient_kernel, count, total, heat_scal...  25.2 us
    psum x2, blocking collectives, on_device(): columns = lax.psum(column_pass(row_totals, expo, total_rows), 'batch')  17.2 us
    psum x1, blocking collectives, on_device(): row_totals, zsum = lax.psum((row_part, zsum), 'proto')  15.9 us
  transfers between devices with their start and end apart: 8, of which 3 were waited for; matrix products, arithmetic and copies ran while one was open for 3% of the time, Pallas kernels for 6%

profile of v1, /device:TPU:0, one launch (start us, length us, event | category | flops | bytes accessed | tf_op | source)
XLA Modules:
  0.0 323.0 jit_solution(561186637748743734)
XLA Ops:
  7.2 2.2 copy-done.7
  11.2 12.5 %scores.1 = (bf16[2048,1024]{1,0:T(8,128)(2,1)S(1)}, bf16[1024,1024]{1,0:T(8,128)(2,1)S(1)}, f32[2048,1024]{1,0:T(8,128)}, bf16[2048,1024]{1,0:T(8,128)(2,1)S(1)...) custom-call(bf16[2048,1024]{1,0:T(8,128)(2,1)} %embeddings_ref.3, bf16[1024,1024]{1,0:T(8,128)(2,1)S(1)} %copy-done.8), custom_call_target="tpu_custom_call" | custom-call | flops 4294967296 | bytes 23068672 | tf_op jit(solution)/shard_map/scores/pallas_call | solution.py:109
  23.6 2.0 copy-done
  25.6 1.9 copy-done.9
  28.9 11.3 %psum.56.column_ref = f32[1,1024]{1,0:T(1,128)S(1)} all-reduce(f32[1,1024]{1,0:T(1,128)S(1)} %get-tuple-element.14), channel_id=1, replica_groups=mesh['batch'=4,'proto'=8] {'batch'}, use_global_device_ids=true, to_apply=%region_0.0 | all-reduce | flops 1024 | bytes 8192 | tf_op jit(solution)/shard_map/psum | solution.py:363
  40.2 2.2 copy-done.1
  44.0 15.9 %psum.57.row_ref = f32[1,2048]{1,0:T(1,128)S(1)} all-reduce(f32[1,2048]{1,0:T(1,128)S(1)} %row_pass.2), channel_id=1, replica_groups=mesh['batch'=4,'proto'=8] {'proto'}, use_global_device_ids=true, to_apply=%region_1.0 | all-reduce | flops 2048 | bytes 16384 | tf_op jit(solution)/shard_map/psum | solution.py:367
  59.9 2.2 copy-done.2
  63.2 8.5 %psum.58.column_ref = f32[1,1024]{1,0:T(1,128)S(1)} all-reduce(f32[1,1024]{1,0:T(1,128)S(1)} %column_pass.2), channel_id=1, replica_groups=mesh['batch'=4,'proto'=8] {'batch'}, use_global_device_ids=true, to_apply=%region_2.0 | all-reduce | flops 1024 | bytes 8192 | tf_op jit(solution)/shard_map/psum | solution.py:370
  71.7 2.2 copy-done.3
  73.9 1.6 row_pass.3
  75.6 14.6 %psum.59.row_ref = f32[1,2048]{1,0:T(1,128)S(1)} all-reduce(f32[1,2048]{1,0:T(1,128)S(1)} %row_pass.3), channel_id=1, replica_groups=mesh['batch'=4,'proto'=8] {'proto'}, use_global_device_ids=true, to_apply=%region_3.0 | all-reduce | flops 2048 | bytes 16384 | tf_op jit(solution)/shard_map/psum | solution.py:369
  90.2 2.2 copy-done.4
  93.5 8.7 %psum.60.column_ref = f32[1,1024]{1,0:T(1,128)S(1)} all-reduce(f32[1,1024]{1,0:T(1,128)S(1)} %column_pass.3), channel_id=1, replica_groups=mesh['batch'=4,'proto'=8] {'batch'}, use_global_device_ids=true, to_apply=%region_4.0 | all-reduce | flops 1024 | bytes 8192 | tf_op jit(solution)/shard_map/psum | solution.py:370
  102.2 27.3 %all-gather.2.cloned.1.call-done.table_ref = bf16[8192,8,128]{2,1,0:T(8,128)(2,1)} async-done(((bf16[256,8,128]{2,1,0:T(8,128)(2,1)}), bf16[8192,8,128]{2,1,0:T(8,128)(2,1)}) %all-gather.2.cloned.1.call-update) | async-done | bytes 16777232 | tf_op jit(solution)/shard_map/all_gather | solution.py:360
  129.5 28.5 %partner_scores.1 = (f32[2048,1024]{1,0:T(8,128)}, f32[2048,1024]{1,0:T(8,128)}) custom-call(s32[2048]{0:T(1024)S(1)} %bitcast.26, s32[2048]{0:T(1024)S(1)} %bitcast.25, bf16[8192,8,128]{2,1,0:T(8,128)(2,1)} %all-gather.2.cloned.1.call-done.table_ref, bf16[1024,1024]{1,0:T(8,128)(2,1)} %copy-done.10), custom_call_target="tpu_custom_call" | custom-call | flops 8589934592 | bytes 37748736 | tf_op jit(solution)/shard_map/partner_scores/pallas_call | solution.py:224
  157.9 3.4 %copy-done.5 = f32[2048,1024]{1,0:T(8,128)S(1)} copy-done((f32[2048,1024]{1,0:T(8,128)S(1)}, f32[2048,1024]{1,0:T(8,128)}, u32[]{:S(2)}) %copy-start.5) | copy-done | bytes 8388632
  161.3 3.4 %copy-done.6 = f32[2048,1024]{1,0:T(8,128)S(1)} copy-done((f32[2048,1024]{1,0:T(8,128)S(1)}, f32[2048,1024]{1,0:T(8,128)}, u32[]{:S(2)}) %copy-start.6) | copy-done | bytes 8388632
  164.7 1.7 partner_row_pass.1
  166.4 27.1 %all-reduce = (f32[2,2048]{1,0:T(2,128)S(1)}, f32[1,2048]{1,0:T(1,128)S(1)}) all-reduce(f32[2,2048]{1,0:T(2,128)S(1)} %partner_row_pass.1, f32[1,2048]{1,0:T(1,128)S(1)} %get-tuple-element.19), channel_id=1, replica_groups=mesh['batch'=4,'proto'=8] {'proto'}, use_global_device_ids=true, to_apply=%region_5.0 | all-reduce | flops 6144 | bytes 49152 | tf_op jit(solution)/shard_map/psum | solution.py:373
  193.5 25.2 %gradients.1 = (f32[2048,1024]{1,0:T(8,128)}, f32[1024,1024]{1,0:T(8,128)}, f32[8,128]{1,0:T(8,128)S(1)}) custom-call(f32[1,1024]{1,0:T(1,128)S(1)} %psum.60.column_ref, f32[2,2048]{1,0:T(2,128)S(1)} %get-tuple-element.27.row_ref, f32[1,2048]{1,0:T(1,128)S(1)} %get-tuple-element.28.zsum_ref, f32[2048,1024]{1,0:T(8,128)} %get-tuple-element.17.first_ref, ...), custom_call_target="tpu_custom_call" | custom-call | flops 8589934592 | bytes 44040192 | tf_op jit(solution)/shard_map/gradients/pallas_call | solution.py:314
  218.8 4.7 %dynamic-slice_bitcast_fusion = f32[4,256,1024]{2,1,0:T(8,128)} fusion(f32[4,2,256,1024]{3,2,1,0:T(8,128)} %bitcast.27, s32[]{:T(128)S(6)} %select_n.53), kind=kLoop, calls=%fused_computation.1 | loop fusion | bytes 8388612 | tf_op jit(solution)/shard_map/jit(dynamic_index_in_dim)/squeeze | solution.py:382
  223.5 2.0 dynamic-slice_convert_fusion.5
  229.1 1.9 collective-permute-done.3
  231.0 4.4 %bitcast_add_fusion = f32[4,256,1024]{2,1,0:T(8,128)S(1)} fusion(f32[4,256,1024]{2,1,0:T(8,128)} %collective-permute-done.3, f32[4,2,256,1024]{3,2,1,0:T(8,128)} %bitcast.28, s32[]{:T(128)S(6)} %select_n.52), kind=kLoop, calls=%fused_computation | loop fusion | flops 1048576 | bytes 12582916 | tf_op jit(solution)/shard_map/add | solution.py:383
  235.4 1.9 copy-done.11
  238.6 1.7 collective-permute-done
  241.1 2.6 collective-permute-start.6
  244.2 62.5 %psum.63 = f32[]{:T(128)} all-reduce(f32[]{:T(128)} %bitcast.3), channel_id=1, replica_groups=mesh['batch'=4,'proto'=8] {'batch','proto'}, use_global_device_ids=true, to_apply=%region_7.0 | all-reduce | flops 1 | bytes 8 | tf_op jit(solution)/shard_map/psum | solution.py:377
  307.3 2.9 convert_add_fusion
  310.2 1.9 fusion
  312.2 2.8 fusion.4
  (39 shorter events, 13.1 us)
Async XLA Ops:
  7.2 122.3 %all-gather.2.cloned.1.call-start = ((), (), s32[]{:S(2)}) async-start(), calls=%async_computation | async-start | bytes 17301504 | tf_op jit(solution)/shard_map/all_gather | solution.py:360
  7.2 2.2 copy-start.7
  9.4 1.8 copy-start.8
  23.6 2.0 copy-start
  25.6 1.9 copy-start.9
  27.5 1.3 copy-start.10
  40.2 2.2 copy-start.1
  59.9 2.2 copy-start.2
  71.7 2.2 copy-start.3
  73.9 28.2 %copy-start.13 = (s32[2048,2]{0,1:T(2,128)S(1)}, s32[2048,2]{0,1:T(2,128)}, u32[]{:S(2)}) copy-start(s32[2048,2]{0,1:T(2,128)} %param.5) | copy-start | bytes 49156
  90.2 2.2 copy-start.4
  157.9 3.4 %copy-start.5 = (f32[2048,1024]{1,0:T(8,128)S(1)}, f32[2048,1024]{1,0:T(8,128)}, u32[]{:S(2)}) copy-start(f32[2048,1024]{1,0:T(8,128)} %get-tuple-element.17.first_ref) | copy-start | bytes 25165828
  161.3 3.4 %copy-start.6 = (f32[2048,1024]{1,0:T(8,128)S(1)}, f32[2048,1024]{1,0:T(8,128)}, u32[]{:S(2)}) copy-start(f32[2048,1024]{1,0:T(8,128)} %get-tuple-element.18.second_ref) | copy-start | bytes 25165828
  223.5 7.5 %collective-permute-start.3 = (f32[4,256,1024]{2,1,0:T(8,128)}, f32[4,256,1024]{2,1,0:T(8,128)}, u32[]{:S(2)}, u32[]{:S(2)}) collective-permute-start(f32[4,256,1024]{2,1,0:T(8,128)} %dynamic-slice_bitcast_fusion), channel_id=1, source_target_pairs={{0,1},{1,0},{2,3},{3,2},{4,5},{5,4},{6,7},{7,6},{8,9},{9,8},{10,11... | collective-permute-start | bytes 12582920 | tf_op jit(solution)/shard_map/ppermute | solution.py:345
  225.5 14.8 %collective-permute-start = (bf16[1024,256]{1,0:T(8,128)(2,1)S(1)}, bf16[1024,256]{1,0:T(8,128)(2,1)S(1)}, u32[]{:S(2)}, u32[]{:S(2)}) collective-permute-start(bf16[1024,256]{1,0:T(8,128)(2,1)S(1)} %get-tuple-element.32), channel_id=1, source_target_pairs={{0,8},{8,0},{16,24},{24,16},{1,9},{9,1},{17,25},{25,17},{2,10},{10... | collective-permute-start | bytes 1572872 | tf_op jit(solution)/shard_map/ppermute | solution.py:345
  226.6 80.7 %collective-permute-start.1 = (bf16[1024,256]{1,0:T(8,128)(2,1)S(1)}, bf16[1024,256]{1,0:T(8,128)(2,1)}, u32[]{:S(2)}, u32[]{:S(2)}) collective-permute-start(bf16[1024,256]{1,0:T(8,128)(2,1)S(1)} %get-tuple-element.34), channel_id=1, source_target_pairs={{0,16},{8,24},{16,0},{24,8},{1,17},{9,25},{17,1},{25,9},{2,18},{10... | collective-permute-start | bytes 1572872 | tf_op jit(solution)/shard_map/ppermute | solution.py:345
  227.6 79.7 %collective-permute-start.2 = (bf16[1024,256]{1,0:T(8,128)(2,1)S(1)}, bf16[1024,256]{1,0:T(8,128)(2,1)}, u32[]{:S(2)}, u32[]{:S(2)}) collective-permute-start(bf16[1024,256]{1,0:T(8,128)(2,1)S(1)} %get-tuple-element.33), channel_id=1, source_target_pairs={{0,24},{8,16},{16,8},{24,0},{1,25},{9,17},{17,9},{25,1},{2,26},{10... | collective-permute-start | bytes 1572872 | tf_op jit(solution)/shard_map/ppermute | solution.py:345
  235.4 1.9 copy-start.11
  238.5 71.7 %collective-permute-start.4 = (bf16[256,1024]{1,0:T(8,128)(2,1)}, bf16[256,1024]{1,0:T(8,128)(2,1)S(1)}, u32[]{:S(2)}, u32[]{:S(2)}) collective-permute-start(bf16[256,1024]{1,0:T(8,128)(2,1)} %get-tuple-element.29), channel_id=1, source_target_pairs={{0,2},{1,3},{2,0},{3,1},{4,6},{5,7},{6,4},{7,5},{8,10},{9,11},{10,... | collective-permute-start | bytes 1572872 | tf_op jit(solution)/shard_map/ppermute | solution.py:345
  238.5 71.7 %collective-permute-start.5 = (bf16[256,1024]{1,0:T(8,128)(2,1)}, bf16[256,1024]{1,0:T(8,128)(2,1)S(1)}, u32[]{:S(2)}, u32[]{:S(2)}) collective-permute-start(bf16[256,1024]{1,0:T(8,128)(2,1)} %get-tuple-element.31), channel_id=1, source_target_pairs={{0,4},{1,5},{2,6},{3,7},{4,0},{5,1},{6,2},{7,3},{8,12},{9,13},{10,... | collective-permute-start | bytes 1572872 | tf_op jit(solution)/shard_map/ppermute | solution.py:345
  240.3 0.8 copy-start.12
  241.1 69.2 %collective-permute-start.6 = (bf16[256,1024]{1,0:T(8,128)(2,1)S(1)}, bf16[256,1024]{1,0:T(8,128)(2,1)S(1)}, u32[]{:S(2)}, u32[]{:S(2)}) collective-permute-start(bf16[256,1024]{1,0:T(8,128)(2,1)S(1)} %get-tuple-element.30), channel_id=1, source_target_pairs={{0,6},{1,7},{2,4},{3,5},{4,2},{5,3},{6,0},{7,1},{8,14},{9,15},{10,... | collective-permute-start | bytes 1572872 | tf_op jit(solution)/shard_map/ppermute | solution.py:345
Sparse Core Ops, SparseCore 0:
  11.6 117.8 all-gather.1

commit v2 on v1

v2 whole, which is shorter than its diff:
```python
import functools

import jax
import jax.numpy as jnp
from jax import lax
from jax.experimental import pallas as pl
from jax.experimental.pallas import tpu as pltpu
from jax.sharding import PartitionSpec as P

ITERS = 3
BALANCE_SMOOTHING = 0.05
SOFTMAX_HEAT = 0.1
NORM_EPSILON = 1e-06
LANES = 128
MIB = 1 << 20
F32 = jnp.float32
BF16 = jnp.bfloat16


def params(mib=60):
    return pltpu.CompilerParams(vmem_limit_bytes=mib * MIB)


def cost(flops, moved, exps=0):
    return pl.CostEstimate(flops=flops, bytes_accessed=moved, transcendentals=exps)


def normalized(block):
    wide = block.astype(F32)
    inverse = 1.0 / jnp.sqrt(jnp.sum(wide * wide, axis=1, keepdims=True) + NORM_EPSILON)
    return wide * inverse


def lane_row_sums(values):
    columns = values.shape[1]
    part = values[:, 0:LANES]
    for start in range(LANES, columns, LANES):
        part = part + values[:, start : start + LANES]
    return jnp.sum(part.T, axis=0, keepdims=True)


def split_rows(row):
    high = row.astype(BF16).astype(F32)
    middle = (row - high).astype(BF16).astype(F32)
    low = row - high - middle
    place = lax.broadcasted_iota(jnp.int32, (16, row.shape[1]), 0)
    stacked = jnp.where(place == 0, high, jnp.where(place == 1, middle, jnp.where(place == 2, low, 0.0)))
    return stacked.astype(BF16)


def total_of(refs):
    total = refs[0][...]
    for ref in refs[1:]:
        total = total + ref[...]
    return total


def own_rows_kernel(index_ref, embeddings_ref, table_ref, stage_ref):
    del index_ref
    rows, columns = embeddings_ref.shape
    unit = normalized(embeddings_ref[...]).astype(BF16).astype(F32)
    groups = columns // LANES
    for k in range(groups):
        stage_ref[pl.ds(k, rows, stride=groups), :] = unit[:, k * LANES : (k + 1) * LANES]
    table_ref[...] = stage_ref[...].reshape(rows, groups, LANES).astype(BF16)


def own_rows(embeddings, index, share):
    columns = embeddings.shape[1]
    groups = columns // LANES
    return pl.pallas_call(
        own_rows_kernel,
        grid_spec=pltpu.PrefetchScalarGridSpec(
            num_scalar_prefetch=1,
            grid=(1,),
            in_specs=[pl.BlockSpec((share, columns), lambda i, index: (index[0], 0))],
            out_specs=pl.BlockSpec((share, groups, LANES), lambda i, index: (0, 0, 0)),
            scratch_shapes=[pltpu.VMEM((share * groups, LANES), F32)],
        ),
        out_shape=jax.ShapeDtypeStruct((share, groups, LANES), BF16),
        compiler_params=params(),
        name="own_rows",
    )(index, embeddings)


def scores_kernel(embeddings_ref, prototypes_ref, unit_ref, wnorm_ref, scores_ref, expo_ref, zsum_ref, column_ref):
    step = pl.program_id(0)

    @pl.when(step == 0)
    def _():
        wnorm_ref[...] = normalized(prototypes_ref[...]).astype(BF16)

    unit = normalized(embeddings_ref[...]).astype(BF16)
    unit_ref[...] = unit
    scores = lax.dot_general(unit, wnorm_ref[...], (((1,), (1,)), ((), ())), preferred_element_type=F32)
    scores_ref[...] = scores
    soft = jnp.exp(scores * (1.0 / SOFTMAX_HEAT))
    zsum_ref[...] = lane_row_sums(soft)
    expo = soft * soft
    expo_ref[...] = expo.astype(BF16)
    sums = jnp.sum(expo, axis=0, keepdims=True)

    @pl.when(step == 0)
    def _():
        column_ref[...] = sums

    @pl.when(step > 0)
    def _():
        column_ref[...] += sums


def scores_of(embeddings, prototypes, share):
    rows, columns = embeddings.shape
    protos = prototypes.shape[0]
    return pl.pallas_call(
        scores_kernel,
        grid=(rows // share,),
        in_specs=[
            pl.BlockSpec((share, columns), lambda i: (i, 0)),
            pl.BlockSpec((protos, columns), lambda i: (0, 0), pipeline_mode=pl.Buffered(1)),
        ],
        out_specs=[
            pl.BlockSpec((share, columns), lambda i: (i, 0)),
            pl.BlockSpec((protos, columns), lambda i: (0, 0)),
            pl.BlockSpec((share, protos), lambda i: (i, 0)),
            pl.BlockSpec((share, protos), lambda i: (i, 0)),
            pl.BlockSpec((None, None, 1, share), lambda i: (i % 2, i // 2, 0, 0)),
            pl.BlockSpec((1, protos), lambda i: (0, 0)),
        ],
        out_shape=[
            jax.ShapeDtypeStruct((rows, columns), BF16),
            jax.ShapeDtypeStruct((protos, columns), BF16),
            jax.ShapeDtypeStruct((rows, protos), F32),
            jax.ShapeDtypeStruct((rows, protos), BF16),
            jax.ShapeDtypeStruct((2, rows // share // 2, 1, share), F32),
            jax.ShapeDtypeStruct((1, protos), F32),
        ],
        compiler_params=params(),
        cost_estimate=cost(2 * rows * columns * protos, 22 * MIB, rows * protos),
        name="scores",
    )(embeddings, prototypes)


def row_kernel(count, *refs):
    *column_refs, expo_ref, row_ref = refs
    scale = 1.0 / (count * total_of(column_refs))
    sums = lax.dot_general(
        split_rows(scale), expo_ref[...], (((1,), (1,)), ((), ())), preferred_element_type=F32
    )
    row_ref[...] = jnp.sum(sums, axis=0, keepdims=True)


def row_pass(columns, expo, count):
    rows, protos = expo.shape
    block = rows // 4
    return pl.pallas_call(
        functools.partial(row_kernel, count),
        grid=(rows // block,),
        in_specs=[pl.BlockSpec((1, protos), lambda i: (0, 0)) for _ in columns]
        + [pl.BlockSpec((block, protos), lambda i: (i, 0))],
        out_specs=pl.BlockSpec((1, block), lambda i: (0, i)),
        out_shape=jax.ShapeDtypeStruct((1, rows), F32),
        compiler_params=params(),
        cost_estimate=cost(2 * rows * protos, 4 * MIB),
        name="row_pass",
    )(*columns, expo)


def column_kernel(count, *refs):
    *row_refs, expo_ref, column_ref = refs
    step = pl.program_id(0)
    scale = 1.0 / (count * total_of(row_refs))
    sums = lax.dot_general(
        split_rows(scale), expo_ref[...], (((1,), (0,)), ((), ())), preferred_element_type=F32
    )
    sums = jnp.sum(sums, axis=0, keepdims=True)

    @pl.when(step == 0)
    def _():
        column_ref[...] = sums

    @pl.when(step > 0)
    def _():
        column_ref[...] += sums


def column_pass(row_totals, expo, count):
    rows, protos = expo.shape
    block = rows // 4
    return pl.pallas_call(
        functools.partial(column_kernel, count),
        grid=(rows // block,),
        in_specs=[pl.BlockSpec((1, block), lambda i: (0, i)) for _ in row_totals]
        + [pl.BlockSpec((block, protos), lambda i: (i, 0))],
        out_specs=pl.BlockSpec((1, protos), lambda i: (0, 0)),
        out_shape=jax.ShapeDtypeStruct((1, protos), F32),
        compiler_params=params(),
        cost_estimate=cost(2 * rows * protos, 4 * MIB),
        name="column_pass",
    )(*row_totals, expo)


CHUNK = 256


def partner_kernel(first_ref, second_ref, table_ref, wnorm_ref, first_expo_ref, second_expo_ref, *stages):
    step = pl.program_id(0)
    groups = table_ref.shape[1]
    rows = first_expo_ref.shape[0]
    wnorm = wnorm_ref[...]
    chunks = [
        (which_ref, out_ref, start)
        for start in range(0, rows, CHUNK)
        for which_ref, out_ref in ((first_ref, first_expo_ref), (second_ref, second_expo_ref))
    ]
    for (which_ref, out_ref, start), stage_ref in zip(chunks, stages):
        for row in range(CHUNK):
            place = which_ref[step * rows + start + row]
            stage_ref[row * groups : (row + 1) * groups, :] = table_ref[place].astype(F32)
        unit = jnp.concatenate(
            [stage_ref[pl.ds(k, CHUNK, stride=groups), :].astype(BF16) for k in range(groups)], axis=1
        )
        scores = lax.dot_general(unit, wnorm, (((1,), (1,)), ((), ())), preferred_element_type=F32)
        soft = jnp.exp(scores * (1.0 / SOFTMAX_HEAT))
        out_ref[start : start + CHUNK, :] = (soft * soft).astype(out_ref.dtype)


def partner_pass(first, second, table, wnorm):
    rows = first.shape[0]
    protos, columns = wnorm.shape
    groups = columns // LANES
    block = 2 * CHUNK
    return pl.pallas_call(
        partner_kernel,
        grid_spec=pltpu.PrefetchScalarGridSpec(
            num_scalar_prefetch=2,
            grid=(rows // block,),
            in_specs=[
                pl.BlockSpec(table.shape, lambda i, *_: (0, 0, 0), pipeline_mode=pl.Buffered(1)),
                pl.BlockSpec((protos, columns), lambda i, *_: (0, 0), pipeline_mode=pl.Buffered(1)),
            ],
            out_specs=[
                pl.BlockSpec((block, protos), lambda i, *_: (i, 0)),
                pl.BlockSpec((block, protos), lambda i, *_: (i, 0)),
            ],
            scratch_shapes=[pltpu.VMEM((CHUNK * groups, LANES), F32)] * 4,
        ),
        out_shape=[jax.ShapeDtypeStruct((rows, protos), BF16)] * 2,
        compiler_params=params(),
        cost_estimate=cost(4 * rows * columns * protos, 28 * MIB, 2 * rows * protos),
        name="partner_scores",
    )(first, second, table, wnorm)


def partner_row_kernel(count, *refs):
    *column_refs, zsum_ref, first_ref, second_ref, row_ref = refs
    scale = 1.0 / (count * total_of(column_refs))
    row_ref[...] = jnp.concatenate(
        [
            lane_row_sums(first_ref[...].astype(F32) * scale),
            lane_row_sums(second_ref[...].astype(F32) * scale),
            zsum_ref[...],
        ],
        axis=0,
    )


def partner_row_pass(columns, zsum, first, second, count):
    rows, protos = first.shape
    share = zsum.shape[-1]
    return pl.pallas_call(
        functools.partial(partner_row_kernel, count),
        grid=(rows // share,),
        in_specs=[pl.BlockSpec((1, protos), lambda i: (0, 0)) for _ in columns]
        + [
            pl.BlockSpec((None, None, 1, share), lambda i: (i % 2, i // 2, 0, 0)),
            pl.BlockSpec((share, protos), lambda i: (i, 0)),
            pl.BlockSpec((share, protos), lambda i: (i, 0)),
        ],
        out_specs=pl.BlockSpec((None, None, 3, share), lambda i: (i % 2, i // 2, 0, 0)),
        out_shape=jax.ShapeDtypeStruct((2, rows // share // 2, 3, share), F32),
        compiler_params=params(),
        cost_estimate=cost(4 * rows * protos, 8 * MIB),
        name="partner_row_pass",
    )(*columns, zsum, first, second)


def gradient_kernel(count, total, heat_scale, proto_size, parts, core_ref, *refs):
    del core_ref
    column_refs, row_refs = refs[: parts[0]], refs[parts[0] : parts[0] + parts[1]]
    first_ref, second_ref, scores_ref, wnorm_ref, gunit_ref, dscore_ref, loss_ref = refs[parts[0] + parts[1] :]
    step = pl.program_id(0)
    scale = 1.0 / (count * total_of(column_refs))
    totals = total_of(row_refs)
    share = totals.shape[-1]
    place = lax.broadcasted_iota(jnp.int32, (8, share), 0)
    loss = jnp.zeros((), F32)
    for group in range(totals.shape[0]):
        row_totals, zsum = totals[group, 0:2], totals[group, 2:3]
        weights = total * (1.0 / (total * row_totals))
        code_totals = 0.5 * jnp.sum(weights * row_totals, axis=0, keepdims=True)
        log_part = jnp.sum(code_totals * jnp.log(zsum)) * (1.0 / proto_size)
        stacked = jnp.where(
            place == 0,
            weights[0:1],
            jnp.where(place == 1, weights[1:2], jnp.where(place == 2, code_totals / zsum, 0.0)),
        ).T
        first = (stacked[:, 0:1] * first_ref[group].astype(F32) * scale).astype(BF16).astype(F32)
        second = (stacked[:, 1:2] * second_ref[group].astype(F32) * scale).astype(BF16).astype(F32)
        targets = 0.5 * (first + second)
        heated = scores_ref[group] * (1.0 / SOFTMAX_HEAT)
        loss = loss + (log_part - jnp.sum(targets * heated))
        dscore = ((jnp.exp(heated) * stacked[:, 2:3] - targets) * heat_scale).astype(BF16)
        dscore_ref[group] = dscore
        gunit = jnp.dot(dscore, wnorm_ref[...], preferred_element_type=F32)
        gunit_ref[group] = gunit.astype(gunit_ref.dtype)

    @pl.when(step == 0)
    def _():
        loss_ref[...] = jnp.full(loss_ref.shape, loss, F32)

    @pl.when(step > 0)
    def _():
        loss_ref[...] += loss


def gradients(core, columns, row_totals, first, second, scores, wnorm, count, total, proto_size, dtype):
    rows, protos = first.shape
    width = wnorm.shape[1]
    heat_scale = count / (32.0 * SOFTMAX_HEAT)
    _, places, _, share = row_totals[0].shape
    group = 2
    by_core = pl.BlockSpec((group, None, share, protos), lambda i, core: (i, core[0], 0, 0))
    first, second, scores = [value.reshape(places, 2, share, protos) for value in (first, second, scores)]
    return pl.pallas_call(
        functools.partial(
            gradient_kernel, count, total, heat_scale, proto_size, (len(columns), len(row_totals))
        ),
        grid_spec=pltpu.PrefetchScalarGridSpec(
            num_scalar_prefetch=1,
            grid=(places // group,),
            in_specs=[pl.BlockSpec((1, protos), lambda i, core: (0, 0)) for _ in columns]
            + [pl.BlockSpec((None, group, 3, share), lambda i, core: (core[0], i, 0, 0)) for _ in row_totals]
            + [
                by_core,
                by_core,
                by_core,
                pl.BlockSpec((protos, width), lambda i, core: (0, 0), pipeline_mode=pl.Buffered(1)),
            ],
            out_specs=[
                pl.BlockSpec((group, share, width), lambda i, core: (i, 0, 0)),
                pl.BlockSpec((group, share, protos), lambda i, core: (i, 0, 0)),
                pl.BlockSpec((1, LANES), lambda i, core: (0, 0)),
            ],
        ),
        out_shape=[
            jax.ShapeDtypeStruct((places, share, width), dtype),
            jax.ShapeDtypeStruct((places, share, protos), BF16),
            jax.ShapeDtypeStruct((1, LANES), F32),
        ],
        compiler_params=params(),
        cost_estimate=cost(rows * width * protos, 16 * MIB, rows * protos // 2),
        name="gradients",
    )(core, *columns, *row_totals, first, second, scores, wnorm)


def combine_kernel(place_ref, kept_ref, received_ref, own_ref, sent_ref):
    del place_ref
    total = kept_ref[...] + received_ref[...].astype(F32)
    sent_ref[...] = total.astype(BF16)
    own_ref[...] = total


def combine(place, kept, received):
    places, share, width = kept.shape
    last = places - 1
    at = pl.BlockSpec((None, share, width), lambda i, place: (place[0] ^ (last - i), 0, 0))
    return pl.pallas_call(
        combine_kernel,
        grid_spec=pltpu.PrefetchScalarGridSpec(
            num_scalar_prefetch=1,
            grid=(places,),
            in_specs=[at, at],
            out_specs=[
                pl.BlockSpec((share, width), lambda i, place: (0, 0)),
                pl.BlockSpec((None, share, width), lambda i, place: (last - i, 0, 0)),
            ],
        ),
        out_shape=[jax.ShapeDtypeStruct((share, width), F32), jax.ShapeDtypeStruct(kept.shape, BF16)],
        compiler_params=params(),
        cost_estimate=cost(places * share * width, 9 * MIB),
        name="combine",
    )(place, kept, received)


def proto_gradient_kernel(index_ref, own_dscore_ref, other_dscore_ref, own_unit_ref, other_unit_ref, own_ref, sent_ref):
    del index_ref
    rows = own_dscore_ref.shape[0]
    part = own_unit_ref.shape[-1]
    both = (((0,), (0,)), ((), ()))
    total = lax.dot_general(
        own_dscore_ref[...], own_unit_ref[...].reshape(rows, part), both, preferred_element_type=F32
    ) + lax.dot_general(
        other_dscore_ref[...], other_unit_ref[...].reshape(rows, part), both, preferred_element_type=F32
    )
    sent_ref[...] = total.astype(BF16)
    own_ref[...] = total


def proto_gradient(index, own_dscore, other_dscore, unit, batch_size):
    places, share, protos = own_dscore.shape
    width = unit.shape[1]
    part = width // batch_size
    rows = places * share
    last = batch_size - 1
    unit = unit.reshape(places, 2, share, width)
    dscore_at = pl.BlockSpec((rows, protos), lambda i, index: (0, 0), pipeline_mode=pl.Buffered(1))
    return pl.pallas_call(
        proto_gradient_kernel,
        grid_spec=pltpu.PrefetchScalarGridSpec(
            num_scalar_prefetch=1,
            grid=(batch_size,),
            in_specs=[
                dscore_at,
                dscore_at,
                pl.BlockSpec((places, None, share, part), lambda i, index: (0, index[1], 0, index[0] ^ (last - i))),
                pl.BlockSpec((places, None, share, part), lambda i, index: (0, 1 - index[1], 0, index[0] ^ (last - i))),
            ],
            out_specs=[
                pl.BlockSpec((protos, part), lambda i, index: (0, 0)),
                pl.BlockSpec((None, protos, part), lambda i, index: (last - i, 0, 0)),
            ],
        ),
        out_shape=[
            jax.ShapeDtypeStruct((protos, part), F32),
            jax.ShapeDtypeStruct((batch_size, protos, part), BF16),
        ],
        compiler_params=params(),
        cost_estimate=cost(4 * rows * protos * width, 12 * MIB),
        name="proto_gradient",
    )(index, own_dscore.reshape(rows, protos), other_dscore.reshape(rows, protos), unit, unit)


def embed_gradient_kernel(index_ref, embeddings_ref, own_ref, *refs):
    del index_ref
    *received_refs, out_ref = refs
    gunit = own_ref[...]
    for ref in received_refs:
        gunit = gunit + ref[...].astype(F32)
    hidden = embeddings_ref[...].astype(F32)
    inverse = 1.0 / jnp.sqrt(jnp.sum(hidden * hidden, axis=1, keepdims=True) + NORM_EPSILON)
    along = jnp.sum(hidden * gunit, axis=1, keepdims=True)
    out_ref[...] = inverse * gunit - hidden * (inverse * inverse * inverse * along)


def embed_gradient(index, embeddings, own, received):
    share, width = own.shape
    whole = pl.BlockSpec((share, width), lambda i, index: (0, 0))
    return pl.pallas_call(
        embed_gradient_kernel,
        grid_spec=pltpu.PrefetchScalarGridSpec(
            num_scalar_prefetch=1,
            grid=(1,),
            in_specs=[pl.BlockSpec((share, width), lambda i, index: (index[0], 0))] + [whole] * (1 + len(received)),
            out_specs=whole,
        ),
        out_shape=jax.ShapeDtypeStruct((share, width), F32),
        compiler_params=params(),
        cost_estimate=cost(8 * share * width, 4 * MIB),
        name="embed_gradient",
    )(index, embeddings, own, *received)


def swap(value, axis, distance):
    size = lax.axis_size(axis)
    return lax.ppermute(value, axis, [(i, i ^ distance) for i in range(size)])


def parts_of(value, axis):
    size = lax.axis_size(axis)
    if size > 8:
        return [lax.psum(value, axis)]
    return [value] + [swap(value, axis, distance) for distance in range(1, size)]


def scalar(value):
    return jnp.full((1,), value, jnp.int32)


def on_device(embeddings, prototypes, partners):
    row_count, width = embeddings.shape
    proto_count = prototypes.shape[0]
    batch_size = lax.axis_size("batch")
    proto_size = lax.axis_size("proto")
    total_rows = row_count * batch_size
    centroids = proto_count * proto_size
    share = row_count // proto_size
    places = proto_size // 2
    batch_index = lax.axis_index("batch")
    proto_index = lax.axis_index("proto")
    core = proto_index % 2
    place = proto_index // 2

    own = own_rows(embeddings, scalar(proto_index), share)
    table = lax.all_gather(own, ("batch", "proto"), axis=0, tiled=True)

    unit, wnorm, scores, expo, zsum, columns = scores_of(embeddings, prototypes, share)
    columns = parts_of(columns, "batch")
    for iteration in range(ITERS - 1):
        row_totals = parts_of(row_pass(columns, expo, centroids), "proto")
        columns = parts_of(column_pass(row_totals, expo, total_rows), "batch")

    first, second = partner_pass(partners[:, 0], partners[:, 1], table, wnorm)
    row_totals = parts_of(partner_row_pass(columns, zsum, first, second, centroids), "proto")
    shared = (columns, row_totals, first, second, scores, wnorm, centroids, total_rows, proto_size)
    other_gunit, other_dscore, other_loss = gradients(scalar(1 - core), *shared, BF16)
    received = swap(other_gunit, "proto", 1)
    kept, own_dscore, own_loss = gradients(scalar(core), *shared, F32)

    own_gunit, sent = combine(scalar(place), kept, received)
    arrived = [swap(sent[distance], "proto", 2 * distance) for distance in range(places - 1, 0, -1)]

    loss = own_loss + other_loss
    for axis in ("batch", "proto"):
        loss = functools.reduce(jnp.add, parts_of(loss, axis))
    loss = loss[0, 0] / total_rows

    grad_proto, sent = proto_gradient(jnp.stack([batch_index, core]).astype(jnp.int32), own_dscore, other_dscore, unit, batch_size)
    for distance in range(batch_size - 1, 0, -1):
        grad_proto = grad_proto + swap(sent[distance], "batch", distance).astype(F32)

    grad_embed = embed_gradient(scalar(proto_index), embeddings, own_gunit, arrived)
    return (loss, grad_proto, grad_embed)


def solution(mesh):
    return jax.shard_map(
        on_device,
        mesh=mesh,
        in_specs=(P("batch", None), P("proto", None), P("batch", None)),
        out_specs=(P(), P("proto", "batch"), P(("batch", "proto"), None)),
        check_vma=False,
    )
```

time: 324 us -> 303 us (0.935)
  blocking collectives: 149 us -> 0 us
  waiting for transfers between devices: 31 us -> 120 us
  starting transfers between devices: 6.28 us -> 53.5 us
  Pallas kernels: 74.5 us -> 101 us
  local copies, waits for them, and re-layouts: 34.7 us -> 9.37 us
  other arithmetic: 12 us -> 2.91 us
    psum x7 -> x0, blocking collectives: 149 us -> none  [the longest x1 62.5 us: on_device(): loss = lax.psum(loss[0, 0], ('batch', 'proto')) / total_rows]
    ppermute x7 -> x47, waiting for transfers between devices: 3.63 us -> 75.8 us  [swap(): return lax.ppermute(value, axis, [(i, i ^ distance) for i in range(size)])]
    ppermute x7 -> x47, starting transfers between devices: 6.24 us -> 53.4 us  [swap(): return lax.ppermute(value, axis, [(i, i ^ distance) for i in range(size)])]
    unnamed x28 -> x76, local copies, waits for them, and re-layouts: 26.2 us -> 4.73 us
    pallas_call x1 -> x4, Pallas kernels: 12.5 us -> 32.8 us  [the longest x1 14.5 us: scores_of(): pl.pallas_call(scores_kernel, grid=(rows // share,), in_specs=[pl.BlockSp...]
    all_gather x1, waiting for transfers between devices: 27.3 us -> 44.2 us  [on_device(): table = lax.all_gather(own, ('batch', 'proto'), axis=0, tiled=True)]
    pallas_call x1, Pallas kernels: 28.5 us -> 21.4 us  [partner_pass(): pl.pallas_call(partner_kernel, grid_spec=pltpu.PrefetchScalarGridSpec(num...]
    pallas_call x2, Pallas kernels: 2.18 us -> 8.23 us  [column_pass(): pl.pallas_call(functools.partial(column_kernel, count), grid=(rows // blo...]
  transfers between devices with their start and end apart: 8 -> 48, of which waited for: 3 -> 21; matrix products, arithmetic and copies ran while one was open for 3% -> 3% of each run, Pallas kernels for 6% -> 26%
where the time goes in v2:
time: 303 us; the launch traced here: 302 us
  waiting for transfers between devices  120 us (40%)
  Pallas kernels  101 us (33%)
  starting transfers between devices  53.5 us (18%)
  between operations  15.5 us (5%)
  local copies, waits for them, and re-layouts  9.37 us (3%)
    ppermute x47, waiting for transfers between devices, swap(): return lax.ppermute(value, axis, [(i, i ^ distance) for i in range(size)])  75.8 us
    ppermute x47, starting transfers between devices, swap(): return lax.ppermute(value, axis, [(i, i ^ distance) for i in range(size)])  53.4 us
    all_gather x1, waiting for transfers between devices, on_device(): table = lax.all_gather(own, ('batch', 'proto'), axis=0, tiled=True)  44.2 us
    pallas_call x1, Pallas kernels, partner_pass(): pl.pallas_call(partner_kernel, grid_spec=pltpu.PrefetchScalarGridSpec(num...  21.4 us
    pallas_call x2, Pallas kernels, gradients(): pl.pallas_call(functools.partial(gradient_kernel, count, total, heat_scal...  19.6 us
    pallas_call x1, Pallas kernels, scores_of(): pl.pallas_call(scores_kernel, grid=(rows // share,), in_specs=[pl.BlockSp...  14.5 us
    pallas_call x1, Pallas kernels, proto_gradient(): pl.pallas_call(proto_gradient_kernel, grid_spec=pltpu.PrefetchScalarGridS...  9.96 us
    pallas_call x2, Pallas kernels, row_pass(): pl.pallas_call(functools.partial(row_kernel, count), grid=(rows // block,...  8.9 us
  transfers between devices with their start and end apart: 48, of which 21 were waited for; matrix products, arithmetic and copies ran while one was open for 3% of the time, Pallas kernels for 26%

profile of v2, /device:TPU:0, one launch (start us, length us, event | category | flops | bytes accessed | tf_op | source)
XLA Modules:
  0.0 302.0 jit_solution(11350929540761703040)
XLA Ops:
  7.2 2.2 own_rows.1
  9.4 14.5 %scores.1 = (bf16[2048,1024]{1,0:T(8,128)(2,1)}, bf16[1024,1024]{1,0:T(8,128)(2,1)}, f32[2048,1024]{1,0:T(8,128)}, bf16[2048,1024]{1,0:T(8,128)(2,1)}, f32[2,4,1,256]{3,2,1,0:T(1,128)}, /*index=5*/f32[1,1024]{1,0:T(1,128)}) custom-call(bf16[2048,1024]{1,0:T(8,128)(2,1)} %embeddings_ref.5, bf16[1024,1024]{1,0:T(8,128)(2,1)} %prototypes_ref.1), custom_call_target="tpu_custom_call" | custom-call | flops 4294967296 | bytes 23068672 | tf_op jit(solution)/shard_map/scores/pallas_call | solution.py:115
  23.9 3.0 collective-permute-start
  30.7 2.4 collective-permute-done.2.refs_3_
  33.7 4.5 %row_pass.2.refs_0_ = f32[1,2048]{1,0:T(1,128)} custom-call(f32[1,1024]{1,0:T(1,128)} %get-tuple-element.21.refs_0_, f32[1,1024]{1,0:T(1,128)} %copy-done.30, f32[1,1024]{1,0:T(1,128)} %copy-done.32, f32[1,1024]{1,0:T(1,128)} %copy-done.34, bf16[2048,1024]{1,0:T(8,128)(2,1)} %get-tuple-element.22.refs_4_.refs_8_), custom_call_target="tpu_custom_call" | custom-call | flops 4194304 | bytes 4194304 | tf_op jit(solution)/shard_map/row_pass/pallas_call | solution.py:156
  40.0 2.6 collective-permute-start.6
  42.6 3.5 %collective-permute-start.8 = (f32[1,2048]{1,0:T(1,128)}, f32[1,2048]{1,0:T(1,128)S(1)}, u32[]{:S(2)}, u32[]{:S(2)}) collective-permute-start(f32[1,2048]{1,0:T(1,128)} %row_pass.2.refs_0_), channel_id=1, source_target_pairs={{0,6},{1,7},{2,4},{3,5},{4,2},{5,3},{6,0},{7,1},{8,14},{9,15},{10,... | collective-permute-start | bytes 24584 | tf_op jit(solution)/shard_map/ppermute | solution.py:476
  48.5 3.0 %collective-permute-done.9.refs_7_ = f32[1,2048]{1,0:T(1,128)S(1)} collective-permute-done((f32[1,2048]{1,0:T(1,128)}, f32[1,2048]{1,0:T(1,128)S(1)}, u32[]{:S(2)}, u32[]{:S(2)}) %collective-permute-start.9) | collective-permute-done | bytes 8224 | tf_op jit(solution)/shard_map/ppermute | solution.py:476
  52.2 4.1 %column_pass.2.refs_0_ = f32[1,1024]{1,0:T(1,128)} custom-call(f32[1,2048]{1,0:T(1,128)} %row_pass.2.refs_0_, f32[1,2048]{1,0:T(1,128)} %copy-done.18, f32[1,2048]{1,0:T(1,128)} %copy-done.20, f32[1,2048]{1,0:T(1,128)} %copy-done.22, f32[1,2048]{1,0:T(1,128)} %copy-done.24, f32[1,2048]{1,0:T(1,128)} %copy-done.25, f32[1,2048]{1,0:T(1,128)} %copy-done.27, ...), custom_call_target="tpu_custom_call" | custom-call | flops 4194304 | bytes 4194304 | tf_op jit(solution)/shard_map/column_pass/pallas_call | solution.py:190
  57.2 2.6 collective-permute-start.12
  62.5 4.5 %row_pass.3.refs_0_ = f32[1,2048]{1,0:T(1,128)} custom-call(f32[1,1024]{1,0:T(1,128)} %column_pass.2.refs_0_, f32[1,1024]{1,0:T(1,128)} %copy-done.31, f32[1,1024]{1,0:T(1,128)} %copy-done.33, f32[1,1024]{1,0:T(1,128)} %copy-done.35, bf16[2048,1024]{1,0:T(8,128)(2,1)} %get-tuple-element.22.refs_4_.refs_8_), custom_call_target="tpu_custom_call" | custom-call | flops 4194304 | bytes 4194304 | tf_op jit(solution)/shard_map/row_pass/pallas_call | solution.py:156
  68.9 2.5 collective-permute-start.17
  72.5 2.6 collective-permute-start.19
  78.2 4.1 %column_pass.3.refs_0_ = f32[1,1024]{1,0:T(1,128)} custom-call(f32[1,2048]{1,0:T(1,128)} %row_pass.3.refs_0_, f32[1,2048]{1,0:T(1,128)} %copy-done.16, f32[1,2048]{1,0:T(1,128)} %copy-done.17, f32[1,2048]{1,0:T(1,128)} %copy-done.19, f32[1,2048]{1,0:T(1,128)} %copy-done.21, f32[1,2048]{1,0:T(1,128)} %copy-done.23, f32[1,2048]{1,0:T(1,128)} %copy-done.26, ...), custom_call_target="tpu_custom_call" | custom-call | flops 4194304 | bytes 4194304 | tf_op jit(solution)/shard_map/column_pass/pallas_call | solution.py:190
  85.8 44.2 %all-gather.2.cloned.1.call-done.table_ref = bf16[8192,8,128]{2,1,0:T(8,128)(2,1)} async-done(((bf16[256,8,128]{2,1,0:T(8,128)(2,1)}), bf16[8192,8,128]{2,1,0:T(8,128)(2,1)}) %all-gather.2.cloned.1.call-update) | async-done | bytes 16777232 | tf_op jit(solution)/shard_map/all_gather | solution.py:505
  130.0 21.4 %partner_scores.1 = (bf16[2048,1024]{1,0:T(8,128)(2,1)}, bf16[2048,1024]{1,0:T(8,128)(2,1)}) custom-call(s32[2048]{0:T(1024)} %bitcast.34, s32[2048]{0:T(1024)} %bitcast.33, bf16[8192,8,128]{2,1,0:T(8,128)(2,1)} %all-gather.2.cloned.1.call-done.table_ref, bf16[1024,1024]{1,0:T(8,128)(2,1)} %get-tuple-element.24.wnorm_ref.refs_15_), custom_call_target="tpu_custom_call" | custom-call | flops 8589934592 | bytes 29360128 | tf_op jit(solution)/shard_map/partner_scores/pallas_call | solution.py:233
  152.1 7.5 %partner_row_pass.1.refs_4_ = f32[2,4,3,256]{3,2,1,0:T(4,128)} custom-call(f32[1,1024]{1,0:T(1,128)} %column_pass.3.refs_0_, f32[1,1024]{1,0:T(1,128)} %copy-done.12, f32[1,1024]{1,0:T(1,128)} %copy-done.13, f32[1,1024]{1,0:T(1,128)} %copy-done.14, f32[2,4,1,256]{3,2,1,0:T(1,128)} %get-tuple-element.23.refs_4_, ...), custom_call_target="tpu_custom_call" | custom-call | flops 8388608 | bytes 8388608 | tf_op jit(solution)/shard_map/partner_row_pass/pallas_call | solution.py:271
  171.8 9.6 %gradients.3 = (bf16[4,256,1024]{2,1,0:T(8,128)(2,1)}, bf16[4,256,1024]{2,1,0:T(8,128)(2,1)}, f32[1,128]{1,0:T(1,128)}) custom-call(s32[1]{0:T(128)} %bitcast.7.core_ref, f32[1,1024]{1,0:T(1,128)} %column_pass.3.refs_0_, f32[1,1024]{1,0:T(1,128)} %copy-done.12, f32[1,1024]{1,0:T(1,128)} %copy-done.13, f32[1,1024]{1,0:T(1,128)} %copy-done.14, ...), custom_call_target="tpu_custom_call" | custom-call | flops 2147483648 | bytes 16777216 | tf_op jit(solution)/shard_map/gradients/pallas_call | solution.py:335
  182.2 10.1 %gradients.2 = (f32[4,256,1024]{2,1,0:T(8,128)}, bf16[4,256,1024]{2,1,0:T(8,128)(2,1)}, f32[1,128]{1,0:T(1,128)}) custom-call(s32[1]{0:T(128)} %bitcast.core_ref, f32[1,1024]{1,0:T(1,128)} %column_pass.3.refs_0_, f32[1,1024]{1,0:T(1,128)} %copy-done.12, f32[1,1024]{1,0:T(1,128)} %copy-done.13, f32[1,1024]{1,0:T(1,128)} %copy-done.14, ...), custom_call_target="tpu_custom_call" | custom-call | flops 2147483648 | bytes 16777216 | tf_op jit(solution)/shard_map/gradients/pallas_call | solution.py:335
  192.2 10.0 %proto_gradient.1 = (f32[1024,256]{1,0:T(8,128)}, bf16[4,1024,256]{2,1,0:T(8,128)(2,1)}) custom-call(s32[2]{0:T(128)} %pad_add_fusion.index_ref, bf16[1024,1024]{1,0:T(8,128)(2,1)} %bitcast.37, bf16[1024,1024]{1,0:T(8,128)(2,1)} %bitcast.36, bf16[4,2,256,1024]{3,2,1,0:T(8,128)(2,1)} %bitcast.38, bf16[4,2,256,1024]{3,2,1,0:T(8,128)(2,1)} %bitcast.39), custom_call_target="tpu_custom_call" | custom-call | flops 4294967296 | bytes 12582912 | tf_op jit(solution)/shard_map/proto_gradient/pallas_call | solution.py:418
  202.2 2.5 slice_bitcast_fusion.5
  209.8 10.3 %collective-permute-done.30 = f32[1,128]{1,0:T(1,128)S(1)} collective-permute-done((f32[1,128]{1,0:T(1,128)S(1)}, f32[1,128]{1,0:T(1,128)S(1)}, u32[]{:S(2)}, u32[]{:S(2)}) %collective-permute-start.30) | collective-permute-done | bytes 544 | tf_op jit(solution)/shard_map/ppermute | solution.py:476
  223.1 3.5 %collective-permute-done.34 = f32[1,128]{1,0:T(1,128)S(1)} collective-permute-done((f32[1,128]{1,0:T(1,128)S(1)}, f32[1,128]{1,0:T(1,128)S(1)}, u32[]{:S(2)}, u32[]{:S(2)}) %collective-permute-start.34) | collective-permute-done | bytes 544 | tf_op jit(solution)/shard_map/ppermute | solution.py:476
  226.6 3.0 collective-permute-done.35
  231.8 5.0 %combine.1 = (f32[256,1024]{1,0:T(8,128)}, bf16[4,256,1024]{2,1,0:T(8,128)(2,1)}) custom-call(s32[1]{0:T(128)} %bitcast.16.place_ref, f32[4,256,1024]{2,1,0:T(8,128)} %get-tuple-element.35.kept_ref, bf16[4,256,1024]{2,1,0:T(8,128)(2,1)} %copy-done), custom_call_target="tpu_custom_call" | custom-call | flops 1048576 | bytes 9437184 | tf_op jit(solution)/shard_map/combine/pallas_call | solution.py:378
  236.9 2.3 collective-permute-start.38
  242.4 2.5 collective-permute-start.44
  244.9 2.0 collective-permute-start.46
  247.0 2.3 convert_add_fusion
  249.2 10.0 %collective-permute-done.44.refs_0_ = bf16[256,1024]{1,0:T(8,128)(2,1)S(1)} collective-permute-done((bf16[256,1024]{1,0:T(8,128)(2,1)S(1)}, bf16[256,1024]{1,0:T(8,128)(2,1)S(1)}, u32[]{:S(2)}, u32[]{:S(2)}) %collective-permute-start.44) | collective-permute-done | bytes 524320 | tf_op jit(solution)/shard_map/ppermute | solution.py:476
  259.2 30.5 %collective-permute-done.45.refs_1_ = bf16[256,1024]{1,0:T(8,128)(2,1)S(1)} collective-permute-done((bf16[256,1024]{1,0:T(8,128)(2,1)S(1)}, bf16[256,1024]{1,0:T(8,128)(2,1)S(1)}, u32[]{:S(2)}, u32[]{:S(2)}) %collective-permute-start.45) | collective-permute-done | bytes 524320 | tf_op jit(solution)/shard_map/ppermute | solution.py:476
  290.7 3.4 %embed_gradient.1 = f32[256,1024]{1,0:T(8,128)} custom-call(s32[1]{0:T(128)} %bitcast.3.index_ref, bf16[2048,1024]{1,0:T(8,128)(2,1)} %embeddings_ref.5, f32[256,1024]{1,0:T(8,128)} %get-tuple-element.37.own_ref, bf16[256,1024]{1,0:T(8,128)(2,1)} %copy-done.2, bf16[256,1024]{1,0:T(8,128)(2,1)} %copy-done.3, bf16[256,1024]{1,0:T(8,128)(2,1)} %copy-done.4), custom_call_target="tpu_custom_call" | custom-call | flops 2097152 | bytes 4194304 | tf_op jit(solution)/shard_map/embed_gradient/pallas_call | solution.py:459
  (162 shorter events, 50.6 us)
Async XLA Ops:
  7.2 122.9 %all-gather.2.cloned.1.call-start = ((), (), s32[]{:S(2)}) async-start(), calls=%async_computation | async-start | bytes 17301504 | tf_op jit(solution)/shard_map/all_gather | solution.py:505
  38.2 8.0 %collective-permute-start.4 = (f32[1,2048]{1,0:T(1,128)}, f32[1,2048]{1,0:T(1,128)S(1)}, u32[]{:S(2)}, u32[]{:S(2)}) collective-permute-start(f32[1,2048]{1,0:T(1,128)} %row_pass.2.refs_0_), channel_id=1, source_target_pairs={{0,2},{1,3},{2,0},{3,1},{4,6},{5,7},{6,4},{7,5},{8,10},{9,11},{10,... | collective-permute-start | bytes 24584 | tf_op jit(solution)/shard_map/ppermute | solution.py:476
  39.8 6.6 %collective-permute-start.5 = (f32[1,2048]{1,0:T(1,128)}, f32[1,2048]{1,0:T(1,128)S(1)}, u32[]{:S(2)}, u32[]{:S(2)}) collective-permute-start(f32[1,2048]{1,0:T(1,128)} %row_pass.2.refs_0_), channel_id=1, source_target_pairs={{0,3},{1,2},{2,1},{3,0},{4,7},{5,6},{6,5},{7,4},{8,11},{9,10},{10,... | collective-permute-start | bytes 24584 | tf_op jit(solution)/shard_map/ppermute | solution.py:476
  40.0 6.4 %collective-permute-start.6 = (f32[1,2048]{1,0:T(1,128)}, f32[1,2048]{1,0:T(1,128)S(1)}, u32[]{:S(2)}, u32[]{:S(2)}) collective-permute-start(f32[1,2048]{1,0:T(1,128)} %row_pass.2.refs_0_), channel_id=1, source_target_pairs={{0,4},{1,5},{2,6},{3,7},{4,0},{5,1},{6,2},{7,3},{8,12},{9,13},{10,... | collective-permute-start | bytes 24584 | tf_op jit(solution)/shard_map/ppermute | solution.py:476
  42.6 5.9 %collective-permute-start.8 = (f32[1,2048]{1,0:T(1,128)}, f32[1,2048]{1,0:T(1,128)S(1)}, u32[]{:S(2)}, u32[]{:S(2)}) collective-permute-start(f32[1,2048]{1,0:T(1,128)} %row_pass.2.refs_0_), channel_id=1, source_target_pairs={{0,6},{1,7},{2,4},{3,5},{4,2},{5,3},{6,0},{7,1},{8,14},{9,15},{10,... | collective-permute-start | bytes 24584 | tf_op jit(solution)/shard_map/ppermute | solution.py:476
  67.0 5.5 %collective-permute-start.14 = (f32[1,2048]{1,0:T(1,128)}, f32[1,2048]{1,0:T(1,128)S(1)}, u32[]{:S(2)}, u32[]{:S(2)}) collective-permute-start(f32[1,2048]{1,0:T(1,128)} %row_pass.3.refs_0_), channel_id=1, source_target_pairs={{0,2},{1,3},{2,0},{3,1},{4,6},{5,7},{6,4},{7,5},{8,10},{9,11},{10,... | collective-permute-start | bytes 24584 | tf_op jit(solution)/shard_map/ppermute | solution.py:476
  67.0 8.7 %collective-permute-start.15 = (f32[1,2048]{1,0:T(1,128)}, f32[1,2048]{1,0:T(1,128)S(1)}, u32[]{:S(2)}, u32[]{:S(2)}) collective-permute-start(f32[1,2048]{1,0:T(1,128)} %row_pass.3.refs_0_), channel_id=1, source_target_pairs={{0,3},{1,2},{2,1},{3,0},{4,7},{5,6},{6,5},{7,4},{8,11},{9,10},{10,... | collective-permute-start | bytes 24584 | tf_op jit(solution)/shard_map/ppermute | solution.py:476
  68.9 6.8 %collective-permute-start.16 = (f32[1,2048]{1,0:T(1,128)}, f32[1,2048]{1,0:T(1,128)S(1)}, u32[]{:S(2)}, u32[]{:S(2)}) collective-permute-start(f32[1,2048]{1,0:T(1,128)} %row_pass.3.refs_0_), channel_id=1, source_target_pairs={{0,4},{1,5},{2,6},{3,7},{4,0},{5,1},{6,2},{7,3},{8,12},{9,13},{10,... | collective-permute-start | bytes 24584 | tf_op jit(solution)/shard_map/ppermute | solution.py:476
  68.9 6.9 %collective-permute-start.17 = (f32[1,2048]{1,0:T(1,128)}, f32[1,2048]{1,0:T(1,128)S(1)}, u32[]{:S(2)}, u32[]{:S(2)}) collective-permute-start(f32[1,2048]{1,0:T(1,128)} %row_pass.3.refs_0_), channel_id=1, source_target_pairs={{0,5},{1,4},{2,7},{3,6},{4,1},{5,0},{6,3},{7,2},{8,13},{9,12},{10,... | collective-permute-start | bytes 24584 | tf_op jit(solution)/shard_map/ppermute | solution.py:476
  71.4 5.7 %collective-permute-start.18 = (f32[1,2048]{1,0:T(1,128)}, f32[1,2048]{1,0:T(1,128)S(1)}, u32[]{:S(2)}, u32[]{:S(2)}) collective-permute-start(f32[1,2048]{1,0:T(1,128)} %row_pass.3.refs_0_), channel_id=1, source_target_pairs={{0,6},{1,7},{2,4},{3,5},{4,2},{5,3},{6,0},{7,1},{8,14},{9,15},{10,... | collective-permute-start | bytes 24584 | tf_op jit(solution)/shard_map/ppermute | solution.py:476
  82.3 69.1 %collective-permute-start.20 = (f32[1,1024]{1,0:T(1,128)}, f32[1,1024]{1,0:T(1,128)S(1)}, u32[]{:S(2)}, u32[]{:S(2)}) collective-permute-start(f32[1,1024]{1,0:T(1,128)} %column_pass.3.refs_0_), channel_id=1, source_target_pairs={{0,8},{8,0},{16,24},{24,16},{1,9},{9,1},{17,25},{25,17},{2,10},{10... | collective-permute-start | bytes 12296 | tf_op jit(solution)/shard_map/ppermute | solution.py:476
  84.0 67.5 %collective-permute-start.21 = (f32[1,1024]{1,0:T(1,128)}, f32[1,1024]{1,0:T(1,128)S(1)}, u32[]{:S(2)}, u32[]{:S(2)}) collective-permute-start(f32[1,1024]{1,0:T(1,128)} %column_pass.3.refs_0_), channel_id=1, source_target_pairs={{0,16},{8,24},{16,0},{24,8},{1,17},{9,25},{17,1},{25,9},{2,18},{10... | collective-permute-start | bytes 12296 | tf_op jit(solution)/shard_map/ppermute | solution.py:476
  85.5 66.0 %collective-permute-start.22 = (f32[1,1024]{1,0:T(1,128)}, f32[1,1024]{1,0:T(1,128)S(1)}, u32[]{:S(2)}, u32[]{:S(2)}) collective-permute-start(f32[1,1024]{1,0:T(1,128)} %column_pass.3.refs_0_), channel_id=1, source_target_pairs={{0,24},{8,16},{16,8},{24,0},{1,25},{9,17},{17,9},{25,1},{2,26},{10... | collective-permute-start | bytes 12296 | tf_op jit(solution)/shard_map/ppermute | solution.py:476
  159.9 5.8 %collective-permute-start.24 = (f32[2,4,3,256]{3,2,1,0:T(4,128)}, f32[2,4,3,256]{3,2,1,0:T(4,128)S(1)}, u32[]{:S(2)}, u32[]{:S(2)}) collective-permute-start(f32[2,4,3,256]{3,2,1,0:T(4,128)} %partner_row_pass.1.refs_4_), channel_id=1, source_target_pairs={{0,2},{1,3},{2,0},{3,1},{4,6},{5,7},{6,4},{7,5},{8,10},{9,11},{10,... | collective-permute-start | bytes 73736 | tf_op jit(solution)/shard_map/ppermute | solution.py:476
  160.2 7.4 %collective-permute-start.25 = (f32[2,4,3,256]{3,2,1,0:T(4,128)}, f32[2,4,3,256]{3,2,1,0:T(4,128)S(1)}, u32[]{:S(2)}, u32[]{:S(2)}) collective-permute-start(f32[2,4,3,256]{3,2,1,0:T(4,128)} %partner_row_pass.1.refs_4_), channel_id=1, source_target_pairs={{0,3},{1,2},{2,1},{3,0},{4,7},{5,6},{6,5},{7,4},{8,11},{9,10},{10,... | collective-permute-start | bytes 73736 | tf_op jit(solution)/shard_map/ppermute | solution.py:476
  161.4 6.2 %collective-permute-start.26 = (f32[2,4,3,256]{3,2,1,0:T(4,128)}, f32[2,4,3,256]{3,2,1,0:T(4,128)S(1)}, u32[]{:S(2)}, u32[]{:S(2)}) collective-permute-start(f32[2,4,3,256]{3,2,1,0:T(4,128)} %partner_row_pass.1.refs_4_), channel_id=1, source_target_pairs={{0,4},{1,5},{2,6},{3,7},{4,0},{5,1},{6,2},{7,3},{8,12},{9,13},{10,... | collective-permute-start | bytes 73736 | tf_op jit(solution)/shard_map/ppermute | solution.py:476
  164.3 6.0 %collective-permute-start.28 = (f32[2,4,3,256]{3,2,1,0:T(4,128)}, f32[2,4,3,256]{3,2,1,0:T(4,128)S(1)}, u32[]{:S(2)}, u32[]{:S(2)}) collective-permute-start(f32[2,4,3,256]{3,2,1,0:T(4,128)} %partner_row_pass.1.refs_4_), channel_id=1, source_target_pairs={{0,6},{1,7},{2,4},{3,5},{4,2},{5,3},{6,0},{7,1},{8,14},{9,15},{10,... | collective-permute-start | bytes 73736 | tf_op jit(solution)/shard_map/ppermute | solution.py:476
  165.7 5.5 %collective-permute-start.29 = (f32[2,4,3,256]{3,2,1,0:T(4,128)}, f32[2,4,3,256]{3,2,1,0:T(4,128)S(1)}, u32[]{:S(2)}, u32[]{:S(2)}) collective-permute-start(f32[2,4,3,256]{3,2,1,0:T(4,128)} %partner_row_pass.1.refs_4_), channel_id=1, source_target_pairs={{0,7},{1,6},{2,5},{3,4},{4,3},{5,2},{6,1},{7,0},{8,15},{9,14},{10,... | collective-permute-start | bytes 73736 | tf_op jit(solution)/shard_map/ppermute | solution.py:476
  181.4 49.2 %collective-permute-start.43 = (bf16[4,256,1024]{2,1,0:T(8,128)(2,1)}, bf16[4,256,1024]{2,1,0:T(8,128)(2,1)S(1)}, u32[]{:S(2)}, u32[]{:S(2)}) collective-permute-start(bf16[4,256,1024]{2,1,0:T(8,128)(2,1)} %get-tuple-element.36), channel_id=1, source_target_pairs={{0,1},{1,0},{2,3},{3,2},{4,5},{5,4},{6,7},{7,6},{8,9},{9,8},{10,11... | collective-permute-start | bytes 6291464 | tf_op jit(solution)/shard_map/ppermute | solution.py:476
  204.7 40.1 %collective-permute-start.40 = (bf16[1024,256]{1,0:T(8,128)(2,1)}, bf16[1024,256]{1,0:T(8,128)(2,1)S(1)}, u32[]{:S(2)}, u32[]{:S(2)}) collective-permute-start(bf16[1024,256]{1,0:T(8,128)(2,1)} %get-tuple-element.42), channel_id=1, source_target_pairs={{0,24},{8,16},{16,8},{24,0},{1,25},{9,17},{17,9},{25,1},{2,26},{10... | collective-permute-start | bytes 1572872 | tf_op jit(solution)/shard_map/ppermute | solution.py:476
  206.3 13.9 %collective-permute-start.30 = (f32[1,128]{1,0:T(1,128)S(1)}, f32[1,128]{1,0:T(1,128)S(1)}, u32[]{:S(2)}, u32[]{:S(2)}) collective-permute-start(f32[1,128]{1,0:T(1,128)S(1)} %add.48), channel_id=1, source_target_pairs={{0,8},{8,0},{16,24},{24,16},{1,9},{9,1},{17,25},{25,17},{2,10},{10... | collective-permute-start | bytes 1544 | tf_op jit(solution)/shard_map/ppermute | solution.py:476
  207.8 12.8 %collective-permute-start.31 = (f32[1,128]{1,0:T(1,128)S(1)}, f32[1,128]{1,0:T(1,128)S(1)}, u32[]{:S(2)}, u32[]{:S(2)}) collective-permute-start(f32[1,128]{1,0:T(1,128)S(1)} %add.48), channel_id=1, source_target_pairs={{0,16},{8,24},{16,0},{24,8},{1,17},{9,25},{17,1},{25,9},{2,18},{10... | collective-permute-start | bytes 1544 | tf_op jit(solution)/shard_map/ppermute | solution.py:476
  208.3 13.6 %collective-permute-start.32 = (f32[1,128]{1,0:T(1,128)S(1)}, f32[1,128]{1,0:T(1,128)S(1)}, u32[]{:S(2)}, u32[]{:S(2)}) collective-permute-start(f32[1,128]{1,0:T(1,128)S(1)} %add.48), channel_id=1, source_target_pairs={{0,24},{8,16},{16,8},{24,0},{1,25},{9,17},{17,9},{25,1},{2,26},{10... | collective-permute-start | bytes 1544 | tf_op jit(solution)/shard_map/ppermute | solution.py:476
  220.1 26.8 %collective-permute-start.41 = (bf16[1024,256]{1,0:T(8,128)(2,1)}, bf16[1024,256]{1,0:T(8,128)(2,1)S(1)}, u32[]{:S(2)}, u32[]{:S(2)}) collective-permute-start(bf16[1024,256]{1,0:T(8,128)(2,1)} %get-tuple-element.44), channel_id=1, source_target_pairs={{0,16},{8,24},{16,0},{24,8},{1,17},{9,25},{17,1},{25,9},{2,18},{10... | collective-permute-start | bytes 1572872 | tf_op jit(solution)/shard_map/ppermute | solution.py:476
  220.7 26.3 %collective-permute-start.42 = (bf16[1024,256]{1,0:T(8,128)(2,1)}, bf16[1024,256]{1,0:T(8,128)(2,1)}, u32[]{:S(2)}, u32[]{:S(2)}) collective-permute-start(bf16[1024,256]{1,0:T(8,128)(2,1)} %get-tuple-element.43), channel_id=1, source_target_pairs={{0,8},{8,0},{16,24},{24,16},{1,9},{9,1},{17,25},{25,17},{2,10},{10... | collective-permute-start | bytes 1572872 | tf_op jit(solution)/shard_map/ppermute | solution.py:476
  229.6 7.3 %collective-permute-start.36 = (f32[1,128]{1,0:T(1,128)S(1)}, f32[1,128]{1,0:T(1,128)S(1)}, u32[]{:S(2)}, u32[]{:S(2)}) collective-permute-start(f32[1,128]{1,0:T(1,128)S(1)} %add_add_fusion.1), channel_id=1, source_target_pairs={{0,4},{1,5},{2,6},{3,7},{4,0},{5,1},{6,2},{7,3},{8,12},{9,13},{10,... | collective-permute-start | bytes 1544 | tf_op jit(solution)/shard_map/ppermute | solution.py:476
  230.5 8.7 %collective-permute-start.37 = (f32[1,128]{1,0:T(1,128)S(1)}, f32[1,128]{1,0:T(1,128)S(1)}, u32[]{:S(2)}, u32[]{:S(2)}) collective-permute-start(f32[1,128]{1,0:T(1,128)S(1)} %add_add_fusion.1), channel_id=1, source_target_pairs={{0,5},{1,4},{2,7},{3,6},{4,1},{5,0},{6,3},{7,2},{8,13},{9,12},{10,... | collective-permute-start | bytes 1544 | tf_op jit(solution)/shard_map/ppermute | solution.py:476
  236.9 5.5 %collective-permute-start.38 = (f32[1,128]{1,0:T(1,128)S(1)}, f32[1,128]{1,0:T(1,128)S(1)}, u32[]{:S(2)}, u32[]{:S(2)}) collective-permute-start(f32[1,128]{1,0:T(1,128)S(1)} %add_add_fusion.1), channel_id=1, source_target_pairs={{0,6},{1,7},{2,4},{3,5},{4,2},{5,3},{6,0},{7,1},{8,14},{9,15},{10,... | collective-permute-start | bytes 1544 | tf_op jit(solution)/shard_map/ppermute | solution.py:476
  239.2 5.6 %collective-permute-start.39 = (f32[1,128]{1,0:T(1,128)S(1)}, f32[1,128]{1,0:T(1,128)S(1)}, u32[]{:S(2)}, u32[]{:S(2)}) collective-permute-start(f32[1,128]{1,0:T(1,128)S(1)} %add_add_fusion.1), channel_id=1, source_target_pairs={{0,7},{1,6},{2,5},{3,4},{4,3},{5,2},{6,1},{7,0},{8,15},{9,14},{10,... | collective-permute-start | bytes 1544 | tf_op jit(solution)/shard_map/ppermute | solution.py:476
  242.4 16.8 %collective-permute-start.44 = (bf16[256,1024]{1,0:T(8,128)(2,1)S(1)}, bf16[256,1024]{1,0:T(8,128)(2,1)S(1)}, u32[]{:S(2)}, u32[]{:S(2)}) collective-permute-start(bf16[256,1024]{1,0:T(8,128)(2,1)S(1)} %get-tuple-element.41), channel_id=1, source_target_pairs={{0,6},{1,7},{2,4},{3,5},{4,2},{5,3},{6,0},{7,1},{8,14},{9,15},{10,... | collective-permute-start | bytes 1572872 | tf_op jit(solution)/shard_map/ppermute | solution.py:476
  244.9 44.8 %collective-permute-start.45 = (bf16[256,1024]{1,0:T(8,128)(2,1)S(1)}, bf16[256,1024]{1,0:T(8,128)(2,1)S(1)}, u32[]{:S(2)}, u32[]{:S(2)}) collective-permute-start(bf16[256,1024]{1,0:T(8,128)(2,1)S(1)} %get-tuple-element.40), channel_id=1, source_target_pairs={{0,4},{1,5},{2,6},{3,7},{4,0},{5,1},{6,2},{7,3},{8,12},{9,13},{10,... | collective-permute-start | bytes 1572872 | tf_op jit(solution)/shard_map/ppermute | solution.py:476
  244.9 44.8 %collective-permute-start.46 = (bf16[256,1024]{1,0:T(8,128)(2,1)S(1)}, bf16[256,1024]{1,0:T(8,128)(2,1)S(1)}, u32[]{:S(2)}, u32[]{:S(2)}) collective-permute-start(bf16[256,1024]{1,0:T(8,128)(2,1)S(1)} %get-tuple-element.39), channel_id=1, source_target_pairs={{0,2},{1,3},{2,0},{3,1},{4,6},{5,7},{6,4},{7,5},{8,10},{9,11},{10,... | collective-permute-start | bytes 1572872 | tf_op jit(solution)/shard_map/ppermute | solution.py:476
  (54 other events, 225.6 us)
Sparse Core Ops, SparseCore 0:
  11.6 118.4 all-gather.1

commit v3 on v2

--- a/solution.py
+++ b/solution.py
@@ -12,6 +12,10 @@
 SOFTMAX_HEAT = 0.1
 NORM_EPSILON = 1e-06
 LANES = 128
+CHUNK = 256
+STREAMS = 4
+OFFLOADED = 768
+OWN_BLOCK = 128
 MIB = 1 << 20
 F32 = jnp.float32
 BF16 = jnp.bfloat16
@@ -65,19 +69,19 @@
     table_ref[...] = stage_ref[...].reshape(rows, groups, LANES).astype(BF16)
 
 
-def own_rows(embeddings, index, share):
+def own_rows(embeddings, index, block, count):
     columns = embeddings.shape[1]
     groups = columns // LANES
     return pl.pallas_call(
         own_rows_kernel,
         grid_spec=pltpu.PrefetchScalarGridSpec(
             num_scalar_prefetch=1,
-            grid=(1,),
-            in_specs=[pl.BlockSpec((share, columns), lambda i, index: (index[0], 0))],
-            out_specs=pl.BlockSpec((share, groups, LANES), lambda i, index: (0, 0, 0)),
-            scratch_shapes=[pltpu.VMEM((share * groups, LANES), F32)],
+            grid=(count,),
+            in_specs=[pl.BlockSpec((block, columns), lambda i, index: (index[0] + i, 0))],
+            out_specs=pl.BlockSpec((block, groups, LANES), lambda i, index: (i, 0, 0)),
+            scratch_shapes=[pltpu.VMEM((block * groups, LANES), F32)],
         ),
-        out_shape=jax.ShapeDtypeStruct((share, groups, LANES), BF16),
+        out_shape=jax.ShapeDtypeStruct((block * count, groups, LANES), BF16),
         compiler_params=params(),
         name="own_rows",
     )(index, embeddings)
@@ -141,71 +145,96 @@
     )(embeddings, prototypes)
 
 
-def row_kernel(count, *refs):
-    *column_refs, expo_ref, row_ref = refs
-    scale = 1.0 / (count * total_of(column_refs))
-    sums = lax.dot_general(
-        split_rows(scale), expo_ref[...], (((1,), (1,)), ((), ())), preferred_element_type=F32
-    )
-    row_ref[...] = jnp.sum(sums, axis=0, keepdims=True)
+def row_kernel(count, parts, *refs):
+    column_refs, expo_refs, row_ref = refs[:parts], refs[parts:-1], refs[-1]
+    scale = split_rows(1.0 / (count * total_of(column_refs)))
+    block = expo_refs[0].shape[0]
+    for k, expo_ref in enumerate(expo_refs):
+        sums = lax.dot_general(scale, expo_ref[...], (((1,), (1,)), ((), ())), preferred_element_type=F32)
+        row_ref[:, k * block : (k + 1) * block] = jnp.sum(sums, axis=0, keepdims=True)
+
+
+def streams_of(shape):
+    return [pl.BlockSpec(shape, functools.partial(lambda k, i: (STREAMS * i + k, 0), k)) for k in range(STREAMS)]
 
 
 def row_pass(columns, expo, count):
     rows, protos = expo.shape
-    block = rows // 4
-    return pl.pallas_call(
-        functools.partial(row_kernel, count),
-        grid=(rows // block,),
-        in_specs=[pl.BlockSpec((1, protos), lambda i: (0, 0)) for _ in columns]
-        + [pl.BlockSpec((block, protos), lambda i: (i, 0))],
-        out_specs=pl.BlockSpec((1, block), lambda i: (0, i)),
+    block = rows // 8
+    return pl.pallas_call(
+        functools.partial(row_kernel, count, len(columns)),
+        grid=(rows // block // STREAMS,),
+        in_specs=[pl.BlockSpec((1, protos), lambda i: (0, 0)) for _ in columns] + streams_of((block, protos)),
+        out_specs=pl.BlockSpec((1, STREAMS * block), lambda i: (0, i)),
         out_shape=jax.ShapeDtypeStruct((1, rows), F32),
         compiler_params=params(),
         cost_estimate=cost(2 * rows * protos, 4 * MIB),
         name="row_pass",
-    )(*columns, expo)
-
-
-def column_kernel(count, *refs):
-    *row_refs, expo_ref, column_ref = refs
+    )(*columns, *[expo] * STREAMS)
+
+
+def column_kernel(count, parts, *refs):
+    row_refs, expo_refs, column_ref = refs[:parts], refs[parts:-1], refs[-1]
     step = pl.program_id(0)
-    scale = 1.0 / (count * total_of(row_refs))
-    sums = lax.dot_general(
-        split_rows(scale), expo_ref[...], (((1,), (0,)), ((), ())), preferred_element_type=F32
-    )
-    sums = jnp.sum(sums, axis=0, keepdims=True)
+    scale = split_rows(1.0 / (count * total_of(row_refs)))
+    block = expo_refs[0].shape[0]
+    total = None
+    for k, expo_ref in enumerate(expo_refs):
+        sums = lax.dot_general(
+            scale[:, k * block : (k + 1) * block], expo_ref[...], (((1,), (0,)), ((), ())), preferred_element_type=F32
+        )
+        total = sums if total is None else total + sums
+    total = jnp.sum(total, axis=0, keepdims=True)
 
     @pl.when(step == 0)
     def _():
-        column_ref[...] = sums
+        column_ref[...] = total
 
     @pl.when(step > 0)
     def _():
-        column_ref[...] += sums
+        column_ref[...] += total
 
 
 def column_pass(row_totals, expo, count):
     rows, protos = expo.shape
-    block = rows // 4
-    return pl.pallas_call(
-        functools.partial(column_kernel, count),
-        grid=(rows // block,),
-        in_specs=[pl.BlockSpec((1, block), lambda i: (0, i)) for _ in row_totals]
-        + [pl.BlockSpec((block, protos), lambda i: (i, 0))],
+    block = rows // 8
+    return pl.pallas_call(
+        functools.partial(column_kernel, count, len(row_totals)),
+        grid=(rows // block // STREAMS,),
+        in_specs=[pl.BlockSpec((1, STREAMS * block), lambda i: (0, i)) for _ in row_totals]
+        + streams_of((block, protos)),
         out_specs=pl.BlockSpec((1, protos), lambda i: (0, 0)),
         out_shape=jax.ShapeDtypeStruct((1, protos), F32),
         compiler_params=params(),
         cost_estimate=cost(2 * rows * protos, 4 * MIB),
         name="column_pass",
-    )(*row_totals, expo)
-
-
-CHUNK = 256
-
-
-def partner_kernel(first_ref, second_ref, table_ref, wnorm_ref, first_expo_ref, second_expo_ref, *stages):
+    )(*row_totals, *[expo] * STREAMS)
+
+
+def partner_kernel(pieces, first_ref, second_ref, places_ref, *refs):
+    piece_refs = refs[: len(pieces)]
+    wnorm_ref, first_expo_ref, second_expo_ref, table_ref, semaphores, *stages = refs[len(pieces) :]
     step = pl.program_id(0)
     groups = table_ref.shape[1]
+
+    @pl.when(step == 0)
+    def _():
+        copies, place = [], 0
+        for piece_ref, (size, count) in zip(piece_refs, pieces):
+            for k in range(count):
+                copies.append(
+                    pltpu.make_async_copy(
+                        piece_ref.at[pl.ds(k * size, size)],
+                        table_ref.at[pl.ds(places_ref[place], size)],
+                        semaphores.at[place],
+                    )
+                )
+                place += 1
+        for copy in copies:
+            copy.start()
+        for copy in copies:
+            copy.wait()
+
     rows = first_expo_ref.shape[0]
     wnorm = wnorm_ref[...]
     chunks = [
@@ -225,64 +254,69 @@
         out_ref[start : start + CHUNK, :] = (soft * soft).astype(out_ref.dtype)
 
 
-def partner_pass(first, second, table, wnorm):
+def partner_pass(first, second, pieces, wnorm, total_rows):
     rows = first.shape[0]
     protos, columns = wnorm.shape
     groups = columns // LANES
     block = 2 * CHUNK
-    return pl.pallas_call(
-        partner_kernel,
+    places = jnp.stack([place for _, _, at in pieces for place in at]).astype(jnp.int32)
+    shapes = tuple((size, len(at)) for _, size, at in pieces)
+    return pl.pallas_call(
+        functools.partial(partner_kernel, shapes),
         grid_spec=pltpu.PrefetchScalarGridSpec(
-            num_scalar_prefetch=2,
+            num_scalar_prefetch=3,
             grid=(rows // block,),
-            in_specs=[
-                pl.BlockSpec(table.shape, lambda i, *_: (0, 0, 0), pipeline_mode=pl.Buffered(1)),
-                pl.BlockSpec((protos, columns), lambda i, *_: (0, 0), pipeline_mode=pl.Buffered(1)),
-            ],
+            in_specs=[pl.BlockSpec(memory_space=pl.ANY) for _ in pieces]
+            + [pl.BlockSpec((protos, columns), lambda i, *_: (0, 0), pipeline_mode=pl.Buffered(1))],
             out_specs=[
                 pl.BlockSpec((block, protos), lambda i, *_: (i, 0)),
                 pl.BlockSpec((block, protos), lambda i, *_: (i, 0)),
             ],
-            scratch_shapes=[pltpu.VMEM((CHUNK * groups, LANES), F32)] * 4,
+            scratch_shapes=[
+                pltpu.VMEM((total_rows, groups, LANES), BF16),
+                pltpu.SemaphoreType.DMA((places.shape[0],)),
+            ]
+            + [pltpu.VMEM((CHUNK * groups, LANES), F32)] * 4,
         ),
         out_shape=[jax.ShapeDtypeStruct((rows, protos), BF16)] * 2,
         compiler_params=params(),
         cost_estimate=cost(4 * rows * columns * protos, 28 * MIB, 2 * rows * protos),
         name="partner_scores",
-    )(first, second, table, wnorm)
-
-
-def partner_row_kernel(count, *refs):
-    *column_refs, zsum_ref, first_ref, second_ref, row_ref = refs
+    )(first, second, places, *[piece for piece, _, _ in pieces], wnorm)
+
+
+def partner_row_kernel(count, parts, *refs):
+    column_refs, zsum_ref, row_ref = refs[:parts], refs[parts], refs[-1]
+    first_refs, second_refs = refs[parts + 1 : parts + 1 + STREAMS], refs[parts + 1 + STREAMS : -1]
     scale = 1.0 / (count * total_of(column_refs))
-    row_ref[...] = jnp.concatenate(
-        [
-            lane_row_sums(first_ref[...].astype(F32) * scale),
-            lane_row_sums(second_ref[...].astype(F32) * scale),
-            zsum_ref[...],
-        ],
-        axis=0,
-    )
+    for k in range(STREAMS):
+        at = (k % 2, k // 2)
+        row_ref[at] = jnp.concatenate(
+            [
+                lane_row_sums(first_refs[k][...].astype(F32) * scale),
+                lane_row_sums(second_refs[k][...].astype(F32) * scale),
+                zsum_ref[at],
+            ],
+            axis=0,
+        )
 
 
 def partner_row_pass(columns, zsum, first, second, count):
     rows, protos = first.shape
     share = zsum.shape[-1]
-    return pl.pallas_call(
-        functools.partial(partner_row_kernel, count),
-        grid=(rows // share,),
+    group = STREAMS // 2
+    return pl.pallas_call(
+        functools.partial(partner_row_kernel, count, len(columns)),
+        grid=(rows // share // STREAMS,),
         in_specs=[pl.BlockSpec((1, protos), lambda i: (0, 0)) for _ in columns]
-        + [
-            pl.BlockSpec((None, None, 1, share), lambda i: (i % 2, i // 2, 0, 0)),
-            pl.BlockSpec((share, protos), lambda i: (i, 0)),
-            pl.BlockSpec((share, protos), lambda i: (i, 0)),
-        ],
-        out_specs=pl.BlockSpec((None, None, 3, share), lambda i: (i % 2, i // 2, 0, 0)),
+        + [pl.BlockSpec((2, group, 1, share), lambda i: (0, i, 0, 0))]
+        + streams_of((share, protos)) * 2,
+        out_specs=pl.BlockSpec((2, group, 3, share), lambda i: (0, i, 0, 0)),
         out_shape=jax.ShapeDtypeStruct((2, rows // share // 2, 3, share), F32),
         compiler_params=params(),
         cost_estimate=cost(4 * rows * protos, 8 * MIB),
         name="partner_row_pass",
-    )(*columns, zsum, first, second)
+    )(*columns, zsum, *[first] * STREAMS, *[second] * STREAMS)
 
 
 def gradient_kernel(count, total, heat_scale, proto_size, parts, core_ref, *refs):
@@ -364,33 +398,34 @@
     )(core, *columns, *row_totals, first, second, scores, wnorm)
 
 
-def combine_kernel(place_ref, kept_ref, received_ref, own_ref, sent_ref):
-    del place_ref
-    total = kept_ref[...] + received_ref[...].astype(F32)
-    sent_ref[...] = total.astype(BF16)
-    own_ref[...] = total
-
-
-def combine(place, kept, received):
-    places, share, width = kept.shape
-    last = places - 1
-    at = pl.BlockSpec((None, share, width), lambda i, place: (place[0] ^ (last - i), 0, 0))
+def combine_kernel(bit_ref, own_kept_ref, own_received_ref, other_kept_ref, other_received_ref, own_ref, sent_ref):
+    del bit_ref
+    sent_ref[...] = (other_kept_ref[...] + other_received_ref[...].astype(F32)).astype(BF16)
+    own_ref[...] = own_kept_ref[...] + own_received_ref[...].astype(F32)
+
+
+def combine(bit, kept, received):
+    count, share, width = kept.shape
+    kept, received = [value.reshape(count // 2, 2, share, width) for value in (kept, received)]
+    own_at = pl.BlockSpec((None, None, share, width), lambda i, bit: (i, bit[0], 0, 0))
+    other_at = pl.BlockSpec((None, None, share, width), lambda i, bit: (i, 1 - bit[0], 0, 0))
+    out_at = pl.BlockSpec((None, share, width), lambda i, bit: (i, 0, 0))
     return pl.pallas_call(
         combine_kernel,
         grid_spec=pltpu.PrefetchScalarGridSpec(
             num_scalar_prefetch=1,
-            grid=(places,),
-            in_specs=[at, at],
-            out_specs=[
-                pl.BlockSpec((share, width), lambda i, place: (0, 0)),
-                pl.BlockSpec((None, share, width), lambda i, place: (last - i, 0, 0)),
-            ],
+            grid=(count // 2,),
+            in_specs=[own_at, own_at, other_at, other_at],
+            out_specs=[out_at, out_at],
         ),
-        out_shape=[jax.ShapeDtypeStruct((share, width), F32), jax.ShapeDtypeStruct(kept.shape, BF16)],
-        compiler_params=params(),
-        cost_estimate=cost(places * share * width, 9 * MIB),
+        out_shape=[
+            jax.ShapeDtypeStruct((count // 2, share, width), F32),
+            jax.ShapeDtypeStruct((count // 2, share, width), BF16),
+        ],
+        compiler_params=params(),
+        cost_estimate=cost(count * share * width, 9 * count * share * width),
         name="combine",
-    )(place, kept, received)
+    )(bit, kept, received, kept, received)
 
 
 def proto_gradient_kernel(index_ref, own_dscore_ref, other_dscore_ref, own_unit_ref, other_unit_ref, own_ref, sent_ref):
@@ -441,12 +476,9 @@
     )(index, own_dscore.reshape(rows, protos), other_dscore.reshape(rows, protos), unit, unit)
 
 
-def embed_gradient_kernel(index_ref, embeddings_ref, own_ref, *refs):
+def embed_gradient_kernel(index_ref, embeddings_ref, own_ref, received_ref, out_ref):
     del index_ref
-    *received_refs, out_ref = refs
-    gunit = own_ref[...]
-    for ref in received_refs:
-        gunit = gunit + ref[...].astype(F32)
+    gunit = own_ref[...] + received_ref[...].astype(F32)
     hidden = embeddings_ref[...].astype(F32)
     inverse = 1.0 / jnp.sqrt(jnp.sum(hidden * hidden, axis=1, keepdims=True) + NORM_EPSILON)
     along = jnp.sum(hidden * gunit, axis=1, keepdims=True)
@@ -461,14 +493,14 @@
         grid_spec=pltpu.PrefetchScalarGridSpec(
             num_scalar_prefetch=1,
             grid=(1,),
-            in_specs=[pl.BlockSpec((share, width), lambda i, index: (index[0], 0))] + [whole] * (1 + len(received)),
+            in_specs=[pl.BlockSpec((share, width), lambda i, index: (index[0], 0)), whole, whole],
             out_specs=whole,
         ),
         out_shape=jax.ShapeDtypeStruct((share, width), F32),
         compiler_params=params(),
         cost_estimate=cost(8 * share * width, 4 * MIB),
         name="embed_gradient",
-    )(index, embeddings, own, *received)
+    )(index, embeddings, own, received)
 
 
 def swap(value, axis, distance):
@@ -501,35 +533,62 @@
     core = proto_index % 2
     place = proto_index // 2
 
-    own = own_rows(embeddings, scalar(proto_index), share)
-    table = lax.all_gather(own, ("batch", "proto"), axis=0, tiled=True)
+    piece = OFFLOADED // proto_size
+    own = own_rows(embeddings, scalar(proto_index), piece, 1)
+    gathered = lax.all_gather(own, ("batch", "proto"), axis=0, tiled=True)
+    rest = row_count - OFFLOADED
+    half = rest // 2
+    own = own_rows(embeddings, scalar(OFFLOADED // OWN_BLOCK), OWN_BLOCK, rest // OWN_BLOCK)
+    own_half = lax.dynamic_slice_in_dim(own, core * half, half, 0)
+    arrived_rows = [swap(own_half, "batch", distance) for distance in range(1, batch_size)]
 
     unit, wnorm, scores, expo, zsum, columns = scores_of(embeddings, prototypes, share)
     columns = parts_of(columns, "batch")
     for iteration in range(ITERS - 1):
         row_totals = parts_of(row_pass(columns, expo, centroids), "proto")
         columns = parts_of(column_pass(row_totals, expo, total_rows), "batch")
-
-    first, second = partner_pass(partners[:, 0], partners[:, 1], table, wnorm)
+        if iteration == 0:
+            columns, arrived_rows = lax.optimization_barrier((columns, arrived_rows))
+            other_rows = [swap(rows, "proto", 1) for rows in arrived_rows]
+
+    pieces = [
+        (gathered, OFFLOADED, [jnp.int32(i * row_count) for i in range(batch_size)]),
+        (own, rest, [batch_index * row_count + OFFLOADED]),
+    ]
+    for distance in range(1, batch_size):
+        start = (batch_index ^ distance) * row_count + OFFLOADED
+        pieces.append((arrived_rows[distance - 1], half, [start + core * half]))
+        pieces.append((other_rows[distance - 1], half, [start + (1 - core) * half]))
+    first, second = partner_pass(partners[:, 0], partners[:, 1], pieces, wnorm, total_rows)
     row_totals = parts_of(partner_row_pass(columns, zsum, first, second, centroids), "proto")
     shared = (columns, row_totals, first, second, scores, wnorm, centroids, total_rows, proto_size)
     other_gunit, other_dscore, other_loss = gradients(scalar(1 - core), *shared, BF16)
     received = swap(other_gunit, "proto", 1)
     kept, own_dscore, own_loss = gradients(scalar(core), *shared, F32)
 
-    own_gunit, sent = combine(scalar(place), kept, received)
-    arrived = [swap(sent[distance], "proto", 2 * distance) for distance in range(places - 1, 0, -1)]
-
-    loss = own_loss + other_loss
+    bit = 0
+    while (2 << bit) <= places:
+        kept, sent = combine(scalar((place >> bit) % 2), kept, received)
+        if bit == 0:
+            sent, own_dscore, other_dscore = lax.optimization_barrier((sent, own_dscore, other_dscore))
+            received = swap(sent, "proto", 2)
+            grad_proto, proto_sent = proto_gradient(
+                jnp.stack([batch_index, core]).astype(jnp.int32), own_dscore, other_dscore, unit, batch_size
+            )
+            kept, grad_proto, proto_sent = lax.optimization_barrier((kept, grad_proto, proto_sent))
+        else:
+            received = swap(sent, "proto", 2 << bit)
+        bit += 1
+    grad_embed = embed_gradient(scalar(proto_index), embeddings, kept[0], received[0])
+
+    loss, proto_sent = lax.optimization_barrier((own_loss + other_loss, proto_sent))
     for axis in ("batch", "proto"):
         loss = functools.reduce(jnp.add, parts_of(loss, axis))
     loss = loss[0, 0] / total_rows
 
-    grad_proto, sent = proto_gradient(jnp.stack([batch_index, core]).astype(jnp.int32), own_dscore, other_dscore, unit, batch_size)
     for distance in range(batch_size - 1, 0, -1):
-        grad_proto = grad_proto + swap(sent[distance], "batch", distance).astype(F32)
-
-    grad_embed = embed_gradient(scalar(proto_index), embeddings, own_gunit, arrived)
+        grad_proto = grad_proto + swap(proto_sent[distance], "batch", distance).astype(F32)
+
     return (loss, grad_proto, grad_embed)
 
 

time: 303 us -> 330 us (1.089)
  waiting for transfers between devices: 120 us -> 139 us
  Pallas kernels: 101 us -> 106 us
    ppermute x47 -> x52, waiting for transfers between devices: 75.8 us -> 139 us  [swap(): return lax.ppermute(value, axis, [(i, i ^ distance) for i in range(size)])]
    all_gather x1, waiting for transfers between devices: 44.2 us -> 0.01 us  [on_device(): gathered = lax.all_gather(own, ('batch', 'proto'), axis=0, tiled=True)]
    pallas_call x1 -> x2, Pallas kernels: 2.21 us -> 9.54 us  [own_rows(): pl.pallas_call(own_rows_kernel, grid_spec=pltpu.PrefetchScalarGridSpec(nu...]
    pallas_call x6, Pallas kernels: 46 us -> 41.9 us  [the longest x1 22.6 us: partner_pass(): pl.pallas_call(functools.partial(partner_kernel, shapes), grid_spec=pltpu...]
    unnamed x76 -> x78, local copies, waits for them, and re-layouts: 4.73 us -> 7.11 us
    pallas_call x1 -> x2, Pallas kernels: 5.04 us -> 7.29 us  [combine(): pl.pallas_call(combine_kernel, grid_spec=pltpu.PrefetchScalarGridSpec(num...]
    ppermute x47 -> x52, starting transfers between devices: 53.4 us -> 53 us  [swap(): return lax.ppermute(value, axis, [(i, i ^ distance) for i in range(size)])]
  transfers between devices with their start and end apart: 48 -> 53, of which waited for: 21 -> 28; matrix products, arithmetic and copies ran while one was open for 3% -> 2% of each run, Pallas kernels for 26% -> 25%
where the time goes in v3:
time: 330 us; the launch traced here: 329 us
  waiting for transfers between devices  139 us (42%)
  Pallas kernels  106 us (32%)
  starting transfers between devices  53.1 us (16%)
  between operations  15.7 us (5%)
  local copies, waits for them, and re-layouts  12.3 us (4%)
    ppermute x52, waiting for transfers between devices, swap(): return lax.ppermute(value, axis, [(i, i ^ distance) for i in range(size)])  139 us
    ppermute x52, starting transfers between devices, swap(): return lax.ppermute(value, axis, [(i, i ^ distance) for i in range(size)])  53 us
    pallas_call x1, Pallas kernels, partner_pass(): pl.pallas_call(functools.partial(partner_kernel, shapes), grid_spec=pltpu...  22.6 us
    pallas_call x2, Pallas kernels, gradients(): pl.pallas_call(functools.partial(gradient_kernel, count, total, heat_scal...  19.8 us
    pallas_call x1, Pallas kernels, scores_of(): pl.pallas_call(scores_kernel, grid=(rows // share,), in_specs=[pl.BlockSp...  14.6 us
    pallas_call x1, Pallas kernels, proto_gradient(): pl.pallas_call(proto_gradient_kernel, grid_spec=pltpu.PrefetchScalarGridS...  9.94 us
    pallas_call x2, Pallas kernels, own_rows(): pl.pallas_call(own_rows_kernel, grid_spec=pltpu.PrefetchScalarGridSpec(nu...  9.54 us
    pallas_call x2, Pallas kernels, row_pass(): pl.pallas_call(functools.partial(row_kernel, count, len(columns)), grid=(...  7.63 us
  transfers between devices with their start and end apart: 53, of which 28 were waited for; matrix products, arithmetic and copies ran while one was open for 2% of the time, Pallas kernels for 25%

profile of v3, /device:TPU:0, one launch (start us, length us, event | category | flops | bytes accessed | tf_op | source)
XLA Modules:
  0.0 328.9 jit_solution(2899536288615687884)
XLA Ops:
  9.1 7.7 %own_rows.2.refs_1_ = bf16[1280,8,128]{2,1,0:T(8,128)(2,1)} custom-call(s32[1]{0:T(128)} %constant.53.clone.1.index_ref, bf16[2048,1024]{1,0:T(8,128)(2,1)} %embeddings_ref.7), custom_call_target="tpu_custom_call" | custom-call | tf_op jit(solution)/shard_map/own_rows/pallas_call | solution.py:75
  18.2 4.0 %collective-permute-start.15 = (bf16[640,8,128]{2,1,0:T(8,128)(2,1)S(1)}, bf16[640,8,128]{2,1,0:T(8,128)(2,1)S(1)}, u32[]{:S(2)}, u32[]{:S(2)}) collective-permute-start(bf16[640,8,128]{2,1,0:T(8,128)(2,1)S(1)} %constant_dynamic-slice_fusion), channel_id=1, source_target_pairs={{0,24},{8,16},{16,8},{24,0},{1,25},{9,17},{17,9},{25,1},{2,26},{10... | collective-permute-start | bytes 3932168 | tf_op jit(solution)/shard_map/ppermute | solution.py:508
  22.8 14.6 %scores.1 = (bf16[2048,1024]{1,0:T(8,128)(2,1)}, bf16[1024,1024]{1,0:T(8,128)(2,1)}, f32[2048,1024]{1,0:T(8,128)}, bf16[2048,1024]{1,0:T(8,128)(2,1)}, f32[2,4,1,256]{3,2,1,0:T(1,128)}, /*index=5*/f32[1,1024]{1,0:T(1,128)}) custom-call(bf16[2048,1024]{1,0:T(8,128)(2,1)} %embeddings_ref.7, bf16[1024,1024]{1,0:T(8,128)(2,1)} %prototypes_ref.1), custom_call_target="tpu_custom_call" | custom-call | flops 4294967296 | bytes 23068672 | tf_op jit(solution)/shard_map/scores/pallas_call | solution.py:119
  37.4 2.8 collective-permute-start.2
  40.8 45.4 %collective-permute-done.2.refs_3_ = f32[1,1024]{1,0:T(1,128)S(1)} collective-permute-done((f32[1,1024]{1,0:T(1,128)}, f32[1,1024]{1,0:T(1,128)S(1)}, u32[]{:S(2)}, u32[]{:S(2)}) %collective-permute-start.2) | collective-permute-done | bytes 4128 | tf_op jit(solution)/shard_map/ppermute | solution.py:508
  90.6 3.9 %row_pass.2.refs_0_ = f32[1,2048]{1,0:T(1,128)} custom-call(f32[1,1024]{1,0:T(1,128)} %get-tuple-element.38.refs_0_, f32[1,1024]{1,0:T(1,128)} %copy-done.34, f32[1,1024]{1,0:T(1,128)} %copy-done.33, f32[1,1024]{1,0:T(1,128)} %copy-done.32, bf16[2048,1024]{1,0:T(8,128)(2,1)} %get-tuple-element.39.refs_4_.refs_5_.refs_6_.refs_7_.refs_8_.refs_9_.refs_10_.refs_11_, ...), custom_call_target="tpu_custom_call" | custom-call | flops 4194304 | bytes 4194304 | tf_op jit(solution)/shard_map/row_pass/pallas_call | solution.py:164
  95.4 3.0 collective-permute-start.8
  111.7 3.4 %column_pass.2.refs_0_ = f32[1,1024]{1,0:T(1,128)} custom-call(f32[1,2048]{1,0:T(1,128)} %row_pass.2.refs_0_, f32[1,2048]{1,0:T(1,128)} %copy-done.28, f32[1,2048]{1,0:T(1,128)} %copy-done.27, f32[1,2048]{1,0:T(1,128)} %copy-done.26, f32[1,2048]{1,0:T(1,128)} %copy-done.25, f32[1,2048]{1,0:T(1,128)} %copy-done.24, f32[1,2048]{1,0:T(1,128)} %copy-done.23, ...), custom_call_target="tpu_custom_call" | custom-call | flops 4194304 | bytes 4194304 | tf_op jit(solution)/shard_map/column_pass/pallas_call | solution.py:201
  124.3 3.7 %row_pass.3.refs_0_ = f32[1,2048]{1,0:T(1,128)} custom-call(f32[1,1024]{1,0:T(1,128)} %column_pass.2.refs_0_, f32[1,1024]{1,0:T(1,128)} %copy-done.31, f32[1,1024]{1,0:T(1,128)} %copy-done.30, f32[1,1024]{1,0:T(1,128)} %copy-done.29, bf16[2048,1024]{1,0:T(8,128)(2,1)} %get-tuple-element.39.refs_4_.refs_5_.refs_6_.refs_7_.refs_8_.refs_9_.refs_10_.refs_11_, ...), custom_call_target="tpu_custom_call" | custom-call | flops 4194304 | bytes 4194304 | tf_op jit(solution)/shard_map/row_pass/pallas_call | solution.py:164
  128.1 2.9 collective-permute-start.22
  133.2 3.4 %collective-permute-done.21.refs_6_ = f32[1,2048]{1,0:T(1,128)S(1)} collective-permute-done((f32[1,2048]{1,0:T(1,128)}, f32[1,2048]{1,0:T(1,128)S(1)}, u32[]{:S(2)}, u32[]{:S(2)}) %collective-permute-start.21) | collective-permute-done | bytes 8224 | tf_op jit(solution)/shard_map/ppermute | solution.py:508
  138.0 3.4 %collective-permute-done.19.refs_4_ = f32[1,2048]{1,0:T(1,128)S(1)} collective-permute-done((f32[1,2048]{1,0:T(1,128)}, f32[1,2048]{1,0:T(1,128)S(1)}, u32[]{:S(2)}, u32[]{:S(2)}) %collective-permute-start.19) | collective-permute-done | bytes 8224 | tf_op jit(solution)/shard_map/ppermute | solution.py:508
  146.5 3.3 column_pass.3.refs_0_
  149.7 2.9 collective-permute-start.25
  153.3 22.6 %partner_scores.1 = (bf16[2048,1024]{1,0:T(8,128)(2,1)}, bf16[2048,1024]{1,0:T(8,128)(2,1)}) custom-call(s32[2048]{0:T(1024)} %bitcast.52, s32[2048]{0:T(1024)} %bitcast.51, s32[11]{0:T(128)} %stack.38.places_ref, bf16[3072,8,128]{2,1,0:T(8,128)(2,1)} %all-gather.2.cloned.1.call-done.refs_0_, bf16[1280,8,128]{2,1,0:T(8,128)(2,1)} %own_rows.2.refs_1_, ...), custom_call_target="tpu_custom_call" | custom-call | flops 8589934592 | bytes 29360128 | tf_op jit(solution)/shard_map/partner_scores/pallas_call | solution.py:264
  176.6 5.0 %partner_row_pass.1.refs_4_ = f32[2,4,3,256]{3,2,1,0:T(4,128)} custom-call(f32[1,1024]{1,0:T(1,128)} %column_pass.3.refs_0_, f32[1,1024]{1,0:T(1,128)} %copy-done.13, f32[1,1024]{1,0:T(1,128)} %copy-done.12, f32[1,1024]{1,0:T(1,128)} %copy-done.11, f32[2,4,1,256]{3,2,1,0:T(1,128)} %get-tuple-element.44.refs_4_, ...), custom_call_target="tpu_custom_call" | custom-call | flops 8388608 | bytes 8388608 | tf_op jit(solution)/shard_map/partner_row_pass/pallas_call | solution.py:308
  183.1 4.7 %collective-permute-start.32 = (f32[2,4,3,256]{3,2,1,0:T(4,128)}, f32[2,4,3,256]{3,2,1,0:T(4,128)S(1)}, u32[]{:S(2)}, u32[]{:S(2)}) collective-permute-start(f32[2,4,3,256]{3,2,1,0:T(4,128)} %partner_row_pass.1.refs_4_), channel_id=1, source_target_pairs={{0,4},{1,5},{2,6},{3,7},{4,0},{5,1},{6,2},{7,3},{8,12},{9,13},{10,... | collective-permute-start | bytes 73736 | tf_op jit(solution)/shard_map/ppermute | solution.py:508
  192.6 9.8 %gradients.3 = (bf16[4,256,1024]{2,1,0:T(8,128)(2,1)}, bf16[4,256,1024]{2,1,0:T(8,128)(2,1)}, f32[1,128]{1,0:T(1,128)}) custom-call(s32[1]{0:T(128)} %bitcast.14.core_ref, f32[1,1024]{1,0:T(1,128)} %column_pass.3.refs_0_, f32[1,1024]{1,0:T(1,128)} %copy-done.13, f32[1,1024]{1,0:T(1,128)} %copy-done.12, f32[1,1024]{1,0:T(1,128)} %copy-done.11, ...), custom_call_target="tpu_custom_call" | custom-call | flops 2147483648 | bytes 16777216 | tf_op jit(solution)/shard_map/gradients/pallas_call | solution.py:369
  202.5 10.0 %gradients.2 = (f32[4,256,1024]{2,1,0:T(8,128)}, bf16[4,256,1024]{2,1,0:T(8,128)(2,1)}, f32[1,128]{1,0:T(1,128)}) custom-call(s32[1]{0:T(128)} %bitcast.core_ref, f32[1,1024]{1,0:T(1,128)} %column_pass.3.refs_0_, f32[1,1024]{1,0:T(1,128)} %copy-done.13, f32[1,1024]{1,0:T(1,128)} %copy-done.12, f32[1,1024]{1,0:T(1,128)} %copy-done.11, ...), custom_call_target="tpu_custom_call" | custom-call | flops 2147483648 | bytes 16777216 | tf_op jit(solution)/shard_map/gradients/pallas_call | solution.py:369
  213.9 4.1 %combine.2 = (f32[2,256,1024]{2,1,0:T(8,128)}, bf16[2,256,1024]{2,1,0:T(8,128)(2,1)}) custom-call(s32[1]{0:T(128)} %bitcast.15.bit_ref, f32[2,2,256,1024]{3,2,1,0:T(8,128)} %bitcast.41, bf16[2,2,256,1024]{3,2,1,0:T(8,128)(2,1)} %bitcast.45, f32[2,2,256,1024]{3,2,1,0:T(8,128)} %bitcast.42, bf16[2,2,256,1024]{3,2,1,0:T(8,128)(2,1)} %bitcast.46), custom_call_target="tpu_custom_call" | custom-call | flops 1048576 | bytes 9437184 | tf_op jit(solution)/shard_map/combine/pallas_call | solution.py:413
  219.5 9.9 %proto_gradient.1 = (f32[1024,256]{1,0:T(8,128)}, bf16[4,1024,256]{2,1,0:T(8,128)(2,1)}) custom-call(s32[2]{0:T(128)} %pad_add_fusion.index_ref, bf16[1024,1024]{1,0:T(8,128)(2,1)} %bitcast.55, bf16[1024,1024]{1,0:T(8,128)(2,1)} %bitcast.54, bf16[4,2,256,1024]{3,2,1,0:T(8,128)(2,1)} %bitcast.56, bf16[4,2,256,1024]{3,2,1,0:T(8,128)(2,1)} %bitcast.57), custom_call_target="tpu_custom_call" | custom-call | flops 4294967296 | bytes 12582912 | tf_op jit(solution)/shard_map/proto_gradient/pallas_call | solution.py:453
  231.9 2.8 collective-permute-start.47
  235.4 2.8 collective-permute-start.39
  238.3 20.0 %collective-permute-done.39 = f32[1,128]{1,0:T(1,128)S(1)} collective-permute-done((f32[1,128]{1,0:T(1,128)S(1)}, f32[1,128]{1,0:T(1,128)S(1)}, u32[]{:S(2)}, u32[]{:S(2)}) %collective-permute-start.39) | collective-permute-done | bytes 544 | tf_op jit(solution)/shard_map/ppermute | solution.py:508
  265.4 4.8 %collective-permute-done.46 = f32[1,128]{1,0:T(1,128)S(1)} collective-permute-done((f32[1,128]{1,0:T(1,128)S(1)}, f32[1,128]{1,0:T(1,128)S(1)}, u32[]{:S(2)}, u32[]{:S(2)}) %collective-permute-start.46) | collective-permute-done | bytes 544 | tf_op jit(solution)/shard_map/ppermute | solution.py:508
  271.8 3.7 %collective-permute-done.45 = f32[1,128]{1,0:T(1,128)S(1)} collective-permute-done((f32[1,128]{1,0:T(1,128)S(1)}, f32[1,128]{1,0:T(1,128)S(1)}, u32[]{:S(2)}, u32[]{:S(2)}) %collective-permute-start.45) | collective-permute-done | bytes 544 | tf_op jit(solution)/shard_map/ppermute | solution.py:508
  275.5 3.9 %collective-permute-done.44 = f32[1,128]{1,0:T(1,128)S(1)} collective-permute-done((f32[1,128]{1,0:T(1,128)S(1)}, f32[1,128]{1,0:T(1,128)S(1)}, u32[]{:S(2)}, u32[]{:S(2)}) %collective-permute-start.44) | collective-permute-done | bytes 544 | tf_op jit(solution)/shard_map/ppermute | solution.py:508
  279.4 4.4 %collective-permute-done.43 = f32[1,128]{1,0:T(1,128)S(1)} collective-permute-done((f32[1,128]{1,0:T(1,128)S(1)}, f32[1,128]{1,0:T(1,128)S(1)}, u32[]{:S(2)}, u32[]{:S(2)}) %collective-permute-start.43) | collective-permute-done | bytes 544 | tf_op jit(solution)/shard_map/ppermute | solution.py:508
  283.8 3.0 collective-permute-done.42
  287.7 3.2 combine.3
  295.5 21.7 %collective-permute-done.51 = bf16[1,256,1024]{2,1,0:T(8,128)(2,1)S(1)} collective-permute-done((bf16[1,256,1024]{2,1,0:T(8,128)(2,1)}, bf16[1,256,1024]{2,1,0:T(8,128)(2,1)S(1)}, u32[]{:S(2)}, u32[]{:S(2)}) %collective-permute-start.51) | collective-permute-done | bytes 524320 | tf_op jit(solution)/shard_map/ppermute | solution.py:508
  318.0 2.9 embed_gradient.1
  (177 shorter events, 69.4 us)
Async XLA Ops:
  7.2 146.1 %all-gather.2.cloned.1.call-start = ((), (), s32[]{:S(2)}) async-start(), calls=%async_computation | async-start | bytes 6488064 | tf_op jit(solution)/shard_map/all_gather | solution.py:538
  18.2 105.4 %collective-permute-start.15 = (bf16[640,8,128]{2,1,0:T(8,128)(2,1)S(1)}, bf16[640,8,128]{2,1,0:T(8,128)(2,1)S(1)}, u32[]{:S(2)}, u32[]{:S(2)}) collective-permute-start(bf16[640,8,128]{2,1,0:T(8,128)(2,1)S(1)} %constant_dynamic-slice_fusion), channel_id=1, source_target_pairs={{0,24},{8,16},{16,8},{24,0},{1,25},{9,17},{17,9},{25,1},{2,26},{10... | collective-permute-start | bytes 3932168 | tf_op jit(solution)/shard_map/ppermute | solution.py:508
  22.2 101.5 %collective-permute-start.14 = (bf16[640,8,128]{2,1,0:T(8,128)(2,1)S(1)}, bf16[640,8,128]{2,1,0:T(8,128)(2,1)S(1)}, u32[]{:S(2)}, u32[]{:S(2)}) collective-permute-start(bf16[640,8,128]{2,1,0:T(8,128)(2,1)S(1)} %constant_dynamic-slice_fusion), channel_id=1, source_target_pairs={{0,16},{8,24},{16,0},{24,8},{1,17},{9,25},{17,1},{25,9},{2,18},{10... | collective-permute-start | bytes 3932168 | tf_op jit(solution)/shard_map/ppermute | solution.py:508
  22.7 101.0 %collective-permute-start.13 = (bf16[640,8,128]{2,1,0:T(8,128)(2,1)S(1)}, bf16[640,8,128]{2,1,0:T(8,128)(2,1)}, u32[]{:S(2)}, u32[]{:S(2)}) collective-permute-start(bf16[640,8,128]{2,1,0:T(8,128)(2,1)S(1)} %constant_dynamic-slice_fusion), channel_id=1, source_target_pairs={{0,8},{8,0},{16,24},{24,16},{1,9},{9,1},{17,25},{25,17},{2,10},{10... | collective-permute-start | bytes 3932168 | tf_op jit(solution)/shard_map/ppermute | solution.py:508
  37.4 48.8 %collective-permute-start.2 = (f32[1,1024]{1,0:T(1,128)}, f32[1,1024]{1,0:T(1,128)S(1)}, u32[]{:S(2)}, u32[]{:S(2)}) collective-permute-start(f32[1,1024]{1,0:T(1,128)} %get-tuple-element.38.refs_0_), channel_id=1, source_target_pairs={{0,24},{8,16},{16,8},{24,0},{1,25},{9,17},{17,9},{25,1},{2,26},{10... | collective-permute-start | bytes 12296 | tf_op jit(solution)/shard_map/ppermute | solution.py:508
  40.2 47.6 %collective-permute-start.1 = (f32[1,1024]{1,0:T(1,128)}, f32[1,1024]{1,0:T(1,128)S(1)}, u32[]{:S(2)}, u32[]{:S(2)}) collective-permute-start(f32[1,1024]{1,0:T(1,128)} %get-tuple-element.38.refs_0_), channel_id=1, source_target_pairs={{0,16},{8,24},{16,0},{24,8},{1,17},{9,25},{17,1},{25,9},{2,18},{10... | collective-permute-start | bytes 12296 | tf_op jit(solution)/shard_map/ppermute | solution.py:508
  94.5 5.2 %collective-permute-start.9 = (f32[1,2048]{1,0:T(1,128)}, f32[1,2048]{1,0:T(1,128)S(1)}, u32[]{:S(2)}, u32[]{:S(2)}) collective-permute-start(f32[1,2048]{1,0:T(1,128)} %row_pass.2.refs_0_), channel_id=1, source_target_pairs={{0,7},{1,6},{2,5},{3,4},{4,3},{5,2},{6,1},{7,0},{8,15},{9,14},{10,... | collective-permute-start | bytes 24584 | tf_op jit(solution)/shard_map/ppermute | solution.py:508
  95.4 5.8 %collective-permute-start.8 = (f32[1,2048]{1,0:T(1,128)}, f32[1,2048]{1,0:T(1,128)S(1)}, u32[]{:S(2)}, u32[]{:S(2)}) collective-permute-start(f32[1,2048]{1,0:T(1,128)} %row_pass.2.refs_0_), channel_id=1, source_target_pairs={{0,6},{1,7},{2,4},{3,5},{4,2},{5,3},{6,0},{7,1},{8,14},{9,15},{10,... | collective-permute-start | bytes 24584 | tf_op jit(solution)/shard_map/ppermute | solution.py:508
  99.7 4.8 %collective-permute-start.7 = (f32[1,2048]{1,0:T(1,128)}, f32[1,2048]{1,0:T(1,128)S(1)}, u32[]{:S(2)}, u32[]{:S(2)}) collective-permute-start(f32[1,2048]{1,0:T(1,128)} %row_pass.2.refs_0_), channel_id=1, source_target_pairs={{0,5},{1,4},{2,7},{3,6},{4,1},{5,0},{6,3},{7,2},{8,13},{9,12},{10,... | collective-permute-start | bytes 24584 | tf_op jit(solution)/shard_map/ppermute | solution.py:508
  101.2 5.1 %collective-permute-start.6 = (f32[1,2048]{1,0:T(1,128)}, f32[1,2048]{1,0:T(1,128)S(1)}, u32[]{:S(2)}, u32[]{:S(2)}) collective-permute-start(f32[1,2048]{1,0:T(1,128)} %row_pass.2.refs_0_), channel_id=1, source_target_pairs={{0,4},{1,5},{2,6},{3,7},{4,0},{5,1},{6,2},{7,3},{8,12},{9,13},{10,... | collective-permute-start | bytes 24584 | tf_op jit(solution)/shard_map/ppermute | solution.py:508
  115.0 4.8 %collective-permute-start.12 = (f32[1,1024]{1,0:T(1,128)}, f32[1,1024]{1,0:T(1,128)S(1)}, u32[]{:S(2)}, u32[]{:S(2)}) collective-permute-start(f32[1,1024]{1,0:T(1,128)} %column_pass.2.refs_0_), channel_id=1, source_target_pairs={{0,24},{8,16},{16,8},{24,0},{1,25},{9,17},{17,9},{25,1},{2,26},{10... | collective-permute-start | bytes 12296 | tf_op jit(solution)/shard_map/ppermute | solution.py:508
  123.7 29.1 %collective-permute-start.26 = (bf16[640,8,128]{2,1,0:T(8,128)(2,1)}, bf16[640,8,128]{2,1,0:T(8,128)(2,1)}, u32[]{:S(2)}, u32[]{:S(2)}) collective-permute-start(bf16[640,8,128]{2,1,0:T(8,128)(2,1)} %collective-permute-done.13.refs_2_), channel_id=1, source_target_pairs={{0,1},{1,0},{2,3},{3,2},{4,5},{5,4},{6,7},{7,6},{8,9},{9,8},{10,11... | collective-permute-start | bytes 3932168 | tf_op jit(solution)/shard_map/ppermute | solution.py:508
  123.8 29.6 %collective-permute-start.27 = (bf16[640,8,128]{2,1,0:T(8,128)(2,1)S(1)}, bf16[640,8,128]{2,1,0:T(8,128)(2,1)}, u32[]{:S(2)}, u32[]{:S(2)}) collective-permute-start(bf16[640,8,128]{2,1,0:T(8,128)(2,1)S(1)} %collective-permute-done.14.refs_4_), channel_id=1, source_target_pairs={{0,1},{1,0},{2,3},{3,2},{4,5},{5,4},{6,7},{7,6},{8,9},{9,8},{10,11... | collective-permute-start | bytes 3932168 | tf_op jit(solution)/shard_map/ppermute | solution.py:508
  124.2 29.1 %collective-permute-start.28 = (bf16[640,8,128]{2,1,0:T(8,128)(2,1)S(1)}, bf16[640,8,128]{2,1,0:T(8,128)(2,1)}, u32[]{:S(2)}, u32[]{:S(2)}) collective-permute-start(bf16[640,8,128]{2,1,0:T(8,128)(2,1)S(1)} %collective-permute-done.15.refs_6_), channel_id=1, source_target_pairs={{0,1},{1,0},{2,3},{3,2},{4,5},{5,4},{6,7},{7,6},{8,9},{9,8},{10,11... | collective-permute-start | bytes 3932168 | tf_op jit(solution)/shard_map/ppermute | solution.py:508
  128.1 5.2 %collective-permute-start.22 = (f32[1,2048]{1,0:T(1,128)}, f32[1,2048]{1,0:T(1,128)S(1)}, u32[]{:S(2)}, u32[]{:S(2)}) collective-permute-start(f32[1,2048]{1,0:T(1,128)} %row_pass.3.refs_0_), channel_id=1, source_target_pairs={{0,7},{1,6},{2,5},{3,4},{4,3},{5,2},{6,1},{7,0},{8,15},{9,14},{10,... | collective-permute-start | bytes 24584 | tf_op jit(solution)/shard_map/ppermute | solution.py:508
  131.0 5.7 %collective-permute-start.21 = (f32[1,2048]{1,0:T(1,128)}, f32[1,2048]{1,0:T(1,128)S(1)}, u32[]{:S(2)}, u32[]{:S(2)}) collective-permute-start(f32[1,2048]{1,0:T(1,128)} %row_pass.3.refs_0_), channel_id=1, source_target_pairs={{0,6},{1,7},{2,4},{3,5},{4,2},{5,3},{6,0},{7,1},{8,14},{9,15},{10,... | collective-permute-start | bytes 24584 | tf_op jit(solution)/shard_map/ppermute | solution.py:508
  149.7 26.2 %collective-permute-start.25 = (f32[1,1024]{1,0:T(1,128)}, f32[1,1024]{1,0:T(1,128)S(1)}, u32[]{:S(2)}, u32[]{:S(2)}) collective-permute-start(f32[1,1024]{1,0:T(1,128)} %column_pass.3.refs_0_), channel_id=1, source_target_pairs={{0,24},{8,16},{16,8},{24,0},{1,25},{9,17},{17,9},{25,1},{2,26},{10... | collective-permute-start | bytes 12296 | tf_op jit(solution)/shard_map/ppermute | solution.py:508
  152.7 23.3 %collective-permute-start.24 = (f32[1,1024]{1,0:T(1,128)}, f32[1,1024]{1,0:T(1,128)S(1)}, u32[]{:S(2)}, u32[]{:S(2)}) collective-permute-start(f32[1,1024]{1,0:T(1,128)} %column_pass.3.refs_0_), channel_id=1, source_target_pairs={{0,16},{8,24},{16,0},{24,8},{1,17},{9,25},{17,1},{25,9},{2,18},{10... | collective-permute-start | bytes 12296 | tf_op jit(solution)/shard_map/ppermute | solution.py:508
  152.8 23.2 %collective-permute-start.23 = (f32[1,1024]{1,0:T(1,128)}, f32[1,1024]{1,0:T(1,128)S(1)}, u32[]{:S(2)}, u32[]{:S(2)}) collective-permute-start(f32[1,1024]{1,0:T(1,128)} %column_pass.3.refs_0_), channel_id=1, source_target_pairs={{0,8},{8,0},{16,24},{24,16},{1,9},{9,1},{17,25},{25,17},{2,10},{10... | collective-permute-start | bytes 12296 | tf_op jit(solution)/shard_map/ppermute | solution.py:508
  181.6 6.2 %collective-permute-start.35 = (f32[2,4,3,256]{3,2,1,0:T(4,128)}, f32[2,4,3,256]{3,2,1,0:T(4,128)S(1)}, u32[]{:S(2)}, u32[]{:S(2)}) collective-permute-start(f32[2,4,3,256]{3,2,1,0:T(4,128)} %partner_row_pass.1.refs_4_), channel_id=1, source_target_pairs={{0,7},{1,6},{2,5},{3,4},{4,3},{5,2},{6,1},{7,0},{8,15},{9,14},{10,... | collective-permute-start | bytes 73736 | tf_op jit(solution)/shard_map/ppermute | solution.py:508
  181.6 6.3 %collective-permute-start.34 = (f32[2,4,3,256]{3,2,1,0:T(4,128)}, f32[2,4,3,256]{3,2,1,0:T(4,128)S(1)}, u32[]{:S(2)}, u32[]{:S(2)}) collective-permute-start(f32[2,4,3,256]{3,2,1,0:T(4,128)} %partner_row_pass.1.refs_4_), channel_id=1, source_target_pairs={{0,6},{1,7},{2,4},{3,5},{4,2},{5,3},{6,0},{7,1},{8,14},{9,15},{10,... | collective-permute-start | bytes 73736 | tf_op jit(solution)/shard_map/ppermute | solution.py:508
  182.5 7.2 %collective-permute-start.33 = (f32[2,4,3,256]{3,2,1,0:T(4,128)}, f32[2,4,3,256]{3,2,1,0:T(4,128)S(1)}, u32[]{:S(2)}, u32[]{:S(2)}) collective-permute-start(f32[2,4,3,256]{3,2,1,0:T(4,128)} %partner_row_pass.1.refs_4_), channel_id=1, source_target_pairs={{0,5},{1,4},{2,7},{3,6},{4,1},{5,0},{6,3},{7,2},{8,13},{9,12},{10,... | collective-permute-start | bytes 73736 | tf_op jit(solution)/shard_map/ppermute | solution.py:508
  183.1 7.3 %collective-permute-start.32 = (f32[2,4,3,256]{3,2,1,0:T(4,128)}, f32[2,4,3,256]{3,2,1,0:T(4,128)S(1)}, u32[]{:S(2)}, u32[]{:S(2)}) collective-permute-start(f32[2,4,3,256]{3,2,1,0:T(4,128)} %partner_row_pass.1.refs_4_), channel_id=1, source_target_pairs={{0,4},{1,5},{2,6},{3,7},{4,0},{5,1},{6,2},{7,3},{8,12},{9,13},{10,... | collective-permute-start | bytes 73736 | tf_op jit(solution)/shard_map/ppermute | solution.py:508
  202.4 10.1 %collective-permute-start.36 = (bf16[4,256,1024]{2,1,0:T(8,128)(2,1)}, bf16[4,256,1024]{2,1,0:T(8,128)(2,1)S(1)}, u32[]{:S(2)}, u32[]{:S(2)}) collective-permute-start(bf16[4,256,1024]{2,1,0:T(8,128)(2,1)} %get-tuple-element.55), channel_id=1, source_target_pairs={{0,1},{1,0},{2,3},{3,2},{4,5},{5,4},{6,7},{7,6},{8,9},{9,8},{10,11... | collective-permute-start | bytes 6291464 | tf_op jit(solution)/shard_map/ppermute | solution.py:508
  218.0 68.7 %collective-permute-start.50 = (bf16[2,256,1024]{2,1,0:T(8,128)(2,1)}, bf16[2,256,1024]{2,1,0:T(8,128)(2,1)S(1)}, u32[]{:S(2)}, u32[]{:S(2)}) collective-permute-start(bf16[2,256,1024]{2,1,0:T(8,128)(2,1)} %get-tuple-element.70), channel_id=1, source_target_pairs={{0,2},{1,3},{2,0},{3,1},{4,6},{5,7},{6,4},{7,5},{8,10},{9,11},{10,... | collective-permute-start | bytes 3145736 | tf_op jit(solution)/shard_map/ppermute | solution.py:508
  231.9 61.3 %collective-permute-start.47 = (bf16[1024,256]{1,0:T(8,128)(2,1)}, bf16[1024,256]{1,0:T(8,128)(2,1)S(1)}, u32[]{:S(2)}, u32[]{:S(2)}) collective-permute-start(bf16[1024,256]{1,0:T(8,128)(2,1)} %get-tuple-element.73), channel_id=1, source_target_pairs={{0,24},{8,16},{16,8},{24,0},{1,25},{9,17},{17,9},{25,1},{2,26},{10... | collective-permute-start | bytes 1572872 | tf_op jit(solution)/shard_map/ppermute | solution.py:508
  234.8 58.4 %collective-permute-start.49 = (bf16[1024,256]{1,0:T(8,128)(2,1)}, bf16[1024,256]{1,0:T(8,128)(2,1)S(1)}, u32[]{:S(2)}, u32[]{:S(2)}) collective-permute-start(bf16[1024,256]{1,0:T(8,128)(2,1)} %get-tuple-element.74), channel_id=1, source_target_pairs={{0,8},{8,0},{16,24},{24,16},{1,9},{9,1},{17,25},{25,17},{2,10},{10... | collective-permute-start | bytes 1572872 | tf_op jit(solution)/shard_map/ppermute | solution.py:508
  234.9 58.3 %collective-permute-start.48 = (bf16[1024,256]{1,0:T(8,128)(2,1)}, bf16[1024,256]{1,0:T(8,128)(2,1)}, u32[]{:S(2)}, u32[]{:S(2)}) collective-permute-start(bf16[1024,256]{1,0:T(8,128)(2,1)} %get-tuple-element.75), channel_id=1, source_target_pairs={{0,16},{8,24},{16,0},{24,8},{1,17},{9,25},{17,1},{25,9},{2,18},{10... | collective-permute-start | bytes 1572872 | tf_op jit(solution)/shard_map/ppermute | solution.py:508
  235.4 22.9 %collective-permute-start.39 = (f32[1,128]{1,0:T(1,128)S(1)}, f32[1,128]{1,0:T(1,128)S(1)}, u32[]{:S(2)}, u32[]{:S(2)}) collective-permute-start(f32[1,128]{1,0:T(1,128)S(1)} %add.98), channel_id=1, source_target_pairs={{0,24},{8,16},{16,8},{24,0},{1,25},{9,17},{17,9},{25,1},{2,26},{10... | collective-permute-start | bytes 1544 | tf_op jit(solution)/shard_map/ppermute | solution.py:508
  270.1 5.3 %collective-permute-start.45 = (f32[1,128]{1,0:T(1,128)S(1)}, f32[1,128]{1,0:T(1,128)S(1)}, u32[]{:S(2)}, u32[]{:S(2)}) collective-permute-start(f32[1,128]{1,0:T(1,128)S(1)} %add_add_fusion.1), channel_id=1, source_target_pairs={{0,6},{1,7},{2,4},{3,5},{4,2},{5,3},{6,0},{7,1},{8,14},{9,15},{10,... | collective-permute-start | bytes 1544 | tf_op jit(solution)/shard_map/ppermute | solution.py:508
  286.8 6.4 %collective-permute-start.40 = (f32[1,128]{1,0:T(1,128)S(1)}, f32[1,128]{1,0:T(1,128)S(1)}, u32[]{:S(2)}, u32[]{:S(2)}) collective-permute-start(f32[1,128]{1,0:T(1,128)S(1)} %add_add_fusion.1), channel_id=1, source_target_pairs={{0,1},{1,0},{2,3},{3,2},{4,5},{5,4},{6,7},{7,6},{8,9},{9,8},{10,11... | collective-permute-start | bytes 1544 | tf_op jit(solution)/shard_map/ppermute | solution.py:508
  290.9 26.3 %collective-permute-start.51 = (bf16[1,256,1024]{2,1,0:T(8,128)(2,1)}, bf16[1,256,1024]{2,1,0:T(8,128)(2,1)S(1)}, u32[]{:S(2)}, u32[]{:S(2)}) collective-permute-start(bf16[1,256,1024]{2,1,0:T(8,128)(2,1)} %get-tuple-element.72), channel_id=1, source_target_pairs={{0,4},{1,5},{2,6},{3,7},{4,0},{5,1},{6,2},{7,3},{8,12},{9,13},{10,... | collective-permute-start | bytes 1572872 | tf_op jit(solution)/shard_map/ppermute | solution.py:508
  (60 other events, 239.0 us)
Sparse Core Ops, SparseCore 0:
  11.6 104.7 all-gather.1

commit v4 on v3

--- a/solution.py
+++ b/solution.py
@@ -14,8 +14,7 @@
 LANES = 128
 CHUNK = 256
 STREAMS = 4
-OFFLOADED = 768
-OWN_BLOCK = 128
+OWN_BLOCK = 256
 MIB = 1 << 20
 F32 = jnp.float32
 BF16 = jnp.bfloat16
@@ -211,25 +210,20 @@
     )(*row_totals, *[expo] * STREAMS)
 
 
-def partner_kernel(pieces, first_ref, second_ref, places_ref, *refs):
-    piece_refs = refs[: len(pieces)]
-    wnorm_ref, first_expo_ref, second_expo_ref, table_ref, semaphores, *stages = refs[len(pieces) :]
+def partner_kernel(first_ref, second_ref, source_ref, wnorm_ref, first_expo_ref, second_expo_ref, table_ref, semaphores, *stages):
     step = pl.program_id(0)
     groups = table_ref.shape[1]
 
     @pl.when(step == 0)
     def _():
-        copies, place = [], 0
-        for piece_ref, (size, count) in zip(piece_refs, pieces):
-            for k in range(count):
-                copies.append(
-                    pltpu.make_async_copy(
-                        piece_ref.at[pl.ds(k * size, size)],
-                        table_ref.at[pl.ds(places_ref[place], size)],
-                        semaphores.at[place],
-                    )
-                )
-                place += 1
+        parts = semaphores.shape[0]
+        size = source_ref.shape[0] // parts
+        copies = [
+            pltpu.make_async_copy(
+                source_ref.at[pl.ds(k * size, size)], table_ref.at[pl.ds(k * size, size)], semaphores.at[k]
+            )
+            for k in range(parts)
+        ]
         for copy in copies:
             copy.start()
         for copy in copies:
@@ -254,27 +248,27 @@
         out_ref[start : start + CHUNK, :] = (soft * soft).astype(out_ref.dtype)
 
 
-def partner_pass(first, second, pieces, wnorm, total_rows):
+def partner_pass(first, second, table, wnorm):
     rows = first.shape[0]
     protos, columns = wnorm.shape
     groups = columns // LANES
     block = 2 * CHUNK
-    places = jnp.stack([place for _, _, at in pieces for place in at]).astype(jnp.int32)
-    shapes = tuple((size, len(at)) for _, size, at in pieces)
-    return pl.pallas_call(
-        functools.partial(partner_kernel, shapes),
+    return pl.pallas_call(
+        partner_kernel,
         grid_spec=pltpu.PrefetchScalarGridSpec(
-            num_scalar_prefetch=3,
+            num_scalar_prefetch=2,
             grid=(rows // block,),
-            in_specs=[pl.BlockSpec(memory_space=pl.ANY) for _ in pieces]
-            + [pl.BlockSpec((protos, columns), lambda i, *_: (0, 0), pipeline_mode=pl.Buffered(1))],
+            in_specs=[
+                pl.BlockSpec(memory_space=pl.ANY),
+                pl.BlockSpec((protos, columns), lambda i, *_: (0, 0), pipeline_mode=pl.Buffered(1)),
+            ],
             out_specs=[
                 pl.BlockSpec((block, protos), lambda i, *_: (i, 0)),
                 pl.BlockSpec((block, protos), lambda i, *_: (i, 0)),
             ],
             scratch_shapes=[
-                pltpu.VMEM((total_rows, groups, LANES), BF16),
-                pltpu.SemaphoreType.DMA((places.shape[0],)),
+                pltpu.VMEM(table.shape, BF16),
+                pltpu.SemaphoreType.DMA((STREAMS,)),
             ]
             + [pltpu.VMEM((CHUNK * groups, LANES), F32)] * 4,
         ),
@@ -282,7 +276,7 @@
         compiler_params=params(),
         cost_estimate=cost(4 * rows * columns * protos, 28 * MIB, 2 * rows * protos),
         name="partner_scores",
-    )(first, second, places, *[piece for piece, _, _ in pieces], wnorm)
+    )(first, second, table, wnorm)
 
 
 def partner_row_kernel(count, parts, *refs):
@@ -510,9 +504,13 @@
 
 def parts_of(value, axis):
     size = lax.axis_size(axis)
-    if size > 8:
+    if size > 4:
         return [lax.psum(value, axis)]
     return [value] + [swap(value, axis, distance) for distance in range(1, size)]
+
+
+def proto_parts_of(value):
+    return parts_of(value + swap(value, "core", 1), "place")
 
 
 def scalar(value):
@@ -523,67 +521,51 @@
     row_count, width = embeddings.shape
     proto_count = prototypes.shape[0]
     batch_size = lax.axis_size("batch")
-    proto_size = lax.axis_size("proto")
+    places = lax.axis_size("place")
+    proto_size = 2 * places
     total_rows = row_count * batch_size
     centroids = proto_count * proto_size
     share = row_count // proto_size
-    places = proto_size // 2
     batch_index = lax.axis_index("batch")
-    proto_index = lax.axis_index("proto")
-    core = proto_index % 2
-    place = proto_index // 2
-
-    piece = OFFLOADED // proto_size
-    own = own_rows(embeddings, scalar(proto_index), piece, 1)
-    gathered = lax.all_gather(own, ("batch", "proto"), axis=0, tiled=True)
-    rest = row_count - OFFLOADED
-    half = rest // 2
-    own = own_rows(embeddings, scalar(OFFLOADED // OWN_BLOCK), OWN_BLOCK, rest // OWN_BLOCK)
-    own_half = lax.dynamic_slice_in_dim(own, core * half, half, 0)
-    arrived_rows = [swap(own_half, "batch", distance) for distance in range(1, batch_size)]
+    place = lax.axis_index("place")
+    core = lax.axis_index("core")
+    proto_index = 2 * place + core
+
+    half = row_count // 2
+    own = own_rows(embeddings, scalar(core * (half // OWN_BLOCK)), OWN_BLOCK, half // OWN_BLOCK)
+    table = lax.all_gather(own, ("batch", "core"), axis=0, tiled=True)
 
     unit, wnorm, scores, expo, zsum, columns = scores_of(embeddings, prototypes, share)
     columns = parts_of(columns, "batch")
     for iteration in range(ITERS - 1):
-        row_totals = parts_of(row_pass(columns, expo, centroids), "proto")
+        row_totals = proto_parts_of(row_pass(columns, expo, centroids))
         columns = parts_of(column_pass(row_totals, expo, total_rows), "batch")
-        if iteration == 0:
-            columns, arrived_rows = lax.optimization_barrier((columns, arrived_rows))
-            other_rows = [swap(rows, "proto", 1) for rows in arrived_rows]
-
-    pieces = [
-        (gathered, OFFLOADED, [jnp.int32(i * row_count) for i in range(batch_size)]),
-        (own, rest, [batch_index * row_count + OFFLOADED]),
-    ]
-    for distance in range(1, batch_size):
-        start = (batch_index ^ distance) * row_count + OFFLOADED
-        pieces.append((arrived_rows[distance - 1], half, [start + core * half]))
-        pieces.append((other_rows[distance - 1], half, [start + (1 - core) * half]))
-    first, second = partner_pass(partners[:, 0], partners[:, 1], pieces, wnorm, total_rows)
-    row_totals = parts_of(partner_row_pass(columns, zsum, first, second, centroids), "proto")
+
+    first, second = partner_pass(partners[:, 0], partners[:, 1], table, wnorm)
+    row_totals = proto_parts_of(partner_row_pass(columns, zsum, first, second, centroids))
     shared = (columns, row_totals, first, second, scores, wnorm, centroids, total_rows, proto_size)
     other_gunit, other_dscore, other_loss = gradients(scalar(1 - core), *shared, BF16)
-    received = swap(other_gunit, "proto", 1)
+    received = swap(other_gunit, "core", 1)
     kept, own_dscore, own_loss = gradients(scalar(core), *shared, F32)
+    loss = functools.reduce(jnp.add, parts_of(own_loss + other_loss, "batch"))
 
     bit = 0
-    while (2 << bit) <= places:
+    while (1 << bit) < places:
         kept, sent = combine(scalar((place >> bit) % 2), kept, received)
         if bit == 0:
-            sent, own_dscore, other_dscore = lax.optimization_barrier((sent, own_dscore, other_dscore))
-            received = swap(sent, "proto", 2)
+            sent, own_dscore, other_dscore, loss = lax.optimization_barrier((sent, own_dscore, other_dscore, loss))
+            received = swap(sent, "place", 1)
             grad_proto, proto_sent = proto_gradient(
                 jnp.stack([batch_index, core]).astype(jnp.int32), own_dscore, other_dscore, unit, batch_size
             )
             kept, grad_proto, proto_sent = lax.optimization_barrier((kept, grad_proto, proto_sent))
+            loss = loss + swap(loss, "core", 1)
         else:
-            received = swap(sent, "proto", 2 << bit)
+            sent, loss = lax.optimization_barrier((sent, loss))
+            received = swap(sent, "place", 1 << bit)
+        loss = loss + swap(loss, "place", 1 << bit)
         bit += 1
     grad_embed = embed_gradient(scalar(proto_index), embeddings, kept[0], received[0])
-
-    loss, proto_sent = lax.optimization_barrier((own_loss + other_loss, proto_sent))
-    for axis in ("batch", "proto"):
-        loss = functools.reduce(jnp.add, parts_of(loss, axis))
     loss = loss[0, 0] / total_rows
 
     for distance in range(batch_size - 1, 0, -1):
@@ -593,10 +575,13 @@
 
 
 def solution(mesh):
+    batch_size, proto_size = mesh.shape["batch"], mesh.shape["proto"]
+    devices = mesh.devices.reshape(batch_size, proto_size // 2, 2)
+    proto = ("place", "core")
     return jax.shard_map(
         on_device,
-        mesh=mesh,
-        in_specs=(P("batch", None), P("proto", None), P("batch", None)),
-        out_specs=(P(), P("proto", "batch"), P(("batch", "proto"), None)),
+        mesh=jax.sharding.Mesh(devices, ("batch", "place", "core")),
+        in_specs=(P("batch", None), P(proto, None), P("batch", None)),
+        out_specs=(P(), P(proto, "batch"), P(("batch", "place", "core"), None)),
         check_vma=False,
     )

time: 330 us -> 243 us (0.74)
  waiting for transfers between devices: 139 us -> 73.6 us
  starting transfers between devices: 53.1 us -> 37.1 us
  Pallas kernels: 106 us -> 100 us
    ppermute x52 -> x33, waiting for transfers between devices: 139 us -> 49.8 us  [swap(): return lax.ppermute(value, axis, [(i, i ^ distance) for i in range(size)])]
    all_gather x1, waiting for transfers between devices: 0.01 us -> 23.7 us  [on_device(): table = lax.all_gather(own, ('batch', 'core'), axis=0, tiled=True)]
    ppermute x52 -> x33, starting transfers between devices: 53 us -> 37.1 us  [swap(): return lax.ppermute(value, axis, [(i, i ^ distance) for i in range(size)])]
    pallas_call x2 -> x1, Pallas kernels: 9.54 us -> 4.48 us  [own_rows(): pl.pallas_call(own_rows_kernel, grid_spec=pltpu.PrefetchScalarGridSpec(nu...]
    unnamed x78 -> x54, local copies, waits for them, and re-layouts: 7.11 us -> 6.77 us
  transfers between devices with their start and end apart: 53 -> 34, of which waited for: 28 -> 23; matrix products, arithmetic and copies ran while one was open for 2% -> 3% of each run, Pallas kernels for 25% -> 31%
where the time goes in v4:
time: 243 us; the launch traced here: 242 us
  Pallas kernels  100 us (41%)
  waiting for transfers between devices  73.6 us (30%)
  starting transfers between devices  37.1 us (15%)
  between operations  15.5 us (6%)
  local copies, waits for them, and re-layouts  9.93 us (4%)
  other arithmetic  5.66 us (2%)
    ppermute x33, waiting for transfers between devices, swap(): return lax.ppermute(value, axis, [(i, i ^ distance) for i in range(size)])  49.8 us
    ppermute x33, starting transfers between devices, swap(): return lax.ppermute(value, axis, [(i, i ^ distance) for i in range(size)])  37.1 us
    all_gather x1, waiting for transfers between devices, on_device(): table = lax.all_gather(own, ('batch', 'core'), axis=0, tiled=True)  23.7 us
    pallas_call x1, Pallas kernels, partner_pass(): pl.pallas_call(partner_kernel, grid_spec=pltpu.PrefetchScalarGridSpec(num...  22.6 us
    pallas_call x2, Pallas kernels, gradients(): pl.pallas_call(functools.partial(gradient_kernel, count, total, heat_scal...  19.5 us
    pallas_call x1, Pallas kernels, scores_of(): pl.pallas_call(scores_kernel, grid=(rows // share,), in_specs=[pl.BlockSp...  14.8 us
    pallas_call x1, Pallas kernels, proto_gradient(): pl.pallas_call(proto_gradient_kernel, grid_spec=pltpu.PrefetchScalarGridS...  9.96 us
    pallas_call x2, Pallas kernels, combine(): pl.pallas_call(combine_kernel, grid_spec=pltpu.PrefetchScalarGridSpec(num...  7.29 us
  transfers between devices with their start and end apart: 34, of which 23 were waited for; matrix products, arithmetic and copies ran while one was open for 3% of the time, Pallas kernels for 31%

profile of v4, /device:TPU:0, one launch (start us, length us, event | category | flops | bytes accessed | tf_op | source)
XLA Modules:
  0.0 241.8 jit_solution(15250322620352404518)
XLA Ops:
  7.2 4.5 %own_rows.1 = bf16[1024,8,128]{2,1,0:T(8,128)(2,1)} custom-call(s32[1]{0:T(128)} %bitcast.5.index_ref, bf16[2048,1024]{1,0:T(8,128)(2,1)} %embeddings_ref.5), custom_call_target="tpu_custom_call" | custom-call | tf_op jit(solution)/shard_map/own_rows/pallas_call | solution.py:74
  11.7 14.8 %scores.1 = (bf16[2048,1024]{1,0:T(8,128)(2,1)}, bf16[1024,1024]{1,0:T(8,128)(2,1)}, f32[2048,1024]{1,0:T(8,128)}, bf16[2048,1024]{1,0:T(8,128)(2,1)}, f32[2,4,1,256]{3,2,1,0:T(1,128)}, /*index=5*/f32[1,1024]{1,0:T(1,128)}) custom-call(bf16[2048,1024]{1,0:T(8,128)(2,1)} %embeddings_ref.5, bf16[1024,1024]{1,0:T(8,128)(2,1)} %prototypes_ref.1), custom_call_target="tpu_custom_call" | custom-call | flops 4294967296 | bytes 23068672 | tf_op jit(solution)/shard_map/scores/pallas_call | solution.py:118
  26.5 2.9 %collective-permute-start = (f32[1,1024]{1,0:T(1,128)}, f32[1,1024]{1,0:T(1,128)S(1)}, u32[]{:S(2)}, u32[]{:S(2)}) collective-permute-start(f32[1,1024]{1,0:T(1,128)} %get-tuple-element.32.refs_0_), channel_id=1, source_target_pairs={{0,8},{8,0},{16,24},{24,16},{1,9},{9,1},{17,25},{25,17},{2,10},{10... | collective-permute-start | bytes 12296 | tf_op jit(solution)/shard_map/ppermute | solution.py:502
  31.3 2.0 collective-permute-done.1.refs_2_
  33.3 2.4 %collective-permute-done.2.refs_3_ = f32[1,1024]{1,0:T(1,128)S(1)} collective-permute-done((f32[1,1024]{1,0:T(1,128)}, f32[1,1024]{1,0:T(1,128)S(1)}, u32[]{:S(2)}, u32[]{:S(2)}) %collective-permute-start.2) | collective-permute-done | bytes 4128 | tf_op jit(solution)/shard_map/ppermute | solution.py:502
  36.4 3.6 %row_pass.2 = f32[1,2048]{1,0:T(1,128)} custom-call(f32[1,1024]{1,0:T(1,128)} %get-tuple-element.32.refs_0_, f32[1,1024]{1,0:T(1,128)} %copy-done.20, f32[1,1024]{1,0:T(1,128)} %copy-done.22, f32[1,1024]{1,0:T(1,128)} %copy-done.24, bf16[2048,1024]{1,0:T(8,128)(2,1)} %get-tuple-element.33.refs_4_.refs_5_.refs_6_.refs_7_, ...), custom_call_target="tpu_custom_call" | custom-call | flops 4194304 | bytes 4194304 | tf_op jit(solution)/shard_map/row_pass/pallas_call | solution.py:163
  43.7 2.6 %collective-permute-start.5 = (f32[1,2048]{1,0:T(1,128)S(1)}, f32[1,2048]{1,0:T(1,128)S(1)}, u32[]{:S(2)}, u32[]{:S(2)}) collective-permute-start(f32[1,2048]{1,0:T(1,128)S(1)} %add.51.refs_0_), channel_id=1, source_target_pairs={{0,4},{2,6},{4,0},{6,2},{1,5},{3,7},{5,1},{7,3},{8,12},{10,14},{12... | collective-permute-start | bytes 24584 | tf_op jit(solution)/shard_map/ppermute | solution.py:502
  48.2 3.5 %collective-permute-done.6.refs_3_ = f32[1,2048]{1,0:T(1,128)S(1)} collective-permute-done((f32[1,2048]{1,0:T(1,128)S(1)}, f32[1,2048]{1,0:T(1,128)S(1)}, u32[]{:S(2)}, u32[]{:S(2)}) %collective-permute-start.6) | collective-permute-done | bytes 8224 | tf_op jit(solution)/shard_map/ppermute | solution.py:502
  52.3 3.2 %column_pass.2.refs_0_ = f32[1,1024]{1,0:T(1,128)} custom-call(f32[1,2048]{1,0:T(1,128)} %copy-done.12, f32[1,2048]{1,0:T(1,128)} %copy-done.16, f32[1,2048]{1,0:T(1,128)} %copy-done.18, f32[1,2048]{1,0:T(1,128)} %copy-done.19, bf16[2048,1024]{1,0:T(8,128)(2,1)} %get-tuple-element.33.refs_4_.refs_5_.refs_6_.refs_7_, ...), custom_call_target="tpu_custom_call" | custom-call | flops 4194304 | bytes 4194304 | tf_op jit(solution)/shard_map/column_pass/pallas_call | solution.py:200
  56.6 2.4 %collective-permute-start.9 = (f32[1,1024]{1,0:T(1,128)}, f32[1,1024]{1,0:T(1,128)S(1)}, u32[]{:S(2)}, u32[]{:S(2)}) collective-permute-start(f32[1,1024]{1,0:T(1,128)} %column_pass.2.refs_0_), channel_id=1, source_target_pairs={{0,24},{8,16},{16,8},{24,0},{1,25},{9,17},{17,9},{25,1},{2,26},{10... | collective-permute-start | bytes 12296 | tf_op jit(solution)/shard_map/ppermute | solution.py:502
  62.0 3.6 %row_pass.3 = f32[1,2048]{1,0:T(1,128)} custom-call(f32[1,1024]{1,0:T(1,128)} %column_pass.2.refs_0_, f32[1,1024]{1,0:T(1,128)} %copy-done.21, f32[1,1024]{1,0:T(1,128)} %copy-done.23, f32[1,1024]{1,0:T(1,128)} %copy-done.25, bf16[2048,1024]{1,0:T(8,128)(2,1)} %get-tuple-element.33.refs_4_.refs_5_.refs_6_.refs_7_, ...), custom_call_target="tpu_custom_call" | custom-call | flops 4194304 | bytes 4194304 | tf_op jit(solution)/shard_map/row_pass/pallas_call | solution.py:163
  68.3 3.8 %collective-permute-start.13 = (f32[1,2048]{1,0:T(1,128)S(1)}, f32[1,2048]{1,0:T(1,128)S(1)}, u32[]{:S(2)}, u32[]{:S(2)}) collective-permute-start(f32[1,2048]{1,0:T(1,128)S(1)} %add.52.refs_0_), channel_id=1, source_target_pairs={{0,6},{2,4},{4,2},{6,0},{1,7},{3,5},{5,3},{7,1},{8,14},{10,12},{12... | collective-permute-start | bytes 24584 | tf_op jit(solution)/shard_map/ppermute | solution.py:502
  74.4 3.3 %column_pass.3.refs_0_ = f32[1,1024]{1,0:T(1,128)} custom-call(f32[1,2048]{1,0:T(1,128)} %copy-done.11, f32[1,2048]{1,0:T(1,128)} %copy-done.14, f32[1,2048]{1,0:T(1,128)} %copy-done.15, f32[1,2048]{1,0:T(1,128)} %copy-done.17, bf16[2048,1024]{1,0:T(8,128)(2,1)} %get-tuple-element.33.refs_4_.refs_5_.refs_6_.refs_7_, ...), custom_call_target="tpu_custom_call" | custom-call | flops 4194304 | bytes 4194304 | tf_op jit(solution)/shard_map/column_pass/pallas_call | solution.py:200
  81.2 23.7 %all-gather.2.cloned.1.call-done.source_ref = bf16[8192,8,128]{2,1,0:T(8,128)(2,1)} async-done(((bf16[1024,8,128]{2,1,0:T(8,128)(2,1)}), bf16[8192,8,128]{2,1,0:T(8,128)(2,1)}) %all-gather.2.cloned.1.call-update) | async-done | bytes 16777232 | tf_op jit(solution)/shard_map/all_gather | solution.py:536
  104.9 22.6 %partner_scores.1 = (bf16[2048,1024]{1,0:T(8,128)(2,1)}, bf16[2048,1024]{1,0:T(8,128)(2,1)}) custom-call(s32[2048]{0:T(1024)} %bitcast.46, s32[2048]{0:T(1024)} %bitcast.45, bf16[8192,8,128]{2,1,0:T(8,128)(2,1)} %all-gather.2.cloned.1.call-done.source_ref, bf16[1024,1024]{1,0:T(8,128)(2,1)} %get-tuple-element.35.wnorm_ref.refs_11_), custom_call_target="tpu_custom_call" | custom-call | flops 8589934592 | bytes 29360128 | tf_op jit(solution)/shard_map/partner_scores/pallas_call | solution.py:256
  128.2 5.0 %partner_row_pass.1 = f32[2,4,3,256]{3,2,1,0:T(4,128)} custom-call(f32[1,1024]{1,0:T(1,128)} %column_pass.3.refs_0_, f32[1,1024]{1,0:T(1,128)} %copy-done.8, f32[1,1024]{1,0:T(1,128)} %copy-done.9, f32[1,1024]{1,0:T(1,128)} %copy-done.10, f32[2,4,1,256]{3,2,1,0:T(1,128)} %get-tuple-element.34.refs_4_, ...), custom_call_target="tpu_custom_call" | custom-call | flops 8388608 | bytes 8388608 | tf_op jit(solution)/shard_map/partner_row_pass/pallas_call | solution.py:302
  136.8 2.4 collective-permute-start.19
  139.8 2.3 collective-permute-done.19.refs_6_
  142.1 2.8 %collective-permute-done.20.refs_7_ = f32[2,4,3,256]{3,2,1,0:T(4,128)S(1)} collective-permute-done((f32[2,4,3,256]{3,2,1,0:T(4,128)S(1)}, f32[2,4,3,256]{3,2,1,0:T(4,128)S(1)}, u32[]{:S(2)}, u32[]{:S(2)}) %collective-permute-start.20) | collective-permute-done | bytes 24608 | tf_op jit(solution)/shard_map/ppermute | solution.py:502
  145.5 9.6 %gradients.3 = (bf16[4,256,1024]{2,1,0:T(8,128)(2,1)}, bf16[4,256,1024]{2,1,0:T(8,128)(2,1)}, f32[1,128]{1,0:T(1,128)}) custom-call(s32[1]{0:T(128)} %bitcast.10.core_ref, f32[1,1024]{1,0:T(1,128)} %column_pass.3.refs_0_, f32[1,1024]{1,0:T(1,128)} %copy-done.8, f32[1,1024]{1,0:T(1,128)} %copy-done.9, f32[1,1024]{1,0:T(1,128)} %copy-done.10, ...), custom_call_target="tpu_custom_call" | custom-call | flops 2147483648 | bytes 16777216 | tf_op jit(solution)/shard_map/gradients/pallas_call | solution.py:363
  155.2 9.9 %gradients.2 = (f32[4,256,1024]{2,1,0:T(8,128)}, bf16[4,256,1024]{2,1,0:T(8,128)(2,1)}, f32[1,128]{1,0:T(1,128)}) custom-call(s32[1]{0:T(128)} %bitcast.2.core_ref, f32[1,1024]{1,0:T(1,128)} %column_pass.3.refs_0_, f32[1,1024]{1,0:T(1,128)} %copy-done.8, f32[1,1024]{1,0:T(1,128)} %copy-done.9, f32[1,1024]{1,0:T(1,128)} %copy-done.10, ...), custom_call_target="tpu_custom_call" | custom-call | flops 2147483648 | bytes 16777216 | tf_op jit(solution)/shard_map/gradients/pallas_call | solution.py:363
  173.7 4.1 %combine.2 = (f32[2,256,1024]{2,1,0:T(8,128)}, bf16[2,256,1024]{2,1,0:T(8,128)(2,1)}) custom-call(s32[1]{0:T(128)} %bitcast.1.bit_ref, f32[2,2,256,1024]{3,2,1,0:T(8,128)} %bitcast.35, bf16[2,2,256,1024]{3,2,1,0:T(8,128)(2,1)} %bitcast.39, f32[2,2,256,1024]{3,2,1,0:T(8,128)} %bitcast.36, bf16[2,2,256,1024]{3,2,1,0:T(8,128)(2,1)} %bitcast.40), custom_call_target="tpu_custom_call" | custom-call | flops 1048576 | bytes 9437184 | tf_op jit(solution)/shard_map/combine/pallas_call | solution.py:407
  178.4 10.0 %proto_gradient.1 = (f32[1024,256]{1,0:T(8,128)}, bf16[4,1024,256]{2,1,0:T(8,128)(2,1)}) custom-call(s32[2]{0:T(128)} %pad_add_fusion.index_ref, bf16[1024,1024]{1,0:T(8,128)(2,1)} %bitcast.48, bf16[1024,1024]{1,0:T(8,128)(2,1)} %bitcast.47, bf16[4,2,256,1024]{3,2,1,0:T(8,128)(2,1)} %bitcast.49, bf16[4,2,256,1024]{3,2,1,0:T(8,128)(2,1)} %bitcast.50), custom_call_target="tpu_custom_call" | custom-call | flops 4294967296 | bytes 12582912 | tf_op jit(solution)/shard_map/proto_gradient/pallas_call | solution.py:447
  188.3 2.6 %slice_bitcast_fusion.2 = (bf16[1024,256]{1,0:T(8,128)(2,1)}, bf16[1024,256]{1,0:T(8,128)(2,1)}, bf16[1024,256]{1,0:T(8,128)(2,1)}) fusion(bf16[4,1024,256]{2,1,0:T(8,128)(2,1)} %get-tuple-element.58), kind=kLoop, calls=%fused_computation.3 | loop fusion | bytes 3145728 | tf_op jit(solution)/shard_map/squeeze | solution.py:572
  195.5 2.0 collective-permute-start.27
  197.5 4.4 %collective-permute-done.27 = f32[1,128]{1,0:T(1,128)S(1)} collective-permute-done((f32[1,128]{1,0:T(1,128)S(1)}, f32[1,128]{1,0:T(1,128)S(1)}, u32[]{:S(2)}, u32[]{:S(2)}) %collective-permute-start.27) | collective-permute-done | bytes 544 | tf_op jit(solution)/shard_map/ppermute | solution.py:502
  202.8 3.2 %combine.3 = (f32[1,256,1024]{2,1,0:T(8,128)}, bf16[1,256,1024]{2,1,0:T(8,128)(2,1)}) custom-call(s32[1]{0:T(128)} %bitcast.bit_ref, f32[1,2,256,1024]{3,2,1,0:T(8,128)} %bitcast.37, bf16[1,2,256,1024]{3,2,1,0:T(8,128)(2,1)} %bitcast.41, f32[1,2,256,1024]{3,2,1,0:T(8,128)} %bitcast.38, bf16[1,2,256,1024]{3,2,1,0:T(8,128)(2,1)} %bitcast.42), custom_call_target="tpu_custom_call" | custom-call | flops 524288 | bytes 4718592 | tf_op jit(solution)/shard_map/combine/pallas_call | solution.py:407
  206.1 2.9 %collective-permute-start.28 = (f32[1,128]{1,0:T(1,128)S(1)}, f32[1,128]{1,0:T(1,128)S(1)}, u32[]{:S(2)}, u32[]{:S(2)}) collective-permute-start(f32[1,128]{1,0:T(1,128)S(1)} %add.59), channel_id=1, source_target_pairs={{0,4},{2,6},{4,0},{6,2},{1,5},{3,7},{5,1},{7,3},{8,12},{10,14},{12... | collective-permute-start | bytes 1544 | tf_op jit(solution)/shard_map/ppermute | solution.py:502
  209.0 6.8 %collective-permute-done.30 = bf16[1024,256]{1,0:T(8,128)(2,1)S(1)} collective-permute-done((bf16[1024,256]{1,0:T(8,128)(2,1)}, bf16[1024,256]{1,0:T(8,128)(2,1)S(1)}, u32[]{:S(2)}, u32[]{:S(2)}) %collective-permute-start.30) | collective-permute-done | bytes 524320 | tf_op jit(solution)/shard_map/ppermute | solution.py:502
  215.9 2.2 convert_add_fusion
  218.2 11.9 %collective-permute-done.28 = f32[1,128]{1,0:T(1,128)S(1)} collective-permute-done((f32[1,128]{1,0:T(1,128)S(1)}, f32[1,128]{1,0:T(1,128)S(1)}, u32[]{:S(2)}, u32[]{:S(2)}) %collective-permute-start.28) | collective-permute-done | bytes 544 | tf_op jit(solution)/shard_map/ppermute | solution.py:502
  230.9 2.9 %embed_gradient.1 = f32[256,1024]{1,0:T(8,128)} custom-call(s32[1]{0:T(128)} %bitcast.22.index_ref, bf16[2048,1024]{1,0:T(8,128)(2,1)} %embeddings_ref.5, f32[256,1024]{1,0:T(8,128)} %bitcast.43, bf16[256,1024]{1,0:T(8,128)(2,1)} %bitcast.44), custom_call_target="tpu_custom_call" | custom-call | flops 2097152 | bytes 4194304 | tf_op jit(solution)/shard_map/embed_gradient/pallas_call | solution.py:485
  (117 shorter events, 42.6 us)
Async XLA Ops:
  7.2 97.8 %all-gather.2.cloned.1.call-start = ((), (), s32[]{:S(2)}) async-start(), calls=%async_computation | async-start | bytes 18874368 | tf_op jit(solution)/shard_map/all_gather | solution.py:536
  26.5 4.8 %collective-permute-start = (f32[1,1024]{1,0:T(1,128)}, f32[1,1024]{1,0:T(1,128)S(1)}, u32[]{:S(2)}, u32[]{:S(2)}) collective-permute-start(f32[1,1024]{1,0:T(1,128)} %get-tuple-element.32.refs_0_), channel_id=1, source_target_pairs={{0,8},{8,0},{16,24},{24,16},{1,9},{9,1},{17,25},{25,17},{2,10},{10... | collective-permute-start | bytes 12296 | tf_op jit(solution)/shard_map/ppermute | solution.py:502
  29.5 3.9 %collective-permute-start.1 = (f32[1,1024]{1,0:T(1,128)}, f32[1,1024]{1,0:T(1,128)S(1)}, u32[]{:S(2)}, u32[]{:S(2)}) collective-permute-start(f32[1,1024]{1,0:T(1,128)} %get-tuple-element.32.refs_0_), channel_id=1, source_target_pairs={{0,16},{8,24},{16,0},{24,8},{1,17},{9,25},{17,1},{25,9},{2,18},{10... | collective-permute-start | bytes 12296 | tf_op jit(solution)/shard_map/ppermute | solution.py:502
  30.9 4.8 %collective-permute-start.2 = (f32[1,1024]{1,0:T(1,128)}, f32[1,1024]{1,0:T(1,128)S(1)}, u32[]{:S(2)}, u32[]{:S(2)}) collective-permute-start(f32[1,1024]{1,0:T(1,128)} %get-tuple-element.32.refs_0_), channel_id=1, source_target_pairs={{0,24},{8,16},{16,8},{24,0},{1,25},{9,17},{17,9},{25,1},{2,26},{10... | collective-permute-start | bytes 12296 | tf_op jit(solution)/shard_map/ppermute | solution.py:502
  39.9 1.4 collective-permute-start.3
  42.0 4.5 %collective-permute-start.4 = (f32[1,2048]{1,0:T(1,128)S(1)}, f32[1,2048]{1,0:T(1,128)S(1)}, u32[]{:S(2)}, u32[]{:S(2)}) collective-permute-start(f32[1,2048]{1,0:T(1,128)S(1)} %add.51.refs_0_), channel_id=1, source_target_pairs={{0,2},{2,0},{4,6},{6,4},{1,3},{3,1},{5,7},{7,5},{8,10},{10,8},{12,... | collective-permute-start | bytes 24584 | tf_op jit(solution)/shard_map/ppermute | solution.py:502
  43.7 4.5 %collective-permute-start.5 = (f32[1,2048]{1,0:T(1,128)S(1)}, f32[1,2048]{1,0:T(1,128)S(1)}, u32[]{:S(2)}, u32[]{:S(2)}) collective-permute-start(f32[1,2048]{1,0:T(1,128)S(1)} %add.51.refs_0_), channel_id=1, source_target_pairs={{0,4},{2,6},{4,0},{6,2},{1,5},{3,7},{5,1},{7,3},{8,12},{10,14},{12... | collective-permute-start | bytes 24584 | tf_op jit(solution)/shard_map/ppermute | solution.py:502
  46.2 5.4 %collective-permute-start.6 = (f32[1,2048]{1,0:T(1,128)S(1)}, f32[1,2048]{1,0:T(1,128)S(1)}, u32[]{:S(2)}, u32[]{:S(2)}) collective-permute-start(f32[1,2048]{1,0:T(1,128)S(1)} %add.51.refs_0_), channel_id=1, source_target_pairs={{0,6},{2,4},{4,2},{6,0},{1,7},{3,5},{5,3},{7,1},{8,14},{10,12},{12... | collective-permute-start | bytes 24584 | tf_op jit(solution)/shard_map/ppermute | solution.py:502
  55.5 3.9 %collective-permute-start.7 = (f32[1,1024]{1,0:T(1,128)}, f32[1,1024]{1,0:T(1,128)S(1)}, u32[]{:S(2)}, u32[]{:S(2)}) collective-permute-start(f32[1,1024]{1,0:T(1,128)} %column_pass.2.refs_0_), channel_id=1, source_target_pairs={{0,8},{8,0},{16,24},{24,16},{1,9},{9,1},{17,25},{25,17},{2,10},{10... | collective-permute-start | bytes 12296 | tf_op jit(solution)/shard_map/ppermute | solution.py:502
  56.1 3.9 %collective-permute-start.8 = (f32[1,1024]{1,0:T(1,128)}, f32[1,1024]{1,0:T(1,128)S(1)}, u32[]{:S(2)}, u32[]{:S(2)}) collective-permute-start(f32[1,1024]{1,0:T(1,128)} %column_pass.2.refs_0_), channel_id=1, source_target_pairs={{0,16},{8,24},{16,0},{24,8},{1,17},{9,25},{17,1},{25,9},{2,18},{10... | collective-permute-start | bytes 12296 | tf_op jit(solution)/shard_map/ppermute | solution.py:502
  56.6 4.8 %collective-permute-start.9 = (f32[1,1024]{1,0:T(1,128)}, f32[1,1024]{1,0:T(1,128)S(1)}, u32[]{:S(2)}, u32[]{:S(2)}) collective-permute-start(f32[1,1024]{1,0:T(1,128)} %column_pass.2.refs_0_), channel_id=1, source_target_pairs={{0,24},{8,16},{16,8},{24,0},{1,25},{9,17},{17,9},{25,1},{2,26},{10... | collective-permute-start | bytes 12296 | tf_op jit(solution)/shard_map/ppermute | solution.py:502
  67.7 5.1 %collective-permute-start.11 = (f32[1,2048]{1,0:T(1,128)S(1)}, f32[1,2048]{1,0:T(1,128)S(1)}, u32[]{:S(2)}, u32[]{:S(2)}) collective-permute-start(f32[1,2048]{1,0:T(1,128)S(1)} %add.52.refs_0_), channel_id=1, source_target_pairs={{0,2},{2,0},{4,6},{6,4},{1,3},{3,1},{5,7},{7,5},{8,10},{10,8},{12,... | collective-permute-start | bytes 24584 | tf_op jit(solution)/shard_map/ppermute | solution.py:502
  67.7 5.0 %collective-permute-start.12 = (f32[1,2048]{1,0:T(1,128)S(1)}, f32[1,2048]{1,0:T(1,128)S(1)}, u32[]{:S(2)}, u32[]{:S(2)}) collective-permute-start(f32[1,2048]{1,0:T(1,128)S(1)} %add.52.refs_0_), channel_id=1, source_target_pairs={{0,4},{2,6},{4,0},{6,2},{1,5},{3,7},{5,1},{7,3},{8,12},{10,14},{12... | collective-permute-start | bytes 24584 | tf_op jit(solution)/shard_map/ppermute | solution.py:502
  68.3 5.5 %collective-permute-start.13 = (f32[1,2048]{1,0:T(1,128)S(1)}, f32[1,2048]{1,0:T(1,128)S(1)}, u32[]{:S(2)}, u32[]{:S(2)}) collective-permute-start(f32[1,2048]{1,0:T(1,128)S(1)} %add.52.refs_0_), channel_id=1, source_target_pairs={{0,6},{2,4},{4,2},{6,0},{1,7},{3,5},{5,3},{7,1},{8,14},{10,12},{12... | collective-permute-start | bytes 24584 | tf_op jit(solution)/shard_map/ppermute | solution.py:502
  77.7 49.8 %collective-permute-start.14 = (f32[1,1024]{1,0:T(1,128)}, f32[1,1024]{1,0:T(1,128)S(1)}, u32[]{:S(2)}, u32[]{:S(2)}) collective-permute-start(f32[1,1024]{1,0:T(1,128)} %column_pass.3.refs_0_), channel_id=1, source_target_pairs={{0,8},{8,0},{16,24},{24,16},{1,9},{9,1},{17,25},{25,17},{2,10},{10... | collective-permute-start | bytes 12296 | tf_op jit(solution)/shard_map/ppermute | solution.py:502
  79.4 48.2 %collective-permute-start.15 = (f32[1,1024]{1,0:T(1,128)}, f32[1,1024]{1,0:T(1,128)S(1)}, u32[]{:S(2)}, u32[]{:S(2)}) collective-permute-start(f32[1,1024]{1,0:T(1,128)} %column_pass.3.refs_0_), channel_id=1, source_target_pairs={{0,16},{8,24},{16,0},{24,8},{1,17},{9,25},{17,1},{25,9},{2,18},{10... | collective-permute-start | bytes 12296 | tf_op jit(solution)/shard_map/ppermute | solution.py:502
  80.8 46.8 %collective-permute-start.16 = (f32[1,1024]{1,0:T(1,128)}, f32[1,1024]{1,0:T(1,128)S(1)}, u32[]{:S(2)}, u32[]{:S(2)}) collective-permute-start(f32[1,1024]{1,0:T(1,128)} %column_pass.3.refs_0_), channel_id=1, source_target_pairs={{0,24},{8,16},{16,8},{24,0},{1,25},{9,17},{17,9},{25,1},{2,26},{10... | collective-permute-start | bytes 12296 | tf_op jit(solution)/shard_map/ppermute | solution.py:502
  133.1 1.4 collective-permute-start.17
  135.3 4.5 %collective-permute-start.18 = (f32[2,4,3,256]{3,2,1,0:T(4,128)S(1)}, f32[2,4,3,256]{3,2,1,0:T(4,128)S(1)}, u32[]{:S(2)}, u32[]{:S(2)}) collective-permute-start(f32[2,4,3,256]{3,2,1,0:T(4,128)S(1)} %add.53.refs_4_), channel_id=1, source_target_pairs={{0,2},{2,0},{4,6},{6,4},{1,3},{3,1},{5,7},{7,5},{8,10},{10,8},{12,... | collective-permute-start | bytes 73736 | tf_op jit(solution)/shard_map/ppermute | solution.py:502
  136.8 5.3 %collective-permute-start.19 = (f32[2,4,3,256]{3,2,1,0:T(4,128)S(1)}, f32[2,4,3,256]{3,2,1,0:T(4,128)S(1)}, u32[]{:S(2)}, u32[]{:S(2)}) collective-permute-start(f32[2,4,3,256]{3,2,1,0:T(4,128)S(1)} %add.53.refs_4_), channel_id=1, source_target_pairs={{0,4},{2,6},{4,0},{6,2},{1,5},{3,7},{5,1},{7,3},{8,12},{10,14},{12... | collective-permute-start | bytes 73736 | tf_op jit(solution)/shard_map/ppermute | solution.py:502
  139.2 5.7 %collective-permute-start.20 = (f32[2,4,3,256]{3,2,1,0:T(4,128)S(1)}, f32[2,4,3,256]{3,2,1,0:T(4,128)S(1)}, u32[]{:S(2)}, u32[]{:S(2)}) collective-permute-start(f32[2,4,3,256]{3,2,1,0:T(4,128)S(1)} %add.53.refs_4_), channel_id=1, source_target_pairs={{0,6},{2,4},{4,2},{6,0},{1,7},{3,5},{5,3},{7,1},{8,14},{10,12},{12... | collective-permute-start | bytes 73736 | tf_op jit(solution)/shard_map/ppermute | solution.py:502
  155.1 17.1 %collective-permute-start.21 = (bf16[4,256,1024]{2,1,0:T(8,128)(2,1)}, bf16[4,256,1024]{2,1,0:T(8,128)(2,1)S(1)}, u32[]{:S(2)}, u32[]{:S(2)}) collective-permute-start(bf16[4,256,1024]{2,1,0:T(8,128)(2,1)} %get-tuple-element.40), channel_id=1, source_target_pairs={{0,1},{1,0},{2,3},{3,2},{4,5},{5,4},{6,7},{7,6},{8,9},{9,8},{10,11... | collective-permute-start | bytes 6291464 | tf_op jit(solution)/shard_map/ppermute | solution.py:502
  165.8 3.5 %collective-permute-start.22 = (f32[1,128]{1,0:T(1,128)S(1)}, f32[1,128]{1,0:T(1,128)S(1)}, u32[]{:S(2)}, u32[]{:S(2)}) collective-permute-start(f32[1,128]{1,0:T(1,128)S(1)} %add.54), channel_id=1, source_target_pairs={{0,8},{8,0},{16,24},{24,16},{1,9},{9,1},{17,25},{25,17},{2,10},{10... | collective-permute-start | bytes 1544 | tf_op jit(solution)/shard_map/ppermute | solution.py:502
  167.2 3.5 %collective-permute-start.23 = (f32[1,128]{1,0:T(1,128)S(1)}, f32[1,128]{1,0:T(1,128)S(1)}, u32[]{:S(2)}, u32[]{:S(2)}) collective-permute-start(f32[1,128]{1,0:T(1,128)S(1)} %add.54), channel_id=1, source_target_pairs={{0,16},{8,24},{16,0},{24,8},{1,17},{9,25},{17,1},{25,9},{2,18},{10... | collective-permute-start | bytes 1544 | tf_op jit(solution)/shard_map/ppermute | solution.py:502
  167.8 4.4 %collective-permute-start.24 = (f32[1,128]{1,0:T(1,128)S(1)}, f32[1,128]{1,0:T(1,128)S(1)}, u32[]{:S(2)}, u32[]{:S(2)}) collective-permute-start(f32[1,128]{1,0:T(1,128)S(1)} %add.54), channel_id=1, source_target_pairs={{0,24},{8,16},{16,8},{24,0},{1,25},{9,17},{17,9},{25,1},{2,26},{10... | collective-permute-start | bytes 1544 | tf_op jit(solution)/shard_map/ppermute | solution.py:502
  177.8 24.1 %collective-permute-start.25 = (bf16[2,256,1024]{2,1,0:T(8,128)(2,1)}, bf16[2,256,1024]{2,1,0:T(8,128)(2,1)S(1)}, u32[]{:S(2)}, u32[]{:S(2)}) collective-permute-start(bf16[2,256,1024]{2,1,0:T(8,128)(2,1)} %get-tuple-element.53), channel_id=1, source_target_pairs={{0,2},{2,0},{4,6},{6,4},{1,3},{3,1},{5,7},{7,5},{8,10},{10,8},{12,... | collective-permute-start | bytes 3145736 | tf_op jit(solution)/shard_map/ppermute | solution.py:502
  190.9 18.1 %collective-permute-start.29 = (bf16[1024,256]{1,0:T(8,128)(2,1)}, bf16[1024,256]{1,0:T(8,128)(2,1)S(1)}, u32[]{:S(2)}, u32[]{:S(2)}) collective-permute-start(bf16[1024,256]{1,0:T(8,128)(2,1)} %get-tuple-element.61), channel_id=1, source_target_pairs={{0,24},{8,16},{16,8},{24,0},{1,25},{9,17},{17,9},{25,1},{2,26},{10... | collective-permute-start | bytes 1572872 | tf_op jit(solution)/shard_map/ppermute | solution.py:502
  192.3 23.5 %collective-permute-start.30 = (bf16[1024,256]{1,0:T(8,128)(2,1)}, bf16[1024,256]{1,0:T(8,128)(2,1)S(1)}, u32[]{:S(2)}, u32[]{:S(2)}) collective-permute-start(bf16[1024,256]{1,0:T(8,128)(2,1)} %get-tuple-element.63), channel_id=1, source_target_pairs={{0,16},{8,24},{16,0},{24,8},{1,17},{9,25},{17,1},{25,9},{2,18},{10... | collective-permute-start | bytes 1572872 | tf_op jit(solution)/shard_map/ppermute | solution.py:502
  193.1 22.9 %collective-permute-start.31 = (bf16[1024,256]{1,0:T(8,128)(2,1)}, bf16[1024,256]{1,0:T(8,128)(2,1)}, u32[]{:S(2)}, u32[]{:S(2)}) collective-permute-start(bf16[1024,256]{1,0:T(8,128)(2,1)} %get-tuple-element.62), channel_id=1, source_target_pairs={{0,8},{8,0},{16,24},{24,16},{1,9},{9,1},{17,25},{25,17},{2,10},{10... | collective-permute-start | bytes 1572872 | tf_op jit(solution)/shard_map/ppermute | solution.py:502
  195.5 6.4 %collective-permute-start.27 = (f32[1,128]{1,0:T(1,128)S(1)}, f32[1,128]{1,0:T(1,128)S(1)}, u32[]{:S(2)}, u32[]{:S(2)}) collective-permute-start(f32[1,128]{1,0:T(1,128)S(1)} %add.58), channel_id=1, source_target_pairs={{0,2},{2,0},{4,6},{6,4},{1,3},{3,1},{5,7},{7,5},{8,10},{10,8},{12,... | collective-permute-start | bytes 1544 | tf_op jit(solution)/shard_map/ppermute | solution.py:502
  206.0 24.1 %collective-permute-start.32 = (bf16[1,256,1024]{2,1,0:T(8,128)(2,1)}, bf16[1,256,1024]{2,1,0:T(8,128)(2,1)S(1)}, u32[]{:S(2)}, u32[]{:S(2)}) collective-permute-start(bf16[1,256,1024]{2,1,0:T(8,128)(2,1)} %get-tuple-element.60), channel_id=1, source_target_pairs={{0,4},{2,6},{4,0},{6,2},{1,5},{3,7},{5,1},{7,3},{8,12},{10,14},{12... | collective-permute-start | bytes 1572872 | tf_op jit(solution)/shard_map/ppermute | solution.py:502
  206.1 24.0 %collective-permute-start.28 = (f32[1,128]{1,0:T(1,128)S(1)}, f32[1,128]{1,0:T(1,128)S(1)}, u32[]{:S(2)}, u32[]{:S(2)}) collective-permute-start(f32[1,128]{1,0:T(1,128)S(1)} %add.59), channel_id=1, source_target_pairs={{0,4},{2,6},{4,0},{6,2},{1,5},{3,7},{5,1},{7,3},{8,12},{10,14},{12... | collective-permute-start | bytes 1544 | tf_op jit(solution)/shard_map/ppermute | solution.py:502
  (29 other events, 104.7 us)
Sparse Core Ops, SparseCore 0:
  11.8 93.0 all-gather.1

commit v5 on v4

--- a/solution.py
+++ b/solution.py
@@ -22,6 +22,10 @@
 
 def params(mib=60):
     return pltpu.CompilerParams(vmem_limit_bytes=mib * MIB)
+
+
+def in_vmem(value):
+    return pltpu.with_memory_space_constraint(value, pltpu.VMEM)
 
 
 def cost(flops, moved, exps=0):
@@ -93,15 +97,20 @@
     def _():
         wnorm_ref[...] = normalized(prototypes_ref[...]).astype(BF16)
 
-    unit = normalized(embeddings_ref[...]).astype(BF16)
-    unit_ref[...] = unit
-    scores = lax.dot_general(unit, wnorm_ref[...], (((1,), (1,)), ((), ())), preferred_element_type=F32)
-    scores_ref[...] = scores
-    soft = jnp.exp(scores * (1.0 / SOFTMAX_HEAT))
-    zsum_ref[...] = lane_row_sums(soft)
-    expo = soft * soft
-    expo_ref[...] = expo.astype(BF16)
-    sums = jnp.sum(expo, axis=0, keepdims=True)
+    share = zsum_ref.shape[-1]
+    sums = None
+    for k in range(2):
+        at = slice(k * share, (k + 1) * share)
+        unit = normalized(embeddings_ref[at]).astype(BF16)
+        unit_ref[at] = unit
+        scores = lax.dot_general(unit, wnorm_ref[...], (((1,), (1,)), ((), ())), preferred_element_type=F32)
+        scores_ref[at] = scores
+        soft = jnp.exp(scores * (1.0 / SOFTMAX_HEAT))
+        zsum_ref[k, 0] = lane_row_sums(soft)
+        expo = soft * soft
+        expo_ref[at] = expo.astype(BF16)
+        part = jnp.sum(expo, axis=0, keepdims=True)
+        sums = part if sums is None else sums + part
 
     @pl.when(step == 0)
     def _():
@@ -117,17 +126,17 @@
     protos = prototypes.shape[0]
     return pl.pallas_call(
         scores_kernel,
-        grid=(rows // share,),
+        grid=(rows // share // 2,),
         in_specs=[
-            pl.BlockSpec((share, columns), lambda i: (i, 0)),
+            pl.BlockSpec((2 * share, columns), lambda i: (i, 0)),
             pl.BlockSpec((protos, columns), lambda i: (0, 0), pipeline_mode=pl.Buffered(1)),
         ],
         out_specs=[
-            pl.BlockSpec((share, columns), lambda i: (i, 0)),
+            pl.BlockSpec((2 * share, columns), lambda i: (i, 0)),
             pl.BlockSpec((protos, columns), lambda i: (0, 0)),
-            pl.BlockSpec((share, protos), lambda i: (i, 0)),
-            pl.BlockSpec((share, protos), lambda i: (i, 0)),
-            pl.BlockSpec((None, None, 1, share), lambda i: (i % 2, i // 2, 0, 0)),
+            pl.BlockSpec((2 * share, protos), lambda i: (i, 0)),
+            pl.BlockSpec((2 * share, protos), lambda i: (i, 0)),
+            pl.BlockSpec((2, 1, 1, share), lambda i: (0, i, 0, 0)),
             pl.BlockSpec((1, protos), lambda i: (0, 0)),
         ],
         out_shape=[
@@ -138,7 +147,7 @@
             jax.ShapeDtypeStruct((2, rows // share // 2, 1, share), F32),
             jax.ShapeDtypeStruct((1, protos), F32),
         ],
-        compiler_params=params(),
+        compiler_params=params(32),
         cost_estimate=cost(2 * rows * columns * protos, 22 * MIB, rows * protos),
         name="scores",
     )(embeddings, prototypes)
@@ -166,10 +175,10 @@
         in_specs=[pl.BlockSpec((1, protos), lambda i: (0, 0)) for _ in columns] + streams_of((block, protos)),
         out_specs=pl.BlockSpec((1, STREAMS * block), lambda i: (0, i)),
         out_shape=jax.ShapeDtypeStruct((1, rows), F32),
-        compiler_params=params(),
+        compiler_params=params(16),
         cost_estimate=cost(2 * rows * protos, 4 * MIB),
         name="row_pass",
-    )(*columns, *[expo] * STREAMS)
+    )(*columns, *[in_vmem(expo)] * STREAMS)
 
 
 def column_kernel(count, parts, *refs):
@@ -204,10 +213,10 @@
         + streams_of((block, protos)),
         out_specs=pl.BlockSpec((1, protos), lambda i: (0, 0)),
         out_shape=jax.ShapeDtypeStruct((1, protos), F32),
-        compiler_params=params(),
+        compiler_params=params(16),
         cost_estimate=cost(2 * rows * protos, 4 * MIB),
         name="column_pass",
-    )(*row_totals, *[expo] * STREAMS)
+    )(*row_totals, *[in_vmem(expo)] * STREAMS)
 
 
 def partner_kernel(first_ref, second_ref, source_ref, wnorm_ref, first_expo_ref, second_expo_ref, table_ref, semaphores, *stages):
@@ -273,7 +282,7 @@
             + [pltpu.VMEM((CHUNK * groups, LANES), F32)] * 4,
         ),
         out_shape=[jax.ShapeDtypeStruct((rows, protos), BF16)] * 2,
-        compiler_params=params(),
+        compiler_params=params(32),
         cost_estimate=cost(4 * rows * columns * protos, 28 * MIB, 2 * rows * protos),
         name="partner_scores",
     )(first, second, table, wnorm)
@@ -307,10 +316,10 @@
         + streams_of((share, protos)) * 2,
         out_specs=pl.BlockSpec((2, group, 3, share), lambda i: (0, i, 0, 0)),
         out_shape=jax.ShapeDtypeStruct((2, rows // share // 2, 3, share), F32),
-        compiler_params=params(),
+        compiler_params=params(16),
         cost_estimate=cost(4 * rows * protos, 8 * MIB),
         name="partner_row_pass",
-    )(*columns, zsum, *[first] * STREAMS, *[second] * STREAMS)
+    )(*columns, zsum, *[in_vmem(first)] * STREAMS, *[in_vmem(second)] * STREAMS)
 
 
 def gradient_kernel(count, total, heat_scale, proto_size, parts, core_ref, *refs):
@@ -352,109 +361,135 @@
         loss_ref[...] += loss
 
 
-def gradients(core, columns, row_totals, first, second, scores, wnorm, count, total, proto_size, dtype):
+def gradients(where, columns, row_totals, first, second, scores, wnorm, count, total, proto_size, dtype):
     rows, protos = first.shape
     width = wnorm.shape[1]
     heat_scale = count / (32.0 * SOFTMAX_HEAT)
     _, places, _, share = row_totals[0].shape
+    half = places // 2
     group = 2
-    by_core = pl.BlockSpec((group, None, share, protos), lambda i, core: (i, core[0], 0, 0))
-    first, second, scores = [value.reshape(places, 2, share, protos) for value in (first, second, scores)]
+    at = pl.BlockSpec((group, None, None, share, protos), lambda i, where: (i, where[0], where[1], 0, 0))
+    first, second, scores = [in_vmem(value.reshape(half, 2, 2, share, protos)) for value in (first, second, scores)]
+    row_totals = [value.reshape(2, half, 2, 3, share) for value in row_totals]
     return pl.pallas_call(
         functools.partial(
             gradient_kernel, count, total, heat_scale, proto_size, (len(columns), len(row_totals))
         ),
         grid_spec=pltpu.PrefetchScalarGridSpec(
             num_scalar_prefetch=1,
-            grid=(places // group,),
-            in_specs=[pl.BlockSpec((1, protos), lambda i, core: (0, 0)) for _ in columns]
-            + [pl.BlockSpec((None, group, 3, share), lambda i, core: (core[0], i, 0, 0)) for _ in row_totals]
+            grid=(half // group,),
+            in_specs=[pl.BlockSpec((1, protos), lambda i, where: (0, 0)) for _ in columns]
             + [
-                by_core,
-                by_core,
-                by_core,
-                pl.BlockSpec((protos, width), lambda i, core: (0, 0), pipeline_mode=pl.Buffered(1)),
-            ],
+                pl.BlockSpec((None, group, None, 3, share), lambda i, where: (where[1], i, where[0], 0, 0))
+                for _ in row_totals
+            ]
+            + [at, at, at, pl.BlockSpec((protos, width), lambda i, where: (0, 0), pipeline_mode=pl.Buffered(1))],
             out_specs=[
-                pl.BlockSpec((group, share, width), lambda i, core: (i, 0, 0)),
-                pl.BlockSpec((group, share, protos), lambda i, core: (i, 0, 0)),
-                pl.BlockSpec((1, LANES), lambda i, core: (0, 0)),
+                pl.BlockSpec((group, share, width), lambda i, where: (i, 0, 0)),
+                pl.BlockSpec((group, share, protos), lambda i, where: (i, 0, 0)),
+                pl.BlockSpec((1, LANES), lambda i, where: (0, 0)),
             ],
         ),
         out_shape=[
-            jax.ShapeDtypeStruct((places, share, width), dtype),
-            jax.ShapeDtypeStruct((places, share, protos), BF16),
+            jax.ShapeDtypeStruct((half, share, width), dtype),
+            jax.ShapeDtypeStruct((half, share, protos), BF16),
             jax.ShapeDtypeStruct((1, LANES), F32),
         ],
-        compiler_params=params(),
-        cost_estimate=cost(rows * width * protos, 16 * MIB, rows * protos // 2),
+        compiler_params=params(32),
+        cost_estimate=cost(MIB, MIB),
         name="gradients",
-    )(core, *columns, *row_totals, first, second, scores, wnorm)
-
-
-def combine_kernel(bit_ref, own_kept_ref, own_received_ref, other_kept_ref, other_received_ref, own_ref, sent_ref):
+    )(where, *columns, *row_totals, first, second, scores, in_vmem(wnorm))
+
+
+def add_kernel(*refs):
+    total = refs[0][...]
+    for ref in refs[1:-1]:
+        total = total + ref[...].astype(F32)
+    refs[-1][...] = total.astype(refs[-1].dtype)
+
+
+def add_blocks(values, dtype):
+    count, share, width = values[0].shape
+    at = pl.BlockSpec((1, share, width), lambda i: (i, 0, 0))
+    return pl.pallas_call(
+        add_kernel,
+        grid=(count,),
+        in_specs=[at for _ in values],
+        out_specs=at,
+        out_shape=jax.ShapeDtypeStruct(values[0].shape, dtype),
+        compiler_params=params(16),
+        cost_estimate=cost(count * share * width, 8 * count * share * width),
+        name="add_blocks",
+    )(*values)
+
+
+def combine_kernel(parts, bit_ref, *refs):
     del bit_ref
-    sent_ref[...] = (other_kept_ref[...] + other_received_ref[...].astype(F32)).astype(BF16)
-    own_ref[...] = own_kept_ref[...] + own_received_ref[...].astype(F32)
-
-
-def combine(bit, kept, received):
-    count, share, width = kept.shape
-    kept, received = [value.reshape(count // 2, 2, share, width) for value in (kept, received)]
+    own_refs, other_refs, (own_ref, sent_ref) = refs[:parts], refs[parts : 2 * parts], refs[2 * parts :]
+    add_kernel(*other_refs, sent_ref)
+    add_kernel(*own_refs, own_ref)
+
+
+def combine(bit, values):
+    count, share, width = values[0].shape
+    values = [value.reshape(count // 2, 2, share, width) for value in values]
     own_at = pl.BlockSpec((None, None, share, width), lambda i, bit: (i, bit[0], 0, 0))
     other_at = pl.BlockSpec((None, None, share, width), lambda i, bit: (i, 1 - bit[0], 0, 0))
     out_at = pl.BlockSpec((None, share, width), lambda i, bit: (i, 0, 0))
     return pl.pallas_call(
-        combine_kernel,
+        functools.partial(combine_kernel, len(values)),
         grid_spec=pltpu.PrefetchScalarGridSpec(
             num_scalar_prefetch=1,
             grid=(count // 2,),
-            in_specs=[own_at, own_at, other_at, other_at],
+            in_specs=[own_at] * len(values) + [other_at] * len(values),
             out_specs=[out_at, out_at],
         ),
         out_shape=[
             jax.ShapeDtypeStruct((count // 2, share, width), F32),
             jax.ShapeDtypeStruct((count // 2, share, width), BF16),
         ],
-        compiler_params=params(),
+        compiler_params=params(16),
         cost_estimate=cost(count * share * width, 9 * count * share * width),
         name="combine",
-    )(bit, kept, received, kept, received)
-
-
-def proto_gradient_kernel(index_ref, own_dscore_ref, other_dscore_ref, own_unit_ref, other_unit_ref, own_ref, sent_ref):
+    )(bit, *values, *values)
+
+
+def proto_gradient_kernel(index_ref, *refs):
     del index_ref
-    rows = own_dscore_ref.shape[0]
-    part = own_unit_ref.shape[-1]
+    dscore_refs, unit_refs, own_ref, sent_ref = refs[:4], refs[4:8], refs[8], refs[9]
     both = (((0,), (0,)), ((), ()))
-    total = lax.dot_general(
-        own_dscore_ref[...], own_unit_ref[...].reshape(rows, part), both, preferred_element_type=F32
-    ) + lax.dot_general(
-        other_dscore_ref[...], other_unit_ref[...].reshape(rows, part), both, preferred_element_type=F32
-    )
+    total = None
+    for dscore_ref, unit_ref in zip(dscore_refs, unit_refs):
+        rows, part = dscore_ref.shape[0], unit_ref.shape[-1]
+        term = lax.dot_general(
+            dscore_ref[...], unit_ref[...].reshape(rows, part), both, preferred_element_type=F32
+        )
+        total = term if total is None else total + term
     sent_ref[...] = total.astype(BF16)
     own_ref[...] = total
 
 
-def proto_gradient(index, own_dscore, other_dscore, unit, batch_size):
-    places, share, protos = own_dscore.shape
+def proto_gradient(index, dscores, unit, batch_size):
+    half, share, protos = dscores[0].shape
     width = unit.shape[1]
     part = width // batch_size
-    rows = places * share
+    rows = half * share
     last = batch_size - 1
-    unit = unit.reshape(places, 2, share, width)
+    unit = unit.reshape(half, 2, 2, share, width)
     dscore_at = pl.BlockSpec((rows, protos), lambda i, index: (0, 0), pipeline_mode=pl.Buffered(1))
+
+    def unit_at(low, core):
+        return pl.BlockSpec(
+            (half, None, None, share, part),
+            lambda i, index: (0, index[1] ^ low, index[2] ^ core, 0, index[0] ^ (last - i)),
+        )
+
     return pl.pallas_call(
         proto_gradient_kernel,
         grid_spec=pltpu.PrefetchScalarGridSpec(
             num_scalar_prefetch=1,
             grid=(batch_size,),
-            in_specs=[
-                dscore_at,
-                dscore_at,
-                pl.BlockSpec((places, None, share, part), lambda i, index: (0, index[1], 0, index[0] ^ (last - i))),
-                pl.BlockSpec((places, None, share, part), lambda i, index: (0, 1 - index[1], 0, index[0] ^ (last - i))),
-            ],
+            in_specs=[dscore_at] * 4 + [unit_at(1, 1), unit_at(1, 0), unit_at(0, 1), unit_at(0, 0)],
             out_specs=[
                 pl.BlockSpec((protos, part), lambda i, index: (0, 0)),
                 pl.BlockSpec((None, protos, part), lambda i, index: (last - i, 0, 0)),
@@ -464,10 +499,10 @@
             jax.ShapeDtypeStruct((protos, part), F32),
             jax.ShapeDtypeStruct((batch_size, protos, part), BF16),
         ],
-        compiler_params=params(),
-        cost_estimate=cost(4 * rows * protos * width, 12 * MIB),
+        compiler_params=params(32),
+        cost_estimate=cost(MIB, MIB),
         name="proto_gradient",
-    )(index, own_dscore.reshape(rows, protos), other_dscore.reshape(rows, protos), unit, unit)
+    )(index, *[in_vmem(dscore.reshape(rows, protos)) for dscore in dscores], *[unit] * 4)
 
 
 def embed_gradient_kernel(index_ref, embeddings_ref, own_ref, received_ref, out_ref):
@@ -497,6 +532,9 @@
     )(index, embeddings, own, received)
 
 
+PLACE = ("high", "low")
+
+
 def swap(value, axis, distance):
     size = lax.axis_size(axis)
     return lax.ppermute(value, axis, [(i, i ^ distance) for i in range(size)])
@@ -510,7 +548,7 @@
 
 
 def proto_parts_of(value):
-    return parts_of(value + swap(value, "core", 1), "place")
+    return parts_of(value + swap(value, "core", 1), PLACE)
 
 
 def scalar(value):
@@ -521,19 +559,21 @@
     row_count, width = embeddings.shape
     proto_count = prototypes.shape[0]
     batch_size = lax.axis_size("batch")
-    places = lax.axis_size("place")
+    places = lax.axis_size(PLACE)
     proto_size = 2 * places
     total_rows = row_count * batch_size
     centroids = proto_count * proto_size
     share = row_count // proto_size
     batch_index = lax.axis_index("batch")
-    place = lax.axis_index("place")
+    low = lax.axis_index("low")
+    place = 2 * lax.axis_index("high") + low
     core = lax.axis_index("core")
     proto_index = 2 * place + core
 
-    half = row_count // 2
-    own = own_rows(embeddings, scalar(core * (half // OWN_BLOCK)), OWN_BLOCK, half // OWN_BLOCK)
-    table = lax.all_gather(own, ("batch", "core"), axis=0, tiled=True)
+    quarter = row_count // 4
+    steps = quarter // OWN_BLOCK
+    own = own_rows(embeddings, scalar((2 * low + core) * steps), OWN_BLOCK, steps)
+    table = lax.all_gather(own, ("batch", "low", "core"), axis=0, tiled=True)
 
     unit, wnorm, scores, expo, zsum, columns = scores_of(embeddings, prototypes, share)
     columns = parts_of(columns, "batch")
@@ -543,29 +583,43 @@
 
     first, second = partner_pass(partners[:, 0], partners[:, 1], table, wnorm)
     row_totals = proto_parts_of(partner_row_pass(columns, zsum, first, second, centroids))
-    shared = (columns, row_totals, first, second, scores, wnorm, centroids, total_rows, proto_size)
-    other_gunit, other_dscore, other_loss = gradients(scalar(1 - core), *shared, BF16)
-    received = swap(other_gunit, "core", 1)
-    kept, own_dscore, own_loss = gradients(scalar(core), *shared, F32)
-    loss = functools.reduce(jnp.add, parts_of(own_loss + other_loss, "batch"))
-
-    bit = 0
+    others = (scores, wnorm, centroids, total_rows, proto_size)
+
+    def quarter_of(low_bit, core_bit, dtype):
+        where = jnp.stack([low_bit, core_bit]).astype(jnp.int32)
+        return gradients(where, columns, row_totals, first, second, *others, dtype)
+
+    gunit, dscore_a, loss_a = quarter_of(1 - low, 1 - core, BF16)
+    received = swap(gunit, "core", 1)
+    kept, dscore_b, loss_b = quarter_of(1 - low, core, F32)
+    sent = add_blocks([kept, received], BF16)
+    sent, first, second = lax.optimization_barrier((sent, first, second))
+    from_neighbor = swap(sent, PLACE, 1)
+
+    gunit, dscore_c, loss_c = quarter_of(low, 1 - core, BF16)
+    received = swap(gunit, "core", 1)
+    kept, dscore_d, loss_d = quarter_of(low, core, F32)
+    grad_proto, proto_sent = proto_gradient(
+        jnp.stack([batch_index, low, core]).astype(jnp.int32),
+        (dscore_a, dscore_b, dscore_c, dscore_d),
+        unit,
+        batch_size,
+    )
+    kept, grad_proto, proto_sent = lax.optimization_barrier((kept, grad_proto, proto_sent))
+
+    loss = loss_a + loss_b + loss_c + loss_d
+    values = [kept, received, from_neighbor]
+    bit = 1
     while (1 << bit) < places:
-        kept, sent = combine(scalar((place >> bit) % 2), kept, received)
-        if bit == 0:
-            sent, own_dscore, other_dscore, loss = lax.optimization_barrier((sent, own_dscore, other_dscore, loss))
-            received = swap(sent, "place", 1)
-            grad_proto, proto_sent = proto_gradient(
-                jnp.stack([batch_index, core]).astype(jnp.int32), own_dscore, other_dscore, unit, batch_size
-            )
-            kept, grad_proto, proto_sent = lax.optimization_barrier((kept, grad_proto, proto_sent))
-            loss = loss + swap(loss, "core", 1)
-        else:
+        kept, sent = combine(scalar((place >> bit) % 2), values)
+        if bit == 1:
             sent, loss = lax.optimization_barrier((sent, loss))
-            received = swap(sent, "place", 1 << bit)
-        loss = loss + swap(loss, "place", 1 << bit)
+            loss = functools.reduce(jnp.add, parts_of(loss, "batch"))
+            loss, proto_sent = lax.optimization_barrier((loss, proto_sent))
+        values = [kept, swap(sent, PLACE, 1 << bit)]
         bit += 1
-    grad_embed = embed_gradient(scalar(proto_index), embeddings, kept[0], received[0])
+    grad_embed = embed_gradient(scalar(proto_index), embeddings, *[value[0] for value in values])
+    loss = functools.reduce(jnp.add, proto_parts_of(loss))
     loss = loss[0, 0] / total_rows
 
     for distance in range(batch_size - 1, 0, -1):
@@ -576,12 +630,12 @@
 
 def solution(mesh):
     batch_size, proto_size = mesh.shape["batch"], mesh.shape["proto"]
-    devices = mesh.devices.reshape(batch_size, proto_size // 2, 2)
-    proto = ("place", "core")
+    devices = mesh.devices.reshape(batch_size, proto_size // 4, 2, 2)
+    proto = ("high", "low", "core")
     return jax.shard_map(
         on_device,
-        mesh=jax.sharding.Mesh(devices, ("batch", "place", "core")),
+        mesh=jax.sharding.Mesh(devices, ("batch",) + proto),
         in_specs=(P("batch", None), P(proto, None), P("batch", None)),
-        out_specs=(P(), P(proto, "batch"), P(("batch", "place", "core"), None)),
+        out_specs=(P(), P(proto, "batch"), P(("batch",) + proto, None)),
         check_vma=False,
     )

time: 243 us -> 230 us (0.947)
  Pallas kernels: 100 us -> 64 us
  waiting for transfers between devices: 73.6 us -> 90.3 us
  local copies, waits for them, and re-layouts: 9.93 us -> 22.8 us
  other arithmetic: 5.66 us -> 1.46 us
    all_gather x1, waiting for transfers between devices: 23.7 us -> 38.6 us  [on_device(): table = lax.all_gather(own, ('batch', 'low', 'core'), axis=0, tiled=True)]
    unnamed x54 -> x40, local copies, waits for them, and re-layouts: 6.77 us -> 21.6 us
    pallas_call x3, Pallas kernels: 22.1 us -> 12.1 us  [the longest x1 9.3 us: scores_of(): pl.pallas_call(scores_kernel, grid=(rows // share // 2,), in_specs=[pl.Bl...]
    pallas_call x2 -> x4, Pallas kernels: 19.5 us -> 13.1 us  [gradients(): pl.pallas_call(functools.partial(gradient_kernel, count, total, heat_scal...]
    pallas_call x2, Pallas kernels: 6.52 us -> 1.67 us  [column_pass(): pl.pallas_call(functools.partial(column_kernel, count, len(row_totals)),...]
    pallas_call x2, Pallas kernels: 7.1 us -> 2.74 us  [row_pass(): pl.pallas_call(functools.partial(row_kernel, count, len(columns)), grid=(...]
    pallas_call x1, Pallas kernels: 9.96 us -> 6.97 us  [proto_gradient(): pl.pallas_call(proto_gradient_kernel, grid_spec=pltpu.PrefetchScalarGridS...]
    pallas_call x1, Pallas kernels: 4.98 us -> 2.04 us  [partner_row_pass(): pl.pallas_call(functools.partial(partner_row_kernel, count, len(columns))...]
  transfers between devices with their start and end apart: 34 -> 36, of which waited for: 23 -> 23; matrix products, arithmetic and copies ran while one was open for 3% -> 1% of each run, Pallas kernels for 31% -> 22%
where the time goes in v5:
time: 230 us
  waiting for transfers between devices  90.3 us (39%)
  Pallas kernels  64 us (28%)
  starting transfers between devices  35.7 us (16%)
  local copies, waits for them, and re-layouts  22.8 us (10%)
  between operations  15.6 us (7%)
    ppermute x35, waiting for transfers between devices, swap(): return lax.ppermute(value, axis, [(i, i ^ distance) for i in range(size)])  51.6 us
    all_gather x1, waiting for transfers between devices, on_device(): table = lax.all_gather(own, ('batch', 'low', 'core'), axis=0, tiled=True)  38.6 us
    ppermute x35, starting transfers between devices, swap(): return lax.ppermute(value, axis, [(i, i ^ distance) for i in range(size)])  35.6 us
    unnamed x40, local copies, waits for them, and re-layouts  21.6 us
    pallas_call x1, Pallas kernels, partner_pass(): pl.pallas_call(partner_kernel, grid_spec=pltpu.PrefetchScalarGridSpec(num...  19.8 us
    pallas_call x4, Pallas kernels, gradients(): pl.pallas_call(functools.partial(gradient_kernel, count, total, heat_scal...  13.1 us
    pallas_call x1, Pallas kernels, scores_of(): pl.pallas_call(scores_kernel, grid=(rows // share // 2,), in_specs=[pl.Bl...  9.3 us
    pallas_call x1, Pallas kernels, proto_gradient(): pl.pallas_call(proto_gradient_kernel, grid_spec=pltpu.PrefetchScalarGridS...  6.97 us
  transfers between devices with their start and end apart: 36, of which 23 were waited for; matrix products, arithmetic and copies ran while one was open for 1% of the time, Pallas kernels for 22%

profile of v5, /device:TPU:0, one launch (start us, length us, event | category | flops | bytes accessed | tf_op | source)
XLA Modules:
  0.0 229.7 jit_solution(8562073712080493857)
XLA Ops:
  7.2 2.6 %own_rows.1 = bf16[512,8,128]{2,1,0:T(8,128)(2,1)} custom-call(s32[1]{0:T(128)} %bitcast.5.index_ref, bf16[2048,1024]{1,0:T(8,128)(2,1)} %embeddings_ref.5), custom_call_target="tpu_custom_call" | custom-call | tf_op jit(solution)/shard_map/own_rows/pallas_call | solution.py:78
  9.9 2.2 copy-done.10
  13.6 9.3 %scores.1 = (bf16[2048,1024]{1,0:T(8,128)(2,1)S(1)}, bf16[1024,1024]{1,0:T(8,128)(2,1)S(1)}, f32[2048,1024]{1,0:T(8,128)}, bf16[2048,1024]{1,0:T(8,128)(2,1)S(1)...) custom-call(bf16[2048,1024]{1,0:T(8,128)(2,1)S(1)} %copy-done.10, bf16[1024,1024]{1,0:T(8,128)(2,1)S(1)} %copy-done.18), custom_call_target="tpu_custom_call" | custom-call | flops 4294967296 | bytes 23068672 | tf_op jit(solution)/shard_map/scores/pallas_call | solution.py:127
  22.9 2.9 %collective-permute-start = (f32[1,1024]{1,0:T(1,128)S(1)}, f32[1,1024]{1,0:T(1,128)S(1)}, u32[]{:S(2)}, u32[]{:S(2)}) collective-permute-start(f32[1,1024]{1,0:T(1,128)S(1)} %get-tuple-element.37.refs_0_), channel_id=1, source_target_pairs={{0,8},{8,0},{16,24},{24,16},{1,9},{9,1},{17,25},{25,17},{2,10},{10... | collective-permute-start | bytes 12296 | tf_op jit(solution)/shard_map/ppermute | solution.py:540
  27.5 2.0 collective-permute-done.1.refs_2_
  29.5 2.5 %collective-permute-done.2.refs_3_ = f32[1,1024]{1,0:T(1,128)S(1)} collective-permute-done((f32[1,1024]{1,0:T(1,128)S(1)}, f32[1,1024]{1,0:T(1,128)S(1)}, u32[]{:S(2)}, u32[]{:S(2)}) %collective-permute-start.2) | collective-permute-done | bytes 4128 | tf_op jit(solution)/shard_map/ppermute | solution.py:540
  36.3 2.6 %collective-permute-start.5 = (f32[1,2048]{1,0:T(1,128)S(1)}, f32[1,2048]{1,0:T(1,128)S(1)}, u32[]{:S(2)}, u32[]{:S(2)}) collective-permute-start(f32[1,2048]{1,0:T(1,128)S(1)} %add.63.refs_0_), channel_id=1, source_target_pairs={{0,4},{2,6},{4,0},{6,2},{1,5},{3,7},{5,1},{7,3},{8,12},{10,14},{12... | collective-permute-start | bytes 24584 | tf_op jit(solution)/shard_map/ppermute | solution.py:540
  39.1 1.8 collective-permute-done.5.refs_2_
  40.9 3.5 %collective-permute-done.6.refs_3_ = f32[1,2048]{1,0:T(1,128)S(1)} collective-permute-done((f32[1,2048]{1,0:T(1,128)S(1)}, f32[1,2048]{1,0:T(1,128)S(1)}, u32[]{:S(2)}, u32[]{:S(2)}) %collective-permute-start.6) | collective-permute-done | bytes 8224 | tf_op jit(solution)/shard_map/ppermute | solution.py:540
  46.3 2.5 %collective-permute-start.9 = (f32[1,1024]{1,0:T(1,128)S(1)}, f32[1,1024]{1,0:T(1,128)S(1)}, u32[]{:S(2)}, u32[]{:S(2)}) collective-permute-start(f32[1,1024]{1,0:T(1,128)S(1)} %column_pass.2.refs_0_), channel_id=1, source_target_pairs={{0,24},{8,16},{16,8},{24,0},{1,25},{9,17},{17,9},{25,1},{2,26},{10... | collective-permute-start | bytes 12296 | tf_op jit(solution)/shard_map/ppermute | solution.py:540
  54.2 3.7 %collective-permute-start.13 = (f32[1,2048]{1,0:T(1,128)S(1)}, f32[1,2048]{1,0:T(1,128)S(1)}, u32[]{:S(2)}, u32[]{:S(2)}) collective-permute-start(f32[1,2048]{1,0:T(1,128)S(1)} %add.64.refs_0_), channel_id=1, source_target_pairs={{0,6},{2,4},{4,2},{6,0},{1,7},{3,5},{5,3},{7,1},{8,14},{10,12},{12... | collective-permute-start | bytes 24584 | tf_op jit(solution)/shard_map/ppermute | solution.py:540
  64.4 38.6 %all-gather.2.cloned.1.call-done.source_ref = bf16[8192,8,128]{2,1,0:T(8,128)(2,1)} async-done(((bf16[512,8,128]{2,1,0:T(8,128)(2,1)}), bf16[8192,8,128]{2,1,0:T(8,128)(2,1)}) %all-gather.2.cloned.1.call-update) | async-done | bytes 16777232 | tf_op jit(solution)/shard_map/all_gather | solution.py:576
  103.0 19.8 %partner_scores.1 = (bf16[2048,1024]{1,0:T(8,128)(2,1)S(1)}, bf16[2048,1024]{1,0:T(8,128)(2,1)S(1)}) custom-call(s32[2048]{0:T(1024)S(1)} %bitcast.79, s32[2048]{0:T(1024)S(1)} %bitcast.78, bf16[8192,8,128]{2,1,0:T(8,128)(2,1)} %all-gather.2.cloned.1.call-done.source_ref, bf16[1024,1024]{1,0:T(8,128)(2,1)S(1)} %get-tuple-element.40.wnorm_ref.refs_11_), custom_call_target="tpu_custom_call" | custom-call | flops 8589934592 | bytes 29360128 | tf_op jit(solution)/shard_map/partner_scores/pallas_call | solution.py:265
  122.9 2.0 partner_row_pass.1
  128.4 2.4 %collective-permute-start.19 = (f32[2,4,3,256]{3,2,1,0:T(4,128)S(1)}, f32[2,4,3,256]{3,2,1,0:T(4,128)S(1)}, u32[]{:S(2)}, u32[]{:S(2)}) collective-permute-start(f32[2,4,3,256]{3,2,1,0:T(4,128)S(1)} %add.66), channel_id=1, source_target_pairs={{0,4},{2,6},{4,0},{6,2},{1,5},{3,7},{5,1},{7,3},{8,12},{10,14},{12... | collective-permute-start | bytes 73736 | tf_op jit(solution)/shard_map/ppermute | solution.py:540
  133.2 3.3 %collective-permute-done.20 = f32[2,4,3,256]{3,2,1,0:T(4,128)S(1)} collective-permute-done((f32[2,4,3,256]{3,2,1,0:T(4,128)S(1)}, f32[2,4,3,256]{3,2,1,0:T(4,128)S(1)}, u32[]{:S(2)}, u32[]{:S(2)}) %collective-permute-start.20) | collective-permute-done | bytes 24608 | tf_op jit(solution)/shard_map/ppermute | solution.py:540
  136.5 2.2 copy-done.1
  138.7 2.2 copy-done.4
  140.9 3.4 %copy-done.6 = f32[2048,1024]{1,0:T(8,128)S(1)} copy-done((f32[2048,1024]{1,0:T(8,128)S(1)}, f32[2048,1024]{1,0:T(8,128)}, u32[]{:S(2)}) %copy-start.6) | copy-done | bytes 8388632
  144.2 3.0 %gradients.5 = (bf16[2,256,1024]{2,1,0:T(8,128)(2,1)S(1)}, bf16[2,256,1024]{2,1,0:T(8,128)(2,1)S(1)}, f32[1,128]{1,0:T(1,128)S(1)}) custom-call(s32[2]{0:T(128)S(1)} %get-tuple-element.79.core_ref, f32[1,1024]{1,0:T(1,128)S(1)} %column_pass.3.refs_0_, f32[1,1024]{1,0:T(1,128)S(1)} %collective-permute-done.14.refs_1_, ...), custom_call_target="tpu_custom_call" | custom-call | flops 1048576 | bytes 1048576 | tf_op jit(solution)/shard_map/gradients/pallas_call | solution.py:374
  147.5 3.0 %gradients.4 = (f32[2,256,1024]{2,1,0:T(8,128)S(1)}, bf16[2,256,1024]{2,1,0:T(8,128)(2,1)S(1)}, f32[1,128]{1,0:T(1,128)S(1)}) custom-call(s32[2]{0:T(128)S(1)} %get-tuple-element.76.core_ref, f32[1,1024]{1,0:T(1,128)S(1)} %column_pass.3.refs_0_, f32[1,1024]{1,0:T(1,128)S(1)} %collective-permute-done.14.refs_1_, ...), custom_call_target="tpu_custom_call" | custom-call | flops 1048576 | bytes 1048576 | tf_op jit(solution)/shard_map/gradients/pallas_call | solution.py:374
  151.8 4.0 %gradients.7 = (bf16[2,256,1024]{2,1,0:T(8,128)(2,1)}, bf16[2,256,1024]{2,1,0:T(8,128)(2,1)S(1)}, f32[1,128]{1,0:T(1,128)S(1)}) custom-call(s32[2]{0:T(128)S(1)} %get-tuple-element.78.core_ref, f32[1,1024]{1,0:T(1,128)S(1)} %column_pass.3.refs_0_, f32[1,1024]{1,0:T(1,128)S(1)} %collective-permute-done.14.refs_1_, ...), custom_call_target="tpu_custom_call" | custom-call | flops 1048576 | bytes 1048576 | tf_op jit(solution)/shard_map/gradients/pallas_call | solution.py:374
  157.4 2.2 copy-done.2
  159.6 2.2 copy-done.5
  161.8 3.4 %copy-done.7 = f32[2048,1024]{1,0:T(8,128)S(1)} copy-done((f32[2048,1024]{1,0:T(8,128)S(1)}, f32[2048,1024]{1,0:T(8,128)}, u32[]{:S(2)}) %copy-start.7) | copy-done | bytes 8388632
  165.2 3.0 %gradients.6 = (f32[2,256,1024]{2,1,0:T(8,128)S(1)}, bf16[2,256,1024]{2,1,0:T(8,128)(2,1)S(1)}, f32[1,128]{1,0:T(1,128)S(1)}) custom-call(s32[2]{0:T(128)S(1)} %get-tuple-element.77.core_ref, f32[1,1024]{1,0:T(1,128)S(1)} %column_pass.3.refs_0_, f32[1,1024]{1,0:T(1,128)S(1)} %collective-permute-done.14.refs_1_, ...), custom_call_target="tpu_custom_call" | custom-call | flops 1048576 | bytes 1048576 | tf_op jit(solution)/shard_map/gradients/pallas_call | solution.py:374
  168.3 7.0 %proto_gradient.1 = (f32[1024,256]{1,0:T(8,128)S(1)}, bf16[4,1024,256]{2,1,0:T(8,128)(2,1)S(1)}) custom-call(s32[3]{0:T(128)S(1)} %pad_add_fusion.index_ref, bf16[512,1024]{1,0:T(8,128)(2,1)S(1)} %bitcast.57, bf16[512,1024]{1,0:T(8,128)(2,1)S(1)} %bitcast.58, bf16[512,1024]{1,0:T(8,128)(2,1)S(1)} %bitcast.59, bf16[512,1024]{1,0:T(8,128)(2,1)S(1)} %bitcast.60, ...), custom_call_target="tpu_custom_call" | custom-call | flops 1048576 | bytes 1048576 | tf_op jit(solution)/shard_map/proto_gradient/pallas_call | solution.py:487
  175.3 7.4 %collective-permute-done.23 = bf16[2,256,1024]{2,1,0:T(8,128)(2,1)} collective-permute-done((bf16[2,256,1024]{2,1,0:T(8,128)(2,1)}, bf16[2,256,1024]{2,1,0:T(8,128)(2,1)}, u32[]{:S(2)}, u32[]{:S(2)}) %collective-permute-start.23) | collective-permute-done | bytes 1048608 | tf_op jit(solution)/shard_map/ppermute | solution.py:540
  197.0 3.3 %collective-permute-done.28 = f32[1,128]{1,0:T(1,128)S(1)} collective-permute-done((f32[1,128]{1,0:T(1,128)S(1)}, f32[1,128]{1,0:T(1,128)S(1)}, u32[]{:S(2)}, u32[]{:S(2)}) %collective-permute-start.28) | collective-permute-done | bytes 544 | tf_op jit(solution)/shard_map/ppermute | solution.py:540
  201.5 10.7 %collective-permute-done.29 = f32[1,128]{1,0:T(1,128)S(1)} collective-permute-done((f32[1,128]{1,0:T(1,128)S(1)}, f32[1,128]{1,0:T(1,128)S(1)}, u32[]{:S(2)}, u32[]{:S(2)}) %collective-permute-start.29) | collective-permute-done | bytes 544 | tf_op jit(solution)/shard_map/ppermute | solution.py:540
  213.4 4.2 %collective-permute-done.30 = f32[1,128]{1,0:T(1,128)S(1)} collective-permute-done((f32[1,128]{1,0:T(1,128)S(1)}, f32[1,128]{1,0:T(1,128)S(1)}, u32[]{:S(2)}, u32[]{:S(2)}) %collective-permute-start.30) | collective-permute-done | bytes 544 | tf_op jit(solution)/shard_map/ppermute | solution.py:540
  217.6 2.9 %embed_gradient.1 = f32[256,1024]{1,0:T(8,128)} custom-call(s32[1]{0:T(128)} %bitcast.30.index_ref, bf16[2048,1024]{1,0:T(8,128)(2,1)} %embeddings_ref.5, f32[256,1024]{1,0:T(8,128)} %bitcast.61, bf16[256,1024]{1,0:T(8,128)(2,1)} %bitcast.32.received_ref), custom_call_target="tpu_custom_call" | custom-call | flops 2097152 | bytes 4194304 | tf_op jit(solution)/shard_map/embed_gradient/pallas_call | solution.py:520
  (110 shorter events, 48.1 us)
Async XLA Ops:
  7.2 95.9 %all-gather.2.cloned.1.call-start = ((), (), s32[]{:S(2)}) async-start(), calls=%async_computation | async-start | bytes 17825792 | tf_op jit(solution)/shard_map/all_gather | solution.py:576
  22.9 4.6 %collective-permute-start = (f32[1,1024]{1,0:T(1,128)S(1)}, f32[1,1024]{1,0:T(1,128)S(1)}, u32[]{:S(2)}, u32[]{:S(2)}) collective-permute-start(f32[1,1024]{1,0:T(1,128)S(1)} %get-tuple-element.37.refs_0_), channel_id=1, source_target_pairs={{0,8},{8,0},{16,24},{24,16},{1,9},{9,1},{17,25},{25,17},{2,10},{10... | collective-permute-start | bytes 12296 | tf_op jit(solution)/shard_map/ppermute | solution.py:540
  25.9 3.6 %collective-permute-start.1 = (f32[1,1024]{1,0:T(1,128)S(1)}, f32[1,1024]{1,0:T(1,128)S(1)}, u32[]{:S(2)}, u32[]{:S(2)}) collective-permute-start(f32[1,1024]{1,0:T(1,128)S(1)} %get-tuple-element.37.refs_0_), channel_id=1, source_target_pairs={{0,16},{8,24},{16,0},{24,8},{1,17},{9,25},{17,1},{25,9},{2,18},{10... | collective-permute-start | bytes 12296 | tf_op jit(solution)/shard_map/ppermute | solution.py:540
  27.4 4.6 %collective-permute-start.2 = (f32[1,1024]{1,0:T(1,128)S(1)}, f32[1,1024]{1,0:T(1,128)S(1)}, u32[]{:S(2)}, u32[]{:S(2)}) collective-permute-start(f32[1,1024]{1,0:T(1,128)S(1)} %get-tuple-element.37.refs_0_), channel_id=1, source_target_pairs={{0,24},{8,16},{16,8},{24,0},{1,25},{9,17},{17,9},{25,1},{2,26},{10... | collective-permute-start | bytes 12296 | tf_op jit(solution)/shard_map/ppermute | solution.py:540
  34.6 4.5 %collective-permute-start.4 = (f32[1,2048]{1,0:T(1,128)S(1)}, f32[1,2048]{1,0:T(1,128)S(1)}, u32[]{:S(2)}, u32[]{:S(2)}) collective-permute-start(f32[1,2048]{1,0:T(1,128)S(1)} %add.63.refs_0_), channel_id=1, source_target_pairs={{0,2},{2,0},{4,6},{6,4},{1,3},{3,1},{5,7},{7,5},{8,10},{10,8},{12,... | collective-permute-start | bytes 24584 | tf_op jit(solution)/shard_map/ppermute | solution.py:540
  36.3 4.7 %collective-permute-start.5 = (f32[1,2048]{1,0:T(1,128)S(1)}, f32[1,2048]{1,0:T(1,128)S(1)}, u32[]{:S(2)}, u32[]{:S(2)}) collective-permute-start(f32[1,2048]{1,0:T(1,128)S(1)} %add.63.refs_0_), channel_id=1, source_target_pairs={{0,4},{2,6},{4,0},{6,2},{1,5},{3,7},{5,1},{7,3},{8,12},{10,14},{12... | collective-permute-start | bytes 24584 | tf_op jit(solution)/shard_map/ppermute | solution.py:540
  38.8 5.6 %collective-permute-start.6 = (f32[1,2048]{1,0:T(1,128)S(1)}, f32[1,2048]{1,0:T(1,128)S(1)}, u32[]{:S(2)}, u32[]{:S(2)}) collective-permute-start(f32[1,2048]{1,0:T(1,128)S(1)} %add.63.refs_0_), channel_id=1, source_target_pairs={{0,6},{2,4},{4,2},{6,0},{1,7},{3,5},{5,3},{7,1},{8,14},{10,12},{12... | collective-permute-start | bytes 24584 | tf_op jit(solution)/shard_map/ppermute | solution.py:540
  45.3 3.7 %collective-permute-start.7 = (f32[1,1024]{1,0:T(1,128)S(1)}, f32[1,1024]{1,0:T(1,128)S(1)}, u32[]{:S(2)}, u32[]{:S(2)}) collective-permute-start(f32[1,1024]{1,0:T(1,128)S(1)} %column_pass.2.refs_0_), channel_id=1, source_target_pairs={{0,8},{8,0},{16,24},{24,16},{1,9},{9,1},{17,25},{25,17},{2,10},{10... | collective-permute-start | bytes 12296 | tf_op jit(solution)/shard_map/ppermute | solution.py:540
  45.8 3.6 %collective-permute-start.8 = (f32[1,1024]{1,0:T(1,128)S(1)}, f32[1,1024]{1,0:T(1,128)S(1)}, u32[]{:S(2)}, u32[]{:S(2)}) collective-permute-start(f32[1,1024]{1,0:T(1,128)S(1)} %column_pass.2.refs_0_), channel_id=1, source_target_pairs={{0,16},{8,24},{16,0},{24,8},{1,17},{9,25},{17,1},{25,9},{2,18},{10... | collective-permute-start | bytes 12296 | tf_op jit(solution)/shard_map/ppermute | solution.py:540
  46.3 4.6 %collective-permute-start.9 = (f32[1,1024]{1,0:T(1,128)S(1)}, f32[1,1024]{1,0:T(1,128)S(1)}, u32[]{:S(2)}, u32[]{:S(2)}) collective-permute-start(f32[1,1024]{1,0:T(1,128)S(1)} %column_pass.2.refs_0_), channel_id=1, source_target_pairs={{0,24},{8,16},{16,8},{24,0},{1,25},{9,17},{17,9},{25,1},{2,26},{10... | collective-permute-start | bytes 12296 | tf_op jit(solution)/shard_map/ppermute | solution.py:540
  53.5 4.5 %collective-permute-start.11 = (f32[1,2048]{1,0:T(1,128)S(1)}, f32[1,2048]{1,0:T(1,128)S(1)}, u32[]{:S(2)}, u32[]{:S(2)}) collective-permute-start(f32[1,2048]{1,0:T(1,128)S(1)} %add.64.refs_0_), channel_id=1, source_target_pairs={{0,2},{2,0},{4,6},{6,4},{1,3},{3,1},{5,7},{7,5},{8,10},{10,8},{12,... | collective-permute-start | bytes 24584 | tf_op jit(solution)/shard_map/ppermute | solution.py:540
  53.6 4.7 %collective-permute-start.12 = (f32[1,2048]{1,0:T(1,128)S(1)}, f32[1,2048]{1,0:T(1,128)S(1)}, u32[]{:S(2)}, u32[]{:S(2)}) collective-permute-start(f32[1,2048]{1,0:T(1,128)S(1)} %add.64.refs_0_), channel_id=1, source_target_pairs={{0,4},{2,6},{4,0},{6,2},{1,5},{3,7},{5,1},{7,3},{8,12},{10,14},{12... | collective-permute-start | bytes 24584 | tf_op jit(solution)/shard_map/ppermute | solution.py:540
  54.2 5.8 %collective-permute-start.13 = (f32[1,2048]{1,0:T(1,128)S(1)}, f32[1,2048]{1,0:T(1,128)S(1)}, u32[]{:S(2)}, u32[]{:S(2)}) collective-permute-start(f32[1,2048]{1,0:T(1,128)S(1)} %add.64.refs_0_), channel_id=1, source_target_pairs={{0,6},{2,4},{4,2},{6,0},{1,7},{3,5},{5,3},{7,1},{8,14},{10,12},{12... | collective-permute-start | bytes 24584 | tf_op jit(solution)/shard_map/ppermute | solution.py:540
  60.8 62.0 %collective-permute-start.14 = (f32[1,1024]{1,0:T(1,128)S(1)}, f32[1,1024]{1,0:T(1,128)S(1)}, u32[]{:S(2)}, u32[]{:S(2)}) collective-permute-start(f32[1,1024]{1,0:T(1,128)S(1)} %column_pass.3.refs_0_), channel_id=1, source_target_pairs={{0,8},{8,0},{16,24},{24,16},{1,9},{9,1},{17,25},{25,17},{2,10},{10... | collective-permute-start | bytes 12296 | tf_op jit(solution)/shard_map/ppermute | solution.py:540
  62.4 60.5 %collective-permute-start.15 = (f32[1,1024]{1,0:T(1,128)S(1)}, f32[1,1024]{1,0:T(1,128)S(1)}, u32[]{:S(2)}, u32[]{:S(2)}) collective-permute-start(f32[1,1024]{1,0:T(1,128)S(1)} %column_pass.3.refs_0_), channel_id=1, source_target_pairs={{0,16},{8,24},{16,0},{24,8},{1,17},{9,25},{17,1},{25,9},{2,18},{10... | collective-permute-start | bytes 12296 | tf_op jit(solution)/shard_map/ppermute | solution.py:540
  63.9 59.0 %collective-permute-start.16 = (f32[1,1024]{1,0:T(1,128)S(1)}, f32[1,1024]{1,0:T(1,128)S(1)}, u32[]{:S(2)}, u32[]{:S(2)}) collective-permute-start(f32[1,1024]{1,0:T(1,128)S(1)} %column_pass.3.refs_0_), channel_id=1, source_target_pairs={{0,24},{8,16},{16,8},{24,0},{1,25},{9,17},{17,9},{25,1},{2,26},{10... | collective-permute-start | bytes 12296 | tf_op jit(solution)/shard_map/ppermute | solution.py:540
  127.4 4.5 %collective-permute-start.18 = (f32[2,4,3,256]{3,2,1,0:T(4,128)S(1)}, f32[2,4,3,256]{3,2,1,0:T(4,128)S(1)}, u32[]{:S(2)}, u32[]{:S(2)}) collective-permute-start(f32[2,4,3,256]{3,2,1,0:T(4,128)S(1)} %add.66), channel_id=1, source_target_pairs={{0,2},{2,0},{4,6},{6,4},{1,3},{3,1},{5,7},{7,5},{8,10},{10,8},{12,... | collective-permute-start | bytes 73736 | tf_op jit(solution)/shard_map/ppermute | solution.py:540
  128.4 4.8 %collective-permute-start.19 = (f32[2,4,3,256]{3,2,1,0:T(4,128)S(1)}, f32[2,4,3,256]{3,2,1,0:T(4,128)S(1)}, u32[]{:S(2)}, u32[]{:S(2)}) collective-permute-start(f32[2,4,3,256]{3,2,1,0:T(4,128)S(1)} %add.66), channel_id=1, source_target_pairs={{0,4},{2,6},{4,0},{6,2},{1,5},{3,7},{5,1},{7,3},{8,12},{10,14},{12... | collective-permute-start | bytes 73736 | tf_op jit(solution)/shard_map/ppermute | solution.py:540
  130.8 5.7 %collective-permute-start.20 = (f32[2,4,3,256]{3,2,1,0:T(4,128)S(1)}, f32[2,4,3,256]{3,2,1,0:T(4,128)S(1)}, u32[]{:S(2)}, u32[]{:S(2)}) collective-permute-start(f32[2,4,3,256]{3,2,1,0:T(4,128)S(1)} %add.66), channel_id=1, source_target_pairs={{0,6},{2,4},{4,2},{6,0},{1,7},{3,5},{5,3},{7,1},{8,14},{10,12},{12... | collective-permute-start | bytes 73736 | tf_op jit(solution)/shard_map/ppermute | solution.py:540
  147.3 3.2 %collective-permute-start.21 = (bf16[2,256,1024]{2,1,0:T(8,128)(2,1)S(1)}, bf16[2,256,1024]{2,1,0:T(8,128)(2,1)S(1)}, u32[]{:S(2)}, u32[]{:S(2)}) collective-permute-start(bf16[2,256,1024]{2,1,0:T(8,128)(2,1)S(1)} %get-tuple-element.45), channel_id=1, source_target_pairs={{0,1},{1,0},{2,3},{3,2},{4,5},{5,4},{6,7},{7,6},{8,9},{9,8},{10,11... | collective-permute-start | bytes 3145736 | tf_op jit(solution)/shard_map/ppermute | solution.py:540
  156.9 18.4 %collective-permute-start.22 = (bf16[2,256,1024]{2,1,0:T(8,128)(2,1)}, bf16[2,256,1024]{2,1,0:T(8,128)(2,1)S(1)}, u32[]{:S(2)}, u32[]{:S(2)}) collective-permute-start(bf16[2,256,1024]{2,1,0:T(8,128)(2,1)} %get-tuple-element.57), channel_id=1, source_target_pairs={{0,1},{1,0},{2,3},{3,2},{4,5},{5,4},{6,7},{7,6},{8,9},{9,8},{10,11... | collective-permute-start | bytes 3145736 | tf_op jit(solution)/shard_map/ppermute | solution.py:540
  157.4 25.4 %collective-permute-start.23 = (bf16[2,256,1024]{2,1,0:T(8,128)(2,1)}, bf16[2,256,1024]{2,1,0:T(8,128)(2,1)}, u32[]{:S(2)}, u32[]{:S(2)}) collective-permute-start(bf16[2,256,1024]{2,1,0:T(8,128)(2,1)} %add_blocks.1), channel_id=1, source_target_pairs={{0,2},{2,0},{4,6},{6,4},{1,3},{3,1},{5,7},{7,5},{8,10},{10,8},{12,... | collective-permute-start | bytes 3145736 | tf_op jit(solution)/shard_map/ppermute | solution.py:540
  184.3 3.6 %collective-permute-start.24 = (f32[1,128]{1,0:T(1,128)S(1)}, f32[1,128]{1,0:T(1,128)S(1)}, u32[]{:S(2)}, u32[]{:S(2)}) collective-permute-start(f32[1,128]{1,0:T(1,128)S(1)} %add_add_fusion.2), channel_id=1, source_target_pairs={{0,8},{8,0},{16,24},{24,16},{1,9},{9,1},{17,25},{25,17},{2,10},{10... | collective-permute-start | bytes 1544 | tf_op jit(solution)/shard_map/ppermute | solution.py:540
  185.8 3.5 %collective-permute-start.25 = (f32[1,128]{1,0:T(1,128)S(1)}, f32[1,128]{1,0:T(1,128)S(1)}, u32[]{:S(2)}, u32[]{:S(2)}) collective-permute-start(f32[1,128]{1,0:T(1,128)S(1)} %add_add_fusion.2), channel_id=1, source_target_pairs={{0,16},{8,24},{16,0},{24,8},{1,17},{9,25},{17,1},{25,9},{2,18},{10... | collective-permute-start | bytes 1544 | tf_op jit(solution)/shard_map/ppermute | solution.py:540
  186.4 4.4 %collective-permute-start.26 = (f32[1,128]{1,0:T(1,128)S(1)}, f32[1,128]{1,0:T(1,128)S(1)}, u32[]{:S(2)}, u32[]{:S(2)}) collective-permute-start(f32[1,128]{1,0:T(1,128)S(1)} %add_add_fusion.2), channel_id=1, source_target_pairs={{0,24},{8,16},{16,8},{24,0},{1,25},{9,17},{17,9},{25,1},{2,26},{10... | collective-permute-start | bytes 1544 | tf_op jit(solution)/shard_map/ppermute | solution.py:540
  187.8 29.8 %collective-permute-start.34 = (bf16[1,256,1024]{2,1,0:T(8,128)(2,1)S(1)}, bf16[1,256,1024]{2,1,0:T(8,128)(2,1)}, u32[]{:S(2)}, u32[]{:S(2)}) collective-permute-start(bf16[1,256,1024]{2,1,0:T(8,128)(2,1)S(1)} %get-tuple-element.70), channel_id=1, source_target_pairs={{0,4},{2,6},{4,0},{6,2},{1,5},{3,7},{5,1},{7,3},{8,12},{10,14},{12... | collective-permute-start | bytes 1572872 | tf_op jit(solution)/shard_map/ppermute | solution.py:540
  192.1 28.5 %collective-permute-start.31 = (bf16[1024,256]{1,0:T(8,128)(2,1)}, bf16[1024,256]{1,0:T(8,128)(2,1)S(1)}, u32[]{:S(2)}, u32[]{:S(2)}) collective-permute-start(bf16[1024,256]{1,0:T(8,128)(2,1)} %get-tuple-element.71), channel_id=1, source_target_pairs={{0,24},{8,16},{16,8},{24,0},{1,25},{9,17},{17,9},{25,1},{2,26},{10... | collective-permute-start | bytes 1572872 | tf_op jit(solution)/shard_map/ppermute | solution.py:540
  193.5 27.1 %collective-permute-start.32 = (bf16[1024,256]{1,0:T(8,128)(2,1)}, bf16[1024,256]{1,0:T(8,128)(2,1)S(1)}, u32[]{:S(2)}, u32[]{:S(2)}) collective-permute-start(bf16[1024,256]{1,0:T(8,128)(2,1)} %get-tuple-element.73), channel_id=1, source_target_pairs={{0,16},{8,24},{16,0},{24,8},{1,17},{9,25},{17,1},{25,9},{2,18},{10... | collective-permute-start | bytes 1572872 | tf_op jit(solution)/shard_map/ppermute | solution.py:540
  194.8 25.7 %collective-permute-start.33 = (bf16[1024,256]{1,0:T(8,128)(2,1)}, bf16[1024,256]{1,0:T(8,128)(2,1)S(1)}, u32[]{:S(2)}, u32[]{:S(2)}) collective-permute-start(bf16[1024,256]{1,0:T(8,128)(2,1)} %get-tuple-element.72), channel_id=1, source_target_pairs={{0,8},{8,0},{16,24},{24,16},{1,9},{9,1},{17,25},{25,17},{2,10},{10... | collective-permute-start | bytes 1572872 | tf_op jit(solution)/shard_map/ppermute | solution.py:540
  196.7 3.5 %collective-permute-start.28 = (f32[1,128]{1,0:T(1,128)S(1)}, f32[1,128]{1,0:T(1,128)S(1)}, u32[]{:S(2)}, u32[]{:S(2)}) collective-permute-start(f32[1,128]{1,0:T(1,128)S(1)} %add.73), channel_id=1, source_target_pairs={{0,2},{2,0},{4,6},{6,4},{1,3},{3,1},{5,7},{7,5},{8,10},{10,8},{12,... | collective-permute-start | bytes 1544 | tf_op jit(solution)/shard_map/ppermute | solution.py:540
  200.2 12.0 %collective-permute-start.29 = (f32[1,128]{1,0:T(1,128)S(1)}, f32[1,128]{1,0:T(1,128)S(1)}, u32[]{:S(2)}, u32[]{:S(2)}) collective-permute-start(f32[1,128]{1,0:T(1,128)S(1)} %add.73), channel_id=1, source_target_pairs={{0,4},{2,6},{4,0},{6,2},{1,5},{3,7},{5,1},{7,3},{8,12},{10,14},{12... | collective-permute-start | bytes 1544 | tf_op jit(solution)/shard_map/ppermute | solution.py:540
  212.2 5.3 %collective-permute-start.30 = (f32[1,128]{1,0:T(1,128)S(1)}, f32[1,128]{1,0:T(1,128)S(1)}, u32[]{:S(2)}, u32[]{:S(2)}) collective-permute-start(f32[1,128]{1,0:T(1,128)S(1)} %add.73), channel_id=1, source_target_pairs={{0,6},{2,4},{4,2},{6,0},{1,7},{3,5},{5,3},{7,1},{8,14},{10,12},{12... | collective-permute-start | bytes 1544 | tf_op jit(solution)/shard_map/ppermute | solution.py:540
  (24 other events, 78.3 us)
Sparse Core Ops, SparseCore 0:
  10.2 92.8 all-gather.1

commit v6 on v5

--- a/solution.py
+++ b/solution.py
@@ -85,7 +85,7 @@
             scratch_shapes=[pltpu.VMEM((block * groups, LANES), F32)],
         ),
         out_shape=jax.ShapeDtypeStruct((block * count, groups, LANES), BF16),
-        compiler_params=params(),
+        compiler_params=params(16),
         name="own_rows",
     )(index, embeddings)
 
@@ -147,7 +147,7 @@
             jax.ShapeDtypeStruct((2, rows // share // 2, 1, share), F32),
             jax.ShapeDtypeStruct((1, protos), F32),
         ],
-        compiler_params=params(32),
+        compiler_params=params(28),
         cost_estimate=cost(2 * rows * columns * protos, 22 * MIB, rows * protos),
         name="scores",
     )(embeddings, prototypes)
@@ -175,7 +175,7 @@
         in_specs=[pl.BlockSpec((1, protos), lambda i: (0, 0)) for _ in columns] + streams_of((block, protos)),
         out_specs=pl.BlockSpec((1, STREAMS * block), lambda i: (0, i)),
         out_shape=jax.ShapeDtypeStruct((1, rows), F32),
-        compiler_params=params(16),
+        compiler_params=params(8),
         cost_estimate=cost(2 * rows * protos, 4 * MIB),
         name="row_pass",
     )(*columns, *[in_vmem(expo)] * STREAMS)
@@ -213,7 +213,7 @@
         + streams_of((block, protos)),
         out_specs=pl.BlockSpec((1, protos), lambda i: (0, 0)),
         out_shape=jax.ShapeDtypeStruct((1, protos), F32),
-        compiler_params=params(16),
+        compiler_params=params(8),
         cost_estimate=cost(2 * rows * protos, 4 * MIB),
         name="column_pass",
     )(*row_totals, *[in_vmem(expo)] * STREAMS)
@@ -245,7 +245,8 @@
         for start in range(0, rows, CHUNK)
         for which_ref, out_ref in ((first_ref, first_expo_ref), (second_ref, second_expo_ref))
     ]
-    for (which_ref, out_ref, start), stage_ref in zip(chunks, stages):
+    for number, (which_ref, out_ref, start) in enumerate(chunks):
+        stage_ref = stages[number % 2]
         for row in range(CHUNK):
             place = which_ref[step * rows + start + row]
             stage_ref[row * groups : (row + 1) * groups, :] = table_ref[place].astype(F32)
@@ -279,10 +280,10 @@
                 pltpu.VMEM(table.shape, BF16),
                 pltpu.SemaphoreType.DMA((STREAMS,)),
             ]
-            + [pltpu.VMEM((CHUNK * groups, LANES), F32)] * 4,
+            + [pltpu.VMEM((CHUNK * groups, LANES), F32)] * 2,
         ),
         out_shape=[jax.ShapeDtypeStruct((rows, protos), BF16)] * 2,
-        compiler_params=params(32),
+        compiler_params=params(28),
         cost_estimate=cost(4 * rows * columns * protos, 28 * MIB, 2 * rows * protos),
         name="partner_scores",
     )(first, second, table, wnorm)
@@ -366,36 +367,37 @@
     width = wnorm.shape[1]
     heat_scale = count / (32.0 * SOFTMAX_HEAT)
     _, places, _, share = row_totals[0].shape
-    half = places // 2
-    group = 2
-    at = pl.BlockSpec((group, None, None, share, protos), lambda i, where: (i, where[0], where[1], 0, 0))
-    first, second, scores = [in_vmem(value.reshape(half, 2, 2, share, protos)) for value in (first, second, scores)]
-    row_totals = [value.reshape(2, half, 2, 3, share) for value in row_totals]
+    top = places // 4
+    at = pl.BlockSpec((1, None, None, None, share, protos), lambda i, where: (i, where[0], where[1], where[2], 0, 0))
+    first, second, scores = [in_vmem(value.reshape(top, 2, 2, 2, share, protos)) for value in (first, second, scores)]
+    row_totals = [value.reshape(2, top, 2, 2, 3, share) for value in row_totals]
     return pl.pallas_call(
         functools.partial(
             gradient_kernel, count, total, heat_scale, proto_size, (len(columns), len(row_totals))
         ),
         grid_spec=pltpu.PrefetchScalarGridSpec(
             num_scalar_prefetch=1,
-            grid=(half // group,),
+            grid=(top,),
             in_specs=[pl.BlockSpec((1, protos), lambda i, where: (0, 0)) for _ in columns]
             + [
-                pl.BlockSpec((None, group, None, 3, share), lambda i, where: (where[1], i, where[0], 0, 0))
+                pl.BlockSpec(
+                    (None, 1, None, None, 3, share), lambda i, where: (where[2], i, where[0], where[1], 0, 0)
+                )
                 for _ in row_totals
             ]
             + [at, at, at, pl.BlockSpec((protos, width), lambda i, where: (0, 0), pipeline_mode=pl.Buffered(1))],
             out_specs=[
-                pl.BlockSpec((group, share, width), lambda i, where: (i, 0, 0)),
-                pl.BlockSpec((group, share, protos), lambda i, where: (i, 0, 0)),
+                pl.BlockSpec((1, share, width), lambda i, where: (i, 0, 0)),
+                pl.BlockSpec((1, share, protos), lambda i, where: (i, 0, 0)),
                 pl.BlockSpec((1, LANES), lambda i, where: (0, 0)),
             ],
         ),
         out_shape=[
-            jax.ShapeDtypeStruct((half, share, width), dtype),
-            jax.ShapeDtypeStruct((half, share, protos), BF16),
+            jax.ShapeDtypeStruct((top, share, width), dtype),
+            jax.ShapeDtypeStruct((top, share, protos), BF16),
             jax.ShapeDtypeStruct((1, LANES), F32),
         ],
-        compiler_params=params(32),
+        compiler_params=params(16),
         cost_estimate=cost(MIB, MIB),
         name="gradients",
     )(where, *columns, *row_totals, first, second, scores, in_vmem(wnorm))
@@ -417,7 +419,7 @@
         in_specs=[at for _ in values],
         out_specs=at,
         out_shape=jax.ShapeDtypeStruct(values[0].shape, dtype),
-        compiler_params=params(16),
+        compiler_params=params(12),
         cost_estimate=cost(count * share * width, 8 * count * share * width),
         name="add_blocks",
     )(*values)
@@ -456,7 +458,7 @@
 
 def proto_gradient_kernel(index_ref, *refs):
     del index_ref
-    dscore_refs, unit_refs, own_ref, sent_ref = refs[:4], refs[4:8], refs[8], refs[9]
+    dscore_refs, unit_refs, own_ref, sent_ref = refs[:8], refs[8:16], refs[16], refs[17]
     both = (((0,), (0,)), ((), ()))
     total = None
     for dscore_ref, unit_ref in zip(dscore_refs, unit_refs):
@@ -470,18 +472,20 @@
 
 
 def proto_gradient(index, dscores, unit, batch_size):
-    half, share, protos = dscores[0].shape
+    top, share, protos = dscores[0].shape
     width = unit.shape[1]
     part = width // batch_size
-    rows = half * share
+    rows = top * share
     last = batch_size - 1
-    unit = unit.reshape(half, 2, 2, share, width)
+    unit = unit.reshape(top, 2, 2, 2, share, width)
     dscore_at = pl.BlockSpec((rows, protos), lambda i, index: (0, 0), pipeline_mode=pl.Buffered(1))
 
-    def unit_at(low, core):
+    def unit_at(number):
         return pl.BlockSpec(
-            (half, None, None, share, part),
-            lambda i, index: (0, index[1] ^ low, index[2] ^ core, 0, index[0] ^ (last - i)),
+            (top, None, None, None, share, part),
+            lambda i, index: (
+                0, index[1] ^ (number >> 2), index[2] ^ (number >> 1 & 1), index[3] ^ (number & 1), 0, index[0] ^ (last - i),
+            ),
         )
 
     return pl.pallas_call(
@@ -489,7 +493,7 @@
         grid_spec=pltpu.PrefetchScalarGridSpec(
             num_scalar_prefetch=1,
             grid=(batch_size,),
-            in_specs=[dscore_at] * 4 + [unit_at(1, 1), unit_at(1, 0), unit_at(0, 1), unit_at(0, 0)],
+            in_specs=[dscore_at] * 8 + [unit_at(number) for number in range(8)],
             out_specs=[
                 pl.BlockSpec((protos, part), lambda i, index: (0, 0)),
                 pl.BlockSpec((None, protos, part), lambda i, index: (last - i, 0, 0)),
@@ -499,40 +503,43 @@
             jax.ShapeDtypeStruct((protos, part), F32),
             jax.ShapeDtypeStruct((batch_size, protos, part), BF16),
         ],
-        compiler_params=params(32),
+        compiler_params=params(20),
         cost_estimate=cost(MIB, MIB),
         name="proto_gradient",
-    )(index, *[in_vmem(dscore.reshape(rows, protos)) for dscore in dscores], *[unit] * 4)
-
-
-def embed_gradient_kernel(index_ref, embeddings_ref, own_ref, received_ref, out_ref):
+    )(index, *[in_vmem(dscore.reshape(rows, protos)) for dscore in dscores], *[unit] * 8)
+
+
+def embed_gradient_kernel(index_ref, embeddings_ref, *refs):
     del index_ref
-    gunit = own_ref[...] + received_ref[...].astype(F32)
+    *part_refs, out_ref = refs
+    gunit = part_refs[0][...]
+    for ref in part_refs[1:]:
+        gunit = gunit + ref[...].astype(F32)
     hidden = embeddings_ref[...].astype(F32)
     inverse = 1.0 / jnp.sqrt(jnp.sum(hidden * hidden, axis=1, keepdims=True) + NORM_EPSILON)
     along = jnp.sum(hidden * gunit, axis=1, keepdims=True)
     out_ref[...] = inverse * gunit - hidden * (inverse * inverse * inverse * along)
 
 
-def embed_gradient(index, embeddings, own, received):
-    share, width = own.shape
+def embed_gradient(index, embeddings, values):
+    share, width = values[0].shape
     whole = pl.BlockSpec((share, width), lambda i, index: (0, 0))
     return pl.pallas_call(
         embed_gradient_kernel,
         grid_spec=pltpu.PrefetchScalarGridSpec(
             num_scalar_prefetch=1,
             grid=(1,),
-            in_specs=[pl.BlockSpec((share, width), lambda i, index: (index[0], 0)), whole, whole],
+            in_specs=[pl.BlockSpec((share, width), lambda i, index: (index[0], 0))] + [whole for _ in values],
             out_specs=whole,
         ),
         out_shape=jax.ShapeDtypeStruct((share, width), F32),
-        compiler_params=params(),
+        compiler_params=params(12),
         cost_estimate=cost(8 * share * width, 4 * MIB),
         name="embed_gradient",
-    )(index, embeddings, own, received)
-
-
-PLACE = ("high", "low")
+    )(index, embeddings, *values)
+
+
+PLACE = ("top", "middle", "low")
 
 
 def swap(value, axis, distance):
@@ -566,7 +573,8 @@
     share = row_count // proto_size
     batch_index = lax.axis_index("batch")
     low = lax.axis_index("low")
-    place = 2 * lax.axis_index("high") + low
+    middle = lax.axis_index("middle")
+    place = lax.axis_index(PLACE)
     core = lax.axis_index("core")
     proto_index = 2 * place + core
 
@@ -585,53 +593,61 @@
     row_totals = proto_parts_of(partner_row_pass(columns, zsum, first, second, centroids))
     others = (scores, wnorm, centroids, total_rows, proto_size)
 
-    def quarter_of(low_bit, core_bit, dtype):
-        where = jnp.stack([low_bit, core_bit]).astype(jnp.int32)
-        return gradients(where, columns, row_totals, first, second, *others, dtype)
-
-    gunit, dscore_a, loss_a = quarter_of(1 - low, 1 - core, BF16)
-    received = swap(gunit, "core", 1)
-    kept, dscore_b, loss_b = quarter_of(1 - low, core, F32)
-    sent = add_blocks([kept, received], BF16)
-    sent, first, second = lax.optimization_barrier((sent, first, second))
-    from_neighbor = swap(sent, PLACE, 1)
-
-    gunit, dscore_c, loss_c = quarter_of(low, 1 - core, BF16)
-    received = swap(gunit, "core", 1)
-    kept, dscore_d, loss_d = quarter_of(low, core, F32)
-    grad_proto, proto_sent = proto_gradient(
-        jnp.stack([batch_index, low, core]).astype(jnp.int32),
-        (dscore_a, dscore_b, dscore_c, dscore_d),
-        unit,
-        batch_size,
-    )
-    kept, grad_proto, proto_sent = lax.optimization_barrier((kept, grad_proto, proto_sent))
-
-    loss = loss_a + loss_b + loss_c + loss_d
-    values = [kept, received, from_neighbor]
-    bit = 1
+    def after(value, *earlier):
+        return lax.optimization_barrier((value, *earlier))[0]
+
+    losses, dscores = [], {}
+
+    def part_of(number, *earlier):
+        place_bits = [middle ^ (number >> 1), low ^ (number & 1)]
+
+        def run(other, dtype):
+            where = after(jnp.stack(place_bits + [core ^ other]).astype(jnp.int32), *earlier)
+            gunit, dscores[2 * number + other], loss = gradients(
+                where, columns, row_totals, first, second, *others, dtype
+            )
+            losses.append(loss)
+            return gunit
+
+        gunit = run(1, BF16)
+        return [run(0, F32), swap(gunit, "core", 1)]
+
+    forwarded = add_blocks(part_of(3), BF16)
+    from_forwarder = swap(forwarded, PLACE, 1)
+    near = add_blocks(part_of(1, forwarded), BF16)
+    from_near = swap(near, PLACE, 1)
+    across = part_of(2, near)
+    values = part_of(0, near)
+
+    loss = functools.reduce(jnp.add, losses)
+    loss = functools.reduce(jnp.add, parts_of(loss, "batch"))
+    index = jnp.stack([batch_index, middle, low, core]).astype(jnp.int32)
+    grad_proto, proto_sent = proto_gradient(index, [dscores[number] for number in range(8)], unit, batch_size)
+    from_forwarder = after(from_forwarder, proto_sent)
+    across = add_blocks(across + [from_forwarder], BF16)
+    values += [from_near, swap(across, PLACE, 2)]
+    proto_sent = after(proto_sent, loss, across, from_near)
+
+    bit = 2
     while (1 << bit) < places:
         kept, sent = combine(scalar((place >> bit) % 2), values)
-        if bit == 1:
-            sent, loss = lax.optimization_barrier((sent, loss))
-            loss = functools.reduce(jnp.add, parts_of(loss, "batch"))
-            loss, proto_sent = lax.optimization_barrier((loss, proto_sent))
         values = [kept, swap(sent, PLACE, 1 << bit)]
         bit += 1
-    grad_embed = embed_gradient(scalar(proto_index), embeddings, *[value[0] for value in values])
-    loss = functools.reduce(jnp.add, proto_parts_of(loss))
+    grad_embed = embed_gradient(scalar(proto_index), embeddings, [value[0] for value in values])
+    loss = loss + swap(loss, "core", 1)
+    arrived = [swap(proto_sent[distance], "batch", distance) for distance in range(batch_size - 1, 0, -1)]
+    loss = functools.reduce(jnp.add, parts_of(after(loss, *arrived), PLACE))
     loss = loss[0, 0] / total_rows
-
-    for distance in range(batch_size - 1, 0, -1):
-        grad_proto = grad_proto + swap(proto_sent[distance], "batch", distance).astype(F32)
+    for block in arrived:
+        grad_proto = grad_proto + block.astype(F32)
 
     return (loss, grad_proto, grad_embed)
 
 
 def solution(mesh):
     batch_size, proto_size = mesh.shape["batch"], mesh.shape["proto"]
-    devices = mesh.devices.reshape(batch_size, proto_size // 4, 2, 2)
-    proto = ("high", "low", "core")
+    devices = mesh.devices.reshape(batch_size, proto_size // 8, 2, 2, 2)
+    proto = PLACE + ("core",)
     return jax.shard_map(
         on_device,
         mesh=jax.sharding.Mesh(devices, ("batch",) + proto),

time: 230 us -> 236 us (1.026)
  waiting for transfers between devices: 90.3 us -> 83.5 us
  local copies, waits for them, and re-layouts: 22.8 us -> 28.9 us
  starting transfers between devices: 35.7 us -> 40.1 us
    ppermute x35 -> x38, waiting for transfers between devices: 51.6 us -> 43.8 us  [swap(): return lax.ppermute(value, axis, [(i, i ^ distance) for i in range(size)])]
    unnamed x40 -> x48, local copies, waits for them, and re-layouts: 21.6 us -> 27.7 us
    ppermute x35 -> x38, starting transfers between devices: 35.6 us -> 40 us  [swap(): return lax.ppermute(value, axis, [(i, i ^ distance) for i in range(size)])]
    pallas_call x4 -> x8, Pallas kernels: 13.1 us -> 16.8 us  [gradients(): pl.pallas_call(functools.partial(gradient_kernel, count, total, heat_scal...]
  transfers between devices with their start and end apart: 36 -> 39, of which waited for: 23 -> 19; matrix products, arithmetic and copies ran while one was open for 1% -> 1% of each run, Pallas kernels for 22% -> 23%
where the time goes in v6:
time: 236 us; the launch traced here: 235 us
  waiting for transfers between devices  83.5 us (35%)
  Pallas kernels  63.8 us (27%)
  starting transfers between devices  40.1 us (17%)
  local copies, waits for them, and re-layouts  28.9 us (12%)
  between operations  15.6 us (7%)
  other arithmetic  2.97 us (1%)
    ppermute x38, waiting for transfers between devices, swap(): return lax.ppermute(value, axis, [(i, i ^ distance) for i in range(size)])  43.8 us
    ppermute x38, starting transfers between devices, swap(): return lax.ppermute(value, axis, [(i, i ^ distance) for i in range(size)])  40 us
    all_gather x1, waiting for transfers between devices, on_device(): table = lax.all_gather(own, ('batch', 'low', 'core'), axis=0, tiled=True)  39.8 us
    unnamed x48, local copies, waits for them, and re-layouts  27.7 us
    pallas_call x1, Pallas kernels, partner_pass(): pl.pallas_call(partner_kernel, grid_spec=pltpu.PrefetchScalarGridSpec(num...  19.8 us
    pallas_call x8, Pallas kernels, gradients(): pl.pallas_call(functools.partial(gradient_kernel, count, total, heat_scal...  16.8 us
    pallas_call x1, Pallas kernels, scores_of(): pl.pallas_call(scores_kernel, grid=(rows // share // 2,), in_specs=[pl.Bl...  7.93 us
    pallas_call x1, Pallas kernels, proto_gradient(): pl.pallas_call(proto_gradient_kernel, grid_spec=pltpu.PrefetchScalarGridS...  7.48 us
  transfers between devices with their start and end apart: 39, of which 19 were waited for; matrix products, arithmetic and copies ran while one was open for 1% of the time, Pallas kernels for 23%

profile of v6, /device:TPU:0, one launch (start us, length us, event | category | flops | bytes accessed | tf_op | source)
XLA Modules:
  0.0 234.9 jit_solution(13487596107369272399)
XLA Ops:
  7.2 2.2 copy-done.11
  11.0 2.2 copy-done.12
  14.8 7.9 %scores.1 = (bf16[2048,1024]{1,0:T(8,128)(2,1)S(1)}, bf16[1024,1024]{1,0:T(8,128)(2,1)S(1)}, f32[2048,1024]{1,0:T(8,128)S(1)}, bf16[2048,1024]{1,0:T(8,128)(2,1)...) custom-call(bf16[2048,1024]{1,0:T(8,128)(2,1)S(1)} %copy-done.12, bf16[1024,1024]{1,0:T(8,128)(2,1)S(1)} %copy-done.22), custom_call_target="tpu_custom_call" | custom-call | flops 4294967296 | bytes 23068672 | tf_op jit(solution)/shard_map/scores/pallas_call | solution.py:127
  22.7 3.0 %collective-permute-start = (f32[1,1024]{1,0:T(1,128)S(1)}, f32[1,1024]{1,0:T(1,128)S(1)}, u32[]{:S(2)}, u32[]{:S(2)}) collective-permute-start(f32[1,1024]{1,0:T(1,128)S(1)} %get-tuple-element.46.refs_0_), channel_id=1, source_target_pairs={{0,8},{8,0},{16,24},{24,16},{1,9},{9,1},{17,25},{25,17},{2,10},{10... | collective-permute-start | bytes 12296 | tf_op jit(solution)/shard_map/ppermute | solution.py:547
  27.4 2.0 collective-permute-done.1.refs_2_
  29.3 2.5 %collective-permute-done.2.refs_3_ = f32[1,1024]{1,0:T(1,128)S(1)} collective-permute-done((f32[1,1024]{1,0:T(1,128)S(1)}, f32[1,1024]{1,0:T(1,128)S(1)}, u32[]{:S(2)}, u32[]{:S(2)}) %collective-permute-start.2) | collective-permute-done | bytes 4128 | tf_op jit(solution)/shard_map/ppermute | solution.py:547
  36.1 2.6 %collective-permute-start.5 = (f32[1,2048]{1,0:T(1,128)S(1)}, f32[1,2048]{1,0:T(1,128)S(1)}, u32[]{:S(2)}, u32[]{:S(2)}) collective-permute-start(f32[1,2048]{1,0:T(1,128)S(1)} %add.70.refs_0_), channel_id=1, source_target_pairs={{0,4},{2,6},{4,0},{6,2},{1,5},{3,7},{5,1},{7,3},{8,12},{10,14},{12... | collective-permute-start | bytes 24584 | tf_op jit(solution)/shard_map/ppermute | solution.py:547
  40.8 3.5 %collective-permute-done.6.refs_3_ = f32[1,2048]{1,0:T(1,128)S(1)} collective-permute-done((f32[1,2048]{1,0:T(1,128)S(1)}, f32[1,2048]{1,0:T(1,128)S(1)}, u32[]{:S(2)}, u32[]{:S(2)}) %collective-permute-start.6) | collective-permute-done | bytes 8224 | tf_op jit(solution)/shard_map/ppermute | solution.py:547
  46.2 2.6 %collective-permute-start.9 = (f32[1,1024]{1,0:T(1,128)S(1)}, f32[1,1024]{1,0:T(1,128)S(1)}, u32[]{:S(2)}, u32[]{:S(2)}) collective-permute-start(f32[1,1024]{1,0:T(1,128)S(1)} %column_pass.2.refs_0_), channel_id=1, source_target_pairs={{0,24},{8,16},{16,8},{24,0},{1,25},{9,17},{17,9},{25,1},{2,26},{10... | collective-permute-start | bytes 12296 | tf_op jit(solution)/shard_map/ppermute | solution.py:547
  54.1 3.7 %collective-permute-start.13 = (f32[1,2048]{1,0:T(1,128)S(1)}, f32[1,2048]{1,0:T(1,128)S(1)}, u32[]{:S(2)}, u32[]{:S(2)}) collective-permute-start(f32[1,2048]{1,0:T(1,128)S(1)} %add.71.refs_0_), channel_id=1, source_target_pairs={{0,6},{2,4},{4,2},{6,0},{1,7},{3,5},{5,3},{7,1},{8,14},{10,12},{12... | collective-permute-start | bytes 24584 | tf_op jit(solution)/shard_map/ppermute | solution.py:547
  64.2 39.8 %all-gather.2.cloned.1.call-done.source_ref = bf16[8192,8,128]{2,1,0:T(8,128)(2,1)} async-done(((bf16[512,8,128]{2,1,0:T(8,128)(2,1)}), bf16[8192,8,128]{2,1,0:T(8,128)(2,1)}) %all-gather.2.cloned.1.call-update) | async-done | bytes 16777232 | tf_op jit(solution)/shard_map/all_gather | solution.py:584
  104.0 19.8 %partner_scores.1 = (bf16[2048,1024]{1,0:T(8,128)(2,1)S(1)}, bf16[2048,1024]{1,0:T(8,128)(2,1)S(1)}) custom-call(s32[2048]{0:T(1024)S(1)} %bitcast.115, s32[2048]{0:T(1024)S(1)} %bitcast.114, bf16[8192,8,128]{2,1,0:T(8,128)(2,1)} %all-gather.2.cloned.1.call-done.source_ref, bf16[1024,1024]{1,0:T(8,128)(2,1)S(1)} %get-tuple-element.49.wnorm_ref.refs_11_), custom_call_target="tpu_custom_call" | custom-call | flops 8589934592 | bytes 29360128 | tf_op jit(solution)/shard_map/partner_scores/pallas_call | solution.py:266
  123.9 2.0 partner_row_pass.1
  129.4 2.4 %collective-permute-start.19 = (f32[2,4,3,256]{3,2,1,0:T(4,128)S(1)}, f32[2,4,3,256]{3,2,1,0:T(4,128)S(1)}, u32[]{:S(2)}, u32[]{:S(2)}) collective-permute-start(f32[2,4,3,256]{3,2,1,0:T(4,128)S(1)} %add.73), channel_id=1, source_target_pairs={{0,4},{2,6},{4,0},{6,2},{1,5},{3,7},{5,1},{7,3},{8,12},{10,14},{12... | collective-permute-start | bytes 73736 | tf_op jit(solution)/shard_map/ppermute | solution.py:547
  134.2 3.3 %collective-permute-done.20 = f32[2,4,3,256]{3,2,1,0:T(4,128)S(1)} collective-permute-done((f32[2,4,3,256]{3,2,1,0:T(4,128)S(1)}, f32[2,4,3,256]{3,2,1,0:T(4,128)S(1)}, u32[]{:S(2)}, u32[]{:S(2)}) %collective-permute-start.20) | collective-permute-done | bytes 24608 | tf_op jit(solution)/shard_map/ppermute | solution.py:547
  137.5 2.2 copy-done.1
  139.7 2.2 copy-done.4
  141.9 3.4 %copy-done.7 = f32[2048,1024]{1,0:T(8,128)S(1)} copy-done((f32[2048,1024]{1,0:T(8,128)S(1)}, f32[2048,1024]{1,0:T(8,128)}, u32[]{:S(2)}) %copy-start.7) | copy-done | bytes 8388632
  151.0 2.7 %gradients.10 = (bf16[1,256,1024]{2,1,0:T(8,128)(2,1)}, bf16[1,256,1024]{2,1,0:T(8,128)(2,1)S(1)}, f32[1,128]{1,0:T(1,128)S(1)}) custom-call(s32[3]{0:T(128)S(1)} %get-tuple-element.57.core_ref, f32[1,1024]{1,0:T(1,128)S(1)} %column_pass.3.refs_0_, f32[1,1024]{1,0:T(1,128)S(1)} %collective-permute-done.14.refs_1_, ...), custom_call_target="tpu_custom_call" | custom-call | flops 1048576 | bytes 1048576 | tf_op jit(solution)/shard_map/gradients/pallas_call | solution.py:374
  155.1 2.2 copy-done.2
  157.3 2.2 copy-done.5
  159.5 3.4 %copy-done.8 = f32[2048,1024]{1,0:T(8,128)S(1)} copy-done((f32[2048,1024]{1,0:T(8,128)S(1)}, f32[2048,1024]{1,0:T(8,128)}, u32[]{:S(2)}) %copy-start.8) | copy-done | bytes 8388632
  164.9 2.1 collective-permute-start.29
  170.9 2.7 %gradients.14 = (bf16[1,256,1024]{2,1,0:T(8,128)(2,1)}, bf16[1,256,1024]{2,1,0:T(8,128)(2,1)S(1)}, f32[1,128]{1,0:T(1,128)S(1)}) custom-call(s32[3]{0:T(128)S(1)} %get-tuple-element.67.core_ref, f32[1,1024]{1,0:T(1,128)S(1)} %column_pass.3.refs_0_, f32[1,1024]{1,0:T(1,128)S(1)} %collective-permute-done.14.refs_1_, ...), custom_call_target="tpu_custom_call" | custom-call | flops 1048576 | bytes 1048576 | tf_op jit(solution)/shard_map/gradients/pallas_call | solution.py:374
  173.7 1.9 gradients.15
  179.1 7.5 %proto_gradient.1 = (f32[1024,256]{1,0:T(8,128)S(1)}, bf16[4,1024,256]{2,1,0:T(8,128)(2,1)S(1)}) custom-call(s32[4]{0:T(128)S(1)} %pad_add_fusion.index_ref, bf16[256,1024]{1,0:T(8,128)(2,1)S(1)} %bitcast.111, bf16[256,1024]{1,0:T(8,128)(2,1)S(1)} %bitcast.110, bf16[256,1024]{1,0:T(8,128)(2,1)S(1)} %bitcast.107, bf16[256,1024]{1,0:T(8,128)(2,1)S(1)} %bitcast.106, ...), custom_call_target="tpu_custom_call" | custom-call | flops 1048576 | bytes 1048576 | tf_op jit(solution)/shard_map/proto_gradient/pallas_call | solution.py:491
  192.9 11.5 %collective-permute-done.30 = bf16[1024,256]{1,0:T(8,128)(2,1)} collective-permute-done((bf16[1024,256]{1,0:T(8,128)(2,1)}, bf16[1024,256]{1,0:T(8,128)(2,1)}, u32[]{:S(2)}, u32[]{:S(2)}) %collective-permute-start.30) | collective-permute-done | bytes 524320 | tf_op jit(solution)/shard_map/ppermute | solution.py:547
  204.3 9.8 %collective-permute-done.31 = bf16[1024,256]{1,0:T(8,128)(2,1)} collective-permute-done((bf16[1024,256]{1,0:T(8,128)(2,1)}, bf16[1024,256]{1,0:T(8,128)(2,1)}, u32[]{:S(2)}, u32[]{:S(2)}) %collective-permute-start.31) | collective-permute-done | bytes 524320 | tf_op jit(solution)/shard_map/ppermute | solution.py:547
  215.7 2.8 %collective-permute-start.35 = (f32[1,128]{1,0:T(1,128)S(1)}, f32[1,128]{1,0:T(1,128)S(1)}, u32[]{:S(2)}, u32[]{:S(2)}) collective-permute-start(f32[1,128]{1,0:T(1,128)S(1)} %add.84), channel_id=1, source_target_pairs={{0,6},{2,4},{4,2},{6,0},{1,7},{3,5},{5,3},{7,1},{8,14},{10,12},{12... | collective-permute-start | bytes 1544 | tf_op jit(solution)/shard_map/ppermute | solution.py:547
  218.6 2.5 %convert_add_fusion = f32[1024,256]{1,0:T(8,128)} fusion(bf16[1024,256]{1,0:T(8,128)(2,1)} %collective-permute-done.32, bf16[1024,256]{1,0:T(8,128)(2,1)} %collective-permute-done.31, f32[1024,256]{1,0:T(8,128)S(1)} %get-tuple-element.86, bf16[1024,256]{1,0:T(8,128)(2,1)} %collective-permute-done.30), kind=kLoop, calls=%fused_computation | loop fusion | flops 1572864 | bytes 3670016 | tf_op jit(solution)/shard_map/add | solution.py:642
  221.1 2.2 copy-done.13
  224.3 2.6 %embed_gradient.1 = f32[256,1024]{1,0:T(8,128)} custom-call(s32[1]{0:T(128)} %bitcast.30.index_ref, bf16[2048,1024]{1,0:T(8,128)(2,1)S(1)} %copy-done.13, f32[256,1024]{1,0:T(8,128)S(1)} %bitcast.103, bf16[256,1024]{1,0:T(8,128)(2,1)S(1)} %bitcast.113, bf16[256,1024]{1,0:T(8,128)(2,1)S(1)} %bitcast.112, bf16[256,1024]{1,0:T(8,128)(2,1)} %bitcast.34.refs_3_), custom_call_target="tpu_custom_call" | custom-call | flops 2097152 | bytes 4194304 | tf_op jit(solution)/shard_map/embed_gradient/pallas_call | solution.py:527
  (131 shorter events, 56.0 us)
Async XLA Ops:
  7.2 96.8 %all-gather.2.cloned.1.call-start = ((), (), s32[]{:S(2)}) async-start(), calls=%async_computation | async-start | bytes 17825792 | tf_op jit(solution)/shard_map/all_gather | solution.py:584
  22.7 4.6 %collective-permute-start = (f32[1,1024]{1,0:T(1,128)S(1)}, f32[1,1024]{1,0:T(1,128)S(1)}, u32[]{:S(2)}, u32[]{:S(2)}) collective-permute-start(f32[1,1024]{1,0:T(1,128)S(1)} %get-tuple-element.46.refs_0_), channel_id=1, source_target_pairs={{0,8},{8,0},{16,24},{24,16},{1,9},{9,1},{17,25},{25,17},{2,10},{10... | collective-permute-start | bytes 12296 | tf_op jit(solution)/shard_map/ppermute | solution.py:547
  27.3 4.6 %collective-permute-start.2 = (f32[1,1024]{1,0:T(1,128)S(1)}, f32[1,1024]{1,0:T(1,128)S(1)}, u32[]{:S(2)}, u32[]{:S(2)}) collective-permute-start(f32[1,1024]{1,0:T(1,128)S(1)} %get-tuple-element.46.refs_0_), channel_id=1, source_target_pairs={{0,24},{8,16},{16,8},{24,0},{1,25},{9,17},{17,9},{25,1},{2,26},{10... | collective-permute-start | bytes 12296 | tf_op jit(solution)/shard_map/ppermute | solution.py:547
  34.5 4.5 %collective-permute-start.4 = (f32[1,2048]{1,0:T(1,128)S(1)}, f32[1,2048]{1,0:T(1,128)S(1)}, u32[]{:S(2)}, u32[]{:S(2)}) collective-permute-start(f32[1,2048]{1,0:T(1,128)S(1)} %add.70.refs_0_), channel_id=1, source_target_pairs={{0,2},{2,0},{4,6},{6,4},{1,3},{3,1},{5,7},{7,5},{8,10},{10,8},{12,... | collective-permute-start | bytes 24584 | tf_op jit(solution)/shard_map/ppermute | solution.py:547
  36.1 4.7 %collective-permute-start.5 = (f32[1,2048]{1,0:T(1,128)S(1)}, f32[1,2048]{1,0:T(1,128)S(1)}, u32[]{:S(2)}, u32[]{:S(2)}) collective-permute-start(f32[1,2048]{1,0:T(1,128)S(1)} %add.70.refs_0_), channel_id=1, source_target_pairs={{0,4},{2,6},{4,0},{6,2},{1,5},{3,7},{5,1},{7,3},{8,12},{10,14},{12... | collective-permute-start | bytes 24584 | tf_op jit(solution)/shard_map/ppermute | solution.py:547
  38.7 5.6 %collective-permute-start.6 = (f32[1,2048]{1,0:T(1,128)S(1)}, f32[1,2048]{1,0:T(1,128)S(1)}, u32[]{:S(2)}, u32[]{:S(2)}) collective-permute-start(f32[1,2048]{1,0:T(1,128)S(1)} %add.70.refs_0_), channel_id=1, source_target_pairs={{0,6},{2,4},{4,2},{6,0},{1,7},{3,5},{5,3},{7,1},{8,14},{10,12},{12... | collective-permute-start | bytes 24584 | tf_op jit(solution)/shard_map/ppermute | solution.py:547
  45.2 3.7 %collective-permute-start.7 = (f32[1,1024]{1,0:T(1,128)S(1)}, f32[1,1024]{1,0:T(1,128)S(1)}, u32[]{:S(2)}, u32[]{:S(2)}) collective-permute-start(f32[1,1024]{1,0:T(1,128)S(1)} %column_pass.2.refs_0_), channel_id=1, source_target_pairs={{0,8},{8,0},{16,24},{24,16},{1,9},{9,1},{17,25},{25,17},{2,10},{10... | collective-permute-start | bytes 12296 | tf_op jit(solution)/shard_map/ppermute | solution.py:547
  46.2 4.6 %collective-permute-start.9 = (f32[1,1024]{1,0:T(1,128)S(1)}, f32[1,1024]{1,0:T(1,128)S(1)}, u32[]{:S(2)}, u32[]{:S(2)}) collective-permute-start(f32[1,1024]{1,0:T(1,128)S(1)} %column_pass.2.refs_0_), channel_id=1, source_target_pairs={{0,24},{8,16},{16,8},{24,0},{1,25},{9,17},{17,9},{25,1},{2,26},{10... | collective-permute-start | bytes 12296 | tf_op jit(solution)/shard_map/ppermute | solution.py:547
  53.3 4.5 %collective-permute-start.11 = (f32[1,2048]{1,0:T(1,128)S(1)}, f32[1,2048]{1,0:T(1,128)S(1)}, u32[]{:S(2)}, u32[]{:S(2)}) collective-permute-start(f32[1,2048]{1,0:T(1,128)S(1)} %add.71.refs_0_), channel_id=1, source_target_pairs={{0,2},{2,0},{4,6},{6,4},{1,3},{3,1},{5,7},{7,5},{8,10},{10,8},{12,... | collective-permute-start | bytes 24584 | tf_op jit(solution)/shard_map/ppermute | solution.py:547
  53.4 4.7 %collective-permute-start.12 = (f32[1,2048]{1,0:T(1,128)S(1)}, f32[1,2048]{1,0:T(1,128)S(1)}, u32[]{:S(2)}, u32[]{:S(2)}) collective-permute-start(f32[1,2048]{1,0:T(1,128)S(1)} %add.71.refs_0_), channel_id=1, source_target_pairs={{0,4},{2,6},{4,0},{6,2},{1,5},{3,7},{5,1},{7,3},{8,12},{10,14},{12... | collective-permute-start | bytes 24584 | tf_op jit(solution)/shard_map/ppermute | solution.py:547
  54.1 5.8 %collective-permute-start.13 = (f32[1,2048]{1,0:T(1,128)S(1)}, f32[1,2048]{1,0:T(1,128)S(1)}, u32[]{:S(2)}, u32[]{:S(2)}) collective-permute-start(f32[1,2048]{1,0:T(1,128)S(1)} %add.71.refs_0_), channel_id=1, source_target_pairs={{0,6},{2,4},{4,2},{6,0},{1,7},{3,5},{5,3},{7,1},{8,14},{10,12},{12... | collective-permute-start | bytes 24584 | tf_op jit(solution)/shard_map/ppermute | solution.py:547
  60.7 63.2 %collective-permute-start.14 = (f32[1,1024]{1,0:T(1,128)S(1)}, f32[1,1024]{1,0:T(1,128)S(1)}, u32[]{:S(2)}, u32[]{:S(2)}) collective-permute-start(f32[1,1024]{1,0:T(1,128)S(1)} %column_pass.3.refs_0_), channel_id=1, source_target_pairs={{0,8},{8,0},{16,24},{24,16},{1,9},{9,1},{17,25},{25,17},{2,10},{10... | collective-permute-start | bytes 12296 | tf_op jit(solution)/shard_map/ppermute | solution.py:547
  62.2 61.6 %collective-permute-start.15 = (f32[1,1024]{1,0:T(1,128)S(1)}, f32[1,1024]{1,0:T(1,128)S(1)}, u32[]{:S(2)}, u32[]{:S(2)}) collective-permute-start(f32[1,1024]{1,0:T(1,128)S(1)} %column_pass.3.refs_0_), channel_id=1, source_target_pairs={{0,16},{8,24},{16,0},{24,8},{1,17},{9,25},{17,1},{25,9},{2,18},{10... | collective-permute-start | bytes 12296 | tf_op jit(solution)/shard_map/ppermute | solution.py:547
  63.8 60.1 %collective-permute-start.16 = (f32[1,1024]{1,0:T(1,128)S(1)}, f32[1,1024]{1,0:T(1,128)S(1)}, u32[]{:S(2)}, u32[]{:S(2)}) collective-permute-start(f32[1,1024]{1,0:T(1,128)S(1)} %column_pass.3.refs_0_), channel_id=1, source_target_pairs={{0,24},{8,16},{16,8},{24,0},{1,25},{9,17},{17,9},{25,1},{2,26},{10... | collective-permute-start | bytes 12296 | tf_op jit(solution)/shard_map/ppermute | solution.py:547
  128.4 4.5 %collective-permute-start.18 = (f32[2,4,3,256]{3,2,1,0:T(4,128)S(1)}, f32[2,4,3,256]{3,2,1,0:T(4,128)S(1)}, u32[]{:S(2)}, u32[]{:S(2)}) collective-permute-start(f32[2,4,3,256]{3,2,1,0:T(4,128)S(1)} %add.73), channel_id=1, source_target_pairs={{0,2},{2,0},{4,6},{6,4},{1,3},{3,1},{5,7},{7,5},{8,10},{10,8},{12,... | collective-permute-start | bytes 73736 | tf_op jit(solution)/shard_map/ppermute | solution.py:547
  129.4 4.8 %collective-permute-start.19 = (f32[2,4,3,256]{3,2,1,0:T(4,128)S(1)}, f32[2,4,3,256]{3,2,1,0:T(4,128)S(1)}, u32[]{:S(2)}, u32[]{:S(2)}) collective-permute-start(f32[2,4,3,256]{3,2,1,0:T(4,128)S(1)} %add.73), channel_id=1, source_target_pairs={{0,4},{2,6},{4,0},{6,2},{1,5},{3,7},{5,1},{7,3},{8,12},{10,14},{12... | collective-permute-start | bytes 73736 | tf_op jit(solution)/shard_map/ppermute | solution.py:547
  131.8 5.7 %collective-permute-start.20 = (f32[2,4,3,256]{3,2,1,0:T(4,128)S(1)}, f32[2,4,3,256]{3,2,1,0:T(4,128)S(1)}, u32[]{:S(2)}, u32[]{:S(2)}) collective-permute-start(f32[2,4,3,256]{3,2,1,0:T(4,128)S(1)} %add.73), channel_id=1, source_target_pairs={{0,6},{2,4},{4,2},{6,0},{1,7},{3,5},{5,3},{7,1},{8,14},{10,12},{12... | collective-permute-start | bytes 73736 | tf_op jit(solution)/shard_map/ppermute | solution.py:547
  154.4 10.3 %collective-permute-start.22 = (bf16[1,256,1024]{2,1,0:T(8,128)(2,1)}, bf16[1,256,1024]{2,1,0:T(8,128)(2,1)S(1)}, u32[]{:S(2)}, u32[]{:S(2)}) collective-permute-start(bf16[1,256,1024]{2,1,0:T(8,128)(2,1)} %get-tuple-element.62), channel_id=1, source_target_pairs={{0,1},{1,0},{2,3},{3,2},{4,5},{5,4},{6,7},{7,6},{8,9},{9,8},{10,11... | collective-permute-start | bytes 1572872 | tf_op jit(solution)/shard_map/ppermute | solution.py:547
  155.0 22.7 %collective-permute-start.28 = (bf16[1,256,1024]{2,1,0:T(8,128)(2,1)}, bf16[1,256,1024]{2,1,0:T(8,128)(2,1)S(1)}, u32[]{:S(2)}, u32[]{:S(2)}) collective-permute-start(bf16[1,256,1024]{2,1,0:T(8,128)(2,1)} %add_blocks.3), channel_id=1, source_target_pairs={{0,2},{2,0},{4,6},{6,4},{1,3},{3,1},{5,7},{7,5},{8,10},{10,8},{12,... | collective-permute-start | bytes 1572872 | tf_op jit(solution)/shard_map/ppermute | solution.py:547
  164.9 22.0 %collective-permute-start.29 = (bf16[1,256,1024]{2,1,0:T(8,128)(2,1)S(1)}, bf16[1,256,1024]{2,1,0:T(8,128)(2,1)S(1)}, u32[]{:S(2)}, u32[]{:S(2)}) collective-permute-start(bf16[1,256,1024]{2,1,0:T(8,128)(2,1)S(1)} %add_blocks.4), channel_id=1, source_target_pairs={{0,2},{2,0},{4,6},{6,4},{1,3},{3,1},{5,7},{7,5},{8,10},{10,8},{12,... | collective-permute-start | bytes 1572872 | tf_op jit(solution)/shard_map/ppermute | solution.py:547
  168.9 17.8 %collective-permute-start.27 = (bf16[1,256,1024]{2,1,0:T(8,128)(2,1)S(1)}, bf16[1,256,1024]{2,1,0:T(8,128)(2,1)S(1)}, u32[]{:S(2)}, u32[]{:S(2)}) collective-permute-start(bf16[1,256,1024]{2,1,0:T(8,128)(2,1)S(1)} %get-tuple-element.82), channel_id=1, source_target_pairs={{0,1},{1,0},{2,3},{3,2},{4,5},{5,4},{6,7},{7,6},{8,9},{9,8},{10,11... | collective-permute-start | bytes 1572872 | tf_op jit(solution)/shard_map/ppermute | solution.py:547
  175.6 11.1 %collective-permute-start.23 = (f32[1,128]{1,0:T(1,128)S(1)}, f32[1,128]{1,0:T(1,128)S(1)}, u32[]{:S(2)}, u32[]{:S(2)}) collective-permute-start(f32[1,128]{1,0:T(1,128)S(1)} %add_add_fusion.2), channel_id=1, source_target_pairs={{0,8},{8,0},{16,24},{24,16},{1,9},{9,1},{17,25},{25,17},{2,10},{10... | collective-permute-start | bytes 1544 | tf_op jit(solution)/shard_map/ppermute | solution.py:547
  177.1 9.5 %collective-permute-start.24 = (f32[1,128]{1,0:T(1,128)S(1)}, f32[1,128]{1,0:T(1,128)S(1)}, u32[]{:S(2)}, u32[]{:S(2)}) collective-permute-start(f32[1,128]{1,0:T(1,128)S(1)} %add_add_fusion.2), channel_id=1, source_target_pairs={{0,16},{8,24},{16,0},{24,8},{1,17},{9,25},{17,1},{25,9},{2,18},{10... | collective-permute-start | bytes 1544 | tf_op jit(solution)/shard_map/ppermute | solution.py:547
  177.7 9.0 %collective-permute-start.25 = (f32[1,128]{1,0:T(1,128)S(1)}, f32[1,128]{1,0:T(1,128)S(1)}, u32[]{:S(2)}, u32[]{:S(2)}) collective-permute-start(f32[1,128]{1,0:T(1,128)S(1)} %add_add_fusion.2), channel_id=1, source_target_pairs={{0,24},{8,16},{16,8},{24,0},{1,25},{9,17},{17,9},{25,1},{2,26},{10... | collective-permute-start | bytes 1544 | tf_op jit(solution)/shard_map/ppermute | solution.py:547
  188.2 16.1 %collective-permute-start.30 = (bf16[1024,256]{1,0:T(8,128)(2,1)}, bf16[1024,256]{1,0:T(8,128)(2,1)}, u32[]{:S(2)}, u32[]{:S(2)}) collective-permute-start(bf16[1024,256]{1,0:T(8,128)(2,1)} %get-tuple-element.91), channel_id=1, source_target_pairs={{0,24},{8,16},{16,8},{24,0},{1,25},{9,17},{17,9},{25,1},{2,26},{10... | collective-permute-start | bytes 1572872 | tf_op jit(solution)/shard_map/ppermute | solution.py:547
  189.7 24.5 %collective-permute-start.31 = (bf16[1024,256]{1,0:T(8,128)(2,1)}, bf16[1024,256]{1,0:T(8,128)(2,1)}, u32[]{:S(2)}, u32[]{:S(2)}) collective-permute-start(bf16[1024,256]{1,0:T(8,128)(2,1)} %get-tuple-element.90), channel_id=1, source_target_pairs={{0,16},{8,24},{16,0},{24,8},{1,17},{9,25},{17,1},{25,9},{2,18},{10... | collective-permute-start | bytes 1572872 | tf_op jit(solution)/shard_map/ppermute | solution.py:547
  191.2 23.0 %collective-permute-start.32 = (bf16[1024,256]{1,0:T(8,128)(2,1)}, bf16[1024,256]{1,0:T(8,128)(2,1)}, u32[]{:S(2)}, u32[]{:S(2)}) collective-permute-start(bf16[1024,256]{1,0:T(8,128)(2,1)} %get-tuple-element.89), channel_id=1, source_target_pairs={{0,8},{8,0},{16,24},{24,16},{1,9},{9,1},{17,25},{25,17},{2,10},{10... | collective-permute-start | bytes 1572872 | tf_op jit(solution)/shard_map/ppermute | solution.py:547
  191.7 29.4 %collective-permute-start.36 = (bf16[1,256,1024]{2,1,0:T(8,128)(2,1)}, bf16[1,256,1024]{2,1,0:T(8,128)(2,1)S(1)}, u32[]{:S(2)}, u32[]{:S(2)}) collective-permute-start(bf16[1,256,1024]{2,1,0:T(8,128)(2,1)} %get-tuple-element.88), channel_id=1, source_target_pairs={{0,1},{1,0},{2,3},{3,2},{4,5},{5,4},{6,7},{7,6},{8,9},{9,8},{10,11... | collective-permute-start | bytes 1572872 | tf_op jit(solution)/shard_map/ppermute | solution.py:547
  192.9 28.3 %collective-permute-start.37 = (bf16[1,256,1024]{2,1,0:T(8,128)(2,1)S(1)}, bf16[1,256,1024]{2,1,0:T(8,128)(2,1)}, u32[]{:S(2)}, u32[]{:S(2)}) collective-permute-start(bf16[1,256,1024]{2,1,0:T(8,128)(2,1)S(1)} %add_blocks.5), channel_id=1, source_target_pairs={{0,4},{2,6},{4,0},{6,2},{1,5},{3,7},{5,1},{7,3},{8,12},{10,14},{12... | collective-permute-start | bytes 1572872 | tf_op jit(solution)/shard_map/ppermute | solution.py:547
  214.2 12.7 %collective-permute-start.33 = (f32[1,128]{1,0:T(1,128)S(1)}, f32[1,128]{1,0:T(1,128)S(1)}, u32[]{:S(2)}, u32[]{:S(2)}) collective-permute-start(f32[1,128]{1,0:T(1,128)S(1)} %add.84), channel_id=1, source_target_pairs={{0,2},{2,0},{4,6},{6,4},{1,3},{3,1},{5,7},{7,5},{8,10},{10,8},{12,... | collective-permute-start | bytes 1544 | tf_op jit(solution)/shard_map/ppermute | solution.py:547
  214.2 12.7 %collective-permute-start.34 = (f32[1,128]{1,0:T(1,128)S(1)}, f32[1,128]{1,0:T(1,128)S(1)}, u32[]{:S(2)}, u32[]{:S(2)}) collective-permute-start(f32[1,128]{1,0:T(1,128)S(1)} %add.84), channel_id=1, source_target_pairs={{0,4},{2,6},{4,0},{6,2},{1,5},{3,7},{5,1},{7,3},{8,12},{10,14},{12... | collective-permute-start | bytes 1544 | tf_op jit(solution)/shard_map/ppermute | solution.py:547
  215.7 11.2 %collective-permute-start.35 = (f32[1,128]{1,0:T(1,128)S(1)}, f32[1,128]{1,0:T(1,128)S(1)}, u32[]{:S(2)}, u32[]{:S(2)}) collective-permute-start(f32[1,128]{1,0:T(1,128)S(1)} %add.84), channel_id=1, source_target_pairs={{0,6},{2,4},{4,2},{6,0},{1,7},{3,5},{5,3},{7,1},{8,14},{10,12},{12... | collective-permute-start | bytes 1544 | tf_op jit(solution)/shard_map/ppermute | solution.py:547
  (31 other events, 103.7 us)
Sparse Core Ops, SparseCore 0:
  11.1 92.8 all-gather.1

commit v7 on v6

--- a/solution.py
+++ b/solution.py
@@ -85,7 +85,7 @@
             scratch_shapes=[pltpu.VMEM((block * groups, LANES), F32)],
         ),
         out_shape=jax.ShapeDtypeStruct((block * count, groups, LANES), BF16),
-        compiler_params=params(16),
+        compiler_params=params(60),
         name="own_rows",
     )(index, embeddings)
 
@@ -97,7 +97,7 @@
     def _():
         wnorm_ref[...] = normalized(prototypes_ref[...]).astype(BF16)
 
-    share = zsum_ref.shape[-1]
+    share = embeddings_ref.shape[0] // 2
     sums = None
     for k in range(2):
         at = slice(k * share, (k + 1) * share)
@@ -106,7 +106,7 @@
         scores = lax.dot_general(unit, wnorm_ref[...], (((1,), (1,)), ((), ())), preferred_element_type=F32)
         scores_ref[at] = scores
         soft = jnp.exp(scores * (1.0 / SOFTMAX_HEAT))
-        zsum_ref[k, 0] = lane_row_sums(soft)
+        zsum_ref[:, at] = lane_row_sums(soft)
         expo = soft * soft
         expo_ref[at] = expo.astype(BF16)
         part = jnp.sum(expo, axis=0, keepdims=True)
@@ -136,7 +136,7 @@
             pl.BlockSpec((protos, columns), lambda i: (0, 0)),
             pl.BlockSpec((2 * share, protos), lambda i: (i, 0)),
             pl.BlockSpec((2 * share, protos), lambda i: (i, 0)),
-            pl.BlockSpec((2, 1, 1, share), lambda i: (0, i, 0, 0)),
+            pl.BlockSpec((1, 2 * share), lambda i: (0, i)),
             pl.BlockSpec((1, protos), lambda i: (0, 0)),
         ],
         out_shape=[
@@ -144,10 +144,10 @@
             jax.ShapeDtypeStruct((protos, columns), BF16),
             jax.ShapeDtypeStruct((rows, protos), F32),
             jax.ShapeDtypeStruct((rows, protos), BF16),
-            jax.ShapeDtypeStruct((2, rows // share // 2, 1, share), F32),
+            jax.ShapeDtypeStruct((1, rows), F32),
             jax.ShapeDtypeStruct((1, protos), F32),
         ],
-        compiler_params=params(28),
+        compiler_params=params(50),
         cost_estimate=cost(2 * rows * columns * protos, 22 * MIB, rows * protos),
         name="scores",
     )(embeddings, prototypes)
@@ -283,44 +283,37 @@
             + [pltpu.VMEM((CHUNK * groups, LANES), F32)] * 2,
         ),
         out_shape=[jax.ShapeDtypeStruct((rows, protos), BF16)] * 2,
-        compiler_params=params(28),
+        compiler_params=params(40),
         cost_estimate=cost(4 * rows * columns * protos, 28 * MIB, 2 * rows * protos),
         name="partner_scores",
     )(first, second, table, wnorm)
 
 
-def partner_row_kernel(count, parts, *refs):
-    column_refs, zsum_ref, row_ref = refs[:parts], refs[parts], refs[-1]
-    first_refs, second_refs = refs[parts + 1 : parts + 1 + STREAMS], refs[parts + 1 + STREAMS : -1]
-    scale = 1.0 / (count * total_of(column_refs))
-    for k in range(STREAMS):
-        at = (k % 2, k // 2)
-        row_ref[at] = jnp.concatenate(
-            [
-                lane_row_sums(first_refs[k][...].astype(F32) * scale),
-                lane_row_sums(second_refs[k][...].astype(F32) * scale),
-                zsum_ref[at],
-            ],
-            axis=0,
-        )
-
-
-def partner_row_pass(columns, zsum, first, second, count):
-    rows, protos = first.shape
-    share = zsum.shape[-1]
-    group = STREAMS // 2
-    return pl.pallas_call(
-        functools.partial(partner_row_kernel, count, len(columns)),
-        grid=(rows // share // STREAMS,),
-        in_specs=[pl.BlockSpec((1, protos), lambda i: (0, 0)) for _ in columns]
-        + [pl.BlockSpec((2, group, 1, share), lambda i: (0, i, 0, 0))]
-        + streams_of((share, protos)) * 2,
-        out_specs=pl.BlockSpec((2, group, 3, share), lambda i: (0, i, 0, 0)),
-        out_shape=jax.ShapeDtypeStruct((2, rows // share // 2, 3, share), F32),
-        compiler_params=params(16),
-        cost_estimate=cost(4 * rows * protos, 8 * MIB),
-        name="partner_row_pass",
-    )(*columns, zsum, *[in_vmem(first)] * STREAMS, *[in_vmem(second)] * STREAMS)
+def lookup_kernel(first_ref, second_ref, totals_ref, out_ref):
+    rows = first_ref.shape[0]
+    for number, which_ref in enumerate((first_ref, second_ref)):
+
+        @pl.loop(0, rows // 16)
+        def _(i):
+            for j in range(16):
+                row = i * 16 + j
+                out_ref[number * rows + row] = totals_ref[which_ref[row]]
+
+
+def lookup(first, second, totals):
+    return pl.pallas_call(
+        lookup_kernel,
+        grid_spec=pltpu.PrefetchScalarGridSpec(
+            num_scalar_prefetch=2,
+            grid=(1,),
+            in_specs=[pl.BlockSpec(memory_space=pltpu.SMEM)],
+            out_specs=pl.BlockSpec(memory_space=pltpu.SMEM),
+        ),
+        out_shape=jax.ShapeDtypeStruct((2 * first.shape[0],), F32),
+        compiler_params=params(8),
+        cost_estimate=cost(MIB, MIB),
+        name="lookup",
+    )(first, second, totals)
 
 
 def gradient_kernel(count, total, heat_scale, proto_size, parts, core_ref, *refs):
@@ -369,7 +362,7 @@
     _, places, _, share = row_totals[0].shape
     top = places // 4
     at = pl.BlockSpec((1, None, None, None, share, protos), lambda i, where: (i, where[0], where[1], where[2], 0, 0))
-    first, second, scores = [in_vmem(value.reshape(top, 2, 2, 2, share, protos)) for value in (first, second, scores)]
+    first, second, scores = [value.reshape(top, 2, 2, 2, share, protos) for value in (first, second, scores)]
     row_totals = [value.reshape(2, top, 2, 2, 3, share) for value in row_totals]
     return pl.pallas_call(
         functools.partial(
@@ -397,10 +390,10 @@
             jax.ShapeDtypeStruct((top, share, protos), BF16),
             jax.ShapeDtypeStruct((1, LANES), F32),
         ],
-        compiler_params=params(16),
+        compiler_params=params(44),
         cost_estimate=cost(MIB, MIB),
         name="gradients",
-    )(where, *columns, *row_totals, first, second, scores, in_vmem(wnorm))
+    )(where, *columns, *row_totals, in_vmem(first), in_vmem(second), scores, in_vmem(wnorm))
 
 
 def add_kernel(*refs):
@@ -533,7 +526,7 @@
             out_specs=whole,
         ),
         out_shape=jax.ShapeDtypeStruct((share, width), F32),
-        compiler_params=params(12),
+        compiler_params=params(60),
         cost_estimate=cost(8 * share * width, 4 * MIB),
         name="embed_gradient",
     )(index, embeddings, *values)
@@ -589,8 +582,16 @@
         row_totals = proto_parts_of(row_pass(columns, expo, centroids))
         columns = parts_of(column_pass(row_totals, expo, total_rows), "batch")
 
+    row_part = row_pass(columns, expo, centroids)
+    row_totals = functools.reduce(jnp.add, proto_parts_of(jnp.concatenate([row_part, zsum], axis=0)))
+    own_totals, zsum = row_totals[0], row_totals[1]
+    all_totals = jnp.concatenate([own_totals] + [swap(own_totals, "batch", distance) for distance in range(1, batch_size)])
+    away = (partners // row_count ^ batch_index) * row_count + partners % row_count
+    partner_totals = lookup(away[:, 0], away[:, 1], all_totals).reshape(2, row_count)
+    row_totals = jnp.concatenate([partner_totals, zsum[None]], axis=0)
+    row_totals = [row_totals.reshape(3, places, 2, share).transpose(2, 1, 0, 3)]
+
     first, second = partner_pass(partners[:, 0], partners[:, 1], table, wnorm)
-    row_totals = proto_parts_of(partner_row_pass(columns, zsum, first, second, centroids))
     others = (scores, wnorm, centroids, total_rows, proto_size)
 
     def after(value, *earlier):

time: 236 us -> 226 us (0.958)
  waiting for transfers between devices: 83.5 us -> 50.6 us
  Pallas kernels: 63.8 us -> 96.1 us
  local copies, waits for them, and re-layouts: 28.9 us -> 11.6 us
  starting transfers between devices: 40.1 us -> 45.6 us
  other arithmetic: 2.97 us -> 5.69 us
    all_gather x1, waiting for transfers between devices: 39.8 us -> 2.62 us  [on_device(): table = lax.all_gather(own, ('batch', 'low', 'core'), axis=0, tiled=True)]
    unnamed x48 -> x60, local copies, waits for them, and re-layouts: 27.7 us -> 9.72 us
    pallas_call x8, Pallas kernels: 16.8 us -> 33.7 us  [gradients(): pl.pallas_call(functools.partial(gradient_kernel, count, total, heat_scal...]
    pallas_call x1, Pallas kernels: 2.04 us -> 10.1 us  [lookup(): pl.pallas_call(lookup_kernel, grid_spec=pltpu.PrefetchScalarGridSpec(num_...]
    ppermute x38 -> x41, starting transfers between devices: 40 us -> 45.6 us  [swap(): return lax.ppermute(value, axis, [(i, i ^ distance) for i in range(size)])]
    pallas_call x1, Pallas kernels: 7.93 us -> 12.2 us  [scores_of(): pl.pallas_call(scores_kernel, grid=(rows // share // 2,), in_specs=[pl.Bl...]
    ppermute x38 -> x41, waiting for transfers between devices: 43.8 us -> 47.9 us  [swap(): return lax.ppermute(value, axis, [(i, i ^ distance) for i in range(size)])]
  transfers between devices with their start and end apart: 39 -> 42, of which waited for: 19 -> 24; matrix products, arithmetic and copies ran while one was open for 1% -> 3% of each run, Pallas kernels for 23% -> 29%
where the time goes in v7:
time: 226 us; the launch traced here: 225 us
  Pallas kernels  96.1 us (43%)
  waiting for transfers between devices  50.6 us (22%)
  starting transfers between devices  45.6 us (20%)
  between operations  15.8 us (7%)
  local copies, waits for them, and re-layouts  11.6 us (5%)
  other arithmetic  5.69 us (3%)
    ppermute x41, waiting for transfers between devices, swap(): return lax.ppermute(value, axis, [(i, i ^ distance) for i in range(size)])  47.9 us
    ppermute x41, starting transfers between devices, swap(): return lax.ppermute(value, axis, [(i, i ^ distance) for i in range(size)])  45.6 us
    pallas_call x8, Pallas kernels, gradients(): pl.pallas_call(functools.partial(gradient_kernel, count, total, heat_scal...  33.7 us
    pallas_call x1, Pallas kernels, partner_pass(): pl.pallas_call(partner_kernel, grid_spec=pltpu.PrefetchScalarGridSpec(num...  20 us
    pallas_call x1, Pallas kernels, scores_of(): pl.pallas_call(scores_kernel, grid=(rows // share // 2,), in_specs=[pl.Bl...  12.2 us
    pallas_call x1, Pallas kernels, lookup(): pl.pallas_call(lookup_kernel, grid_spec=pltpu.PrefetchScalarGridSpec(num_...  10.1 us
    unnamed x60, local copies, waits for them, and re-layouts  9.72 us
    pallas_call x1, Pallas kernels, proto_gradient(): pl.pallas_call(proto_gradient_kernel, grid_spec=pltpu.PrefetchScalarGridS...  7.19 us
  transfers between devices with their start and end apart: 42, of which 24 were waited for; matrix products, arithmetic and copies ran while one was open for 3% of the time, Pallas kernels for 29%

profile of v7, /device:TPU:0, one launch (start us, length us, event | category | flops | bytes accessed | tf_op | source)
XLA Modules:
  0.0 225.3 jit_solution(17821777257054015495)
XLA Ops:
  7.2 2.6 %own_rows.1 = bf16[512,8,128]{2,1,0:T(8,128)(2,1)} custom-call(s32[1]{0:T(128)} %bitcast.10.index_ref, bf16[2048,1024]{1,0:T(8,128)(2,1)} %embeddings_ref.5), custom_call_target="tpu_custom_call" | custom-call | tf_op jit(solution)/shard_map/own_rows/pallas_call | solution.py:78
  9.9 12.2 %scores.1 = (bf16[2048,1024]{1,0:T(8,128)(2,1)}, bf16[1024,1024]{1,0:T(8,128)(2,1)S(1)}, f32[2048,1024]{1,0:T(8,128)}, bf16[2048,1024]{1,0:T(8,128)(2,1)}, f32[1,2048]{1,0:T(1,128)S(1)}, /*index=5*/f32[1,1024]{1,0:T(1,128)S(1)}) custom-call(bf16[2048,1024]{1,0:T(8,128)(2,1)} %embeddings_ref.5, bf16[1024,1024]{1,0:T(8,128)(2,1)} %prototypes_ref.1), custom_call_target="tpu_custom_call" | custom-call | flops 4294967296 | bytes 23068672 | tf_op jit(solution)/shard_map/scores/pallas_call | solution.py:127
  22.1 3.0 %collective-permute-start = (f32[1,1024]{1,0:T(1,128)S(1)}, f32[1,1024]{1,0:T(1,128)S(1)}, u32[]{:S(2)}, u32[]{:S(2)}) collective-permute-start(f32[1,1024]{1,0:T(1,128)S(1)} %get-tuple-element.46.refs_0_), channel_id=1, source_target_pairs={{0,8},{8,0},{16,24},{24,16},{1,9},{9,1},{17,25},{25,17},{2,10},{10... | collective-permute-start | bytes 12296 | tf_op jit(solution)/shard_map/ppermute | solution.py:540
  28.6 2.5 %collective-permute-done.2.refs_3_ = f32[1,1024]{1,0:T(1,128)S(1)} collective-permute-done((f32[1,1024]{1,0:T(1,128)S(1)}, f32[1,1024]{1,0:T(1,128)S(1)}, u32[]{:S(2)}, u32[]{:S(2)}) %collective-permute-start.2) | collective-permute-done | bytes 4128 | tf_op jit(solution)/shard_map/ppermute | solution.py:540
  31.1 2.2 copy-done
  37.7 2.6 %collective-permute-start.5 = (f32[1,2048]{1,0:T(1,128)S(1)}, f32[1,2048]{1,0:T(1,128)S(1)}, u32[]{:S(2)}, u32[]{:S(2)}) collective-permute-start(f32[1,2048]{1,0:T(1,128)S(1)} %add.89.refs_0_), channel_id=1, source_target_pairs={{0,4},{2,6},{4,0},{6,2},{1,5},{3,7},{5,1},{7,3},{8,12},{10,14},{12... | collective-permute-start | bytes 24584 | tf_op jit(solution)/shard_map/ppermute | solution.py:540
  42.4 3.5 %collective-permute-done.6.refs_3_ = f32[1,2048]{1,0:T(1,128)S(1)} collective-permute-done((f32[1,2048]{1,0:T(1,128)S(1)}, f32[1,2048]{1,0:T(1,128)S(1)}, u32[]{:S(2)}, u32[]{:S(2)}) %collective-permute-start.6) | collective-permute-done | bytes 8224 | tf_op jit(solution)/shard_map/ppermute | solution.py:540
  47.9 2.4 %collective-permute-start.9 = (f32[1,1024]{1,0:T(1,128)S(1)}, f32[1,1024]{1,0:T(1,128)S(1)}, u32[]{:S(2)}, u32[]{:S(2)}) collective-permute-start(f32[1,1024]{1,0:T(1,128)S(1)} %column_pass.2.refs_0_), channel_id=1, source_target_pairs={{0,24},{8,16},{16,8},{24,0},{1,25},{9,17},{17,9},{25,1},{2,26},{10... | collective-permute-start | bytes 12296 | tf_op jit(solution)/shard_map/ppermute | solution.py:540
  55.8 3.7 %collective-permute-start.13 = (f32[1,2048]{1,0:T(1,128)S(1)}, f32[1,2048]{1,0:T(1,128)S(1)}, u32[]{:S(2)}, u32[]{:S(2)}) collective-permute-start(f32[1,2048]{1,0:T(1,128)S(1)} %add.90.refs_0_), channel_id=1, source_target_pairs={{0,6},{2,4},{4,2},{6,0},{1,7},{3,5},{5,3},{7,1},{8,14},{10,12},{12... | collective-permute-start | bytes 24584 | tf_op jit(solution)/shard_map/ppermute | solution.py:540
  67.5 2.4 %collective-permute-done.16.refs_3_ = f32[1,1024]{1,0:T(1,128)S(1)} collective-permute-done((f32[1,1024]{1,0:T(1,128)S(1)}, f32[1,1024]{1,0:T(1,128)S(1)}, u32[]{:S(2)}, u32[]{:S(2)}) %collective-permute-start.16) | collective-permute-done | bytes 4128 | tf_op jit(solution)/shard_map/ppermute | solution.py:540
  69.9 2.3 %copy-done.2 = bf16[2048,1024]{1,0:T(8,128)(2,1)S(1)} copy-done((bf16[2048,1024]{1,0:T(8,128)(2,1)S(1)}, bf16[2048,1024]{1,0:T(8,128)(2,1)}, u32[]{:S(2)}) %copy-start.2) | copy-done | bytes 4194328
  75.2 4.0 %collective-permute-start.19 = (f32[2,2048]{1,0:T(2,128)S(1)}, f32[2,2048]{1,0:T(2,128)S(1)}, u32[]{:S(2)}, u32[]{:S(2)}) collective-permute-start(f32[2,2048]{1,0:T(2,128)S(1)} %fusion.1), channel_id=1, source_target_pairs={{0,4},{2,6},{4,0},{6,2},{1,5},{3,7},{5,1},{7,3},{8,12},{10,14},{12... | collective-permute-start | bytes 49160 | tf_op jit(solution)/shard_map/ppermute | solution.py:540
  81.0 4.0 %collective-permute-done.20 = f32[2,2048]{1,0:T(2,128)S(1)} collective-permute-done((f32[2,2048]{1,0:T(2,128)S(1)}, f32[2,2048]{1,0:T(2,128)S(1)}, u32[]{:S(2)}, u32[]{:S(2)}) %collective-permute-start.20) | collective-permute-done | bytes 16416 | tf_op jit(solution)/shard_map/ppermute | solution.py:540
  86.0 2.7 %collective-permute-start.23 = (f32[2048]{0:T(1024)S(1)}, f32[2048]{0:T(1024)S(1)}, u32[]{:S(2)}, u32[]{:S(2)}) collective-permute-start(f32[2048]{0:T(1024)S(1)} %bitcast.96), channel_id=1, source_target_pairs={{0,24},{8,16},{16,8},{24,0},{1,25},{9,17},{17,9},{25,1},{2,26},{10... | collective-permute-start | bytes 24584 | tf_op jit(solution)/shard_map/ppermute | solution.py:540
  90.7 10.1 %lookup.1 = f32[4096]{0:T(1024)S(1)} custom-call(s32[2048]{0:T(1024)S(1)} %bitcast.74, s32[2048]{0:T(1024)S(1)} %bitcast.73, f32[8192]{0:T(1024)S(1)} %pad_maximum_fusion.totals_ref), custom_call_target="tpu_custom_call" | custom-call | flops 1048576 | bytes 1048576 | tf_op jit(solution)/shard_map/lookup/pallas_call | solution.py:304
  101.5 2.6 %all-gather.2.cloned.1.call-done.source_ref = bf16[8192,8,128]{2,1,0:T(8,128)(2,1)} async-done(((bf16[512,8,128]{2,1,0:T(8,128)(2,1)}), bf16[8192,8,128]{2,1,0:T(8,128)(2,1)}) %all-gather.2.cloned.1.call-update) | async-done | bytes 16777232 | tf_op jit(solution)/shard_map/all_gather | solution.py:577
  105.7 20.0 %partner_scores.1 = (bf16[2048,1024]{1,0:T(8,128)(2,1)S(1)}, bf16[2048,1024]{1,0:T(8,128)(2,1)S(1)}) custom-call(s32[2048]{0:T(1024)S(1)} %bitcast.76, s32[2048]{0:T(1024)S(1)} %bitcast.75, bf16[8192,8,128]{2,1,0:T(8,128)(2,1)} %all-gather.2.cloned.1.call-done.source_ref, bf16[1024,1024]{1,0:T(8,128)(2,1)S(1)} %copy-done.5), custom_call_target="tpu_custom_call" | custom-call | flops 8589934592 | bytes 29360128 | tf_op jit(solution)/shard_map/partner_scores/pallas_call | solution.py:266
  125.7 4.1 %gradients.8 = (bf16[1,256,1024]{2,1,0:T(8,128)(2,1)}, bf16[1,256,1024]{2,1,0:T(8,128)(2,1)}, f32[1,128]{1,0:T(1,128)}) custom-call(s32[3]{0:T(128)} %get-tuple-element.104.core_ref, f32[1,1024]{1,0:T(1,128)} %copy-done.18, f32[1,1024]{1,0:T(1,128)} %copy-done.19, f32[1,1024]{1,0:T(1,128)} %copy-done.20, f32[1,1024]{1,0:T(1,128)} %copy-done.21, ...), custom_call_target="tpu_custom_call" | custom-call | flops 1048576 | bytes 1048576 | tf_op jit(solution)/shard_map/gradients/pallas_call | solution.py:367
  130.7 4.2 %gradients.9 = (f32[1,256,1024]{2,1,0:T(8,128)}, bf16[1,256,1024]{2,1,0:T(8,128)(2,1)}, f32[1,128]{1,0:T(1,128)}) custom-call(s32[3]{0:T(128)} %get-tuple-element.105.core_ref, f32[1,1024]{1,0:T(1,128)} %copy-done.18, f32[1,1024]{1,0:T(1,128)} %copy-done.19, f32[1,1024]{1,0:T(1,128)} %copy-done.20, f32[1,1024]{1,0:T(1,128)} %copy-done.21, ...), custom_call_target="tpu_custom_call" | custom-call | flops 1048576 | bytes 1048576 | tf_op jit(solution)/shard_map/gradients/pallas_call | solution.py:367
  136.3 4.1 %gradients.10 = (bf16[1,256,1024]{2,1,0:T(8,128)(2,1)}, bf16[1,256,1024]{2,1,0:T(8,128)(2,1)}, f32[1,128]{1,0:T(1,128)}) custom-call(s32[3]{0:T(128)} %get-tuple-element.57.core_ref, f32[1,1024]{1,0:T(1,128)} %copy-done.18, f32[1,1024]{1,0:T(1,128)} %copy-done.19, f32[1,1024]{1,0:T(1,128)} %copy-done.20, f32[1,1024]{1,0:T(1,128)} %copy-done.21, ...), custom_call_target="tpu_custom_call" | custom-call | flops 1048576 | bytes 1048576 | tf_op jit(solution)/shard_map/gradients/pallas_call | solution.py:367
  142.1 4.2 %gradients.11 = (f32[1,256,1024]{2,1,0:T(8,128)}, bf16[1,256,1024]{2,1,0:T(8,128)(2,1)}, f32[1,128]{1,0:T(1,128)}) custom-call(s32[3]{0:T(128)} %get-tuple-element.59.core_ref, f32[1,1024]{1,0:T(1,128)} %copy-done.18, f32[1,1024]{1,0:T(1,128)} %copy-done.19, f32[1,1024]{1,0:T(1,128)} %copy-done.20, f32[1,1024]{1,0:T(1,128)} %copy-done.21, ...), custom_call_target="tpu_custom_call" | custom-call | flops 1048576 | bytes 1048576 | tf_op jit(solution)/shard_map/gradients/pallas_call | solution.py:367
  150.2 4.1 %gradients.12 = (bf16[1,256,1024]{2,1,0:T(8,128)(2,1)}, bf16[1,256,1024]{2,1,0:T(8,128)(2,1)}, f32[1,128]{1,0:T(1,128)}) custom-call(s32[3]{0:T(128)} %get-tuple-element.63.core_ref, f32[1,1024]{1,0:T(1,128)} %copy-done.18, f32[1,1024]{1,0:T(1,128)} %copy-done.19, f32[1,1024]{1,0:T(1,128)} %copy-done.20, f32[1,1024]{1,0:T(1,128)} %copy-done.21, ...), custom_call_target="tpu_custom_call" | custom-call | flops 1048576 | bytes 1048576 | tf_op jit(solution)/shard_map/gradients/pallas_call | solution.py:367
  154.4 4.2 %gradients.13 = (f32[1,256,1024]{2,1,0:T(8,128)}, bf16[1,256,1024]{2,1,0:T(8,128)(2,1)}, f32[1,128]{1,0:T(1,128)}) custom-call(s32[3]{0:T(128)} %get-tuple-element.65.core_ref, f32[1,1024]{1,0:T(1,128)} %copy-done.18, f32[1,1024]{1,0:T(1,128)} %copy-done.19, f32[1,1024]{1,0:T(1,128)} %copy-done.20, f32[1,1024]{1,0:T(1,128)} %copy-done.21, ...), custom_call_target="tpu_custom_call" | custom-call | flops 1048576 | bytes 1048576 | tf_op jit(solution)/shard_map/gradients/pallas_call | solution.py:367
  158.6 4.1 %gradients.14 = (bf16[1,256,1024]{2,1,0:T(8,128)(2,1)}, bf16[1,256,1024]{2,1,0:T(8,128)(2,1)}, f32[1,128]{1,0:T(1,128)}) custom-call(s32[3]{0:T(128)} %get-tuple-element.67.core_ref, f32[1,1024]{1,0:T(1,128)} %copy-done.18, f32[1,1024]{1,0:T(1,128)} %copy-done.19, f32[1,1024]{1,0:T(1,128)} %copy-done.20, f32[1,1024]{1,0:T(1,128)} %copy-done.21, ...), custom_call_target="tpu_custom_call" | custom-call | flops 1048576 | bytes 1048576 | tf_op jit(solution)/shard_map/gradients/pallas_call | solution.py:367
  162.8 4.8 %gradients.15 = (f32[1,256,1024]{2,1,0:T(8,128)}, bf16[1,256,1024]{2,1,0:T(8,128)(2,1)}, f32[1,128]{1,0:T(1,128)}) custom-call(s32[3]{0:T(128)} %get-tuple-element.69.core_ref, f32[1,1024]{1,0:T(1,128)} %copy-done.18, f32[1,1024]{1,0:T(1,128)} %copy-done.19, f32[1,1024]{1,0:T(1,128)} %copy-done.20, f32[1,1024]{1,0:T(1,128)} %copy-done.21, ...), custom_call_target="tpu_custom_call" | custom-call | flops 1048576 | bytes 1048576 | tf_op jit(solution)/shard_map/gradients/pallas_call | solution.py:367
  172.9 7.2 %proto_gradient.1 = (f32[1024,256]{1,0:T(8,128)S(1)}, bf16[4,1024,256]{2,1,0:T(8,128)(2,1)S(1)}) custom-call(s32[4]{0:T(128)S(1)} %pad_add_fusion.index_ref, bf16[256,1024]{1,0:T(8,128)(2,1)S(1)} %bitcast.72, bf16[256,1024]{1,0:T(8,128)(2,1)S(1)} %bitcast.71, bf16[256,1024]{1,0:T(8,128)(2,1)S(1)} %bitcast.68, bf16[256,1024]{1,0:T(8,128)(2,1)S(1)} %bitcast.67, ...), custom_call_target="tpu_custom_call" | custom-call | flops 1048576 | bytes 1048576 | tf_op jit(solution)/shard_map/proto_gradient/pallas_call | solution.py:484
  186.1 2.4 %collective-permute-start.40 = (bf16[1,256,1024]{2,1,0:T(8,128)(2,1)S(1)}, bf16[1,256,1024]{2,1,0:T(8,128)(2,1)}, u32[]{:S(2)}, u32[]{:S(2)}) collective-permute-start(bf16[1,256,1024]{2,1,0:T(8,128)(2,1)S(1)} %add_blocks.5), channel_id=1, source_target_pairs={{0,4},{2,6},{4,0},{6,2},{1,5},{3,7},{5,1},{7,3},{8,12},{10,14},{12... | collective-permute-start | bytes 1572872 | tf_op jit(solution)/shard_map/ppermute | solution.py:540
  188.5 8.9 %collective-permute-done.33 = bf16[1024,256]{1,0:T(8,128)(2,1)S(1)} collective-permute-done((bf16[1024,256]{1,0:T(8,128)(2,1)}, bf16[1024,256]{1,0:T(8,128)(2,1)S(1)}, u32[]{:S(2)}, u32[]{:S(2)}) %collective-permute-start.33) | collective-permute-done | bytes 524320 | tf_op jit(solution)/shard_map/ppermute | solution.py:540
  197.4 9.8 %collective-permute-done.34 = bf16[1024,256]{1,0:T(8,128)(2,1)S(1)} collective-permute-done((bf16[1024,256]{1,0:T(8,128)(2,1)}, bf16[1024,256]{1,0:T(8,128)(2,1)S(1)}, u32[]{:S(2)}, u32[]{:S(2)}) %collective-permute-start.34) | collective-permute-done | bytes 524320 | tf_op jit(solution)/shard_map/ppermute | solution.py:540
  208.0 2.4 %collective-permute-start.37 = (f32[1,128]{1,0:T(1,128)S(1)}, f32[1,128]{1,0:T(1,128)S(1)}, u32[]{:S(2)}, u32[]{:S(2)}) collective-permute-start(f32[1,128]{1,0:T(1,128)S(1)} %add.108), channel_id=1, source_target_pairs={{0,4},{2,6},{4,0},{6,2},{1,5},{3,7},{5,1},{7,3},{8,12},{10,14},{12... | collective-permute-start | bytes 1544 | tf_op jit(solution)/shard_map/ppermute | solution.py:540
  211.7 2.2 convert_add_fusion
  213.9 3.4 %embed_gradient.1 = f32[256,1024]{1,0:T(8,128)} custom-call(s32[1]{0:T(128)} %bitcast.31.index_ref, bf16[2048,1024]{1,0:T(8,128)(2,1)} %embeddings_ref.5, f32[256,1024]{1,0:T(8,128)} %bitcast.93, bf16[256,1024]{1,0:T(8,128)(2,1)} %bitcast.33.refs_1_, bf16[256,1024]{1,0:T(8,128)(2,1)} %bitcast.34.refs_2_, bf16[256,1024]{1,0:T(8,128)(2,1)} %bitcast.35.refs_3_), custom_call_target="tpu_custom_call" | custom-call | flops 2097152 | bytes 4194304 | tf_op jit(solution)/shard_map/embed_gradient/pallas_call | solution.py:520
  (160 shorter events, 56.7 us)
Async XLA Ops:
  7.2 96.9 %all-gather.2.cloned.1.call-start = ((), (), s32[]{:S(2)}) async-start(), calls=%async_computation | async-start | bytes 17825792 | tf_op jit(solution)/shard_map/all_gather | solution.py:577
  22.1 4.6 %collective-permute-start = (f32[1,1024]{1,0:T(1,128)S(1)}, f32[1,1024]{1,0:T(1,128)S(1)}, u32[]{:S(2)}, u32[]{:S(2)}) collective-permute-start(f32[1,1024]{1,0:T(1,128)S(1)} %get-tuple-element.46.refs_0_), channel_id=1, source_target_pairs={{0,8},{8,0},{16,24},{24,16},{1,9},{9,1},{17,25},{25,17},{2,10},{10... | collective-permute-start | bytes 12296 | tf_op jit(solution)/shard_map/ppermute | solution.py:540
  26.6 4.6 %collective-permute-start.2 = (f32[1,1024]{1,0:T(1,128)S(1)}, f32[1,1024]{1,0:T(1,128)S(1)}, u32[]{:S(2)}, u32[]{:S(2)}) collective-permute-start(f32[1,1024]{1,0:T(1,128)S(1)} %get-tuple-element.46.refs_0_), channel_id=1, source_target_pairs={{0,24},{8,16},{16,8},{24,0},{1,25},{9,17},{17,9},{25,1},{2,26},{10... | collective-permute-start | bytes 12296 | tf_op jit(solution)/shard_map/ppermute | solution.py:540
  36.0 4.5 %collective-permute-start.4 = (f32[1,2048]{1,0:T(1,128)S(1)}, f32[1,2048]{1,0:T(1,128)S(1)}, u32[]{:S(2)}, u32[]{:S(2)}) collective-permute-start(f32[1,2048]{1,0:T(1,128)S(1)} %add.89.refs_0_), channel_id=1, source_target_pairs={{0,2},{2,0},{4,6},{6,4},{1,3},{3,1},{5,7},{7,5},{8,10},{10,8},{12,... | collective-permute-start | bytes 24584 | tf_op jit(solution)/shard_map/ppermute | solution.py:540
  37.7 4.7 %collective-permute-start.5 = (f32[1,2048]{1,0:T(1,128)S(1)}, f32[1,2048]{1,0:T(1,128)S(1)}, u32[]{:S(2)}, u32[]{:S(2)}) collective-permute-start(f32[1,2048]{1,0:T(1,128)S(1)} %add.89.refs_0_), channel_id=1, source_target_pairs={{0,4},{2,6},{4,0},{6,2},{1,5},{3,7},{5,1},{7,3},{8,12},{10,14},{12... | collective-permute-start | bytes 24584 | tf_op jit(solution)/shard_map/ppermute | solution.py:540
  40.3 5.6 %collective-permute-start.6 = (f32[1,2048]{1,0:T(1,128)S(1)}, f32[1,2048]{1,0:T(1,128)S(1)}, u32[]{:S(2)}, u32[]{:S(2)}) collective-permute-start(f32[1,2048]{1,0:T(1,128)S(1)} %add.89.refs_0_), channel_id=1, source_target_pairs={{0,6},{2,4},{4,2},{6,0},{1,7},{3,5},{5,3},{7,1},{8,14},{10,12},{12... | collective-permute-start | bytes 24584 | tf_op jit(solution)/shard_map/ppermute | solution.py:540
  47.9 4.6 %collective-permute-start.9 = (f32[1,1024]{1,0:T(1,128)S(1)}, f32[1,1024]{1,0:T(1,128)S(1)}, u32[]{:S(2)}, u32[]{:S(2)}) collective-permute-start(f32[1,1024]{1,0:T(1,128)S(1)} %column_pass.2.refs_0_), channel_id=1, source_target_pairs={{0,24},{8,16},{16,8},{24,0},{1,25},{9,17},{17,9},{25,1},{2,26},{10... | collective-permute-start | bytes 12296 | tf_op jit(solution)/shard_map/ppermute | solution.py:540
  55.1 4.5 %collective-permute-start.11 = (f32[1,2048]{1,0:T(1,128)S(1)}, f32[1,2048]{1,0:T(1,128)S(1)}, u32[]{:S(2)}, u32[]{:S(2)}) collective-permute-start(f32[1,2048]{1,0:T(1,128)S(1)} %add.90.refs_0_), channel_id=1, source_target_pairs={{0,2},{2,0},{4,6},{6,4},{1,3},{3,1},{5,7},{7,5},{8,10},{10,8},{12,... | collective-permute-start | bytes 24584 | tf_op jit(solution)/shard_map/ppermute | solution.py:540
  55.2 4.7 %collective-permute-start.12 = (f32[1,2048]{1,0:T(1,128)S(1)}, f32[1,2048]{1,0:T(1,128)S(1)}, u32[]{:S(2)}, u32[]{:S(2)}) collective-permute-start(f32[1,2048]{1,0:T(1,128)S(1)} %add.90.refs_0_), channel_id=1, source_target_pairs={{0,4},{2,6},{4,0},{6,2},{1,5},{3,7},{5,1},{7,3},{8,12},{10,14},{12... | collective-permute-start | bytes 24584 | tf_op jit(solution)/shard_map/ppermute | solution.py:540
  55.8 5.8 %collective-permute-start.13 = (f32[1,2048]{1,0:T(1,128)S(1)}, f32[1,2048]{1,0:T(1,128)S(1)}, u32[]{:S(2)}, u32[]{:S(2)}) collective-permute-start(f32[1,2048]{1,0:T(1,128)S(1)} %add.90.refs_0_), channel_id=1, source_target_pairs={{0,6},{2,4},{4,2},{6,0},{1,7},{3,5},{5,3},{7,1},{8,14},{10,12},{12... | collective-permute-start | bytes 24584 | tf_op jit(solution)/shard_map/ppermute | solution.py:540
  65.4 4.6 %collective-permute-start.16 = (f32[1,1024]{1,0:T(1,128)S(1)}, f32[1,1024]{1,0:T(1,128)S(1)}, u32[]{:S(2)}, u32[]{:S(2)}) collective-permute-start(f32[1,1024]{1,0:T(1,128)S(1)} %column_pass.3.refs_0_), channel_id=1, source_target_pairs={{0,24},{8,16},{16,8},{24,0},{1,25},{9,17},{17,9},{25,1},{2,26},{10... | collective-permute-start | bytes 12296 | tf_op jit(solution)/shard_map/ppermute | solution.py:540
  75.0 4.5 %collective-permute-start.18 = (f32[2,2048]{1,0:T(2,128)S(1)}, f32[2,2048]{1,0:T(2,128)S(1)}, u32[]{:S(2)}, u32[]{:S(2)}) collective-permute-start(f32[2,2048]{1,0:T(2,128)S(1)} %fusion.1), channel_id=1, source_target_pairs={{0,2},{2,0},{4,6},{6,4},{1,3},{3,1},{5,7},{7,5},{8,10},{10,8},{12,... | collective-permute-start | bytes 49160 | tf_op jit(solution)/shard_map/ppermute | solution.py:540
  75.2 5.8 %collective-permute-start.19 = (f32[2,2048]{1,0:T(2,128)S(1)}, f32[2,2048]{1,0:T(2,128)S(1)}, u32[]{:S(2)}, u32[]{:S(2)}) collective-permute-start(f32[2,2048]{1,0:T(2,128)S(1)} %fusion.1), channel_id=1, source_target_pairs={{0,4},{2,6},{4,0},{6,2},{1,5},{3,7},{5,1},{7,3},{8,12},{10,14},{12... | collective-permute-start | bytes 49160 | tf_op jit(solution)/shard_map/ppermute | solution.py:540
  79.2 5.9 %collective-permute-start.20 = (f32[2,2048]{1,0:T(2,128)S(1)}, f32[2,2048]{1,0:T(2,128)S(1)}, u32[]{:S(2)}, u32[]{:S(2)}) collective-permute-start(f32[2,2048]{1,0:T(2,128)S(1)} %fusion.1), channel_id=1, source_target_pairs={{0,6},{2,4},{4,2},{6,0},{1,7},{3,5},{5,3},{7,1},{8,14},{10,12},{12... | collective-permute-start | bytes 49160 | tf_op jit(solution)/shard_map/ppermute | solution.py:540
  85.1 4.2 %collective-permute-start.21 = (f32[2048]{0:T(1024)S(1)}, f32[2048]{0:T(1024)S(1)}, u32[]{:S(2)}, u32[]{:S(2)}) collective-permute-start(f32[2048]{0:T(1024)S(1)} %bitcast.94), channel_id=1, source_target_pairs={{0,8},{8,0},{16,24},{24,16},{1,9},{9,1},{17,25},{25,17},{2,10},{10... | collective-permute-start | bytes 24584 | tf_op jit(solution)/shard_map/ppermute | solution.py:540
  86.0 4.7 %collective-permute-start.23 = (f32[2048]{0:T(1024)S(1)}, f32[2048]{0:T(1024)S(1)}, u32[]{:S(2)}, u32[]{:S(2)}) collective-permute-start(f32[2048]{0:T(1024)S(1)} %bitcast.96), channel_id=1, source_target_pairs={{0,24},{8,16},{16,8},{24,0},{1,25},{9,17},{17,9},{25,1},{2,26},{10... | collective-permute-start | bytes 24584 | tf_op jit(solution)/shard_map/ppermute | solution.py:540
  129.8 5.2 %collective-permute-start.24 = (bf16[1,256,1024]{2,1,0:T(8,128)(2,1)}, bf16[1,256,1024]{2,1,0:T(8,128)(2,1)S(1)}, u32[]{:S(2)}, u32[]{:S(2)}) collective-permute-start(bf16[1,256,1024]{2,1,0:T(8,128)(2,1)} %get-tuple-element.56), channel_id=1, source_target_pairs={{0,1},{1,0},{2,3},{3,2},{4,5},{5,4},{6,7},{7,6},{8,9},{9,8},{10,11... | collective-permute-start | bytes 1572872 | tf_op jit(solution)/shard_map/ppermute | solution.py:540
  140.3 6.0 %collective-permute-start.25 = (bf16[1,256,1024]{2,1,0:T(8,128)(2,1)}, bf16[1,256,1024]{2,1,0:T(8,128)(2,1)S(1)}, u32[]{:S(2)}, u32[]{:S(2)}) collective-permute-start(bf16[1,256,1024]{2,1,0:T(8,128)(2,1)} %get-tuple-element.62), channel_id=1, source_target_pairs={{0,1},{1,0},{2,3},{3,2},{4,5},{5,4},{6,7},{7,6},{8,9},{9,8},{10,11... | collective-permute-start | bytes 1572872 | tf_op jit(solution)/shard_map/ppermute | solution.py:540
  140.6 29.1 %collective-permute-start.31 = (bf16[1,256,1024]{2,1,0:T(8,128)(2,1)S(1)}, bf16[1,256,1024]{2,1,0:T(8,128)(2,1)S(1)}, u32[]{:S(2)}, u32[]{:S(2)}) collective-permute-start(bf16[1,256,1024]{2,1,0:T(8,128)(2,1)S(1)} %add_blocks.3), channel_id=1, source_target_pairs={{0,2},{2,0},{4,6},{6,4},{1,3},{3,1},{5,7},{7,5},{8,10},{10,8},{12,... | collective-permute-start | bytes 1572872 | tf_op jit(solution)/shard_map/ppermute | solution.py:540
  148.4 31.9 %collective-permute-start.32 = (bf16[1,256,1024]{2,1,0:T(8,128)(2,1)}, bf16[1,256,1024]{2,1,0:T(8,128)(2,1)}, u32[]{:S(2)}, u32[]{:S(2)}) collective-permute-start(bf16[1,256,1024]{2,1,0:T(8,128)(2,1)} %add_blocks.4), channel_id=1, source_target_pairs={{0,2},{2,0},{4,6},{6,4},{1,3},{3,1},{5,7},{7,5},{8,10},{10,8},{12,... | collective-permute-start | bytes 1572872 | tf_op jit(solution)/shard_map/ppermute | solution.py:540
  154.3 25.8 %collective-permute-start.30 = (bf16[1,256,1024]{2,1,0:T(8,128)(2,1)}, bf16[1,256,1024]{2,1,0:T(8,128)(2,1)S(1)}, u32[]{:S(2)}, u32[]{:S(2)}) collective-permute-start(bf16[1,256,1024]{2,1,0:T(8,128)(2,1)} %get-tuple-element.82), channel_id=1, source_target_pairs={{0,1},{1,0},{2,3},{3,2},{4,5},{5,4},{6,7},{7,6},{8,9},{9,8},{10,11... | collective-permute-start | bytes 1572872 | tf_op jit(solution)/shard_map/ppermute | solution.py:540
  168.3 11.8 %collective-permute-start.26 = (f32[1,128]{1,0:T(1,128)S(1)}, f32[1,128]{1,0:T(1,128)S(1)}, u32[]{:S(2)}, u32[]{:S(2)}) collective-permute-start(f32[1,128]{1,0:T(1,128)S(1)} %add_add_fusion.3), channel_id=1, source_target_pairs={{0,8},{8,0},{16,24},{24,16},{1,9},{9,1},{17,25},{25,17},{2,10},{10... | collective-permute-start | bytes 1544 | tf_op jit(solution)/shard_map/ppermute | solution.py:540
  168.4 11.7 %collective-permute-start.27 = (f32[1,128]{1,0:T(1,128)S(1)}, f32[1,128]{1,0:T(1,128)S(1)}, u32[]{:S(2)}, u32[]{:S(2)}) collective-permute-start(f32[1,128]{1,0:T(1,128)S(1)} %add_add_fusion.3), channel_id=1, source_target_pairs={{0,16},{8,24},{16,0},{24,8},{1,17},{9,25},{17,1},{25,9},{2,18},{10... | collective-permute-start | bytes 1544 | tf_op jit(solution)/shard_map/ppermute | solution.py:540
  169.6 10.4 %collective-permute-start.28 = (f32[1,128]{1,0:T(1,128)S(1)}, f32[1,128]{1,0:T(1,128)S(1)}, u32[]{:S(2)}, u32[]{:S(2)}) collective-permute-start(f32[1,128]{1,0:T(1,128)S(1)} %add_add_fusion.3), channel_id=1, source_target_pairs={{0,24},{8,16},{16,8},{24,0},{1,25},{9,17},{17,9},{25,1},{2,26},{10... | collective-permute-start | bytes 1544 | tf_op jit(solution)/shard_map/ppermute | solution.py:540
  181.5 15.9 %collective-permute-start.33 = (bf16[1024,256]{1,0:T(8,128)(2,1)}, bf16[1024,256]{1,0:T(8,128)(2,1)S(1)}, u32[]{:S(2)}, u32[]{:S(2)}) collective-permute-start(bf16[1024,256]{1,0:T(8,128)(2,1)} %get-tuple-element.91), channel_id=1, source_target_pairs={{0,24},{8,16},{16,8},{24,0},{1,25},{9,17},{17,9},{25,1},{2,26},{10... | collective-permute-start | bytes 1572872 | tf_op jit(solution)/shard_map/ppermute | solution.py:540
  182.3 24.9 %collective-permute-start.34 = (bf16[1024,256]{1,0:T(8,128)(2,1)}, bf16[1024,256]{1,0:T(8,128)(2,1)S(1)}, u32[]{:S(2)}, u32[]{:S(2)}) collective-permute-start(bf16[1024,256]{1,0:T(8,128)(2,1)} %get-tuple-element.90), channel_id=1, source_target_pairs={{0,16},{8,24},{16,0},{24,8},{1,17},{9,25},{17,1},{25,9},{2,18},{10... | collective-permute-start | bytes 1572872 | tf_op jit(solution)/shard_map/ppermute | solution.py:540
  183.0 24.3 %collective-permute-start.35 = (bf16[1024,256]{1,0:T(8,128)(2,1)}, bf16[1024,256]{1,0:T(8,128)(2,1)}, u32[]{:S(2)}, u32[]{:S(2)}) collective-permute-start(bf16[1024,256]{1,0:T(8,128)(2,1)} %get-tuple-element.89), channel_id=1, source_target_pairs={{0,8},{8,0},{16,24},{24,16},{1,9},{9,1},{17,25},{25,17},{2,10},{10... | collective-permute-start | bytes 1572872 | tf_op jit(solution)/shard_map/ppermute | solution.py:540
  185.0 28.9 %collective-permute-start.39 = (bf16[1,256,1024]{2,1,0:T(8,128)(2,1)}, bf16[1,256,1024]{2,1,0:T(8,128)(2,1)}, u32[]{:S(2)}, u32[]{:S(2)}) collective-permute-start(bf16[1,256,1024]{2,1,0:T(8,128)(2,1)} %get-tuple-element.88), channel_id=1, source_target_pairs={{0,1},{1,0},{2,3},{3,2},{4,5},{5,4},{6,7},{7,6},{8,9},{9,8},{10,11... | collective-permute-start | bytes 1572872 | tf_op jit(solution)/shard_map/ppermute | solution.py:540
  186.1 27.8 %collective-permute-start.40 = (bf16[1,256,1024]{2,1,0:T(8,128)(2,1)S(1)}, bf16[1,256,1024]{2,1,0:T(8,128)(2,1)}, u32[]{:S(2)}, u32[]{:S(2)}) collective-permute-start(bf16[1,256,1024]{2,1,0:T(8,128)(2,1)S(1)} %add_blocks.5), channel_id=1, source_target_pairs={{0,4},{2,6},{4,0},{6,2},{1,5},{3,7},{5,1},{7,3},{8,12},{10,14},{12... | collective-permute-start | bytes 1572872 | tf_op jit(solution)/shard_map/ppermute | solution.py:540
  207.3 10.0 %collective-permute-start.36 = (f32[1,128]{1,0:T(1,128)S(1)}, f32[1,128]{1,0:T(1,128)S(1)}, u32[]{:S(2)}, u32[]{:S(2)}) collective-permute-start(f32[1,128]{1,0:T(1,128)S(1)} %add.108), channel_id=1, source_target_pairs={{0,2},{2,0},{4,6},{6,4},{1,3},{3,1},{5,7},{7,5},{8,10},{10,8},{12,... | collective-permute-start | bytes 1544 | tf_op jit(solution)/shard_map/ppermute | solution.py:540
  208.0 9.3 %collective-permute-start.37 = (f32[1,128]{1,0:T(1,128)S(1)}, f32[1,128]{1,0:T(1,128)S(1)}, u32[]{:S(2)}, u32[]{:S(2)}) collective-permute-start(f32[1,128]{1,0:T(1,128)S(1)} %add.108), channel_id=1, source_target_pairs={{0,4},{2,6},{4,0},{6,2},{1,5},{3,7},{5,1},{7,3},{8,12},{10,14},{12... | collective-permute-start | bytes 1544 | tf_op jit(solution)/shard_map/ppermute | solution.py:540
  210.4 6.9 %collective-permute-start.38 = (f32[1,128]{1,0:T(1,128)S(1)}, f32[1,128]{1,0:T(1,128)S(1)}, u32[]{:S(2)}, u32[]{:S(2)}) collective-permute-start(f32[1,128]{1,0:T(1,128)S(1)} %add.108), channel_id=1, source_target_pairs={{0,6},{2,4},{4,2},{6,0},{1,7},{3,5},{5,3},{7,1},{8,14},{10,12},{12... | collective-permute-start | bytes 1544 | tf_op jit(solution)/shard_map/ppermute | solution.py:540
  (40 other events, 233.2 us)
Sparse Core Ops, SparseCore 0:
  10.2 93.8 all-gather.1

commit v8 on v7

--- a/solution.py
+++ b/solution.py
@@ -147,7 +147,7 @@
             jax.ShapeDtypeStruct((1, rows), F32),
             jax.ShapeDtypeStruct((1, protos), F32),
         ],
-        compiler_params=params(50),
+        compiler_params=params(28),
         cost_estimate=cost(2 * rows * columns * protos, 22 * MIB, rows * protos),
         name="scores",
     )(embeddings, prototypes)
@@ -219,7 +219,9 @@
     )(*row_totals, *[in_vmem(expo)] * STREAMS)
 
 
-def partner_kernel(first_ref, second_ref, source_ref, wnorm_ref, first_expo_ref, second_expo_ref, table_ref, semaphores, *stages):
+def partner_kernel(count, total, heat_scale, proto_size, parts, first_ref, second_ref, *refs):
+    column_refs = refs[:parts]
+    totals_ref, source_ref, wnorm_ref, scores_ref, dscore_ref, loss_ref, table_ref, semaphores, *stages = refs[parts:]
     step = pl.program_id(0)
     groups = table_ref.shape[1]
 
@@ -238,43 +240,70 @@
         for copy in copies:
             copy.wait()
 
-    rows = first_expo_ref.shape[0]
+    rows = dscore_ref.shape[0]
     wnorm = wnorm_ref[...]
-    chunks = [
-        (which_ref, out_ref, start)
-        for start in range(0, rows, CHUNK)
-        for which_ref, out_ref in ((first_ref, first_expo_ref), (second_ref, second_expo_ref))
-    ]
-    for number, (which_ref, out_ref, start) in enumerate(chunks):
-        stage_ref = stages[number % 2]
-        for row in range(CHUNK):
-            place = which_ref[step * rows + start + row]
-            stage_ref[row * groups : (row + 1) * groups, :] = table_ref[place].astype(F32)
-        unit = jnp.concatenate(
-            [stage_ref[pl.ds(k, CHUNK, stride=groups), :].astype(BF16) for k in range(groups)], axis=1
-        )
-        scores = lax.dot_general(unit, wnorm, (((1,), (1,)), ((), ())), preferred_element_type=F32)
-        soft = jnp.exp(scores * (1.0 / SOFTMAX_HEAT))
-        out_ref[start : start + CHUNK, :] = (soft * soft).astype(out_ref.dtype)
-
-
-def partner_pass(first, second, table, wnorm):
+    scale = 1.0 / (count * total_of(column_refs))
+    place_in = lax.broadcasted_iota(jnp.int32, (8, CHUNK), 0)
+    loss = jnp.zeros((), F32)
+    for start in range(0, rows, CHUNK):
+        at = slice(start, start + CHUNK)
+        row_totals, zsum = totals_ref[0:2, at], totals_ref[2:3, at]
+        weights = total * (1.0 / (total * row_totals))
+        code_totals = 0.5 * jnp.sum(weights * row_totals, axis=0, keepdims=True)
+        log_part = jnp.sum(code_totals * jnp.log(zsum)) * (1.0 / proto_size)
+        stacked = jnp.where(
+            place_in == 0,
+            weights[0:1],
+            jnp.where(place_in == 1, weights[1:2], jnp.where(place_in == 2, code_totals / zsum, 0.0)),
+        ).T
+        codes = []
+        for number, which_ref in enumerate((first_ref, second_ref)):
+            stage_ref = stages[number]
+            for row in range(CHUNK):
+                place = which_ref[step * rows + start + row]
+                stage_ref[row * groups : (row + 1) * groups, :] = table_ref[place].astype(F32)
+            unit = jnp.concatenate(
+                [stage_ref[pl.ds(k, CHUNK, stride=groups), :].astype(BF16) for k in range(groups)], axis=1
+            )
+            scores = lax.dot_general(unit, wnorm, (((1,), (1,)), ((), ())), preferred_element_type=F32)
+            soft = jnp.exp(scores * (1.0 / SOFTMAX_HEAT))
+            expo = soft * soft
+            codes.append((stacked[:, number : number + 1] * expo * scale).astype(BF16).astype(F32))
+        targets = 0.5 * (codes[0] + codes[1])
+        heated = scores_ref[at] * (1.0 / SOFTMAX_HEAT)
+        loss = loss + (log_part - jnp.sum(targets * heated))
+        dscore_ref[at] = ((jnp.exp(heated) * stacked[:, 2:3] - targets) * heat_scale).astype(BF16)
+
+    @pl.when(step == 0)
+    def _():
+        loss_ref[...] = jnp.full(loss_ref.shape, loss, F32)
+
+    @pl.when(step > 0)
+    def _():
+        loss_ref[...] += loss
+
+
+def partner_pass(first, second, columns, totals, table, wnorm, scores, count, total, proto_size):
     rows = first.shape[0]
-    protos, columns = wnorm.shape
-    groups = columns // LANES
+    protos, columns_of_table = wnorm.shape
+    groups = columns_of_table // LANES
     block = 2 * CHUNK
-    return pl.pallas_call(
-        partner_kernel,
+    heat_scale = count / (32.0 * SOFTMAX_HEAT)
+    return pl.pallas_call(
+        functools.partial(partner_kernel, count, total, heat_scale, proto_size, len(columns)),
         grid_spec=pltpu.PrefetchScalarGridSpec(
             num_scalar_prefetch=2,
             grid=(rows // block,),
-            in_specs=[
+            in_specs=[pl.BlockSpec((1, protos), lambda i, *_: (0, 0)) for _ in columns]
+            + [
+                pl.BlockSpec((3, block), lambda i, *_: (0, i)),
                 pl.BlockSpec(memory_space=pl.ANY),
-                pl.BlockSpec((protos, columns), lambda i, *_: (0, 0), pipeline_mode=pl.Buffered(1)),
+                pl.BlockSpec(wnorm.shape, lambda i, *_: (0, 0), pipeline_mode=pl.Buffered(1)),
+                pl.BlockSpec((block, protos), lambda i, *_: (i, 0)),
             ],
             out_specs=[
                 pl.BlockSpec((block, protos), lambda i, *_: (i, 0)),
-                pl.BlockSpec((block, protos), lambda i, *_: (i, 0)),
+                pl.BlockSpec((1, LANES), lambda i, *_: (0, 0)),
             ],
             scratch_shapes=[
                 pltpu.VMEM(table.shape, BF16),
@@ -282,11 +311,11 @@
             ]
             + [pltpu.VMEM((CHUNK * groups, LANES), F32)] * 2,
         ),
-        out_shape=[jax.ShapeDtypeStruct((rows, protos), BF16)] * 2,
-        compiler_params=params(40),
-        cost_estimate=cost(4 * rows * columns * protos, 28 * MIB, 2 * rows * protos),
+        out_shape=[jax.ShapeDtypeStruct((rows, protos), BF16), jax.ShapeDtypeStruct((1, LANES), F32)],
+        compiler_params=params(46),
+        cost_estimate=cost(4 * rows * columns_of_table * protos, 32 * MIB, 3 * rows * protos),
         name="partner_scores",
-    )(first, second, table, wnorm)
+    )(first, second, *columns, totals, table, wnorm, scores)
 
 
 def lookup_kernel(first_ref, second_ref, totals_ref, out_ref):
@@ -316,84 +345,32 @@
     )(first, second, totals)
 
 
-def gradient_kernel(count, total, heat_scale, proto_size, parts, core_ref, *refs):
-    del core_ref
-    column_refs, row_refs = refs[: parts[0]], refs[parts[0] : parts[0] + parts[1]]
-    first_ref, second_ref, scores_ref, wnorm_ref, gunit_ref, dscore_ref, loss_ref = refs[parts[0] + parts[1] :]
-    step = pl.program_id(0)
-    scale = 1.0 / (count * total_of(column_refs))
-    totals = total_of(row_refs)
-    share = totals.shape[-1]
-    place = lax.broadcasted_iota(jnp.int32, (8, share), 0)
-    loss = jnp.zeros((), F32)
-    for group in range(totals.shape[0]):
-        row_totals, zsum = totals[group, 0:2], totals[group, 2:3]
-        weights = total * (1.0 / (total * row_totals))
-        code_totals = 0.5 * jnp.sum(weights * row_totals, axis=0, keepdims=True)
-        log_part = jnp.sum(code_totals * jnp.log(zsum)) * (1.0 / proto_size)
-        stacked = jnp.where(
-            place == 0,
-            weights[0:1],
-            jnp.where(place == 1, weights[1:2], jnp.where(place == 2, code_totals / zsum, 0.0)),
-        ).T
-        first = (stacked[:, 0:1] * first_ref[group].astype(F32) * scale).astype(BF16).astype(F32)
-        second = (stacked[:, 1:2] * second_ref[group].astype(F32) * scale).astype(BF16).astype(F32)
-        targets = 0.5 * (first + second)
-        heated = scores_ref[group] * (1.0 / SOFTMAX_HEAT)
-        loss = loss + (log_part - jnp.sum(targets * heated))
-        dscore = ((jnp.exp(heated) * stacked[:, 2:3] - targets) * heat_scale).astype(BF16)
-        dscore_ref[group] = dscore
-        gunit = jnp.dot(dscore, wnorm_ref[...], preferred_element_type=F32)
-        gunit_ref[group] = gunit.astype(gunit_ref.dtype)
-
-    @pl.when(step == 0)
-    def _():
-        loss_ref[...] = jnp.full(loss_ref.shape, loss, F32)
-
-    @pl.when(step > 0)
-    def _():
-        loss_ref[...] += loss
-
-
-def gradients(where, columns, row_totals, first, second, scores, wnorm, count, total, proto_size, dtype):
-    rows, protos = first.shape
+def gradient_kernel(where_ref, dscore_ref, wnorm_ref, gunit_ref):
+    del where_ref
+    gunit_ref[0] = jnp.dot(dscore_ref[0], wnorm_ref[...], preferred_element_type=F32).astype(gunit_ref.dtype)
+
+
+def gradients(where, dscore, wnorm, dtype):
+    top, share, protos = dscore.shape[0], *dscore.shape[4:]
     width = wnorm.shape[1]
-    heat_scale = count / (32.0 * SOFTMAX_HEAT)
-    _, places, _, share = row_totals[0].shape
-    top = places // 4
-    at = pl.BlockSpec((1, None, None, None, share, protos), lambda i, where: (i, where[0], where[1], where[2], 0, 0))
-    first, second, scores = [value.reshape(top, 2, 2, 2, share, protos) for value in (first, second, scores)]
-    row_totals = [value.reshape(2, top, 2, 2, 3, share) for value in row_totals]
-    return pl.pallas_call(
-        functools.partial(
-            gradient_kernel, count, total, heat_scale, proto_size, (len(columns), len(row_totals))
-        ),
+    return pl.pallas_call(
+        gradient_kernel,
         grid_spec=pltpu.PrefetchScalarGridSpec(
             num_scalar_prefetch=1,
             grid=(top,),
-            in_specs=[pl.BlockSpec((1, protos), lambda i, where: (0, 0)) for _ in columns]
-            + [
+            in_specs=[
                 pl.BlockSpec(
-                    (None, 1, None, None, 3, share), lambda i, where: (where[2], i, where[0], where[1], 0, 0)
-                )
-                for _ in row_totals
-            ]
-            + [at, at, at, pl.BlockSpec((protos, width), lambda i, where: (0, 0), pipeline_mode=pl.Buffered(1))],
-            out_specs=[
-                pl.BlockSpec((1, share, width), lambda i, where: (i, 0, 0)),
-                pl.BlockSpec((1, share, protos), lambda i, where: (i, 0, 0)),
-                pl.BlockSpec((1, LANES), lambda i, where: (0, 0)),
+                    (1, None, None, None, share, protos), lambda i, where: (i, where[0], where[1], where[2], 0, 0)
+                ),
+                pl.BlockSpec((protos, width), lambda i, where: (0, 0), pipeline_mode=pl.Buffered(1)),
             ],
+            out_specs=pl.BlockSpec((1, share, width), lambda i, where: (i, 0, 0)),
         ),
-        out_shape=[
-            jax.ShapeDtypeStruct((top, share, width), dtype),
-            jax.ShapeDtypeStruct((top, share, protos), BF16),
-            jax.ShapeDtypeStruct((1, LANES), F32),
-        ],
-        compiler_params=params(44),
+        out_shape=jax.ShapeDtypeStruct((top, share, width), dtype),
+        compiler_params=params(16),
         cost_estimate=cost(MIB, MIB),
         name="gradients",
-    )(where, *columns, *row_totals, in_vmem(first), in_vmem(second), scores, in_vmem(wnorm))
+    )(where, in_vmem(dscore), in_vmem(wnorm))
 
 
 def add_kernel(*refs):
@@ -455,29 +432,35 @@
     both = (((0,), (0,)), ((), ()))
     total = None
     for dscore_ref, unit_ref in zip(dscore_refs, unit_refs):
-        rows, part = dscore_ref.shape[0], unit_ref.shape[-1]
+        rows, protos, part = dscore_ref.shape[0] * dscore_ref.shape[1], dscore_ref.shape[2], unit_ref.shape[-1]
         term = lax.dot_general(
-            dscore_ref[...], unit_ref[...].reshape(rows, part), both, preferred_element_type=F32
+            dscore_ref[...].reshape(rows, protos), unit_ref[...].reshape(rows, part), both, preferred_element_type=F32
         )
         total = term if total is None else total + term
     sent_ref[...] = total.astype(BF16)
     own_ref[...] = total
 
 
-def proto_gradient(index, dscores, unit, batch_size):
-    top, share, protos = dscores[0].shape
+def proto_gradient(dscore, unit, index, batch_size):
+    top, share, protos = dscore.shape[0], *dscore.shape[4:]
     width = unit.shape[1]
     part = width // batch_size
     rows = top * share
     last = batch_size - 1
     unit = unit.reshape(top, 2, 2, 2, share, width)
-    dscore_at = pl.BlockSpec((rows, protos), lambda i, index: (0, 0), pipeline_mode=pl.Buffered(1))
+
+    def dscore_at(number):
+        return pl.BlockSpec(
+            (top, None, None, None, share, protos),
+            lambda i, index: (0, number >> 2, number >> 1 & 1, number & 1, 0, 0),
+            pipeline_mode=pl.Buffered(1),
+        )
 
     def unit_at(number):
         return pl.BlockSpec(
             (top, None, None, None, share, part),
             lambda i, index: (
-                0, index[1] ^ (number >> 2), index[2] ^ (number >> 1 & 1), index[3] ^ (number & 1), 0, index[0] ^ (last - i),
+                0, number >> 2, number >> 1 & 1, number & 1, 0, index[0] ^ (last - i),
             ),
         )
 
@@ -486,7 +469,7 @@
         grid_spec=pltpu.PrefetchScalarGridSpec(
             num_scalar_prefetch=1,
             grid=(batch_size,),
-            in_specs=[dscore_at] * 8 + [unit_at(number) for number in range(8)],
+            in_specs=[dscore_at(number) for number in range(8)] + [unit_at(number) for number in range(8)],
             out_specs=[
                 pl.BlockSpec((protos, part), lambda i, index: (0, 0)),
                 pl.BlockSpec((None, protos, part), lambda i, index: (last - i, 0, 0)),
@@ -499,7 +482,7 @@
         compiler_params=params(20),
         cost_estimate=cost(MIB, MIB),
         name="proto_gradient",
-    )(index, *[in_vmem(dscore.reshape(rows, protos)) for dscore in dscores], *[unit] * 8)
+    )(index, *[in_vmem(dscore)] * 8, *[unit] * 8)
 
 
 def embed_gradient_kernel(index_ref, embeddings_ref, *refs):
@@ -589,26 +572,20 @@
     away = (partners // row_count ^ batch_index) * row_count + partners % row_count
     partner_totals = lookup(away[:, 0], away[:, 1], all_totals).reshape(2, row_count)
     row_totals = jnp.concatenate([partner_totals, zsum[None]], axis=0)
-    row_totals = [row_totals.reshape(3, places, 2, share).transpose(2, 1, 0, 3)]
-
-    first, second = partner_pass(partners[:, 0], partners[:, 1], table, wnorm)
-    others = (scores, wnorm, centroids, total_rows, proto_size)
+    dscore, loss = partner_pass(
+        partners[:, 0], partners[:, 1], columns, row_totals, table, wnorm, scores, centroids, total_rows, proto_size
+    )
+    dscore = dscore.reshape(places // 4, 2, 2, 2, share, proto_count)
 
     def after(value, *earlier):
         return lax.optimization_barrier((value, *earlier))[0]
 
-    losses, dscores = [], {}
-
     def part_of(number, *earlier):
         place_bits = [middle ^ (number >> 1), low ^ (number & 1)]
 
         def run(other, dtype):
             where = after(jnp.stack(place_bits + [core ^ other]).astype(jnp.int32), *earlier)
-            gunit, dscores[2 * number + other], loss = gradients(
-                where, columns, row_totals, first, second, *others, dtype
-            )
-            losses.append(loss)
-            return gunit
+            return gradients(where, dscore, wnorm, dtype)
 
         gunit = run(1, BF16)
         return [run(0, F32), swap(gunit, "core", 1)]
@@ -620,10 +597,8 @@
     across = part_of(2, near)
     values = part_of(0, near)
 
-    loss = functools.reduce(jnp.add, losses)
     loss = functools.reduce(jnp.add, parts_of(loss, "batch"))
-    index = jnp.stack([batch_index, middle, low, core]).astype(jnp.int32)
-    grad_proto, proto_sent = proto_gradient(index, [dscores[number] for number in range(8)], unit, batch_size)
+    grad_proto, proto_sent = proto_gradient(dscore, unit, scalar(batch_index), batch_size)
     from_forwarder = after(from_forwarder, proto_sent)
     across = add_blocks(across + [from_forwarder], BF16)
     values += [from_near, swap(across, PLACE, 2)]

time: 226 us -> 205 us (0.907)
  Pallas kernels: 96.1 us -> 73.5 us
  waiting for transfers between devices: 50.6 us -> 58 us
  other arithmetic: 5.69 us -> 3.04 us
    pallas_call x9, Pallas kernels: 53.7 us -> 36.3 us  [the longest x1 25.6 us: partner_pass(): pl.pallas_call(functools.partial(partner_kernel, count, total, heat_scale...]
    pallas_call x1, Pallas kernels: 12.2 us -> 7.93 us  [scores_of(): pl.pallas_call(scores_kernel, grid=(rows // share // 2,), in_specs=[pl.Bl...]
    ppermute x41, waiting for transfers between devices: 47.9 us -> 51.8 us  [swap(): return lax.ppermute(value, axis, [(i, i ^ distance) for i in range(size)])]
    all_gather x1, waiting for transfers between devices: 2.62 us -> 6.14 us  [on_device(): table = lax.all_gather(own, ('batch', 'low', 'core'), axis=0, tiled=True)]
    unnamed x60 -> x24, local copies, waits for them, and re-layouts: 9.72 us -> 9.31 us
  transfers between devices with their start and end apart: 42 -> 42, of which waited for: 24 -> 28; matrix products, arithmetic and copies ran while one was open for 3% -> 2% of each run, Pallas kernels for 29% -> 21%
where the time goes in v8:
time: 205 us
  Pallas kernels  73.5 us (36%)
  waiting for transfers between devices  58 us (28%)
  starting transfers between devices  44.4 us (22%)
  between operations  15.6 us (8%)
  local copies, waits for them, and re-layouts  10.6 us (5%)
  other arithmetic  3.04 us (1%)
    ppermute x41, waiting for transfers between devices, swap(): return lax.ppermute(value, axis, [(i, i ^ distance) for i in range(size)])  51.8 us
    ppermute x41, starting transfers between devices, swap(): return lax.ppermute(value, axis, [(i, i ^ distance) for i in range(size)])  44.3 us
    pallas_call x1, Pallas kernels, partner_pass(): pl.pallas_call(functools.partial(partner_kernel, count, total, heat_scale...  25.6 us
    pallas_call x8, Pallas kernels, gradients(): pl.pallas_call(gradient_kernel, grid_spec=pltpu.PrefetchScalarGridSpec(nu...  10.7 us
    pallas_call x1, Pallas kernels, lookup(): pl.pallas_call(lookup_kernel, grid_spec=pltpu.PrefetchScalarGridSpec(num_...  10.1 us
    unnamed x24, local copies, waits for them, and re-layouts  9.31 us
    pallas_call x1, Pallas kernels, scores_of(): pl.pallas_call(scores_kernel, grid=(rows // share // 2,), in_specs=[pl.Bl...  7.93 us
    pallas_call x1, Pallas kernels, proto_gradient(): pl.pallas_call(proto_gradient_kernel, grid_spec=pltpu.PrefetchScalarGridS...  6.28 us
  transfers between devices with their start and end apart: 42, of which 28 were waited for; matrix products, arithmetic and copies ran while one was open for 2% of the time, Pallas kernels for 21%

profile of v8, /device:TPU:0, one launch (start us, length us, event | category | flops | bytes accessed | tf_op | source)
XLA Modules:
  0.0 205.1 jit_solution(11452849730027275636)
XLA Ops:
  7.2 2.6 %own_rows.1 = bf16[512,8,128]{2,1,0:T(8,128)(2,1)} custom-call(s32[1]{0:T(128)} %bitcast.5.index_ref, bf16[2048,1024]{1,0:T(8,128)(2,1)} %embeddings_ref.5), custom_call_target="tpu_custom_call" | custom-call | tf_op jit(solution)/shard_map/own_rows/pallas_call | solution.py:78
  9.9 2.2 %copy-done.6 = bf16[2048,1024]{1,0:T(8,128)(2,1)S(1)} copy-done((bf16[2048,1024]{1,0:T(8,128)(2,1)S(1)}, bf16[2048,1024]{1,0:T(8,128)(2,1)}, u32[]{:S(2)}) %copy-start.6) | copy-done | bytes 4194328
  13.6 7.9 %scores.1 = (bf16[2048,1024]{1,0:T(8,128)(2,1)S(1)}, bf16[1024,1024]{1,0:T(8,128)(2,1)S(1)}, f32[2048,1024]{1,0:T(8,128)S(1)}, bf16[2048,1024]{1,0:T(8,128)(2,1)...) custom-call(bf16[2048,1024]{1,0:T(8,128)(2,1)S(1)} %copy-done.6, bf16[1024,1024]{1,0:T(8,128)(2,1)S(1)} %copy-done.8), custom_call_target="tpu_custom_call" | custom-call | flops 4294967296 | bytes 23068672 | tf_op jit(solution)/shard_map/scores/pallas_call | solution.py:127
  21.6 3.0 %collective-permute-start = (f32[1,1024]{1,0:T(1,128)S(1)}, f32[1,1024]{1,0:T(1,128)S(1)}, u32[]{:S(2)}, u32[]{:S(2)}) collective-permute-start(f32[1,1024]{1,0:T(1,128)S(1)} %get-tuple-element.22.refs_0_), channel_id=1, source_target_pairs={{0,8},{8,0},{16,24},{24,16},{1,9},{9,1},{17,25},{25,17},{2,10},{10... | collective-permute-start | bytes 12296 | tf_op jit(solution)/shard_map/ppermute | solution.py:523
  26.3 2.0 collective-permute-done.1.refs_2_
  28.2 2.5 %collective-permute-done.2.refs_3_ = f32[1,1024]{1,0:T(1,128)S(1)} collective-permute-done((f32[1,1024]{1,0:T(1,128)S(1)}, f32[1,1024]{1,0:T(1,128)S(1)}, u32[]{:S(2)}, u32[]{:S(2)}) %collective-permute-start.2) | collective-permute-done | bytes 4128 | tf_op jit(solution)/shard_map/ppermute | solution.py:523
  35.0 2.6 %collective-permute-start.5 = (f32[1,2048]{1,0:T(1,128)S(1)}, f32[1,2048]{1,0:T(1,128)S(1)}, u32[]{:S(2)}, u32[]{:S(2)}) collective-permute-start(f32[1,2048]{1,0:T(1,128)S(1)} %add.68.refs_0_), channel_id=1, source_target_pairs={{0,4},{2,6},{4,0},{6,2},{1,5},{3,7},{5,1},{7,3},{8,12},{10,14},{12... | collective-permute-start | bytes 24584 | tf_op jit(solution)/shard_map/ppermute | solution.py:523
  37.8 1.8 collective-permute-done.5.refs_2_
  39.7 3.5 %collective-permute-done.6.refs_3_ = f32[1,2048]{1,0:T(1,128)S(1)} collective-permute-done((f32[1,2048]{1,0:T(1,128)S(1)}, f32[1,2048]{1,0:T(1,128)S(1)}, u32[]{:S(2)}, u32[]{:S(2)}) %collective-permute-start.6) | collective-permute-done | bytes 8224 | tf_op jit(solution)/shard_map/ppermute | solution.py:523
  45.0 2.5 %collective-permute-start.9 = (f32[1,1024]{1,0:T(1,128)S(1)}, f32[1,1024]{1,0:T(1,128)S(1)}, u32[]{:S(2)}, u32[]{:S(2)}) collective-permute-start(f32[1,1024]{1,0:T(1,128)S(1)} %column_pass.2.refs_0_), channel_id=1, source_target_pairs={{0,24},{8,16},{16,8},{24,0},{1,25},{9,17},{17,9},{25,1},{2,26},{10... | collective-permute-start | bytes 12296 | tf_op jit(solution)/shard_map/ppermute | solution.py:523
  53.0 3.7 %collective-permute-start.13 = (f32[1,2048]{1,0:T(1,128)S(1)}, f32[1,2048]{1,0:T(1,128)S(1)}, u32[]{:S(2)}, u32[]{:S(2)}) collective-permute-start(f32[1,2048]{1,0:T(1,128)S(1)} %add.69.refs_0_), channel_id=1, source_target_pairs={{0,6},{2,4},{4,2},{6,0},{1,7},{3,5},{5,3},{7,1},{8,14},{10,12},{12... | collective-permute-start | bytes 24584 | tf_op jit(solution)/shard_map/ppermute | solution.py:523
  57.0 1.7 collective-permute-done.13.refs_3_
  64.7 2.5 %collective-permute-done.16.refs_3_ = f32[1,1024]{1,0:T(1,128)S(1)} collective-permute-done((f32[1,1024]{1,0:T(1,128)S(1)}, f32[1,1024]{1,0:T(1,128)S(1)}, u32[]{:S(2)}, u32[]{:S(2)}) %collective-permute-start.16) | collective-permute-done | bytes 4128 | tf_op jit(solution)/shard_map/ppermute | solution.py:523
  67.2 2.3 %copy-done.1 = bf16[2048,1024]{1,0:T(8,128)(2,1)S(1)} copy-done((bf16[2048,1024]{1,0:T(8,128)(2,1)S(1)}, bf16[2048,1024]{1,0:T(8,128)(2,1)}, u32[]{:S(2)}) %copy-start.1) | copy-done | bytes 4194328
  72.5 4.0 %collective-permute-start.19 = (f32[2,2048]{1,0:T(2,128)S(1)}, f32[2,2048]{1,0:T(2,128)S(1)}, u32[]{:S(2)}, u32[]{:S(2)}) collective-permute-start(f32[2,2048]{1,0:T(2,128)S(1)} %fusion.1), channel_id=1, source_target_pairs={{0,4},{2,6},{4,0},{6,2},{1,5},{3,7},{5,1},{7,3},{8,12},{10,14},{12... | collective-permute-start | bytes 49160 | tf_op jit(solution)/shard_map/ppermute | solution.py:523
  78.3 4.0 %collective-permute-done.20 = f32[2,2048]{1,0:T(2,128)S(1)} collective-permute-done((f32[2,2048]{1,0:T(2,128)S(1)}, f32[2,2048]{1,0:T(2,128)S(1)}, u32[]{:S(2)}, u32[]{:S(2)}) %collective-permute-start.20) | collective-permute-done | bytes 16416 | tf_op jit(solution)/shard_map/ppermute | solution.py:523
  83.1 2.8 %collective-permute-start.23 = (f32[2048]{0:T(1024)S(1)}, f32[2048]{0:T(1024)S(1)}, u32[]{:S(2)}, u32[]{:S(2)}) collective-permute-start(f32[2048]{0:T(1024)S(1)} %bitcast.60), channel_id=1, source_target_pairs={{0,24},{8,16},{16,8},{24,0},{1,25},{9,17},{17,9},{25,1},{2,26},{10... | collective-permute-start | bytes 24584 | tf_op jit(solution)/shard_map/ppermute | solution.py:523
  87.8 10.1 %lookup.1 = f32[4096]{0:T(1024)S(1)} custom-call(s32[2048]{0:T(1024)S(1)} %bitcast.54, s32[2048]{0:T(1024)S(1)} %bitcast.53, f32[8192]{0:T(1024)S(1)} %pad_maximum_fusion.totals_ref), custom_call_target="tpu_custom_call" | custom-call | flops 1048576 | bytes 1048576 | tf_op jit(solution)/shard_map/lookup/pallas_call | solution.py:333
  97.9 6.1 %all-gather.2.cloned.1.call-done.refs_5_ = bf16[8192,8,128]{2,1,0:T(8,128)(2,1)} async-done(((bf16[512,8,128]{2,1,0:T(8,128)(2,1)}), bf16[8192,8,128]{2,1,0:T(8,128)(2,1)}) %all-gather.2.cloned.1.call-update) | async-done | bytes 16777232 | tf_op jit(solution)/shard_map/all_gather | solution.py:560
  104.1 25.6 %partner_scores.1 = (bf16[2048,1024]{1,0:T(8,128)(2,1)S(1)}, f32[1,128]{1,0:T(1,128)S(1)}) custom-call(s32[2048]{0:T(1024)S(1)} %bitcast.56, s32[2048]{0:T(1024)S(1)} %bitcast.55, f32[1,1024]{1,0:T(1,128)S(1)} %column_pass.3.refs_0_, f32[1,1024]{1,0:T(1,128)S(1)} %collective-permute-done.14.refs_1_, f32[1,1024]{1,0:T(1,128)S(1)} %collective-permute-done.15.refs_2_, ...), custom_call_target="tpu_custom_call" | custom-call | flops 8589934592 | bytes 33554432 | tf_op jit(solution)/shard_map/partner_scores/pallas_call | solution.py:292
  140.8 2.3 %collective-permute-done.24 = f32[1,128]{1,0:T(1,128)S(1)} collective-permute-done((f32[1,128]{1,0:T(1,128)S(1)}, f32[1,128]{1,0:T(1,128)S(1)}, u32[]{:S(2)}, u32[]{:S(2)}) %collective-permute-start.24) | collective-permute-done | bytes 544 | tf_op jit(solution)/shard_map/ppermute | solution.py:523
  143.8 6.3 %proto_gradient.1 = (f32[1024,256]{1,0:T(8,128)S(1)}, bf16[4,1024,256]{2,1,0:T(8,128)(2,1)S(1)}) custom-call(s32[1]{0:T(128)} %bitcast.6.index_ref, bf16[1,2,2,2,256,1024]{5,4,3,2,1,0:T(8,128)(2,1)S(1)} %bitcast.33, bf16[1,2,2,2,256,1024]{5,4,3,2,1,0:T(8,128)(2,1)S(1)} %bitcast.34, bf16[1,2,2,2,256,1024]{5,4,3,2,1,0:T(8,128)(2,1)S(1)} %bitcast.35, ...), custom_call_target="tpu_custom_call" | custom-call | flops 1048576 | bytes 1048576 | tf_op jit(solution)/shard_map/proto_gradient/pallas_call | solution.py:467
  152.4 7.6 %collective-permute-done.32 = bf16[1,256,1024]{2,1,0:T(8,128)(2,1)S(1)} collective-permute-done((bf16[1,256,1024]{2,1,0:T(8,128)(2,1)S(1)}, bf16[1,256,1024]{2,1,0:T(8,128)(2,1)S(1)}, u32[]{:S(2)}, u32[]{:S(2)}) %collective-permute-start.32) | collective-permute-done | bytes 524320 | tf_op jit(solution)/shard_map/ppermute | solution.py:523
  162.7 1.9 collective-permute-start.35
  164.7 2.0 gradients.15
  167.2 2.4 %collective-permute-start.40 = (bf16[1,256,1024]{2,1,0:T(8,128)(2,1)}, bf16[1,256,1024]{2,1,0:T(8,128)(2,1)}, u32[]{:S(2)}, u32[]{:S(2)}) collective-permute-start(bf16[1,256,1024]{2,1,0:T(8,128)(2,1)} %add_blocks.5), channel_id=1, source_target_pairs={{0,4},{2,6},{4,0},{6,2},{1,5},{3,7},{5,1},{7,3},{8,12},{10,14},{12... | collective-permute-start | bytes 1572872 | tf_op jit(solution)/shard_map/ppermute | solution.py:523
  169.6 2.2 %copy-done.3 = bf16[2048,1024]{1,0:T(8,128)(2,1)S(1)} copy-done((bf16[2048,1024]{1,0:T(8,128)(2,1)S(1)}, bf16[2048,1024]{1,0:T(8,128)(2,1)}, u32[]{:S(2)}) %copy-start.3) | copy-done | bytes 4194328
  174.1 3.2 %collective-permute-done.33 = bf16[1024,256]{1,0:T(8,128)(2,1)} collective-permute-done((bf16[1024,256]{1,0:T(8,128)(2,1)}, bf16[1024,256]{1,0:T(8,128)(2,1)}, u32[]{:S(2)}, u32[]{:S(2)}) %collective-permute-start.33) | collective-permute-done | bytes 524320 | tf_op jit(solution)/shard_map/ppermute | solution.py:523
  177.2 8.7 %collective-permute-done.34 = bf16[1024,256]{1,0:T(8,128)(2,1)} collective-permute-done((bf16[1024,256]{1,0:T(8,128)(2,1)}, bf16[1024,256]{1,0:T(8,128)(2,1)}, u32[]{:S(2)}, u32[]{:S(2)}) %collective-permute-start.34) | collective-permute-done | bytes 524320 | tf_op jit(solution)/shard_map/ppermute | solution.py:523
  187.5 2.4 %collective-permute-start.37 = (f32[1,128]{1,0:T(1,128)S(1)}, f32[1,128]{1,0:T(1,128)S(1)}, u32[]{:S(2)}, u32[]{:S(2)}) collective-permute-start(f32[1,128]{1,0:T(1,128)S(1)} %add.80), channel_id=1, source_target_pairs={{0,4},{2,6},{4,0},{6,2},{1,5},{3,7},{5,1},{7,3},{8,12},{10,14},{12... | collective-permute-start | bytes 1544 | tf_op jit(solution)/shard_map/ppermute | solution.py:523
  191.2 2.5 %convert_add_fusion = f32[1024,256]{1,0:T(8,128)} fusion(bf16[1024,256]{1,0:T(8,128)(2,1)} %collective-permute-done.35, bf16[1024,256]{1,0:T(8,128)(2,1)} %collective-permute-done.34, f32[1024,256]{1,0:T(8,128)S(1)} %get-tuple-element.38, bf16[1024,256]{1,0:T(8,128)(2,1)} %collective-permute-done.33), kind=kLoop, calls=%fused_computation | loop fusion | flops 1572864 | bytes 3670016 | tf_op jit(solution)/shard_map/add | solution.py:618
  193.7 3.4 %embed_gradient.1 = f32[256,1024]{1,0:T(8,128)} custom-call(s32[1]{0:T(128)} %bitcast.19.index_ref, bf16[2048,1024]{1,0:T(8,128)(2,1)} %embeddings_ref.5, f32[256,1024]{1,0:T(8,128)} %bitcast.52, bf16[256,1024]{1,0:T(8,128)(2,1)} %bitcast.21.refs_1_, bf16[256,1024]{1,0:T(8,128)(2,1)} %bitcast.57, bf16[256,1024]{1,0:T(8,128)(2,1)} %bitcast.23.refs_3_), custom_call_target="tpu_custom_call" | custom-call | flops 2097152 | bytes 4194304 | tf_op jit(solution)/shard_map/embed_gradient/pallas_call | solution.py:503
  (120 shorter events, 51.2 us)
Async XLA Ops:
  7.2 96.9 %all-gather.2.cloned.1.call-start = ((), (), s32[]{:S(2)}) async-start(), calls=%async_computation | async-start | bytes 17825792 | tf_op jit(solution)/shard_map/all_gather | solution.py:560
  21.6 4.7 %collective-permute-start = (f32[1,1024]{1,0:T(1,128)S(1)}, f32[1,1024]{1,0:T(1,128)S(1)}, u32[]{:S(2)}, u32[]{:S(2)}) collective-permute-start(f32[1,1024]{1,0:T(1,128)S(1)} %get-tuple-element.22.refs_0_), channel_id=1, source_target_pairs={{0,8},{8,0},{16,24},{24,16},{1,9},{9,1},{17,25},{25,17},{2,10},{10... | collective-permute-start | bytes 12296 | tf_op jit(solution)/shard_map/ppermute | solution.py:523
  26.1 4.6 %collective-permute-start.2 = (f32[1,1024]{1,0:T(1,128)S(1)}, f32[1,1024]{1,0:T(1,128)S(1)}, u32[]{:S(2)}, u32[]{:S(2)}) collective-permute-start(f32[1,1024]{1,0:T(1,128)S(1)} %get-tuple-element.22.refs_0_), channel_id=1, source_target_pairs={{0,24},{8,16},{16,8},{24,0},{1,25},{9,17},{17,9},{25,1},{2,26},{10... | collective-permute-start | bytes 12296 | tf_op jit(solution)/shard_map/ppermute | solution.py:523
  33.4 4.5 %collective-permute-start.4 = (f32[1,2048]{1,0:T(1,128)S(1)}, f32[1,2048]{1,0:T(1,128)S(1)}, u32[]{:S(2)}, u32[]{:S(2)}) collective-permute-start(f32[1,2048]{1,0:T(1,128)S(1)} %add.68.refs_0_), channel_id=1, source_target_pairs={{0,2},{2,0},{4,6},{6,4},{1,3},{3,1},{5,7},{7,5},{8,10},{10,8},{12,... | collective-permute-start | bytes 24584 | tf_op jit(solution)/shard_map/ppermute | solution.py:523
  35.0 4.7 %collective-permute-start.5 = (f32[1,2048]{1,0:T(1,128)S(1)}, f32[1,2048]{1,0:T(1,128)S(1)}, u32[]{:S(2)}, u32[]{:S(2)}) collective-permute-start(f32[1,2048]{1,0:T(1,128)S(1)} %add.68.refs_0_), channel_id=1, source_target_pairs={{0,4},{2,6},{4,0},{6,2},{1,5},{3,7},{5,1},{7,3},{8,12},{10,14},{12... | collective-permute-start | bytes 24584 | tf_op jit(solution)/shard_map/ppermute | solution.py:523
  37.6 5.6 %collective-permute-start.6 = (f32[1,2048]{1,0:T(1,128)S(1)}, f32[1,2048]{1,0:T(1,128)S(1)}, u32[]{:S(2)}, u32[]{:S(2)}) collective-permute-start(f32[1,2048]{1,0:T(1,128)S(1)} %add.68.refs_0_), channel_id=1, source_target_pairs={{0,6},{2,4},{4,2},{6,0},{1,7},{3,5},{5,3},{7,1},{8,14},{10,12},{12... | collective-permute-start | bytes 24584 | tf_op jit(solution)/shard_map/ppermute | solution.py:523
  44.0 3.7 %collective-permute-start.7 = (f32[1,1024]{1,0:T(1,128)S(1)}, f32[1,1024]{1,0:T(1,128)S(1)}, u32[]{:S(2)}, u32[]{:S(2)}) collective-permute-start(f32[1,1024]{1,0:T(1,128)S(1)} %column_pass.2.refs_0_), channel_id=1, source_target_pairs={{0,8},{8,0},{16,24},{24,16},{1,9},{9,1},{17,25},{25,17},{2,10},{10... | collective-permute-start | bytes 12296 | tf_op jit(solution)/shard_map/ppermute | solution.py:523
  45.0 4.6 %collective-permute-start.9 = (f32[1,1024]{1,0:T(1,128)S(1)}, f32[1,1024]{1,0:T(1,128)S(1)}, u32[]{:S(2)}, u32[]{:S(2)}) collective-permute-start(f32[1,1024]{1,0:T(1,128)S(1)} %column_pass.2.refs_0_), channel_id=1, source_target_pairs={{0,24},{8,16},{16,8},{24,0},{1,25},{9,17},{17,9},{25,1},{2,26},{10... | collective-permute-start | bytes 12296 | tf_op jit(solution)/shard_map/ppermute | solution.py:523
  52.2 4.5 %collective-permute-start.11 = (f32[1,2048]{1,0:T(1,128)S(1)}, f32[1,2048]{1,0:T(1,128)S(1)}, u32[]{:S(2)}, u32[]{:S(2)}) collective-permute-start(f32[1,2048]{1,0:T(1,128)S(1)} %add.69.refs_0_), channel_id=1, source_target_pairs={{0,2},{2,0},{4,6},{6,4},{1,3},{3,1},{5,7},{7,5},{8,10},{10,8},{12,... | collective-permute-start | bytes 24584 | tf_op jit(solution)/shard_map/ppermute | solution.py:523
  52.3 4.7 %collective-permute-start.12 = (f32[1,2048]{1,0:T(1,128)S(1)}, f32[1,2048]{1,0:T(1,128)S(1)}, u32[]{:S(2)}, u32[]{:S(2)}) collective-permute-start(f32[1,2048]{1,0:T(1,128)S(1)} %add.69.refs_0_), channel_id=1, source_target_pairs={{0,4},{2,6},{4,0},{6,2},{1,5},{3,7},{5,1},{7,3},{8,12},{10,14},{12... | collective-permute-start | bytes 24584 | tf_op jit(solution)/shard_map/ppermute | solution.py:523
  53.0 5.8 %collective-permute-start.13 = (f32[1,2048]{1,0:T(1,128)S(1)}, f32[1,2048]{1,0:T(1,128)S(1)}, u32[]{:S(2)}, u32[]{:S(2)}) collective-permute-start(f32[1,2048]{1,0:T(1,128)S(1)} %add.69.refs_0_), channel_id=1, source_target_pairs={{0,6},{2,4},{4,2},{6,0},{1,7},{3,5},{5,3},{7,1},{8,14},{10,12},{12... | collective-permute-start | bytes 24584 | tf_op jit(solution)/shard_map/ppermute | solution.py:523
  59.6 3.8 %collective-permute-start.14 = (f32[1,1024]{1,0:T(1,128)S(1)}, f32[1,1024]{1,0:T(1,128)S(1)}, u32[]{:S(2)}, u32[]{:S(2)}) collective-permute-start(f32[1,1024]{1,0:T(1,128)S(1)} %column_pass.3.refs_0_), channel_id=1, source_target_pairs={{0,8},{8,0},{16,24},{24,16},{1,9},{9,1},{17,25},{25,17},{2,10},{10... | collective-permute-start | bytes 12296 | tf_op jit(solution)/shard_map/ppermute | solution.py:523
  62.6 4.6 %collective-permute-start.16 = (f32[1,1024]{1,0:T(1,128)S(1)}, f32[1,1024]{1,0:T(1,128)S(1)}, u32[]{:S(2)}, u32[]{:S(2)}) collective-permute-start(f32[1,1024]{1,0:T(1,128)S(1)} %column_pass.3.refs_0_), channel_id=1, source_target_pairs={{0,24},{8,16},{16,8},{24,0},{1,25},{9,17},{17,9},{25,1},{2,26},{10... | collective-permute-start | bytes 12296 | tf_op jit(solution)/shard_map/ppermute | solution.py:523
  72.2 4.5 %collective-permute-start.18 = (f32[2,2048]{1,0:T(2,128)S(1)}, f32[2,2048]{1,0:T(2,128)S(1)}, u32[]{:S(2)}, u32[]{:S(2)}) collective-permute-start(f32[2,2048]{1,0:T(2,128)S(1)} %fusion.1), channel_id=1, source_target_pairs={{0,2},{2,0},{4,6},{6,4},{1,3},{3,1},{5,7},{7,5},{8,10},{10,8},{12,... | collective-permute-start | bytes 49160 | tf_op jit(solution)/shard_map/ppermute | solution.py:523
  72.5 5.8 %collective-permute-start.19 = (f32[2,2048]{1,0:T(2,128)S(1)}, f32[2,2048]{1,0:T(2,128)S(1)}, u32[]{:S(2)}, u32[]{:S(2)}) collective-permute-start(f32[2,2048]{1,0:T(2,128)S(1)} %fusion.1), channel_id=1, source_target_pairs={{0,4},{2,6},{4,0},{6,2},{1,5},{3,7},{5,1},{7,3},{8,12},{10,14},{12... | collective-permute-start | bytes 49160 | tf_op jit(solution)/shard_map/ppermute | solution.py:523
  76.4 5.9 %collective-permute-start.20 = (f32[2,2048]{1,0:T(2,128)S(1)}, f32[2,2048]{1,0:T(2,128)S(1)}, u32[]{:S(2)}, u32[]{:S(2)}) collective-permute-start(f32[2,2048]{1,0:T(2,128)S(1)} %fusion.1), channel_id=1, source_target_pairs={{0,6},{2,4},{4,2},{6,0},{1,7},{3,5},{5,3},{7,1},{8,14},{10,12},{12... | collective-permute-start | bytes 49160 | tf_op jit(solution)/shard_map/ppermute | solution.py:523
  82.4 3.9 %collective-permute-start.21 = (f32[2048]{0:T(1024)S(1)}, f32[2048]{0:T(1024)S(1)}, u32[]{:S(2)}, u32[]{:S(2)}) collective-permute-start(f32[2048]{0:T(1024)S(1)} %bitcast.58), channel_id=1, source_target_pairs={{0,8},{8,0},{16,24},{24,16},{1,9},{9,1},{17,25},{25,17},{2,10},{10... | collective-permute-start | bytes 24584 | tf_op jit(solution)/shard_map/ppermute | solution.py:523
  82.6 3.7 %collective-permute-start.22 = (f32[2048]{0:T(1024)S(1)}, f32[2048]{0:T(1024)S(1)}, u32[]{:S(2)}, u32[]{:S(2)}) collective-permute-start(f32[2048]{0:T(1024)S(1)} %bitcast.59), channel_id=1, source_target_pairs={{0,16},{8,24},{16,0},{24,8},{1,17},{9,25},{17,1},{25,9},{2,18},{10... | collective-permute-start | bytes 24584 | tf_op jit(solution)/shard_map/ppermute | solution.py:523
  83.1 4.7 %collective-permute-start.23 = (f32[2048]{0:T(1024)S(1)}, f32[2048]{0:T(1024)S(1)}, u32[]{:S(2)}, u32[]{:S(2)}) collective-permute-start(f32[2048]{0:T(1024)S(1)} %bitcast.60), channel_id=1, source_target_pairs={{0,24},{8,16},{16,8},{24,0},{1,25},{9,17},{17,9},{25,1},{2,26},{10... | collective-permute-start | bytes 24584 | tf_op jit(solution)/shard_map/ppermute | solution.py:523
  134.6 15.5 %collective-permute-start.31 = (bf16[1,256,1024]{2,1,0:T(8,128)(2,1)S(1)}, bf16[1,256,1024]{2,1,0:T(8,128)(2,1)S(1)}, u32[]{:S(2)}, u32[]{:S(2)}) collective-permute-start(bf16[1,256,1024]{2,1,0:T(8,128)(2,1)S(1)} %add_blocks.3), channel_id=1, source_target_pairs={{0,2},{2,0},{4,6},{6,4},{1,3},{3,1},{5,7},{7,5},{8,10},{10,8},{12,... | collective-permute-start | bytes 1572872 | tf_op jit(solution)/shard_map/ppermute | solution.py:523
  137.6 13.8 %collective-permute-start.30 = (bf16[1,256,1024]{2,1,0:T(8,128)(2,1)S(1)}, bf16[1,256,1024]{2,1,0:T(8,128)(2,1)S(1)}, u32[]{:S(2)}, u32[]{:S(2)}) collective-permute-start(bf16[1,256,1024]{2,1,0:T(8,128)(2,1)S(1)} %gradients.13), channel_id=1, source_target_pairs={{0,1},{1,0},{2,3},{3,2},{4,5},{5,4},{6,7},{7,6},{8,9},{9,8},{10,11... | collective-permute-start | bytes 1572872 | tf_op jit(solution)/shard_map/ppermute | solution.py:523
  137.9 22.0 %collective-permute-start.32 = (bf16[1,256,1024]{2,1,0:T(8,128)(2,1)S(1)}, bf16[1,256,1024]{2,1,0:T(8,128)(2,1)S(1)}, u32[]{:S(2)}, u32[]{:S(2)}) collective-permute-start(bf16[1,256,1024]{2,1,0:T(8,128)(2,1)S(1)} %add_blocks.4), channel_id=1, source_target_pairs={{0,2},{2,0},{4,6},{6,4},{1,3},{3,1},{5,7},{7,5},{8,10},{10,8},{12,... | collective-permute-start | bytes 1572872 | tf_op jit(solution)/shard_map/ppermute | solution.py:523
  139.7 10.4 %collective-permute-start.25 = (f32[1,128]{1,0:T(1,128)S(1)}, f32[1,128]{1,0:T(1,128)S(1)}, u32[]{:S(2)}, u32[]{:S(2)}) collective-permute-start(f32[1,128]{1,0:T(1,128)S(1)} %get-tuple-element.27), channel_id=1, source_target_pairs={{0,16},{8,24},{16,0},{24,8},{1,17},{9,25},{17,1},{25,9},{2,18},{10... | collective-permute-start | bytes 1544 | tf_op jit(solution)/shard_map/ppermute | solution.py:523
  143.0 7.1 %collective-permute-start.26 = (f32[1,128]{1,0:T(1,128)S(1)}, f32[1,128]{1,0:T(1,128)S(1)}, u32[]{:S(2)}, u32[]{:S(2)}) collective-permute-start(f32[1,128]{1,0:T(1,128)S(1)} %get-tuple-element.27), channel_id=1, source_target_pairs={{0,24},{8,16},{16,8},{24,0},{1,25},{9,17},{17,9},{25,1},{2,26},{10... | collective-permute-start | bytes 1544 | tf_op jit(solution)/shard_map/ppermute | solution.py:523
  161.2 16.1 %collective-permute-start.33 = (bf16[1024,256]{1,0:T(8,128)(2,1)}, bf16[1024,256]{1,0:T(8,128)(2,1)}, u32[]{:S(2)}, u32[]{:S(2)}) collective-permute-start(bf16[1024,256]{1,0:T(8,128)(2,1)} %get-tuple-element.43), channel_id=1, source_target_pairs={{0,24},{8,16},{16,8},{24,0},{1,25},{9,17},{17,9},{25,1},{2,26},{10... | collective-permute-start | bytes 1572872 | tf_op jit(solution)/shard_map/ppermute | solution.py:523
  161.4 24.6 %collective-permute-start.34 = (bf16[1024,256]{1,0:T(8,128)(2,1)}, bf16[1024,256]{1,0:T(8,128)(2,1)}, u32[]{:S(2)}, u32[]{:S(2)}) collective-permute-start(bf16[1024,256]{1,0:T(8,128)(2,1)} %get-tuple-element.42), channel_id=1, source_target_pairs={{0,16},{8,24},{16,0},{24,8},{1,17},{9,25},{17,1},{25,9},{2,18},{10... | collective-permute-start | bytes 1572872 | tf_op jit(solution)/shard_map/ppermute | solution.py:523
  162.7 24.1 %collective-permute-start.35 = (bf16[1024,256]{1,0:T(8,128)(2,1)}, bf16[1024,256]{1,0:T(8,128)(2,1)}, u32[]{:S(2)}, u32[]{:S(2)}) collective-permute-start(bf16[1024,256]{1,0:T(8,128)(2,1)} %get-tuple-element.41), channel_id=1, source_target_pairs={{0,8},{8,0},{16,24},{24,16},{1,9},{9,1},{17,25},{25,17},{2,10},{10... | collective-permute-start | bytes 1572872 | tf_op jit(solution)/shard_map/ppermute | solution.py:523
  166.7 27.0 %collective-permute-start.39 = (bf16[1,256,1024]{2,1,0:T(8,128)(2,1)}, bf16[1,256,1024]{2,1,0:T(8,128)(2,1)}, u32[]{:S(2)}, u32[]{:S(2)}) collective-permute-start(bf16[1,256,1024]{2,1,0:T(8,128)(2,1)} %gradients.15), channel_id=1, source_target_pairs={{0,1},{1,0},{2,3},{3,2},{4,5},{5,4},{6,7},{7,6},{8,9},{9,8},{10,11... | collective-permute-start | bytes 1572872 | tf_op jit(solution)/shard_map/ppermute | solution.py:523
  167.2 26.5 %collective-permute-start.40 = (bf16[1,256,1024]{2,1,0:T(8,128)(2,1)}, bf16[1,256,1024]{2,1,0:T(8,128)(2,1)}, u32[]{:S(2)}, u32[]{:S(2)}) collective-permute-start(bf16[1,256,1024]{2,1,0:T(8,128)(2,1)} %add_blocks.5), channel_id=1, source_target_pairs={{0,4},{2,6},{4,0},{6,2},{1,5},{3,7},{5,1},{7,3},{8,12},{10,14},{12... | collective-permute-start | bytes 1572872 | tf_op jit(solution)/shard_map/ppermute | solution.py:523
  186.8 10.3 %collective-permute-start.36 = (f32[1,128]{1,0:T(1,128)S(1)}, f32[1,128]{1,0:T(1,128)S(1)}, u32[]{:S(2)}, u32[]{:S(2)}) collective-permute-start(f32[1,128]{1,0:T(1,128)S(1)} %add.80), channel_id=1, source_target_pairs={{0,2},{2,0},{4,6},{6,4},{1,3},{3,1},{5,7},{7,5},{8,10},{10,8},{12,... | collective-permute-start | bytes 1544 | tf_op jit(solution)/shard_map/ppermute | solution.py:523
  187.5 9.6 %collective-permute-start.37 = (f32[1,128]{1,0:T(1,128)S(1)}, f32[1,128]{1,0:T(1,128)S(1)}, u32[]{:S(2)}, u32[]{:S(2)}) collective-permute-start(f32[1,128]{1,0:T(1,128)S(1)} %add.80), channel_id=1, source_target_pairs={{0,4},{2,6},{4,0},{6,2},{1,5},{3,7},{5,1},{7,3},{8,12},{10,14},{12... | collective-permute-start | bytes 1544 | tf_op jit(solution)/shard_map/ppermute | solution.py:523
  189.9 7.2 %collective-permute-start.38 = (f32[1,128]{1,0:T(1,128)S(1)}, f32[1,128]{1,0:T(1,128)S(1)}, u32[]{:S(2)}, u32[]{:S(2)}) collective-permute-start(f32[1,128]{1,0:T(1,128)S(1)} %add.80), channel_id=1, source_target_pairs={{0,6},{2,4},{4,2},{6,0},{1,7},{3,5},{5,3},{7,1},{8,14},{10,12},{12... | collective-permute-start | bytes 1544 | tf_op jit(solution)/shard_map/ppermute | solution.py:523
  (22 other events, 152.4 us)
Sparse Core Ops, SparseCore 0:
  10.2 93.8 all-gather.1

commit v9 on v8

--- a/solution.py
+++ b/solution.py
@@ -580,29 +580,31 @@
     def after(value, *earlier):
         return lax.optimization_barrier((value, *earlier))[0]
 
-    def part_of(number, *earlier):
+    def part_of(number, other_after=(), own_after=()):
         place_bits = [middle ^ (number >> 1), low ^ (number & 1)]
 
-        def run(other, dtype):
+        def run(other, dtype, earlier):
             where = after(jnp.stack(place_bits + [core ^ other]).astype(jnp.int32), *earlier)
             return gradients(where, dscore, wnorm, dtype)
 
-        gunit = run(1, BF16)
-        return [run(0, F32), swap(gunit, "core", 1)]
-
-    forwarded = add_blocks(part_of(3), BF16)
+        gunit = run(1, BF16, other_after)
+        return [run(0, F32, own_after), swap(gunit, "core", 1)]
+
+    loss = functools.reduce(jnp.add, parts_of(loss, PLACE))
+    forwarded = after(add_blocks(part_of(3), BF16), loss)
     from_forwarder = swap(forwarded, PLACE, 1)
-    near = add_blocks(part_of(1, forwarded), BF16)
+    near = add_blocks(part_of(1, [forwarded], [forwarded]), BF16)
     from_near = swap(near, PLACE, 1)
-    across = part_of(2, near)
-    values = part_of(0, near)
-
+    across = part_of(2, [near], [near])
+    values = part_of(0, [near], [from_near])
+
+    loss = loss + swap(loss, "core", 1)
     loss = functools.reduce(jnp.add, parts_of(loss, "batch"))
-    grad_proto, proto_sent = proto_gradient(dscore, unit, scalar(batch_index), batch_size)
+    grad_proto, proto_sent = proto_gradient(dscore, unit, after(scalar(batch_index), values[1]), batch_size)
     from_forwarder = after(from_forwarder, proto_sent)
     across = add_blocks(across + [from_forwarder], BF16)
     values += [from_near, swap(across, PLACE, 2)]
-    proto_sent = after(proto_sent, loss, across, from_near)
+    proto_sent = after(proto_sent, loss, across)
 
     bit = 2
     while (1 << bit) < places:
@@ -610,9 +612,7 @@
         values = [kept, swap(sent, PLACE, 1 << bit)]
         bit += 1
     grad_embed = embed_gradient(scalar(proto_index), embeddings, [value[0] for value in values])
-    loss = loss + swap(loss, "core", 1)
     arrived = [swap(proto_sent[distance], "batch", distance) for distance in range(batch_size - 1, 0, -1)]
-    loss = functools.reduce(jnp.add, parts_of(after(loss, *arrived), PLACE))
     loss = loss[0, 0] / total_rows
     for block in arrived:
         grad_proto = grad_proto + block.astype(F32)

time: 205 us -> 206 us (level)
  transfers between devices with their start and end apart: 42 -> 42, of which waited for: 28 -> 27; matrix products, arithmetic and copies ran while one was open for 2% -> 1% of each run, Pallas kernels for 21% -> 20%
where the time goes in v9:
time: 206 us
  Pallas kernels  73.5 us (36%)
  waiting for transfers between devices  58.7 us (28%)
  starting transfers between devices  43.3 us (21%)
  between operations  15.7 us (8%)
  local copies, waits for them, and re-layouts  11.3 us (5%)
  other arithmetic  3.11 us (2%)
    ppermute x41, waiting for transfers between devices, swap(): return lax.ppermute(value, axis, [(i, i ^ distance) for i in range(size)])  52.5 us
    ppermute x41, starting transfers between devices, swap(): return lax.ppermute(value, axis, [(i, i ^ distance) for i in range(size)])  43.3 us
    pallas_call x1, Pallas kernels, partner_pass(): pl.pallas_call(functools.partial(partner_kernel, count, total, heat_scale...  25.6 us
    pallas_call x1, Pallas kernels, lookup(): pl.pallas_call(lookup_kernel, grid_spec=pltpu.PrefetchScalarGridSpec(num_...  10.1 us
    unnamed x24, local copies, waits for them, and re-layouts  10.1 us
    pallas_call x8, Pallas kernels, gradients(): pl.pallas_call(gradient_kernel, grid_spec=pltpu.PrefetchScalarGridSpec(nu...  9.95 us
    pallas_call x1, Pallas kernels, scores_of(): pl.pallas_call(scores_kernel, grid=(rows // share // 2,), in_specs=[pl.Bl...  7.93 us
    pallas_call x1, Pallas kernels, proto_gradient(): pl.pallas_call(proto_gradient_kernel, grid_spec=pltpu.PrefetchScalarGridS...  6.28 us
  transfers between devices with their start and end apart: 42, of which 27 were waited for; matrix products, arithmetic and copies ran while one was open for 1% of the time, Pallas kernels for 20%

profile of v9, /device:TPU:0, one launch (start us, length us, event | category | flops | bytes accessed | tf_op | source)
XLA Modules:
  0.0 205.6 jit_solution(13886153043190491165)
XLA Ops:
  7.2 2.6 %own_rows.1 = bf16[512,8,128]{2,1,0:T(8,128)(2,1)} custom-call(s32[1]{0:T(128)} %bitcast.5.index_ref, bf16[2048,1024]{1,0:T(8,128)(2,1)} %embeddings_ref.5), custom_call_target="tpu_custom_call" | custom-call | tf_op jit(solution)/shard_map/own_rows/pallas_call | solution.py:78
  9.9 2.2 %copy-done.6 = bf16[2048,1024]{1,0:T(8,128)(2,1)S(1)} copy-done((bf16[2048,1024]{1,0:T(8,128)(2,1)S(1)}, bf16[2048,1024]{1,0:T(8,128)(2,1)}, u32[]{:S(2)}) %copy-start.6) | copy-done | bytes 4194328
  13.6 7.9 %scores.1 = (bf16[2048,1024]{1,0:T(8,128)(2,1)S(1)}, bf16[1024,1024]{1,0:T(8,128)(2,1)S(1)}, f32[2048,1024]{1,0:T(8,128)S(1)}, bf16[2048,1024]{1,0:T(8,128)(2,1)...) custom-call(bf16[2048,1024]{1,0:T(8,128)(2,1)S(1)} %copy-done.6, bf16[1024,1024]{1,0:T(8,128)(2,1)S(1)} %copy-done.8), custom_call_target="tpu_custom_call" | custom-call | flops 4294967296 | bytes 23068672 | tf_op jit(solution)/shard_map/scores/pallas_call | solution.py:127
  21.6 3.0 %collective-permute-start = (f32[1,1024]{1,0:T(1,128)S(1)}, f32[1,1024]{1,0:T(1,128)S(1)}, u32[]{:S(2)}, u32[]{:S(2)}) collective-permute-start(f32[1,1024]{1,0:T(1,128)S(1)} %get-tuple-element.23.refs_0_), channel_id=1, source_target_pairs={{0,8},{8,0},{16,24},{24,16},{1,9},{9,1},{17,25},{25,17},{2,10},{10... | collective-permute-start | bytes 12296 | tf_op jit(solution)/shard_map/ppermute | solution.py:523
  26.3 2.0 collective-permute-done.1.refs_2_
  28.2 2.5 %collective-permute-done.2.refs_3_ = f32[1,1024]{1,0:T(1,128)S(1)} collective-permute-done((f32[1,1024]{1,0:T(1,128)S(1)}, f32[1,1024]{1,0:T(1,128)S(1)}, u32[]{:S(2)}, u32[]{:S(2)}) %collective-permute-start.2) | collective-permute-done | bytes 4128 | tf_op jit(solution)/shard_map/ppermute | solution.py:523
  33.4 1.6 collective-permute-start.4
  35.0 2.6 %collective-permute-start.5 = (f32[1,2048]{1,0:T(1,128)S(1)}, f32[1,2048]{1,0:T(1,128)S(1)}, u32[]{:S(2)}, u32[]{:S(2)}) collective-permute-start(f32[1,2048]{1,0:T(1,128)S(1)} %add.68.refs_0_), channel_id=1, source_target_pairs={{0,4},{2,6},{4,0},{6,2},{1,5},{3,7},{5,1},{7,3},{8,12},{10,14},{12... | collective-permute-start | bytes 24584 | tf_op jit(solution)/shard_map/ppermute | solution.py:523
  37.8 1.8 collective-permute-done.5.refs_2_
  39.7 3.5 %collective-permute-done.6.refs_3_ = f32[1,2048]{1,0:T(1,128)S(1)} collective-permute-done((f32[1,2048]{1,0:T(1,128)S(1)}, f32[1,2048]{1,0:T(1,128)S(1)}, u32[]{:S(2)}, u32[]{:S(2)}) %collective-permute-start.6) | collective-permute-done | bytes 8224 | tf_op jit(solution)/shard_map/ppermute | solution.py:523
  45.0 2.5 %collective-permute-start.9 = (f32[1,1024]{1,0:T(1,128)S(1)}, f32[1,1024]{1,0:T(1,128)S(1)}, u32[]{:S(2)}, u32[]{:S(2)}) collective-permute-start(f32[1,1024]{1,0:T(1,128)S(1)} %column_pass.2.refs_0_), channel_id=1, source_target_pairs={{0,24},{8,16},{16,8},{24,0},{1,25},{9,17},{17,9},{25,1},{2,26},{10... | collective-permute-start | bytes 12296 | tf_op jit(solution)/shard_map/ppermute | solution.py:523
  53.0 3.7 %collective-permute-start.13 = (f32[1,2048]{1,0:T(1,128)S(1)}, f32[1,2048]{1,0:T(1,128)S(1)}, u32[]{:S(2)}, u32[]{:S(2)}) collective-permute-start(f32[1,2048]{1,0:T(1,128)S(1)} %add.69.refs_0_), channel_id=1, source_target_pairs={{0,6},{2,4},{4,2},{6,0},{1,7},{3,5},{5,3},{7,1},{8,14},{10,12},{12... | collective-permute-start | bytes 24584 | tf_op jit(solution)/shard_map/ppermute | solution.py:523
  57.0 1.7 collective-permute-done.13.refs_3_
  64.7 2.5 %collective-permute-done.16.refs_3_ = f32[1,1024]{1,0:T(1,128)S(1)} collective-permute-done((f32[1,1024]{1,0:T(1,128)S(1)}, f32[1,1024]{1,0:T(1,128)S(1)}, u32[]{:S(2)}, u32[]{:S(2)}) %collective-permute-start.16) | collective-permute-done | bytes 4128 | tf_op jit(solution)/shard_map/ppermute | solution.py:523
  67.2 2.3 %copy-done.1 = bf16[2048,1024]{1,0:T(8,128)(2,1)S(1)} copy-done((bf16[2048,1024]{1,0:T(8,128)(2,1)S(1)}, bf16[2048,1024]{1,0:T(8,128)(2,1)}, u32[]{:S(2)}) %copy-start.1) | copy-done | bytes 4194328
  72.5 4.0 %collective-permute-start.19 = (f32[2,2048]{1,0:T(2,128)S(1)}, f32[2,2048]{1,0:T(2,128)S(1)}, u32[]{:S(2)}, u32[]{:S(2)}) collective-permute-start(f32[2,2048]{1,0:T(2,128)S(1)} %fusion.1), channel_id=1, source_target_pairs={{0,4},{2,6},{4,0},{6,2},{1,5},{3,7},{5,1},{7,3},{8,12},{10,14},{12... | collective-permute-start | bytes 49160 | tf_op jit(solution)/shard_map/ppermute | solution.py:523
  78.3 4.0 %collective-permute-done.20 = f32[2,2048]{1,0:T(2,128)S(1)} collective-permute-done((f32[2,2048]{1,0:T(2,128)S(1)}, f32[2,2048]{1,0:T(2,128)S(1)}, u32[]{:S(2)}, u32[]{:S(2)}) %collective-permute-start.20) | collective-permute-done | bytes 16416 | tf_op jit(solution)/shard_map/ppermute | solution.py:523
  83.1 2.8 %collective-permute-start.23 = (f32[2048]{0:T(1024)S(1)}, f32[2048]{0:T(1024)S(1)}, u32[]{:S(2)}, u32[]{:S(2)}) collective-permute-start(f32[2048]{0:T(1024)S(1)} %bitcast.60), channel_id=1, source_target_pairs={{0,24},{8,16},{16,8},{24,0},{1,25},{9,17},{17,9},{25,1},{2,26},{10... | collective-permute-start | bytes 24584 | tf_op jit(solution)/shard_map/ppermute | solution.py:523
  87.8 10.1 %lookup.1 = f32[4096]{0:T(1024)S(1)} custom-call(s32[2048]{0:T(1024)S(1)} %bitcast.54, s32[2048]{0:T(1024)S(1)} %bitcast.53, f32[8192]{0:T(1024)S(1)} %pad_maximum_fusion.totals_ref), custom_call_target="tpu_custom_call" | custom-call | flops 1048576 | bytes 1048576 | tf_op jit(solution)/shard_map/lookup/pallas_call | solution.py:333
  97.9 6.1 %all-gather.2.cloned.1.call-done.refs_5_ = bf16[8192,8,128]{2,1,0:T(8,128)(2,1)} async-done(((bf16[512,8,128]{2,1,0:T(8,128)(2,1)}), bf16[8192,8,128]{2,1,0:T(8,128)(2,1)}) %all-gather.2.cloned.1.call-update) | async-done | bytes 16777232 | tf_op jit(solution)/shard_map/all_gather | solution.py:560
  104.1 25.6 %partner_scores.1 = (bf16[2048,1024]{1,0:T(8,128)(2,1)S(1)}, f32[1,128]{1,0:T(1,128)S(1)}) custom-call(s32[2048]{0:T(1024)S(1)} %bitcast.56, s32[2048]{0:T(1024)S(1)} %bitcast.55, f32[1,1024]{1,0:T(1,128)S(1)} %column_pass.3.refs_0_, f32[1,1024]{1,0:T(1,128)S(1)} %collective-permute-done.14.refs_1_, f32[1,1024]{1,0:T(1,128)S(1)} %collective-permute-done.15.refs_2_, ...), custom_call_target="tpu_custom_call" | custom-call | flops 8589934592 | bytes 33554432 | tf_op jit(solution)/shard_map/partner_scores/pallas_call | solution.py:292
  131.5 2.5 %collective-permute-start.25 = (f32[1,128]{1,0:T(1,128)S(1)}, f32[1,128]{1,0:T(1,128)S(1)}, u32[]{:S(2)}, u32[]{:S(2)}) collective-permute-start(f32[1,128]{1,0:T(1,128)S(1)} %get-tuple-element.28), channel_id=1, source_target_pairs={{0,4},{2,6},{4,0},{6,2},{1,5},{3,7},{5,1},{7,3},{8,12},{10,14},{12... | collective-permute-start | bytes 1544 | tf_op jit(solution)/shard_map/ppermute | solution.py:523
  134.0 1.6 collective-permute-start.26
  137.0 2.4 %collective-permute-done.26 = f32[1,128]{1,0:T(1,128)S(1)} collective-permute-done((f32[1,128]{1,0:T(1,128)S(1)}, f32[1,128]{1,0:T(1,128)S(1)}, u32[]{:S(2)}, u32[]{:S(2)}) %collective-permute-start.26) | collective-permute-done | bytes 544 | tf_op jit(solution)/shard_map/ppermute | solution.py:523
  150.2 1.6 collective-permute-done.28
  153.3 3.0 %collective-permute-done.30 = f32[1,128]{1,0:T(1,128)S(1)} collective-permute-done((f32[1,128]{1,0:T(1,128)S(1)}, f32[1,128]{1,0:T(1,128)S(1)}, u32[]{:S(2)}, u32[]{:S(2)}) %collective-permute-start.30) | collective-permute-done | bytes 544 | tf_op jit(solution)/shard_map/ppermute | solution.py:523
  156.3 2.0 collective-permute-start.39
  160.4 6.3 %proto_gradient.1 = (f32[1024,256]{1,0:T(8,128)S(1)}, bf16[4,1024,256]{2,1,0:T(8,128)(2,1)S(1)}) custom-call(s32[1]{0:T(128)} %bitcast.7.index_ref, bf16[1,2,2,2,256,1024]{5,4,3,2,1,0:T(8,128)(2,1)S(1)} %bitcast.35, bf16[1,2,2,2,256,1024]{5,4,3,2,1,0:T(8,128)(2,1)S(1)} %bitcast.36, bf16[1,2,2,2,256,1024]{5,4,3,2,1,0:T(8,128)(2,1)S(1)} %bitcast.37, ...), custom_call_target="tpu_custom_call" | custom-call | flops 1048576 | bytes 1048576 | tf_op jit(solution)/shard_map/proto_gradient/pallas_call | solution.py:467
  172.6 2.2 %copy-done.3 = bf16[2048,1024]{1,0:T(8,128)(2,1)S(1)} copy-done((bf16[2048,1024]{1,0:T(8,128)(2,1)S(1)}, bf16[2048,1024]{1,0:T(8,128)(2,1)}, u32[]{:S(2)}) %copy-start.3) | copy-done | bytes 4194328
  177.0 14.6 %collective-permute-done.40 = bf16[1,256,1024]{2,1,0:T(8,128)(2,1)} collective-permute-done((bf16[1,256,1024]{2,1,0:T(8,128)(2,1)}, bf16[1,256,1024]{2,1,0:T(8,128)(2,1)}, u32[]{:S(2)}, u32[]{:S(2)}) %collective-permute-start.40) | collective-permute-done | bytes 524320 | tf_op jit(solution)/shard_map/ppermute | solution.py:523
  191.7 3.4 %embed_gradient.1 = f32[256,1024]{1,0:T(8,128)} custom-call(s32[1]{0:T(128)} %bitcast.19.index_ref, bf16[2048,1024]{1,0:T(8,128)(2,1)} %embeddings_ref.5, f32[256,1024]{1,0:T(8,128)} %bitcast.52, bf16[256,1024]{1,0:T(8,128)(2,1)} %bitcast.57, bf16[256,1024]{1,0:T(8,128)(2,1)} %bitcast.22.refs_2_, bf16[256,1024]{1,0:T(8,128)(2,1)} %bitcast.23.refs_3_), custom_call_target="tpu_custom_call" | custom-call | flops 2097152 | bytes 4194304 | tf_op jit(solution)/shard_map/embed_gradient/pallas_call | solution.py:503
  195.1 2.5 %convert_add_fusion = f32[1024,256]{1,0:T(8,128)} fusion(bf16[1024,256]{1,0:T(8,128)(2,1)} %collective-permute-done.38, bf16[1024,256]{1,0:T(8,128)(2,1)} %collective-permute-done.37, f32[1024,256]{1,0:T(8,128)S(1)} %get-tuple-element.36, bf16[1024,256]{1,0:T(8,128)(2,1)} %collective-permute-done.36), kind=kLoop, calls=%fused_computation | loop fusion | flops 1572864 | bytes 3670016 | tf_op jit(solution)/shard_map/add | solution.py:618
  (121 shorter events, 52.7 us)
Async XLA Ops:
  7.2 96.9 %all-gather.2.cloned.1.call-start = ((), (), s32[]{:S(2)}) async-start(), calls=%async_computation | async-start | bytes 17825792 | tf_op jit(solution)/shard_map/all_gather | solution.py:560
  21.6 4.7 %collective-permute-start = (f32[1,1024]{1,0:T(1,128)S(1)}, f32[1,1024]{1,0:T(1,128)S(1)}, u32[]{:S(2)}, u32[]{:S(2)}) collective-permute-start(f32[1,1024]{1,0:T(1,128)S(1)} %get-tuple-element.23.refs_0_), channel_id=1, source_target_pairs={{0,8},{8,0},{16,24},{24,16},{1,9},{9,1},{17,25},{25,17},{2,10},{10... | collective-permute-start | bytes 12296 | tf_op jit(solution)/shard_map/ppermute | solution.py:523
  26.1 4.6 %collective-permute-start.2 = (f32[1,1024]{1,0:T(1,128)S(1)}, f32[1,1024]{1,0:T(1,128)S(1)}, u32[]{:S(2)}, u32[]{:S(2)}) collective-permute-start(f32[1,1024]{1,0:T(1,128)S(1)} %get-tuple-element.23.refs_0_), channel_id=1, source_target_pairs={{0,24},{8,16},{16,8},{24,0},{1,25},{9,17},{17,9},{25,1},{2,26},{10... | collective-permute-start | bytes 12296 | tf_op jit(solution)/shard_map/ppermute | solution.py:523
  33.4 4.5 %collective-permute-start.4 = (f32[1,2048]{1,0:T(1,128)S(1)}, f32[1,2048]{1,0:T(1,128)S(1)}, u32[]{:S(2)}, u32[]{:S(2)}) collective-permute-start(f32[1,2048]{1,0:T(1,128)S(1)} %add.68.refs_0_), channel_id=1, source_target_pairs={{0,2},{2,0},{4,6},{6,4},{1,3},{3,1},{5,7},{7,5},{8,10},{10,8},{12,... | collective-permute-start | bytes 24584 | tf_op jit(solution)/shard_map/ppermute | solution.py:523
  35.0 4.7 %collective-permute-start.5 = (f32[1,2048]{1,0:T(1,128)S(1)}, f32[1,2048]{1,0:T(1,128)S(1)}, u32[]{:S(2)}, u32[]{:S(2)}) collective-permute-start(f32[1,2048]{1,0:T(1,128)S(1)} %add.68.refs_0_), channel_id=1, source_target_pairs={{0,4},{2,6},{4,0},{6,2},{1,5},{3,7},{5,1},{7,3},{8,12},{10,14},{12... | collective-permute-start | bytes 24584 | tf_op jit(solution)/shard_map/ppermute | solution.py:523
  37.6 5.6 %collective-permute-start.6 = (f32[1,2048]{1,0:T(1,128)S(1)}, f32[1,2048]{1,0:T(1,128)S(1)}, u32[]{:S(2)}, u32[]{:S(2)}) collective-permute-start(f32[1,2048]{1,0:T(1,128)S(1)} %add.68.refs_0_), channel_id=1, source_target_pairs={{0,6},{2,4},{4,2},{6,0},{1,7},{3,5},{5,3},{7,1},{8,14},{10,12},{12... | collective-permute-start | bytes 24584 | tf_op jit(solution)/shard_map/ppermute | solution.py:523
  44.0 3.7 %collective-permute-start.7 = (f32[1,1024]{1,0:T(1,128)S(1)}, f32[1,1024]{1,0:T(1,128)S(1)}, u32[]{:S(2)}, u32[]{:S(2)}) collective-permute-start(f32[1,1024]{1,0:T(1,128)S(1)} %column_pass.2.refs_0_), channel_id=1, source_target_pairs={{0,8},{8,0},{16,24},{24,16},{1,9},{9,1},{17,25},{25,17},{2,10},{10... | collective-permute-start | bytes 12296 | tf_op jit(solution)/shard_map/ppermute | solution.py:523
  45.0 4.6 %collective-permute-start.9 = (f32[1,1024]{1,0:T(1,128)S(1)}, f32[1,1024]{1,0:T(1,128)S(1)}, u32[]{:S(2)}, u32[]{:S(2)}) collective-permute-start(f32[1,1024]{1,0:T(1,128)S(1)} %column_pass.2.refs_0_), channel_id=1, source_target_pairs={{0,24},{8,16},{16,8},{24,0},{1,25},{9,17},{17,9},{25,1},{2,26},{10... | collective-permute-start | bytes 12296 | tf_op jit(solution)/shard_map/ppermute | solution.py:523
  52.2 4.5 %collective-permute-start.11 = (f32[1,2048]{1,0:T(1,128)S(1)}, f32[1,2048]{1,0:T(1,128)S(1)}, u32[]{:S(2)}, u32[]{:S(2)}) collective-permute-start(f32[1,2048]{1,0:T(1,128)S(1)} %add.69.refs_0_), channel_id=1, source_target_pairs={{0,2},{2,0},{4,6},{6,4},{1,3},{3,1},{5,7},{7,5},{8,10},{10,8},{12,... | collective-permute-start | bytes 24584 | tf_op jit(solution)/shard_map/ppermute | solution.py:523
  52.3 4.7 %collective-permute-start.12 = (f32[1,2048]{1,0:T(1,128)S(1)}, f32[1,2048]{1,0:T(1,128)S(1)}, u32[]{:S(2)}, u32[]{:S(2)}) collective-permute-start(f32[1,2048]{1,0:T(1,128)S(1)} %add.69.refs_0_), channel_id=1, source_target_pairs={{0,4},{2,6},{4,0},{6,2},{1,5},{3,7},{5,1},{7,3},{8,12},{10,14},{12... | collective-permute-start | bytes 24584 | tf_op jit(solution)/shard_map/ppermute | solution.py:523
  53.0 5.8 %collective-permute-start.13 = (f32[1,2048]{1,0:T(1,128)S(1)}, f32[1,2048]{1,0:T(1,128)S(1)}, u32[]{:S(2)}, u32[]{:S(2)}) collective-permute-start(f32[1,2048]{1,0:T(1,128)S(1)} %add.69.refs_0_), channel_id=1, source_target_pairs={{0,6},{2,4},{4,2},{6,0},{1,7},{3,5},{5,3},{7,1},{8,14},{10,12},{12... | collective-permute-start | bytes 24584 | tf_op jit(solution)/shard_map/ppermute | solution.py:523
  59.6 3.8 %collective-permute-start.14 = (f32[1,1024]{1,0:T(1,128)S(1)}, f32[1,1024]{1,0:T(1,128)S(1)}, u32[]{:S(2)}, u32[]{:S(2)}) collective-permute-start(f32[1,1024]{1,0:T(1,128)S(1)} %column_pass.3.refs_0_), channel_id=1, source_target_pairs={{0,8},{8,0},{16,24},{24,16},{1,9},{9,1},{17,25},{25,17},{2,10},{10... | collective-permute-start | bytes 12296 | tf_op jit(solution)/shard_map/ppermute | solution.py:523
  62.6 4.6 %collective-permute-start.16 = (f32[1,1024]{1,0:T(1,128)S(1)}, f32[1,1024]{1,0:T(1,128)S(1)}, u32[]{:S(2)}, u32[]{:S(2)}) collective-permute-start(f32[1,1024]{1,0:T(1,128)S(1)} %column_pass.3.refs_0_), channel_id=1, source_target_pairs={{0,24},{8,16},{16,8},{24,0},{1,25},{9,17},{17,9},{25,1},{2,26},{10... | collective-permute-start | bytes 12296 | tf_op jit(solution)/shard_map/ppermute | solution.py:523
  72.2 4.5 %collective-permute-start.18 = (f32[2,2048]{1,0:T(2,128)S(1)}, f32[2,2048]{1,0:T(2,128)S(1)}, u32[]{:S(2)}, u32[]{:S(2)}) collective-permute-start(f32[2,2048]{1,0:T(2,128)S(1)} %fusion.1), channel_id=1, source_target_pairs={{0,2},{2,0},{4,6},{6,4},{1,3},{3,1},{5,7},{7,5},{8,10},{10,8},{12,... | collective-permute-start | bytes 49160 | tf_op jit(solution)/shard_map/ppermute | solution.py:523
  72.5 5.8 %collective-permute-start.19 = (f32[2,2048]{1,0:T(2,128)S(1)}, f32[2,2048]{1,0:T(2,128)S(1)}, u32[]{:S(2)}, u32[]{:S(2)}) collective-permute-start(f32[2,2048]{1,0:T(2,128)S(1)} %fusion.1), channel_id=1, source_target_pairs={{0,4},{2,6},{4,0},{6,2},{1,5},{3,7},{5,1},{7,3},{8,12},{10,14},{12... | collective-permute-start | bytes 49160 | tf_op jit(solution)/shard_map/ppermute | solution.py:523
  76.4 5.9 %collective-permute-start.20 = (f32[2,2048]{1,0:T(2,128)S(1)}, f32[2,2048]{1,0:T(2,128)S(1)}, u32[]{:S(2)}, u32[]{:S(2)}) collective-permute-start(f32[2,2048]{1,0:T(2,128)S(1)} %fusion.1), channel_id=1, source_target_pairs={{0,6},{2,4},{4,2},{6,0},{1,7},{3,5},{5,3},{7,1},{8,14},{10,12},{12... | collective-permute-start | bytes 49160 | tf_op jit(solution)/shard_map/ppermute | solution.py:523
  82.4 3.9 %collective-permute-start.21 = (f32[2048]{0:T(1024)S(1)}, f32[2048]{0:T(1024)S(1)}, u32[]{:S(2)}, u32[]{:S(2)}) collective-permute-start(f32[2048]{0:T(1024)S(1)} %bitcast.58), channel_id=1, source_target_pairs={{0,8},{8,0},{16,24},{24,16},{1,9},{9,1},{17,25},{25,17},{2,10},{10... | collective-permute-start | bytes 24584 | tf_op jit(solution)/shard_map/ppermute | solution.py:523
  82.6 3.7 %collective-permute-start.22 = (f32[2048]{0:T(1024)S(1)}, f32[2048]{0:T(1024)S(1)}, u32[]{:S(2)}, u32[]{:S(2)}) collective-permute-start(f32[2048]{0:T(1024)S(1)} %bitcast.59), channel_id=1, source_target_pairs={{0,16},{8,24},{16,0},{24,8},{1,17},{9,25},{17,1},{25,9},{2,18},{10... | collective-permute-start | bytes 24584 | tf_op jit(solution)/shard_map/ppermute | solution.py:523
  83.1 4.7 %collective-permute-start.23 = (f32[2048]{0:T(1024)S(1)}, f32[2048]{0:T(1024)S(1)}, u32[]{:S(2)}, u32[]{:S(2)}) collective-permute-start(f32[2048]{0:T(1024)S(1)} %bitcast.60), channel_id=1, source_target_pairs={{0,24},{8,16},{16,8},{24,0},{1,25},{9,17},{17,9},{25,1},{2,26},{10... | collective-permute-start | bytes 24584 | tf_op jit(solution)/shard_map/ppermute | solution.py:523
  130.9 8.4 %collective-permute-start.31 = (bf16[1,256,1024]{2,1,0:T(8,128)(2,1)S(1)}, bf16[1,256,1024]{2,1,0:T(8,128)(2,1)S(1)}, u32[]{:S(2)}, u32[]{:S(2)}) collective-permute-start(bf16[1,256,1024]{2,1,0:T(8,128)(2,1)S(1)} %gradients.9), channel_id=1, source_target_pairs={{0,1},{1,0},{2,3},{3,2},{4,5},{5,4},{6,7},{7,6},{8,9},{9,8},{10,11... | collective-permute-start | bytes 1572872 | tf_op jit(solution)/shard_map/ppermute | solution.py:523
  131.3 5.7 %collective-permute-start.24 = (f32[1,128]{1,0:T(1,128)S(1)}, f32[1,128]{1,0:T(1,128)S(1)}, u32[]{:S(2)}, u32[]{:S(2)}) collective-permute-start(f32[1,128]{1,0:T(1,128)S(1)} %get-tuple-element.28), channel_id=1, source_target_pairs={{0,2},{2,0},{4,6},{6,4},{1,3},{3,1},{5,7},{7,5},{8,10},{10,8},{12,... | collective-permute-start | bytes 1544 | tf_op jit(solution)/shard_map/ppermute | solution.py:523
  131.5 5.5 %collective-permute-start.25 = (f32[1,128]{1,0:T(1,128)S(1)}, f32[1,128]{1,0:T(1,128)S(1)}, u32[]{:S(2)}, u32[]{:S(2)}) collective-permute-start(f32[1,128]{1,0:T(1,128)S(1)} %get-tuple-element.28), channel_id=1, source_target_pairs={{0,4},{2,6},{4,0},{6,2},{1,5},{3,7},{5,1},{7,3},{8,12},{10,14},{12... | collective-permute-start | bytes 1544 | tf_op jit(solution)/shard_map/ppermute | solution.py:523
  134.0 5.3 %collective-permute-start.26 = (f32[1,128]{1,0:T(1,128)S(1)}, f32[1,128]{1,0:T(1,128)S(1)}, u32[]{:S(2)}, u32[]{:S(2)}) collective-permute-start(f32[1,128]{1,0:T(1,128)S(1)} %get-tuple-element.28), channel_id=1, source_target_pairs={{0,6},{2,4},{4,2},{6,0},{1,7},{3,5},{5,3},{7,1},{8,14},{10,12},{12... | collective-permute-start | bytes 1544 | tf_op jit(solution)/shard_map/ppermute | solution.py:523
  144.8 14.7 %collective-permute-start.33 = (bf16[1,256,1024]{2,1,0:T(8,128)(2,1)S(1)}, bf16[1,256,1024]{2,1,0:T(8,128)(2,1)S(1)}, u32[]{:S(2)}, u32[]{:S(2)}) collective-permute-start(bf16[1,256,1024]{2,1,0:T(8,128)(2,1)S(1)} %gradients.12), channel_id=1, source_target_pairs={{0,1},{1,0},{2,3},{3,2},{4,5},{5,4},{6,7},{7,6},{8,9},{9,8},{10,11... | collective-permute-start | bytes 1572872 | tf_op jit(solution)/shard_map/ppermute | solution.py:523
  145.0 21.6 %collective-permute-start.35 = (bf16[1,256,1024]{2,1,0:T(8,128)(2,1)S(1)}, bf16[1,256,1024]{2,1,0:T(8,128)(2,1)S(1)}, u32[]{:S(2)}, u32[]{:S(2)}) collective-permute-start(bf16[1,256,1024]{2,1,0:T(8,128)(2,1)S(1)} %add_blocks.3), channel_id=1, source_target_pairs={{0,2},{2,0},{4,6},{6,4},{1,3},{3,1},{5,7},{7,5},{8,10},{10,8},{12,... | collective-permute-start | bytes 1572872 | tf_op jit(solution)/shard_map/ppermute | solution.py:523
  146.3 20.4 %collective-permute-start.34 = (bf16[1,256,1024]{2,1,0:T(8,128)(2,1)S(1)}, bf16[1,256,1024]{2,1,0:T(8,128)(2,1)S(1)}, u32[]{:S(2)}, u32[]{:S(2)}) collective-permute-start(bf16[1,256,1024]{2,1,0:T(8,128)(2,1)S(1)} %gradients.14), channel_id=1, source_target_pairs={{0,1},{1,0},{2,3},{3,2},{4,5},{5,4},{6,7},{7,6},{8,9},{9,8},{10,11... | collective-permute-start | bytes 1572872 | tf_op jit(solution)/shard_map/ppermute | solution.py:523
  151.8 4.4 %collective-permute-start.30 = (f32[1,128]{1,0:T(1,128)S(1)}, f32[1,128]{1,0:T(1,128)S(1)}, u32[]{:S(2)}, u32[]{:S(2)}) collective-permute-start(f32[1,128]{1,0:T(1,128)S(1)} %add.80), channel_id=1, source_target_pairs={{0,24},{8,16},{16,8},{24,0},{1,25},{9,17},{17,9},{25,1},{2,26},{10... | collective-permute-start | bytes 1544 | tf_op jit(solution)/shard_map/ppermute | solution.py:523
  156.3 16.3 %collective-permute-start.39 = (bf16[1,256,1024]{2,1,0:T(8,128)(2,1)}, bf16[1,256,1024]{2,1,0:T(8,128)(2,1)}, u32[]{:S(2)}, u32[]{:S(2)}) collective-permute-start(bf16[1,256,1024]{2,1,0:T(8,128)(2,1)} %add_blocks.4), channel_id=1, source_target_pairs={{0,2},{2,0},{4,6},{6,4},{1,3},{3,1},{5,7},{7,5},{8,10},{10,8},{12,... | collective-permute-start | bytes 1572872 | tf_op jit(solution)/shard_map/ppermute | solution.py:523
  167.7 24.0 %collective-permute-start.40 = (bf16[1,256,1024]{2,1,0:T(8,128)(2,1)}, bf16[1,256,1024]{2,1,0:T(8,128)(2,1)}, u32[]{:S(2)}, u32[]{:S(2)}) collective-permute-start(bf16[1,256,1024]{2,1,0:T(8,128)(2,1)} %add_blocks.5), channel_id=1, source_target_pairs={{0,4},{2,6},{4,0},{6,2},{1,5},{3,7},{5,1},{7,3},{8,12},{10,14},{12... | collective-permute-start | bytes 1572872 | tf_op jit(solution)/shard_map/ppermute | solution.py:523
  169.0 26.0 %collective-permute-start.36 = (bf16[1024,256]{1,0:T(8,128)(2,1)}, bf16[1024,256]{1,0:T(8,128)(2,1)}, u32[]{:S(2)}, u32[]{:S(2)}) collective-permute-start(bf16[1024,256]{1,0:T(8,128)(2,1)} %get-tuple-element.43), channel_id=1, source_target_pairs={{0,24},{8,16},{16,8},{24,0},{1,25},{9,17},{17,9},{25,1},{2,26},{10... | collective-permute-start | bytes 1572872 | tf_op jit(solution)/shard_map/ppermute | solution.py:523
  170.2 24.9 %collective-permute-start.37 = (bf16[1024,256]{1,0:T(8,128)(2,1)}, bf16[1024,256]{1,0:T(8,128)(2,1)}, u32[]{:S(2)}, u32[]{:S(2)}) collective-permute-start(bf16[1024,256]{1,0:T(8,128)(2,1)} %get-tuple-element.45), channel_id=1, source_target_pairs={{0,16},{8,24},{16,0},{24,8},{1,17},{9,25},{17,1},{25,9},{2,18},{10... | collective-permute-start | bytes 1572872 | tf_op jit(solution)/shard_map/ppermute | solution.py:523
  171.7 23.4 %collective-permute-start.38 = (bf16[1024,256]{1,0:T(8,128)(2,1)}, bf16[1024,256]{1,0:T(8,128)(2,1)}, u32[]{:S(2)}, u32[]{:S(2)}) collective-permute-start(bf16[1024,256]{1,0:T(8,128)(2,1)} %get-tuple-element.44), channel_id=1, source_target_pairs={{0,8},{8,0},{16,24},{24,16},{1,9},{9,1},{17,25},{25,17},{2,10},{10... | collective-permute-start | bytes 1572872 | tf_op jit(solution)/shard_map/ppermute | solution.py:523
  (22 other events, 149.1 us)
Sparse Core Ops, SparseCore 0:
  10.2 93.8 all-gather.1

commit v10 on v9

--- a/solution.py
+++ b/solution.py
@@ -428,7 +428,7 @@
 
 def proto_gradient_kernel(index_ref, *refs):
     del index_ref
-    dscore_refs, unit_refs, own_ref, sent_ref = refs[:8], refs[8:16], refs[16], refs[17]
+    dscore_refs, unit_refs, loss_ref, own_ref, sent_ref = refs[:8], refs[8:16], *refs[16:]
     both = (((0,), (0,)), ((), ()))
     total = None
     for dscore_ref, unit_ref in zip(dscore_refs, unit_refs):
@@ -437,11 +437,13 @@
             dscore_ref[...].reshape(rows, protos), unit_ref[...].reshape(rows, part), both, preferred_element_type=F32
         )
         total = term if total is None else total + term
-    sent_ref[...] = total.astype(BF16)
+    protos, part = total.shape
+    sent_ref[0:protos] = total.astype(BF16)
+    sent_ref[protos:] = split_rows(jnp.concatenate([loss_ref[...]] * (part // LANES), axis=1))
     own_ref[...] = total
 
 
-def proto_gradient(dscore, unit, index, batch_size):
+def proto_gradient(dscore, unit, loss, index, batch_size):
     top, share, protos = dscore.shape[0], *dscore.shape[4:]
     width = unit.shape[1]
     part = width // batch_size
@@ -469,20 +471,21 @@
         grid_spec=pltpu.PrefetchScalarGridSpec(
             num_scalar_prefetch=1,
             grid=(batch_size,),
-            in_specs=[dscore_at(number) for number in range(8)] + [unit_at(number) for number in range(8)],
+            in_specs=[dscore_at(number) for number in range(8)] + [unit_at(number) for number in range(8)]
+            + [pl.BlockSpec((1, LANES), lambda i, index: (0, 0))],
             out_specs=[
                 pl.BlockSpec((protos, part), lambda i, index: (0, 0)),
-                pl.BlockSpec((None, protos, part), lambda i, index: (last - i, 0, 0)),
+                pl.BlockSpec((None, protos + 16, part), lambda i, index: (last - i, 0, 0)),
             ],
         ),
         out_shape=[
             jax.ShapeDtypeStruct((protos, part), F32),
-            jax.ShapeDtypeStruct((batch_size, protos, part), BF16),
+            jax.ShapeDtypeStruct((batch_size, protos + 16, part), BF16),
         ],
         compiler_params=params(20),
         cost_estimate=cost(MIB, MIB),
         name="proto_gradient",
-    )(index, *[in_vmem(dscore)] * 8, *[unit] * 8)
+    )(index, *[in_vmem(dscore)] * 8, *[unit] * 8, loss)
 
 
 def embed_gradient_kernel(index_ref, embeddings_ref, *refs):
@@ -590,21 +593,19 @@
         gunit = run(1, BF16, other_after)
         return [run(0, F32, own_after), swap(gunit, "core", 1)]
 
-    loss = functools.reduce(jnp.add, parts_of(loss, PLACE))
-    forwarded = after(add_blocks(part_of(3), BF16), loss)
+    loss = loss + swap(loss, "core", 1)
+    forwarded = add_blocks(part_of(3), BF16)
     from_forwarder = swap(forwarded, PLACE, 1)
     near = add_blocks(part_of(1, [forwarded], [forwarded]), BF16)
     from_near = swap(near, PLACE, 1)
     across = part_of(2, [near], [near])
     values = part_of(0, [near], [from_near])
 
-    loss = loss + swap(loss, "core", 1)
-    loss = functools.reduce(jnp.add, parts_of(loss, "batch"))
-    grad_proto, proto_sent = proto_gradient(dscore, unit, after(scalar(batch_index), values[1]), batch_size)
+    grad_proto, proto_sent = proto_gradient(dscore, unit, loss, after(scalar(batch_index), values[1]), batch_size)
     from_forwarder = after(from_forwarder, proto_sent)
     across = add_blocks(across + [from_forwarder], BF16)
     values += [from_near, swap(across, PLACE, 2)]
-    proto_sent = after(proto_sent, loss, across)
+    proto_sent = after(proto_sent, across)
 
     bit = 2
     while (1 << bit) < places:
@@ -613,9 +614,11 @@
         bit += 1
     grad_embed = embed_gradient(scalar(proto_index), embeddings, [value[0] for value in values])
     arrived = [swap(proto_sent[distance], "batch", distance) for distance in range(batch_size - 1, 0, -1)]
+    for block in arrived:
+        grad_proto = grad_proto + block[:proto_count].astype(F32)
+        loss = loss + jnp.sum(block[proto_count : proto_count + 3, :LANES].astype(F32), axis=0, keepdims=True)
+    loss = functools.reduce(jnp.add, parts_of(loss, PLACE))
     loss = loss[0, 0] / total_rows
-    for block in arrived:
-        grad_proto = grad_proto + block.astype(F32)
 
     return (loss, grad_proto, grad_embed)
 

time: 206 us -> 206 us (level)
  other arithmetic: 3.11 us -> 5.18 us
    reduce_sum x0 -> x3, other arithmetic: none -> 2.07 us  [on_device(): jnp.sum(block[proto_count:proto_count + 3, :LANES].astype(F32), axis=0, k...]
    ppermute x41 -> x38, starting transfers between devices: 43.3 us -> 41.3 us  [swap(): return lax.ppermute(value, axis, [(i, i ^ distance) for i in range(size)])]
    ppermute x41 -> x38, waiting for transfers between devices: 52.5 us -> 52.6 us  [swap(): return lax.ppermute(value, axis, [(i, i ^ distance) for i in range(size)])]
  transfers between devices with their start and end apart: 42 -> 39, of which waited for: 27 -> 27; matrix products, arithmetic and copies ran while one was open for 1% -> 2% of each run, Pallas kernels for 20% -> 19%
where the time goes in v10:
time: 206 us
  Pallas kernels  73.6 us (36%)
  waiting for transfers between devices  58.8 us (29%)
  starting transfers between devices  41.3 us (20%)
  between operations  15.6 us (8%)
  local copies, waits for them, and re-layouts  11.4 us (6%)
  other arithmetic  5.18 us (3%)
    ppermute x38, waiting for transfers between devices, swap(): return lax.ppermute(value, axis, [(i, i ^ distance) for i in range(size)])  52.6 us
    ppermute x38, starting transfers between devices, swap(): return lax.ppermute(value, axis, [(i, i ^ distance) for i in range(size)])  41.3 us
    pallas_call x1, Pallas kernels, partner_pass(): pl.pallas_call(functools.partial(partner_kernel, count, total, heat_scale...  25.6 us
    unnamed x24, local copies, waits for them, and re-layouts  10.1 us
    pallas_call x1, Pallas kernels, lookup(): pl.pallas_call(lookup_kernel, grid_spec=pltpu.PrefetchScalarGridSpec(num_...  10.1 us
    pallas_call x8, Pallas kernels, gradients(): pl.pallas_call(gradient_kernel, grid_spec=pltpu.PrefetchScalarGridSpec(nu...  9.94 us
    pallas_call x1, Pallas kernels, scores_of(): pl.pallas_call(scores_kernel, grid=(rows // share // 2,), in_specs=[pl.Bl...  7.93 us
    pallas_call x1, Pallas kernels, proto_gradient(): pl.pallas_call(proto_gradient_kernel, grid_spec=pltpu.PrefetchScalarGridS...  6.28 us
  transfers between devices with their start and end apart: 39, of which 27 were waited for; matrix products, arithmetic and copies ran while one was open for 2% of the time, Pallas kernels for 19%

profile of v10, /device:TPU:0, one launch (start us, length us, event | category | flops | bytes accessed | tf_op | source)
XLA Modules:
  0.0 205.8 jit_solution(9724064822907835019)
XLA Ops:
  7.2 2.6 %own_rows.1 = bf16[512,8,128]{2,1,0:T(8,128)(2,1)} custom-call(s32[1]{0:T(128)} %bitcast.5.index_ref, bf16[2048,1024]{1,0:T(8,128)(2,1)} %embeddings_ref.5), custom_call_target="tpu_custom_call" | custom-call | tf_op jit(solution)/shard_map/own_rows/pallas_call | solution.py:78
  9.9 2.2 %copy-done.6 = bf16[2048,1024]{1,0:T(8,128)(2,1)S(1)} copy-done((bf16[2048,1024]{1,0:T(8,128)(2,1)S(1)}, bf16[2048,1024]{1,0:T(8,128)(2,1)}, u32[]{:S(2)}) %copy-start.6) | copy-done | bytes 4194328
  12.1 1.6 copy-done.8
  13.6 7.9 %scores.1 = (bf16[2048,1024]{1,0:T(8,128)(2,1)S(1)}, bf16[1024,1024]{1,0:T(8,128)(2,1)S(1)}, f32[2048,1024]{1,0:T(8,128)S(1)}, bf16[2048,1024]{1,0:T(8,128)(2,1)...) custom-call(bf16[2048,1024]{1,0:T(8,128)(2,1)S(1)} %copy-done.6, bf16[1024,1024]{1,0:T(8,128)(2,1)S(1)} %copy-done.8), custom_call_target="tpu_custom_call" | custom-call | flops 4294967296 | bytes 23068672 | tf_op jit(solution)/shard_map/scores/pallas_call | solution.py:127
  21.6 3.0 %collective-permute-start = (f32[1,1024]{1,0:T(1,128)S(1)}, f32[1,1024]{1,0:T(1,128)S(1)}, u32[]{:S(2)}, u32[]{:S(2)}) collective-permute-start(f32[1,1024]{1,0:T(1,128)S(1)} %get-tuple-element.22.refs_0_), channel_id=1, source_target_pairs={{0,8},{8,0},{16,24},{24,16},{1,9},{9,1},{17,25},{25,17},{2,10},{10... | collective-permute-start | bytes 12296 | tf_op jit(solution)/shard_map/ppermute | solution.py:526
  26.3 2.0 collective-permute-done.1.refs_2_
  28.2 2.5 %collective-permute-done.2.refs_3_ = f32[1,1024]{1,0:T(1,128)S(1)} collective-permute-done((f32[1,1024]{1,0:T(1,128)S(1)}, f32[1,1024]{1,0:T(1,128)S(1)}, u32[]{:S(2)}, u32[]{:S(2)}) %collective-permute-start.2) | collective-permute-done | bytes 4128 | tf_op jit(solution)/shard_map/ppermute | solution.py:526
  33.4 1.6 collective-permute-start.4
  35.0 2.6 %collective-permute-start.5 = (f32[1,2048]{1,0:T(1,128)S(1)}, f32[1,2048]{1,0:T(1,128)S(1)}, u32[]{:S(2)}, u32[]{:S(2)}) collective-permute-start(f32[1,2048]{1,0:T(1,128)S(1)} %add.68.refs_0_), channel_id=1, source_target_pairs={{0,4},{2,6},{4,0},{6,2},{1,5},{3,7},{5,1},{7,3},{8,12},{10,14},{12... | collective-permute-start | bytes 24584 | tf_op jit(solution)/shard_map/ppermute | solution.py:526
  37.8 1.8 collective-permute-done.5.refs_2_
  39.7 3.5 %collective-permute-done.6.refs_3_ = f32[1,2048]{1,0:T(1,128)S(1)} collective-permute-done((f32[1,2048]{1,0:T(1,128)S(1)}, f32[1,2048]{1,0:T(1,128)S(1)}, u32[]{:S(2)}, u32[]{:S(2)}) %collective-permute-start.6) | collective-permute-done | bytes 8224 | tf_op jit(solution)/shard_map/ppermute | solution.py:526
  45.0 2.5 %collective-permute-start.9 = (f32[1,1024]{1,0:T(1,128)S(1)}, f32[1,1024]{1,0:T(1,128)S(1)}, u32[]{:S(2)}, u32[]{:S(2)}) collective-permute-start(f32[1,1024]{1,0:T(1,128)S(1)} %column_pass.2.refs_0_), channel_id=1, source_target_pairs={{0,24},{8,16},{16,8},{24,0},{1,25},{9,17},{17,9},{25,1},{2,26},{10... | collective-permute-start | bytes 12296 | tf_op jit(solution)/shard_map/ppermute | solution.py:526
  53.0 3.7 %collective-permute-start.13 = (f32[1,2048]{1,0:T(1,128)S(1)}, f32[1,2048]{1,0:T(1,128)S(1)}, u32[]{:S(2)}, u32[]{:S(2)}) collective-permute-start(f32[1,2048]{1,0:T(1,128)S(1)} %add.69.refs_0_), channel_id=1, source_target_pairs={{0,6},{2,4},{4,2},{6,0},{1,7},{3,5},{5,3},{7,1},{8,14},{10,12},{12... | collective-permute-start | bytes 24584 | tf_op jit(solution)/shard_map/ppermute | solution.py:526
  57.0 1.7 collective-permute-done.13.refs_3_
  64.7 2.5 %collective-permute-done.16.refs_3_ = f32[1,1024]{1,0:T(1,128)S(1)} collective-permute-done((f32[1,1024]{1,0:T(1,128)S(1)}, f32[1,1024]{1,0:T(1,128)S(1)}, u32[]{:S(2)}, u32[]{:S(2)}) %collective-permute-start.16) | collective-permute-done | bytes 4128 | tf_op jit(solution)/shard_map/ppermute | solution.py:526
  67.2 2.3 %copy-done.1 = bf16[2048,1024]{1,0:T(8,128)(2,1)S(1)} copy-done((bf16[2048,1024]{1,0:T(8,128)(2,1)S(1)}, bf16[2048,1024]{1,0:T(8,128)(2,1)}, u32[]{:S(2)}) %copy-start.1) | copy-done | bytes 4194328
  72.5 4.0 %collective-permute-start.19 = (f32[2,2048]{1,0:T(2,128)S(1)}, f32[2,2048]{1,0:T(2,128)S(1)}, u32[]{:S(2)}, u32[]{:S(2)}) collective-permute-start(f32[2,2048]{1,0:T(2,128)S(1)} %fusion.1), channel_id=1, source_target_pairs={{0,4},{2,6},{4,0},{6,2},{1,5},{3,7},{5,1},{7,3},{8,12},{10,14},{12... | collective-permute-start | bytes 49160 | tf_op jit(solution)/shard_map/ppermute | solution.py:526
  78.3 4.0 %collective-permute-done.20 = f32[2,2048]{1,0:T(2,128)S(1)} collective-permute-done((f32[2,2048]{1,0:T(2,128)S(1)}, f32[2,2048]{1,0:T(2,128)S(1)}, u32[]{:S(2)}, u32[]{:S(2)}) %collective-permute-start.20) | collective-permute-done | bytes 16416 | tf_op jit(solution)/shard_map/ppermute | solution.py:526
  83.1 2.8 %collective-permute-start.23 = (f32[2048]{0:T(1024)S(1)}, f32[2048]{0:T(1024)S(1)}, u32[]{:S(2)}, u32[]{:S(2)}) collective-permute-start(f32[2048]{0:T(1024)S(1)} %bitcast.70), channel_id=1, source_target_pairs={{0,24},{8,16},{16,8},{24,0},{1,25},{9,17},{17,9},{25,1},{2,26},{10... | collective-permute-start | bytes 24584 | tf_op jit(solution)/shard_map/ppermute | solution.py:526
  87.8 10.1 %lookup.1 = f32[4096]{0:T(1024)S(1)} custom-call(s32[2048]{0:T(1024)S(1)} %bitcast.64, s32[2048]{0:T(1024)S(1)} %bitcast.63, f32[8192]{0:T(1024)S(1)} %pad_maximum_fusion.totals_ref), custom_call_target="tpu_custom_call" | custom-call | flops 1048576 | bytes 1048576 | tf_op jit(solution)/shard_map/lookup/pallas_call | solution.py:333
  97.9 6.1 %all-gather.2.cloned.1.call-done.refs_5_ = bf16[8192,8,128]{2,1,0:T(8,128)(2,1)} async-done(((bf16[512,8,128]{2,1,0:T(8,128)(2,1)}), bf16[8192,8,128]{2,1,0:T(8,128)(2,1)}) %all-gather.2.cloned.1.call-update) | async-done | bytes 16777232 | tf_op jit(solution)/shard_map/all_gather | solution.py:563
  104.1 25.6 %partner_scores.1 = (bf16[2048,1024]{1,0:T(8,128)(2,1)S(1)}, f32[1,128]{1,0:T(1,128)S(1)}) custom-call(s32[2048]{0:T(1024)S(1)} %bitcast.66, s32[2048]{0:T(1024)S(1)} %bitcast.65, f32[1,1024]{1,0:T(1,128)S(1)} %column_pass.3.refs_0_, f32[1,1024]{1,0:T(1,128)S(1)} %collective-permute-done.14.refs_1_, f32[1,1024]{1,0:T(1,128)S(1)} %collective-permute-done.15.refs_2_, ...), custom_call_target="tpu_custom_call" | custom-call | flops 8589934592 | bytes 33554432 | tf_op jit(solution)/shard_map/partner_scores/pallas_call | solution.py:292
  144.3 6.3 %proto_gradient.1 = (f32[1024,256]{1,0:T(8,128)S(1)}, bf16[4,1040,256]{2,1,0:T(8,128)(2,1)S(1)}) custom-call(s32[1]{0:T(128)} %bitcast.6.index_ref, bf16[1,2,2,2,256,1024]{5,4,3,2,1,0:T(8,128)(2,1)S(1)} %bitcast.45, bf16[1,2,2,2,256,1024]{5,4,3,2,1,0:T(8,128)(2,1)S(1)} %bitcast.46, bf16[1,2,2,2,256,1024]{5,4,3,2,1,0:T(8,128)(2,1)S(1)} %bitcast.47, ...), custom_call_target="tpu_custom_call" | custom-call | flops 1048576 | bytes 1048576 | tf_op jit(solution)/shard_map/proto_gradient/pallas_call | solution.py:469
  150.6 2.2 %collective-permute-done.29.refs_2_ = bf16[1,256,1024]{2,1,0:T(8,128)(2,1)S(1)} collective-permute-done((bf16[1,256,1024]{2,1,0:T(8,128)(2,1)S(1)}, bf16[1,256,1024]{2,1,0:T(8,128)(2,1)S(1)}, u32[]{:S(2)}, u32[]{:S(2)}) %collective-permute-start.29) | collective-permute-done | bytes 524320 | tf_op jit(solution)/shard_map/ppermute | solution.py:526
  155.1 1.6 collective-permute-start.36
  156.7 2.4 %collective-permute-start.37 = (bf16[1,256,1024]{2,1,0:T(8,128)(2,1)}, bf16[1,256,1024]{2,1,0:T(8,128)(2,1)}, u32[]{:S(2)}, u32[]{:S(2)}) collective-permute-start(bf16[1,256,1024]{2,1,0:T(8,128)(2,1)} %add_blocks.5), channel_id=1, source_target_pairs={{0,4},{2,6},{4,0},{6,2},{1,5},{3,7},{5,1},{7,3},{8,12},{10,14},{12... | collective-permute-start | bytes 1572872 | tf_op jit(solution)/shard_map/ppermute | solution.py:526
  159.7 1.6 collective-permute-start.30
  161.4 18.3 %collective-permute-done.36 = bf16[1,256,1024]{2,1,0:T(8,128)(2,1)} collective-permute-done((bf16[1,256,1024]{2,1,0:T(8,128)(2,1)}, bf16[1,256,1024]{2,1,0:T(8,128)(2,1)}, u32[]{:S(2)}, u32[]{:S(2)}) %collective-permute-start.36) | collective-permute-done | bytes 524320 | tf_op jit(solution)/shard_map/ppermute | solution.py:526
  179.7 2.2 %copy-done.3 = bf16[2048,1024]{1,0:T(8,128)(2,1)S(1)} copy-done((bf16[2048,1024]{1,0:T(8,128)(2,1)S(1)}, bf16[2048,1024]{1,0:T(8,128)(2,1)}, u32[]{:S(2)}) %copy-start.3) | copy-done | bytes 4194328
  184.1 3.4 %embed_gradient.1 = f32[256,1024]{1,0:T(8,128)} custom-call(s32[1]{0:T(128)} %bitcast.22.index_ref, bf16[2048,1024]{1,0:T(8,128)(2,1)} %embeddings_ref.5, f32[256,1024]{1,0:T(8,128)} %bitcast.62, bf16[256,1024]{1,0:T(8,128)(2,1)} %bitcast.67, bf16[256,1024]{1,0:T(8,128)(2,1)} %bitcast.25.refs_2_, bf16[256,1024]{1,0:T(8,128)(2,1)} %bitcast.26.refs_3_), custom_call_target="tpu_custom_call" | custom-call | flops 2097152 | bytes 4194304 | tf_op jit(solution)/shard_map/embed_gradient/pallas_call | solution.py:506
  189.6 2.8 %collective-permute-start.34 = (f32[1,128]{1,0:T(1,128)S(1)}, f32[1,128]{1,0:T(1,128)S(1)}, u32[]{:S(2)}, u32[]{:S(2)}) collective-permute-start(f32[1,128]{1,0:T(1,128)S(1)} %bitcast_add_fusion), channel_id=1, source_target_pairs={{0,4},{2,6},{4,0},{6,2},{1,5},{3,7},{5,1},{7,3},{8,12},{10,14},{12... | collective-permute-start | bytes 1544 | tf_op jit(solution)/shard_map/ppermute | solution.py:526
  194.0 2.5 %convert_add_fusion = f32[1024,256]{1,0:T(8,128)} fusion(f32[1024,256]{1,0:T(8,128)S(1)} %get-tuple-element.39, bf16[1040,256]{1,0:T(8,128)(2,1)} %collective-permute-done.32, bf16[1040,256]{1,0:T(8,128)(2,1)} %collective-permute-done.31, bf16[1040,256]{1,0:T(8,128)(2,1)} %collective-permute-done.30), kind=kLoop, calls=%fused_computation | loop fusion | flops 1572864 | bytes 3670016 | tf_op jit(solution)/shard_map/add | solution.py:618
  (118 shorter events, 50.2 us)
Async XLA Ops:
  7.2 96.9 %all-gather.2.cloned.1.call-start = ((), (), s32[]{:S(2)}) async-start(), calls=%async_computation | async-start | bytes 17825792 | tf_op jit(solution)/shard_map/all_gather | solution.py:563
  21.6 4.7 %collective-permute-start = (f32[1,1024]{1,0:T(1,128)S(1)}, f32[1,1024]{1,0:T(1,128)S(1)}, u32[]{:S(2)}, u32[]{:S(2)}) collective-permute-start(f32[1,1024]{1,0:T(1,128)S(1)} %get-tuple-element.22.refs_0_), channel_id=1, source_target_pairs={{0,8},{8,0},{16,24},{24,16},{1,9},{9,1},{17,25},{25,17},{2,10},{10... | collective-permute-start | bytes 12296 | tf_op jit(solution)/shard_map/ppermute | solution.py:526
  24.6 3.6 %collective-permute-start.1 = (f32[1,1024]{1,0:T(1,128)S(1)}, f32[1,1024]{1,0:T(1,128)S(1)}, u32[]{:S(2)}, u32[]{:S(2)}) collective-permute-start(f32[1,1024]{1,0:T(1,128)S(1)} %get-tuple-element.22.refs_0_), channel_id=1, source_target_pairs={{0,16},{8,24},{16,0},{24,8},{1,17},{9,25},{17,1},{25,9},{2,18},{10... | collective-permute-start | bytes 12296 | tf_op jit(solution)/shard_map/ppermute | solution.py:526
  26.1 4.6 %collective-permute-start.2 = (f32[1,1024]{1,0:T(1,128)S(1)}, f32[1,1024]{1,0:T(1,128)S(1)}, u32[]{:S(2)}, u32[]{:S(2)}) collective-permute-start(f32[1,1024]{1,0:T(1,128)S(1)} %get-tuple-element.22.refs_0_), channel_id=1, source_target_pairs={{0,24},{8,16},{16,8},{24,0},{1,25},{9,17},{17,9},{25,1},{2,26},{10... | collective-permute-start | bytes 12296 | tf_op jit(solution)/shard_map/ppermute | solution.py:526
  33.4 4.5 %collective-permute-start.4 = (f32[1,2048]{1,0:T(1,128)S(1)}, f32[1,2048]{1,0:T(1,128)S(1)}, u32[]{:S(2)}, u32[]{:S(2)}) collective-permute-start(f32[1,2048]{1,0:T(1,128)S(1)} %add.68.refs_0_), channel_id=1, source_target_pairs={{0,2},{2,0},{4,6},{6,4},{1,3},{3,1},{5,7},{7,5},{8,10},{10,8},{12,... | collective-permute-start | bytes 24584 | tf_op jit(solution)/shard_map/ppermute | solution.py:526
  35.0 4.7 %collective-permute-start.5 = (f32[1,2048]{1,0:T(1,128)S(1)}, f32[1,2048]{1,0:T(1,128)S(1)}, u32[]{:S(2)}, u32[]{:S(2)}) collective-permute-start(f32[1,2048]{1,0:T(1,128)S(1)} %add.68.refs_0_), channel_id=1, source_target_pairs={{0,4},{2,6},{4,0},{6,2},{1,5},{3,7},{5,1},{7,3},{8,12},{10,14},{12... | collective-permute-start | bytes 24584 | tf_op jit(solution)/shard_map/ppermute | solution.py:526
  37.6 5.6 %collective-permute-start.6 = (f32[1,2048]{1,0:T(1,128)S(1)}, f32[1,2048]{1,0:T(1,128)S(1)}, u32[]{:S(2)}, u32[]{:S(2)}) collective-permute-start(f32[1,2048]{1,0:T(1,128)S(1)} %add.68.refs_0_), channel_id=1, source_target_pairs={{0,6},{2,4},{4,2},{6,0},{1,7},{3,5},{5,3},{7,1},{8,14},{10,12},{12... | collective-permute-start | bytes 24584 | tf_op jit(solution)/shard_map/ppermute | solution.py:526
  44.0 3.7 %collective-permute-start.7 = (f32[1,1024]{1,0:T(1,128)S(1)}, f32[1,1024]{1,0:T(1,128)S(1)}, u32[]{:S(2)}, u32[]{:S(2)}) collective-permute-start(f32[1,1024]{1,0:T(1,128)S(1)} %column_pass.2.refs_0_), channel_id=1, source_target_pairs={{0,8},{8,0},{16,24},{24,16},{1,9},{9,1},{17,25},{25,17},{2,10},{10... | collective-permute-start | bytes 12296 | tf_op jit(solution)/shard_map/ppermute | solution.py:526
  44.5 3.6 %collective-permute-start.8 = (f32[1,1024]{1,0:T(1,128)S(1)}, f32[1,1024]{1,0:T(1,128)S(1)}, u32[]{:S(2)}, u32[]{:S(2)}) collective-permute-start(f32[1,1024]{1,0:T(1,128)S(1)} %column_pass.2.refs_0_), channel_id=1, source_target_pairs={{0,16},{8,24},{16,0},{24,8},{1,17},{9,25},{17,1},{25,9},{2,18},{10... | collective-permute-start | bytes 12296 | tf_op jit(solution)/shard_map/ppermute | solution.py:526
  45.0 4.6 %collective-permute-start.9 = (f32[1,1024]{1,0:T(1,128)S(1)}, f32[1,1024]{1,0:T(1,128)S(1)}, u32[]{:S(2)}, u32[]{:S(2)}) collective-permute-start(f32[1,1024]{1,0:T(1,128)S(1)} %column_pass.2.refs_0_), channel_id=1, source_target_pairs={{0,24},{8,16},{16,8},{24,0},{1,25},{9,17},{17,9},{25,1},{2,26},{10... | collective-permute-start | bytes 12296 | tf_op jit(solution)/shard_map/ppermute | solution.py:526
  52.2 4.5 %collective-permute-start.11 = (f32[1,2048]{1,0:T(1,128)S(1)}, f32[1,2048]{1,0:T(1,128)S(1)}, u32[]{:S(2)}, u32[]{:S(2)}) collective-permute-start(f32[1,2048]{1,0:T(1,128)S(1)} %add.69.refs_0_), channel_id=1, source_target_pairs={{0,2},{2,0},{4,6},{6,4},{1,3},{3,1},{5,7},{7,5},{8,10},{10,8},{12,... | collective-permute-start | bytes 24584 | tf_op jit(solution)/shard_map/ppermute | solution.py:526
  52.3 4.7 %collective-permute-start.12 = (f32[1,2048]{1,0:T(1,128)S(1)}, f32[1,2048]{1,0:T(1,128)S(1)}, u32[]{:S(2)}, u32[]{:S(2)}) collective-permute-start(f32[1,2048]{1,0:T(1,128)S(1)} %add.69.refs_0_), channel_id=1, source_target_pairs={{0,4},{2,6},{4,0},{6,2},{1,5},{3,7},{5,1},{7,3},{8,12},{10,14},{12... | collective-permute-start | bytes 24584 | tf_op jit(solution)/shard_map/ppermute | solution.py:526
  53.0 5.8 %collective-permute-start.13 = (f32[1,2048]{1,0:T(1,128)S(1)}, f32[1,2048]{1,0:T(1,128)S(1)}, u32[]{:S(2)}, u32[]{:S(2)}) collective-permute-start(f32[1,2048]{1,0:T(1,128)S(1)} %add.69.refs_0_), channel_id=1, source_target_pairs={{0,6},{2,4},{4,2},{6,0},{1,7},{3,5},{5,3},{7,1},{8,14},{10,12},{12... | collective-permute-start | bytes 24584 | tf_op jit(solution)/shard_map/ppermute | solution.py:526
  59.6 3.8 %collective-permute-start.14 = (f32[1,1024]{1,0:T(1,128)S(1)}, f32[1,1024]{1,0:T(1,128)S(1)}, u32[]{:S(2)}, u32[]{:S(2)}) collective-permute-start(f32[1,1024]{1,0:T(1,128)S(1)} %column_pass.3.refs_0_), channel_id=1, source_target_pairs={{0,8},{8,0},{16,24},{24,16},{1,9},{9,1},{17,25},{25,17},{2,10},{10... | collective-permute-start | bytes 12296 | tf_op jit(solution)/shard_map/ppermute | solution.py:526
  62.6 4.6 %collective-permute-start.16 = (f32[1,1024]{1,0:T(1,128)S(1)}, f32[1,1024]{1,0:T(1,128)S(1)}, u32[]{:S(2)}, u32[]{:S(2)}) collective-permute-start(f32[1,1024]{1,0:T(1,128)S(1)} %column_pass.3.refs_0_), channel_id=1, source_target_pairs={{0,24},{8,16},{16,8},{24,0},{1,25},{9,17},{17,9},{25,1},{2,26},{10... | collective-permute-start | bytes 12296 | tf_op jit(solution)/shard_map/ppermute | solution.py:526
  72.2 4.5 %collective-permute-start.18 = (f32[2,2048]{1,0:T(2,128)S(1)}, f32[2,2048]{1,0:T(2,128)S(1)}, u32[]{:S(2)}, u32[]{:S(2)}) collective-permute-start(f32[2,2048]{1,0:T(2,128)S(1)} %fusion.1), channel_id=1, source_target_pairs={{0,2},{2,0},{4,6},{6,4},{1,3},{3,1},{5,7},{7,5},{8,10},{10,8},{12,... | collective-permute-start | bytes 49160 | tf_op jit(solution)/shard_map/ppermute | solution.py:526
  72.5 5.8 %collective-permute-start.19 = (f32[2,2048]{1,0:T(2,128)S(1)}, f32[2,2048]{1,0:T(2,128)S(1)}, u32[]{:S(2)}, u32[]{:S(2)}) collective-permute-start(f32[2,2048]{1,0:T(2,128)S(1)} %fusion.1), channel_id=1, source_target_pairs={{0,4},{2,6},{4,0},{6,2},{1,5},{3,7},{5,1},{7,3},{8,12},{10,14},{12... | collective-permute-start | bytes 49160 | tf_op jit(solution)/shard_map/ppermute | solution.py:526
  76.4 5.9 %collective-permute-start.20 = (f32[2,2048]{1,0:T(2,128)S(1)}, f32[2,2048]{1,0:T(2,128)S(1)}, u32[]{:S(2)}, u32[]{:S(2)}) collective-permute-start(f32[2,2048]{1,0:T(2,128)S(1)} %fusion.1), channel_id=1, source_target_pairs={{0,6},{2,4},{4,2},{6,0},{1,7},{3,5},{5,3},{7,1},{8,14},{10,12},{12... | collective-permute-start | bytes 49160 | tf_op jit(solution)/shard_map/ppermute | solution.py:526
  82.4 3.9 %collective-permute-start.21 = (f32[2048]{0:T(1024)S(1)}, f32[2048]{0:T(1024)S(1)}, u32[]{:S(2)}, u32[]{:S(2)}) collective-permute-start(f32[2048]{0:T(1024)S(1)} %bitcast.68), channel_id=1, source_target_pairs={{0,8},{8,0},{16,24},{24,16},{1,9},{9,1},{17,25},{25,17},{2,10},{10... | collective-permute-start | bytes 24584 | tf_op jit(solution)/shard_map/ppermute | solution.py:526
  82.6 3.7 %collective-permute-start.22 = (f32[2048]{0:T(1024)S(1)}, f32[2048]{0:T(1024)S(1)}, u32[]{:S(2)}, u32[]{:S(2)}) collective-permute-start(f32[2048]{0:T(1024)S(1)} %bitcast.69), channel_id=1, source_target_pairs={{0,16},{8,24},{16,0},{24,8},{1,17},{9,25},{17,1},{25,9},{2,18},{10... | collective-permute-start | bytes 24584 | tf_op jit(solution)/shard_map/ppermute | solution.py:526
  83.1 4.7 %collective-permute-start.23 = (f32[2048]{0:T(1024)S(1)}, f32[2048]{0:T(1024)S(1)}, u32[]{:S(2)}, u32[]{:S(2)}) collective-permute-start(f32[2048]{0:T(1024)S(1)} %bitcast.70), channel_id=1, source_target_pairs={{0,24},{8,16},{16,8},{24,0},{1,25},{9,17},{17,9},{25,1},{2,26},{10... | collective-permute-start | bytes 24584 | tf_op jit(solution)/shard_map/ppermute | solution.py:526
  138.4 5.1 %collective-permute-start.27 = (bf16[1,256,1024]{2,1,0:T(8,128)(2,1)S(1)}, bf16[1,256,1024]{2,1,0:T(8,128)(2,1)S(1)}, u32[]{:S(2)}, u32[]{:S(2)}) collective-permute-start(bf16[1,256,1024]{2,1,0:T(8,128)(2,1)S(1)} %gradients.12), channel_id=1, source_target_pairs={{0,1},{1,0},{2,3},{3,2},{4,5},{5,4},{6,7},{7,6},{8,9},{9,8},{10,11... | collective-permute-start | bytes 1572872 | tf_op jit(solution)/shard_map/ppermute | solution.py:526
  138.7 14.1 %collective-permute-start.29 = (bf16[1,256,1024]{2,1,0:T(8,128)(2,1)S(1)}, bf16[1,256,1024]{2,1,0:T(8,128)(2,1)S(1)}, u32[]{:S(2)}, u32[]{:S(2)}) collective-permute-start(bf16[1,256,1024]{2,1,0:T(8,128)(2,1)S(1)} %add_blocks.3), channel_id=1, source_target_pairs={{0,2},{2,0},{4,6},{6,4},{1,3},{3,1},{5,7},{7,5},{8,10},{10,8},{12,... | collective-permute-start | bytes 1572872 | tf_op jit(solution)/shard_map/ppermute | solution.py:526
  140.2 12.6 %collective-permute-start.28 = (bf16[1,256,1024]{2,1,0:T(8,128)(2,1)S(1)}, bf16[1,256,1024]{2,1,0:T(8,128)(2,1)S(1)}, u32[]{:S(2)}, u32[]{:S(2)}) collective-permute-start(bf16[1,256,1024]{2,1,0:T(8,128)(2,1)S(1)} %gradients.14), channel_id=1, source_target_pairs={{0,1},{1,0},{2,3},{3,2},{4,5},{5,4},{6,7},{7,6},{8,9},{9,8},{10,11... | collective-permute-start | bytes 1572872 | tf_op jit(solution)/shard_map/ppermute | solution.py:526
  155.0 32.4 %collective-permute-start.32 = (bf16[1040,256]{1,0:T(8,128)(2,1)}, bf16[1040,256]{1,0:T(8,128)(2,1)}, u32[]{:S(2)}, u32[]{:S(2)}) collective-permute-start(bf16[1040,256]{1,0:T(8,128)(2,1)} %get-tuple-element.42), channel_id=1, source_target_pairs={{0,8},{8,0},{16,24},{24,16},{1,9},{9,1},{17,25},{25,17},{2,10},{10... | collective-permute-start | bytes 1597448 | tf_op jit(solution)/shard_map/ppermute | solution.py:526
  155.1 24.6 %collective-permute-start.36 = (bf16[1,256,1024]{2,1,0:T(8,128)(2,1)}, bf16[1,256,1024]{2,1,0:T(8,128)(2,1)}, u32[]{:S(2)}, u32[]{:S(2)}) collective-permute-start(bf16[1,256,1024]{2,1,0:T(8,128)(2,1)} %add_blocks.4), channel_id=1, source_target_pairs={{0,2},{2,0},{4,6},{6,4},{1,3},{3,1},{5,7},{7,5},{8,10},{10,8},{12,... | collective-permute-start | bytes 1572872 | tf_op jit(solution)/shard_map/ppermute | solution.py:526
  156.7 27.4 %collective-permute-start.37 = (bf16[1,256,1024]{2,1,0:T(8,128)(2,1)}, bf16[1,256,1024]{2,1,0:T(8,128)(2,1)}, u32[]{:S(2)}, u32[]{:S(2)}) collective-permute-start(bf16[1,256,1024]{2,1,0:T(8,128)(2,1)} %add_blocks.5), channel_id=1, source_target_pairs={{0,4},{2,6},{4,0},{6,2},{1,5},{3,7},{5,1},{7,3},{8,12},{10,14},{12... | collective-permute-start | bytes 1572872 | tf_op jit(solution)/shard_map/ppermute | solution.py:526
  159.2 29.0 %collective-permute-start.31 = (bf16[1040,256]{1,0:T(8,128)(2,1)}, bf16[1040,256]{1,0:T(8,128)(2,1)}, u32[]{:S(2)}, u32[]{:S(2)}) collective-permute-start(bf16[1040,256]{1,0:T(8,128)(2,1)} %get-tuple-element.43), channel_id=1, source_target_pairs={{0,16},{8,24},{16,0},{24,8},{1,17},{9,25},{17,1},{25,9},{2,18},{10... | collective-permute-start | bytes 1597448 | tf_op jit(solution)/shard_map/ppermute | solution.py:526
  159.7 29.1 %collective-permute-start.30 = (bf16[1040,256]{1,0:T(8,128)(2,1)}, bf16[1040,256]{1,0:T(8,128)(2,1)}, u32[]{:S(2)}, u32[]{:S(2)}) collective-permute-start(bf16[1040,256]{1,0:T(8,128)(2,1)} %get-tuple-element.41), channel_id=1, source_target_pairs={{0,24},{8,16},{16,8},{24,0},{1,25},{9,17},{17,9},{25,1},{2,26},{10... | collective-permute-start | bytes 1597448 | tf_op jit(solution)/shard_map/ppermute | solution.py:526
  189.5 7.0 %collective-permute-start.33 = (f32[1,128]{1,0:T(1,128)S(1)}, f32[1,128]{1,0:T(1,128)S(1)}, u32[]{:S(2)}, u32[]{:S(2)}) collective-permute-start(f32[1,128]{1,0:T(1,128)S(1)} %bitcast_add_fusion), channel_id=1, source_target_pairs={{0,2},{2,0},{4,6},{6,4},{1,3},{3,1},{5,7},{7,5},{8,10},{10,8},{12,... | collective-permute-start | bytes 1544 | tf_op jit(solution)/shard_map/ppermute | solution.py:526
  189.6 6.9 %collective-permute-start.34 = (f32[1,128]{1,0:T(1,128)S(1)}, f32[1,128]{1,0:T(1,128)S(1)}, u32[]{:S(2)}, u32[]{:S(2)}) collective-permute-start(f32[1,128]{1,0:T(1,128)S(1)} %bitcast_add_fusion), channel_id=1, source_target_pairs={{0,4},{2,6},{4,0},{6,2},{1,5},{3,7},{5,1},{7,3},{8,12},{10,14},{12... | collective-permute-start | bytes 1544 | tf_op jit(solution)/shard_map/ppermute | solution.py:526
  192.4 5.3 %collective-permute-start.35 = (f32[1,128]{1,0:T(1,128)S(1)}, f32[1,128]{1,0:T(1,128)S(1)}, u32[]{:S(2)}, u32[]{:S(2)}) collective-permute-start(f32[1,128]{1,0:T(1,128)S(1)} %bitcast_add_fusion), channel_id=1, source_target_pairs={{0,6},{2,4},{4,2},{6,0},{1,7},{3,5},{5,3},{7,1},{8,14},{10,12},{12... | collective-permute-start | bytes 1544 | tf_op jit(solution)/shard_map/ppermute | solution.py:526
  (19 other events, 111.1 us)
Sparse Core Ops, SparseCore 0:
  10.2 93.8 all-gather.1

commit v11 on v10

--- a/solution.py
+++ b/solution.py
@@ -599,10 +599,11 @@
     near = add_blocks(part_of(1, [forwarded], [forwarded]), BF16)
     from_near = swap(near, PLACE, 1)
     across = part_of(2, [near], [near])
-    values = part_of(0, [near], [from_near])
+    values = part_of(0, [near], [near])
 
     grad_proto, proto_sent = proto_gradient(dscore, unit, loss, after(scalar(batch_index), values[1]), batch_size)
     from_forwarder = after(from_forwarder, proto_sent)
+    from_near = after(from_near, proto_sent)
     across = add_blocks(across + [from_forwarder], BF16)
     values += [from_near, swap(across, PLACE, 2)]
     proto_sent = after(proto_sent, across)
@@ -616,7 +617,8 @@
     arrived = [swap(proto_sent[distance], "batch", distance) for distance in range(batch_size - 1, 0, -1)]
     for block in arrived:
         grad_proto = grad_proto + block[:proto_count].astype(F32)
-        loss = loss + jnp.sum(block[proto_count : proto_count + 3, :LANES].astype(F32), axis=0, keepdims=True)
+    rows = functools.reduce(jnp.add, [block[proto_count : proto_count + 3, :LANES].astype(F32) for block in arrived])
+    loss = loss + jnp.sum(rows, axis=0, keepdims=True)
     loss = functools.reduce(jnp.add, parts_of(loss, PLACE))
     loss = loss[0, 0] / total_rows
 

time: 206 us -> 205 us (level)
  no operation moved by 1% of the time
where the time goes in v11:
time: 205 us
  Pallas kernels  73.6 us (36%)
  waiting for transfers between devices  58.8 us (29%)
  starting transfers between devices  42 us (20%)
  between operations  15.6 us (8%)
  local copies, waits for them, and re-layouts  11.4 us (6%)
  other arithmetic  3.73 us (2%)
    ppermute x38, waiting for transfers between devices, swap(): return lax.ppermute(value, axis, [(i, i ^ distance) for i in range(size)])  52.7 us
    ppermute x38, starting transfers between devices, swap(): return lax.ppermute(value, axis, [(i, i ^ distance) for i in range(size)])  42 us
    pallas_call x1, Pallas kernels, partner_pass(): pl.pallas_call(functools.partial(partner_kernel, count, total, heat_scale...  25.6 us
    unnamed x24, local copies, waits for them, and re-layouts  10.1 us
    pallas_call x1, Pallas kernels, lookup(): pl.pallas_call(lookup_kernel, grid_spec=pltpu.PrefetchScalarGridSpec(num_...  10.1 us
    pallas_call x8, Pallas kernels, gradients(): pl.pallas_call(gradient_kernel, grid_spec=pltpu.PrefetchScalarGridSpec(nu...  9.96 us
    pallas_call x1, Pallas kernels, scores_of(): pl.pallas_call(scores_kernel, grid=(rows // share // 2,), in_specs=[pl.Bl...  7.93 us
    pallas_call x1, Pallas kernels, proto_gradient(): pl.pallas_call(proto_gradient_kernel, grid_spec=pltpu.PrefetchScalarGridS...  6.28 us
  transfers between devices with their start and end apart: 39, of which 27 were waited for; matrix products, arithmetic and copies ran while one was open for 2% of the time, Pallas kernels for 19%

profile of v11, /device:TPU:0, one launch (start us, length us, event | category | flops | bytes accessed | tf_op | source)
XLA Modules:
  0.0 205.1 jit_solution(4878212220946424770)
XLA Ops:
  7.2 2.6 %own_rows.1 = bf16[512,8,128]{2,1,0:T(8,128)(2,1)} custom-call(s32[1]{0:T(128)} %bitcast.5.index_ref, bf16[2048,1024]{1,0:T(8,128)(2,1)} %embeddings_ref.5), custom_call_target="tpu_custom_call" | custom-call | tf_op jit(solution)/shard_map/own_rows/pallas_call | solution.py:78
  9.9 2.2 %copy-done.6 = bf16[2048,1024]{1,0:T(8,128)(2,1)S(1)} copy-done((bf16[2048,1024]{1,0:T(8,128)(2,1)S(1)}, bf16[2048,1024]{1,0:T(8,128)(2,1)}, u32[]{:S(2)}) %copy-start.6) | copy-done | bytes 4194328
  13.6 7.9 %scores.1 = (bf16[2048,1024]{1,0:T(8,128)(2,1)S(1)}, bf16[1024,1024]{1,0:T(8,128)(2,1)S(1)}, f32[2048,1024]{1,0:T(8,128)S(1)}, bf16[2048,1024]{1,0:T(8,128)(2,1)...) custom-call(bf16[2048,1024]{1,0:T(8,128)(2,1)S(1)} %copy-done.6, bf16[1024,1024]{1,0:T(8,128)(2,1)S(1)} %copy-done.8), custom_call_target="tpu_custom_call" | custom-call | flops 4294967296 | bytes 23068672 | tf_op jit(solution)/shard_map/scores/pallas_call | solution.py:127
  21.6 3.0 %collective-permute-start = (f32[1,1024]{1,0:T(1,128)S(1)}, f32[1,1024]{1,0:T(1,128)S(1)}, u32[]{:S(2)}, u32[]{:S(2)}) collective-permute-start(f32[1,1024]{1,0:T(1,128)S(1)} %get-tuple-element.23.refs_0_), channel_id=1, source_target_pairs={{0,8},{8,0},{16,24},{24,16},{1,9},{9,1},{17,25},{25,17},{2,10},{10... | collective-permute-start | bytes 12296 | tf_op jit(solution)/shard_map/ppermute | solution.py:526
  26.3 2.0 collective-permute-done.1.refs_2_
  28.2 2.5 %collective-permute-done.2.refs_3_ = f32[1,1024]{1,0:T(1,128)S(1)} collective-permute-done((f32[1,1024]{1,0:T(1,128)S(1)}, f32[1,1024]{1,0:T(1,128)S(1)}, u32[]{:S(2)}, u32[]{:S(2)}) %collective-permute-start.2) | collective-permute-done | bytes 4128 | tf_op jit(solution)/shard_map/ppermute | solution.py:526
  33.4 1.6 collective-permute-start.4
  35.0 2.6 %collective-permute-start.5 = (f32[1,2048]{1,0:T(1,128)S(1)}, f32[1,2048]{1,0:T(1,128)S(1)}, u32[]{:S(2)}, u32[]{:S(2)}) collective-permute-start(f32[1,2048]{1,0:T(1,128)S(1)} %add.68.refs_0_), channel_id=1, source_target_pairs={{0,4},{2,6},{4,0},{6,2},{1,5},{3,7},{5,1},{7,3},{8,12},{10,14},{12... | collective-permute-start | bytes 24584 | tf_op jit(solution)/shard_map/ppermute | solution.py:526
  37.8 1.8 collective-permute-done.5.refs_2_
  39.7 3.5 %collective-permute-done.6.refs_3_ = f32[1,2048]{1,0:T(1,128)S(1)} collective-permute-done((f32[1,2048]{1,0:T(1,128)S(1)}, f32[1,2048]{1,0:T(1,128)S(1)}, u32[]{:S(2)}, u32[]{:S(2)}) %collective-permute-start.6) | collective-permute-done | bytes 8224 | tf_op jit(solution)/shard_map/ppermute | solution.py:526
  45.0 2.5 %collective-permute-start.9 = (f32[1,1024]{1,0:T(1,128)S(1)}, f32[1,1024]{1,0:T(1,128)S(1)}, u32[]{:S(2)}, u32[]{:S(2)}) collective-permute-start(f32[1,1024]{1,0:T(1,128)S(1)} %column_pass.2.refs_0_), channel_id=1, source_target_pairs={{0,24},{8,16},{16,8},{24,0},{1,25},{9,17},{17,9},{25,1},{2,26},{10... | collective-permute-start | bytes 12296 | tf_op jit(solution)/shard_map/ppermute | solution.py:526
  53.0 3.7 %collective-permute-start.13 = (f32[1,2048]{1,0:T(1,128)S(1)}, f32[1,2048]{1,0:T(1,128)S(1)}, u32[]{:S(2)}, u32[]{:S(2)}) collective-permute-start(f32[1,2048]{1,0:T(1,128)S(1)} %add.69.refs_0_), channel_id=1, source_target_pairs={{0,6},{2,4},{4,2},{6,0},{1,7},{3,5},{5,3},{7,1},{8,14},{10,12},{12... | collective-permute-start | bytes 24584 | tf_op jit(solution)/shard_map/ppermute | solution.py:526
  57.0 1.7 collective-permute-done.13.refs_3_
  64.7 2.5 %collective-permute-done.16.refs_3_ = f32[1,1024]{1,0:T(1,128)S(1)} collective-permute-done((f32[1,1024]{1,0:T(1,128)S(1)}, f32[1,1024]{1,0:T(1,128)S(1)}, u32[]{:S(2)}, u32[]{:S(2)}) %collective-permute-start.16) | collective-permute-done | bytes 4128 | tf_op jit(solution)/shard_map/ppermute | solution.py:526
  67.2 2.3 %copy-done.1 = bf16[2048,1024]{1,0:T(8,128)(2,1)S(1)} copy-done((bf16[2048,1024]{1,0:T(8,128)(2,1)S(1)}, bf16[2048,1024]{1,0:T(8,128)(2,1)}, u32[]{:S(2)}) %copy-start.1) | copy-done | bytes 4194328
  72.5 4.0 %collective-permute-start.19 = (f32[2,2048]{1,0:T(2,128)S(1)}, f32[2,2048]{1,0:T(2,128)S(1)}, u32[]{:S(2)}, u32[]{:S(2)}) collective-permute-start(f32[2,2048]{1,0:T(2,128)S(1)} %fusion.1), channel_id=1, source_target_pairs={{0,4},{2,6},{4,0},{6,2},{1,5},{3,7},{5,1},{7,3},{8,12},{10,14},{12... | collective-permute-start | bytes 49160 | tf_op jit(solution)/shard_map/ppermute | solution.py:526
  78.3 4.0 %collective-permute-done.20 = f32[2,2048]{1,0:T(2,128)S(1)} collective-permute-done((f32[2,2048]{1,0:T(2,128)S(1)}, f32[2,2048]{1,0:T(2,128)S(1)}, u32[]{:S(2)}, u32[]{:S(2)}) %collective-permute-start.20) | collective-permute-done | bytes 16416 | tf_op jit(solution)/shard_map/ppermute | solution.py:526
  83.1 2.8 %collective-permute-start.23 = (f32[2048]{0:T(1024)S(1)}, f32[2048]{0:T(1024)S(1)}, u32[]{:S(2)}, u32[]{:S(2)}) collective-permute-start(f32[2048]{0:T(1024)S(1)} %bitcast.62), channel_id=1, source_target_pairs={{0,24},{8,16},{16,8},{24,0},{1,25},{9,17},{17,9},{25,1},{2,26},{10... | collective-permute-start | bytes 24584 | tf_op jit(solution)/shard_map/ppermute | solution.py:526
  87.8 10.1 %lookup.1 = f32[4096]{0:T(1024)S(1)} custom-call(s32[2048]{0:T(1024)S(1)} %bitcast.56, s32[2048]{0:T(1024)S(1)} %bitcast.55, f32[8192]{0:T(1024)S(1)} %pad_maximum_fusion.totals_ref), custom_call_target="tpu_custom_call" | custom-call | flops 1048576 | bytes 1048576 | tf_op jit(solution)/shard_map/lookup/pallas_call | solution.py:333
  97.9 6.1 %all-gather.2.cloned.1.call-done.refs_5_ = bf16[8192,8,128]{2,1,0:T(8,128)(2,1)} async-done(((bf16[512,8,128]{2,1,0:T(8,128)(2,1)}), bf16[8192,8,128]{2,1,0:T(8,128)(2,1)}) %all-gather.2.cloned.1.call-update) | async-done | bytes 16777232 | tf_op jit(solution)/shard_map/all_gather | solution.py:563
  104.1 25.6 %partner_scores.1 = (bf16[2048,1024]{1,0:T(8,128)(2,1)S(1)}, f32[1,128]{1,0:T(1,128)S(1)}) custom-call(s32[2048]{0:T(1024)S(1)} %bitcast.58, s32[2048]{0:T(1024)S(1)} %bitcast.57, f32[1,1024]{1,0:T(1,128)S(1)} %column_pass.3.refs_0_, f32[1,1024]{1,0:T(1,128)S(1)} %collective-permute-done.14.refs_1_, f32[1,1024]{1,0:T(1,128)S(1)} %collective-permute-done.15.refs_2_, ...), custom_call_target="tpu_custom_call" | custom-call | flops 8589934592 | bytes 33554432 | tf_op jit(solution)/shard_map/partner_scores/pallas_call | solution.py:292
  144.3 6.3 %proto_gradient.1 = (f32[1024,256]{1,0:T(8,128)S(1)}, bf16[4,1040,256]{2,1,0:T(8,128)(2,1)S(1)}) custom-call(s32[1]{0:T(128)} %bitcast.6.index_ref, bf16[1,2,2,2,256,1024]{5,4,3,2,1,0:T(8,128)(2,1)S(1)} %bitcast.37, bf16[1,2,2,2,256,1024]{5,4,3,2,1,0:T(8,128)(2,1)S(1)} %bitcast.38, bf16[1,2,2,2,256,1024]{5,4,3,2,1,0:T(8,128)(2,1)S(1)} %bitcast.39, ...), custom_call_target="tpu_custom_call" | custom-call | flops 1048576 | bytes 1048576 | tf_op jit(solution)/shard_map/proto_gradient/pallas_call | solution.py:469
  150.6 2.2 %collective-permute-done.29.refs_2_ = bf16[1,256,1024]{2,1,0:T(8,128)(2,1)S(1)} collective-permute-done((bf16[1,256,1024]{2,1,0:T(8,128)(2,1)S(1)}, bf16[1,256,1024]{2,1,0:T(8,128)(2,1)S(1)}, u32[]{:S(2)}, u32[]{:S(2)}) %collective-permute-start.29) | collective-permute-done | bytes 524320 | tf_op jit(solution)/shard_map/ppermute | solution.py:526
  156.6 2.0 collective-permute-start.32
  158.8 2.5 %collective-permute-start.37 = (bf16[1,256,1024]{2,1,0:T(8,128)(2,1)}, bf16[1,256,1024]{2,1,0:T(8,128)(2,1)}, u32[]{:S(2)}, u32[]{:S(2)}) collective-permute-start(bf16[1,256,1024]{2,1,0:T(8,128)(2,1)} %add_blocks.5), channel_id=1, source_target_pairs={{0,4},{2,6},{4,0},{6,2},{1,5},{3,7},{5,1},{7,3},{8,12},{10,14},{12... | collective-permute-start | bytes 1572872 | tf_op jit(solution)/shard_map/ppermute | solution.py:526
  161.3 2.2 %copy-done.3 = bf16[2048,1024]{1,0:T(8,128)(2,1)S(1)} copy-done((bf16[2048,1024]{1,0:T(8,128)(2,1)S(1)}, bf16[2048,1024]{1,0:T(8,128)(2,1)}, u32[]{:S(2)}) %copy-start.3) | copy-done | bytes 4194328
  165.7 16.8 %collective-permute-done.36 = bf16[1,256,1024]{2,1,0:T(8,128)(2,1)} collective-permute-done((bf16[1,256,1024]{2,1,0:T(8,128)(2,1)}, bf16[1,256,1024]{2,1,0:T(8,128)(2,1)}, u32[]{:S(2)}, u32[]{:S(2)}) %collective-permute-start.36) | collective-permute-done | bytes 524320 | tf_op jit(solution)/shard_map/ppermute | solution.py:526
  182.5 3.4 %embed_gradient.1 = f32[256,1024]{1,0:T(8,128)} custom-call(s32[1]{0:T(128)} %bitcast.20.index_ref, bf16[2048,1024]{1,0:T(8,128)(2,1)} %embeddings_ref.5, f32[256,1024]{1,0:T(8,128)} %bitcast.54, bf16[256,1024]{1,0:T(8,128)(2,1)} %bitcast.59, bf16[256,1024]{1,0:T(8,128)(2,1)} %bitcast.23.refs_2_, bf16[256,1024]{1,0:T(8,128)(2,1)} %bitcast.24.refs_3_), custom_call_target="tpu_custom_call" | custom-call | flops 2097152 | bytes 4194304 | tf_op jit(solution)/shard_map/embed_gradient/pallas_call | solution.py:506
  186.6 2.5 %collective-permute-start.33 = (f32[1,128]{1,0:T(1,128)S(1)}, f32[1,128]{1,0:T(1,128)S(1)}, u32[]{:S(2)}, u32[]{:S(2)}) collective-permute-start(f32[1,128]{1,0:T(1,128)S(1)} %bitcast_add_fusion), channel_id=1, source_target_pairs={{0,2},{2,0},{4,6},{6,4},{1,3},{3,1},{5,7},{7,5},{8,10},{10,8},{12,... | collective-permute-start | bytes 1544 | tf_op jit(solution)/shard_map/ppermute | solution.py:526
  189.1 2.7 %collective-permute-start.34 = (f32[1,128]{1,0:T(1,128)S(1)}, f32[1,128]{1,0:T(1,128)S(1)}, u32[]{:S(2)}, u32[]{:S(2)}) collective-permute-start(f32[1,128]{1,0:T(1,128)S(1)} %bitcast_add_fusion), channel_id=1, source_target_pairs={{0,4},{2,6},{4,0},{6,2},{1,5},{3,7},{5,1},{7,3},{8,12},{10,14},{12... | collective-permute-start | bytes 1544 | tf_op jit(solution)/shard_map/ppermute | solution.py:526
  191.7 2.5 %convert_add_fusion = f32[1024,256]{1,0:T(8,128)} fusion(f32[1024,256]{1,0:T(8,128)S(1)} %get-tuple-element.40, bf16[1040,256]{1,0:T(8,128)(2,1)} %collective-permute-done.32, bf16[1040,256]{1,0:T(8,128)(2,1)} %collective-permute-done.31, bf16[1040,256]{1,0:T(8,128)(2,1)} %collective-permute-done.30), kind=kLoop, calls=%fused_computation | loop fusion | flops 1572864 | bytes 3670016 | tf_op jit(solution)/shard_map/add | solution.py:619
  194.3 2.8 %collective-permute-done.35 = f32[1,128]{1,0:T(1,128)S(1)} collective-permute-done((f32[1,128]{1,0:T(1,128)S(1)}, f32[1,128]{1,0:T(1,128)S(1)}, u32[]{:S(2)}, u32[]{:S(2)}) %collective-permute-start.35) | collective-permute-done | bytes 544 | tf_op jit(solution)/shard_map/ppermute | solution.py:526
  (115 shorter events, 48.6 us)
Async XLA Ops:
  7.2 96.9 %all-gather.2.cloned.1.call-start = ((), (), s32[]{:S(2)}) async-start(), calls=%async_computation | async-start | bytes 17825792 | tf_op jit(solution)/shard_map/all_gather | solution.py:563
  21.6 4.7 %collective-permute-start = (f32[1,1024]{1,0:T(1,128)S(1)}, f32[1,1024]{1,0:T(1,128)S(1)}, u32[]{:S(2)}, u32[]{:S(2)}) collective-permute-start(f32[1,1024]{1,0:T(1,128)S(1)} %get-tuple-element.23.refs_0_), channel_id=1, source_target_pairs={{0,8},{8,0},{16,24},{24,16},{1,9},{9,1},{17,25},{25,17},{2,10},{10... | collective-permute-start | bytes 12296 | tf_op jit(solution)/shard_map/ppermute | solution.py:526
  24.6 3.6 %collective-permute-start.1 = (f32[1,1024]{1,0:T(1,128)S(1)}, f32[1,1024]{1,0:T(1,128)S(1)}, u32[]{:S(2)}, u32[]{:S(2)}) collective-permute-start(f32[1,1024]{1,0:T(1,128)S(1)} %get-tuple-element.23.refs_0_), channel_id=1, source_target_pairs={{0,16},{8,24},{16,0},{24,8},{1,17},{9,25},{17,1},{25,9},{2,18},{10... | collective-permute-start | bytes 12296 | tf_op jit(solution)/shard_map/ppermute | solution.py:526
  26.1 4.6 %collective-permute-start.2 = (f32[1,1024]{1,0:T(1,128)S(1)}, f32[1,1024]{1,0:T(1,128)S(1)}, u32[]{:S(2)}, u32[]{:S(2)}) collective-permute-start(f32[1,1024]{1,0:T(1,128)S(1)} %get-tuple-element.23.refs_0_), channel_id=1, source_target_pairs={{0,24},{8,16},{16,8},{24,0},{1,25},{9,17},{17,9},{25,1},{2,26},{10... | collective-permute-start | bytes 12296 | tf_op jit(solution)/shard_map/ppermute | solution.py:526
  33.4 4.5 %collective-permute-start.4 = (f32[1,2048]{1,0:T(1,128)S(1)}, f32[1,2048]{1,0:T(1,128)S(1)}, u32[]{:S(2)}, u32[]{:S(2)}) collective-permute-start(f32[1,2048]{1,0:T(1,128)S(1)} %add.68.refs_0_), channel_id=1, source_target_pairs={{0,2},{2,0},{4,6},{6,4},{1,3},{3,1},{5,7},{7,5},{8,10},{10,8},{12,... | collective-permute-start | bytes 24584 | tf_op jit(solution)/shard_map/ppermute | solution.py:526
  35.0 4.7 %collective-permute-start.5 = (f32[1,2048]{1,0:T(1,128)S(1)}, f32[1,2048]{1,0:T(1,128)S(1)}, u32[]{:S(2)}, u32[]{:S(2)}) collective-permute-start(f32[1,2048]{1,0:T(1,128)S(1)} %add.68.refs_0_), channel_id=1, source_target_pairs={{0,4},{2,6},{4,0},{6,2},{1,5},{3,7},{5,1},{7,3},{8,12},{10,14},{12... | collective-permute-start | bytes 24584 | tf_op jit(solution)/shard_map/ppermute | solution.py:526
  37.6 5.6 %collective-permute-start.6 = (f32[1,2048]{1,0:T(1,128)S(1)}, f32[1,2048]{1,0:T(1,128)S(1)}, u32[]{:S(2)}, u32[]{:S(2)}) collective-permute-start(f32[1,2048]{1,0:T(1,128)S(1)} %add.68.refs_0_), channel_id=1, source_target_pairs={{0,6},{2,4},{4,2},{6,0},{1,7},{3,5},{5,3},{7,1},{8,14},{10,12},{12... | collective-permute-start | bytes 24584 | tf_op jit(solution)/shard_map/ppermute | solution.py:526
  44.0 3.7 %collective-permute-start.7 = (f32[1,1024]{1,0:T(1,128)S(1)}, f32[1,1024]{1,0:T(1,128)S(1)}, u32[]{:S(2)}, u32[]{:S(2)}) collective-permute-start(f32[1,1024]{1,0:T(1,128)S(1)} %column_pass.2.refs_0_), channel_id=1, source_target_pairs={{0,8},{8,0},{16,24},{24,16},{1,9},{9,1},{17,25},{25,17},{2,10},{10... | collective-permute-start | bytes 12296 | tf_op jit(solution)/shard_map/ppermute | solution.py:526
  44.5 3.6 %collective-permute-start.8 = (f32[1,1024]{1,0:T(1,128)S(1)}, f32[1,1024]{1,0:T(1,128)S(1)}, u32[]{:S(2)}, u32[]{:S(2)}) collective-permute-start(f32[1,1024]{1,0:T(1,128)S(1)} %column_pass.2.refs_0_), channel_id=1, source_target_pairs={{0,16},{8,24},{16,0},{24,8},{1,17},{9,25},{17,1},{25,9},{2,18},{10... | collective-permute-start | bytes 12296 | tf_op jit(solution)/shard_map/ppermute | solution.py:526
  45.0 4.6 %collective-permute-start.9 = (f32[1,1024]{1,0:T(1,128)S(1)}, f32[1,1024]{1,0:T(1,128)S(1)}, u32[]{:S(2)}, u32[]{:S(2)}) collective-permute-start(f32[1,1024]{1,0:T(1,128)S(1)} %column_pass.2.refs_0_), channel_id=1, source_target_pairs={{0,24},{8,16},{16,8},{24,0},{1,25},{9,17},{17,9},{25,1},{2,26},{10... | collective-permute-start | bytes 12296 | tf_op jit(solution)/shard_map/ppermute | solution.py:526
  52.2 4.5 %collective-permute-start.11 = (f32[1,2048]{1,0:T(1,128)S(1)}, f32[1,2048]{1,0:T(1,128)S(1)}, u32[]{:S(2)}, u32[]{:S(2)}) collective-permute-start(f32[1,2048]{1,0:T(1,128)S(1)} %add.69.refs_0_), channel_id=1, source_target_pairs={{0,2},{2,0},{4,6},{6,4},{1,3},{3,1},{5,7},{7,5},{8,10},{10,8},{12,... | collective-permute-start | bytes 24584 | tf_op jit(solution)/shard_map/ppermute | solution.py:526
  52.3 4.7 %collective-permute-start.12 = (f32[1,2048]{1,0:T(1,128)S(1)}, f32[1,2048]{1,0:T(1,128)S(1)}, u32[]{:S(2)}, u32[]{:S(2)}) collective-permute-start(f32[1,2048]{1,0:T(1,128)S(1)} %add.69.refs_0_), channel_id=1, source_target_pairs={{0,4},{2,6},{4,0},{6,2},{1,5},{3,7},{5,1},{7,3},{8,12},{10,14},{12... | collective-permute-start | bytes 24584 | tf_op jit(solution)/shard_map/ppermute | solution.py:526
  53.0 5.8 %collective-permute-start.13 = (f32[1,2048]{1,0:T(1,128)S(1)}, f32[1,2048]{1,0:T(1,128)S(1)}, u32[]{:S(2)}, u32[]{:S(2)}) collective-permute-start(f32[1,2048]{1,0:T(1,128)S(1)} %add.69.refs_0_), channel_id=1, source_target_pairs={{0,6},{2,4},{4,2},{6,0},{1,7},{3,5},{5,3},{7,1},{8,14},{10,12},{12... | collective-permute-start | bytes 24584 | tf_op jit(solution)/shard_map/ppermute | solution.py:526
  59.6 3.8 %collective-permute-start.14 = (f32[1,1024]{1,0:T(1,128)S(1)}, f32[1,1024]{1,0:T(1,128)S(1)}, u32[]{:S(2)}, u32[]{:S(2)}) collective-permute-start(f32[1,1024]{1,0:T(1,128)S(1)} %column_pass.3.refs_0_), channel_id=1, source_target_pairs={{0,8},{8,0},{16,24},{24,16},{1,9},{9,1},{17,25},{25,17},{2,10},{10... | collective-permute-start | bytes 12296 | tf_op jit(solution)/shard_map/ppermute | solution.py:526
  62.6 4.6 %collective-permute-start.16 = (f32[1,1024]{1,0:T(1,128)S(1)}, f32[1,1024]{1,0:T(1,128)S(1)}, u32[]{:S(2)}, u32[]{:S(2)}) collective-permute-start(f32[1,1024]{1,0:T(1,128)S(1)} %column_pass.3.refs_0_), channel_id=1, source_target_pairs={{0,24},{8,16},{16,8},{24,0},{1,25},{9,17},{17,9},{25,1},{2,26},{10... | collective-permute-start | bytes 12296 | tf_op jit(solution)/shard_map/ppermute | solution.py:526
  72.2 4.5 %collective-permute-start.18 = (f32[2,2048]{1,0:T(2,128)S(1)}, f32[2,2048]{1,0:T(2,128)S(1)}, u32[]{:S(2)}, u32[]{:S(2)}) collective-permute-start(f32[2,2048]{1,0:T(2,128)S(1)} %fusion.1), channel_id=1, source_target_pairs={{0,2},{2,0},{4,6},{6,4},{1,3},{3,1},{5,7},{7,5},{8,10},{10,8},{12,... | collective-permute-start | bytes 49160 | tf_op jit(solution)/shard_map/ppermute | solution.py:526
  72.5 5.8 %collective-permute-start.19 = (f32[2,2048]{1,0:T(2,128)S(1)}, f32[2,2048]{1,0:T(2,128)S(1)}, u32[]{:S(2)}, u32[]{:S(2)}) collective-permute-start(f32[2,2048]{1,0:T(2,128)S(1)} %fusion.1), channel_id=1, source_target_pairs={{0,4},{2,6},{4,0},{6,2},{1,5},{3,7},{5,1},{7,3},{8,12},{10,14},{12... | collective-permute-start | bytes 49160 | tf_op jit(solution)/shard_map/ppermute | solution.py:526
  76.4 5.9 %collective-permute-start.20 = (f32[2,2048]{1,0:T(2,128)S(1)}, f32[2,2048]{1,0:T(2,128)S(1)}, u32[]{:S(2)}, u32[]{:S(2)}) collective-permute-start(f32[2,2048]{1,0:T(2,128)S(1)} %fusion.1), channel_id=1, source_target_pairs={{0,6},{2,4},{4,2},{6,0},{1,7},{3,5},{5,3},{7,1},{8,14},{10,12},{12... | collective-permute-start | bytes 49160 | tf_op jit(solution)/shard_map/ppermute | solution.py:526
  82.4 3.9 %collective-permute-start.21 = (f32[2048]{0:T(1024)S(1)}, f32[2048]{0:T(1024)S(1)}, u32[]{:S(2)}, u32[]{:S(2)}) collective-permute-start(f32[2048]{0:T(1024)S(1)} %bitcast.60), channel_id=1, source_target_pairs={{0,8},{8,0},{16,24},{24,16},{1,9},{9,1},{17,25},{25,17},{2,10},{10... | collective-permute-start | bytes 24584 | tf_op jit(solution)/shard_map/ppermute | solution.py:526
  82.6 3.7 %collective-permute-start.22 = (f32[2048]{0:T(1024)S(1)}, f32[2048]{0:T(1024)S(1)}, u32[]{:S(2)}, u32[]{:S(2)}) collective-permute-start(f32[2048]{0:T(1024)S(1)} %bitcast.61), channel_id=1, source_target_pairs={{0,16},{8,24},{16,0},{24,8},{1,17},{9,25},{17,1},{25,9},{2,18},{10... | collective-permute-start | bytes 24584 | tf_op jit(solution)/shard_map/ppermute | solution.py:526
  83.1 4.7 %collective-permute-start.23 = (f32[2048]{0:T(1024)S(1)}, f32[2048]{0:T(1024)S(1)}, u32[]{:S(2)}, u32[]{:S(2)}) collective-permute-start(f32[2048]{0:T(1024)S(1)} %bitcast.62), channel_id=1, source_target_pairs={{0,24},{8,16},{16,8},{24,0},{1,25},{9,17},{17,9},{25,1},{2,26},{10... | collective-permute-start | bytes 24584 | tf_op jit(solution)/shard_map/ppermute | solution.py:526
  138.4 5.1 %collective-permute-start.27 = (bf16[1,256,1024]{2,1,0:T(8,128)(2,1)S(1)}, bf16[1,256,1024]{2,1,0:T(8,128)(2,1)S(1)}, u32[]{:S(2)}, u32[]{:S(2)}) collective-permute-start(bf16[1,256,1024]{2,1,0:T(8,128)(2,1)S(1)} %gradients.12), channel_id=1, source_target_pairs={{0,1},{1,0},{2,3},{3,2},{4,5},{5,4},{6,7},{7,6},{8,9},{9,8},{10,11... | collective-permute-start | bytes 1572872 | tf_op jit(solution)/shard_map/ppermute | solution.py:526
  138.7 14.1 %collective-permute-start.29 = (bf16[1,256,1024]{2,1,0:T(8,128)(2,1)S(1)}, bf16[1,256,1024]{2,1,0:T(8,128)(2,1)S(1)}, u32[]{:S(2)}, u32[]{:S(2)}) collective-permute-start(bf16[1,256,1024]{2,1,0:T(8,128)(2,1)S(1)} %add_blocks.3), channel_id=1, source_target_pairs={{0,2},{2,0},{4,6},{6,4},{1,3},{3,1},{5,7},{7,5},{8,10},{10,8},{12,... | collective-permute-start | bytes 1572872 | tf_op jit(solution)/shard_map/ppermute | solution.py:526
  140.2 12.6 %collective-permute-start.28 = (bf16[1,256,1024]{2,1,0:T(8,128)(2,1)S(1)}, bf16[1,256,1024]{2,1,0:T(8,128)(2,1)S(1)}, u32[]{:S(2)}, u32[]{:S(2)}) collective-permute-start(bf16[1,256,1024]{2,1,0:T(8,128)(2,1)S(1)} %gradients.14), channel_id=1, source_target_pairs={{0,1},{1,0},{2,3},{3,2},{4,5},{5,4},{6,7},{7,6},{8,9},{9,8},{10,11... | collective-permute-start | bytes 1572872 | tf_op jit(solution)/shard_map/ppermute | solution.py:526
  155.0 30.8 %collective-permute-start.30 = (bf16[1040,256]{1,0:T(8,128)(2,1)}, bf16[1040,256]{1,0:T(8,128)(2,1)}, u32[]{:S(2)}, u32[]{:S(2)}) collective-permute-start(bf16[1040,256]{1,0:T(8,128)(2,1)} %get-tuple-element.43), channel_id=1, source_target_pairs={{0,24},{8,16},{16,8},{24,0},{1,25},{9,17},{17,9},{25,1},{2,26},{10... | collective-permute-start | bytes 1597448 | tf_op jit(solution)/shard_map/ppermute | solution.py:526
  155.2 30.6 %collective-permute-start.31 = (bf16[1040,256]{1,0:T(8,128)(2,1)}, bf16[1040,256]{1,0:T(8,128)(2,1)}, u32[]{:S(2)}, u32[]{:S(2)}) collective-permute-start(bf16[1040,256]{1,0:T(8,128)(2,1)} %get-tuple-element.45), channel_id=1, source_target_pairs={{0,16},{8,24},{16,0},{24,8},{1,17},{9,25},{17,1},{25,9},{2,18},{10... | collective-permute-start | bytes 1597448 | tf_op jit(solution)/shard_map/ppermute | solution.py:526
  156.6 29.3 %collective-permute-start.32 = (bf16[1040,256]{1,0:T(8,128)(2,1)}, bf16[1040,256]{1,0:T(8,128)(2,1)}, u32[]{:S(2)}, u32[]{:S(2)}) collective-permute-start(bf16[1040,256]{1,0:T(8,128)(2,1)} %get-tuple-element.44), channel_id=1, source_target_pairs={{0,8},{8,0},{16,24},{24,16},{1,9},{9,1},{17,25},{25,17},{2,10},{10... | collective-permute-start | bytes 1597448 | tf_op jit(solution)/shard_map/ppermute | solution.py:526
  158.5 24.0 %collective-permute-start.36 = (bf16[1,256,1024]{2,1,0:T(8,128)(2,1)}, bf16[1,256,1024]{2,1,0:T(8,128)(2,1)}, u32[]{:S(2)}, u32[]{:S(2)}) collective-permute-start(bf16[1,256,1024]{2,1,0:T(8,128)(2,1)} %add_blocks.4), channel_id=1, source_target_pairs={{0,2},{2,0},{4,6},{6,4},{1,3},{3,1},{5,7},{7,5},{8,10},{10,8},{12,... | collective-permute-start | bytes 1572872 | tf_op jit(solution)/shard_map/ppermute | solution.py:526
  158.8 23.7 %collective-permute-start.37 = (bf16[1,256,1024]{2,1,0:T(8,128)(2,1)}, bf16[1,256,1024]{2,1,0:T(8,128)(2,1)}, u32[]{:S(2)}, u32[]{:S(2)}) collective-permute-start(bf16[1,256,1024]{2,1,0:T(8,128)(2,1)} %add_blocks.5), channel_id=1, source_target_pairs={{0,4},{2,6},{4,0},{6,2},{1,5},{3,7},{5,1},{7,3},{8,12},{10,14},{12... | collective-permute-start | bytes 1572872 | tf_op jit(solution)/shard_map/ppermute | solution.py:526
  186.6 7.7 %collective-permute-start.33 = (f32[1,128]{1,0:T(1,128)S(1)}, f32[1,128]{1,0:T(1,128)S(1)}, u32[]{:S(2)}, u32[]{:S(2)}) collective-permute-start(f32[1,128]{1,0:T(1,128)S(1)} %bitcast_add_fusion), channel_id=1, source_target_pairs={{0,2},{2,0},{4,6},{6,4},{1,3},{3,1},{5,7},{7,5},{8,10},{10,8},{12,... | collective-permute-start | bytes 1544 | tf_op jit(solution)/shard_map/ppermute | solution.py:526
  189.1 5.2 %collective-permute-start.34 = (f32[1,128]{1,0:T(1,128)S(1)}, f32[1,128]{1,0:T(1,128)S(1)}, u32[]{:S(2)}, u32[]{:S(2)}) collective-permute-start(f32[1,128]{1,0:T(1,128)S(1)} %bitcast_add_fusion), channel_id=1, source_target_pairs={{0,4},{2,6},{4,0},{6,2},{1,5},{3,7},{5,1},{7,3},{8,12},{10,14},{12... | collective-permute-start | bytes 1544 | tf_op jit(solution)/shard_map/ppermute | solution.py:526
  191.7 5.3 %collective-permute-start.35 = (f32[1,128]{1,0:T(1,128)S(1)}, f32[1,128]{1,0:T(1,128)S(1)}, u32[]{:S(2)}, u32[]{:S(2)}) collective-permute-start(f32[1,128]{1,0:T(1,128)S(1)} %bitcast_add_fusion), channel_id=1, source_target_pairs={{0,6},{2,4},{4,2},{6,0},{1,7},{3,5},{5,3},{7,1},{8,14},{10,12},{12... | collective-permute-start | bytes 1544 | tf_op jit(solution)/shard_map/ppermute | solution.py:526
  (19 other events, 111.0 us)
Sparse Core Ops, SparseCore 0:
  10.2 93.8 all-gather.1

commit v12 on v11

--- a/solution.py
+++ b/solution.py
@@ -602,11 +602,9 @@
     values = part_of(0, [near], [near])
 
     grad_proto, proto_sent = proto_gradient(dscore, unit, loss, after(scalar(batch_index), values[1]), batch_size)
-    from_forwarder = after(from_forwarder, proto_sent)
-    from_near = after(from_near, proto_sent)
+    from_forwarder = after(from_forwarder, proto_sent, from_near)
     across = add_blocks(across + [from_forwarder], BF16)
     values += [from_near, swap(across, PLACE, 2)]
-    proto_sent = after(proto_sent, across)
 
     bit = 2
     while (1 << bit) < places:

time: 205 us -> 212 us (1.034)
  waiting for transfers between devices: 58.8 us -> 67.5 us
    ppermute x38, waiting for transfers between devices: 52.7 us -> 61.3 us  [swap(): return lax.ppermute(value, axis, [(i, i ^ distance) for i in range(size)])]
    unnamed x24 -> x26, local copies, waits for them, and re-layouts: 10.1 us -> 10.1 us
  transfers between devices with their start and end apart: 39 -> 39, of which waited for: 27 -> 28; matrix products, arithmetic and copies ran while one was open for 2% -> 2% of each run, Pallas kernels for 19% -> 19%
where the time goes in v12:
time: 212 us
  Pallas kernels  72.7 us (34%)
  waiting for transfers between devices  67.5 us (32%)
  starting transfers between devices  41 us (19%)
  between operations  15.6 us (7%)
  local copies, waits for them, and re-layouts  11.4 us (5%)
  other arithmetic  3.73 us (2%)
    ppermute x38, waiting for transfers between devices, swap(): return lax.ppermute(value, axis, [(i, i ^ distance) for i in range(size)])  61.3 us
    ppermute x38, starting transfers between devices, swap(): return lax.ppermute(value, axis, [(i, i ^ distance) for i in range(size)])  41 us
    pallas_call x1, Pallas kernels, partner_pass(): pl.pallas_call(functools.partial(partner_kernel, count, total, heat_scale...  25.6 us
    unnamed x26, local copies, waits for them, and re-layouts  10.1 us
    pallas_call x1, Pallas kernels, lookup(): pl.pallas_call(lookup_kernel, grid_spec=pltpu.PrefetchScalarGridSpec(num_...  10.1 us
    pallas_call x8, Pallas kernels, gradients(): pl.pallas_call(gradient_kernel, grid_spec=pltpu.PrefetchScalarGridSpec(nu...  9.95 us
    pallas_call x1, Pallas kernels, scores_of(): pl.pallas_call(scores_kernel, grid=(rows // share // 2,), in_specs=[pl.Bl...  7.93 us
    pallas_call x1, Pallas kernels, proto_gradient(): pl.pallas_call(proto_gradient_kernel, grid_spec=pltpu.PrefetchScalarGridS...  6.28 us
  transfers between devices with their start and end apart: 39, of which 28 were waited for; matrix products, arithmetic and copies ran while one was open for 2% of the time, Pallas kernels for 19%

profile of v12, /device:TPU:0, one launch (start us, length us, event | category | flops | bytes accessed | tf_op | source)
XLA Modules:
  0.0 212.0 jit_solution(7574997138072164073)
XLA Ops:
  7.2 2.6 %own_rows.1 = bf16[512,8,128]{2,1,0:T(8,128)(2,1)} custom-call(s32[1]{0:T(128)} %bitcast.5.index_ref, bf16[2048,1024]{1,0:T(8,128)(2,1)} %embeddings_ref.5), custom_call_target="tpu_custom_call" | custom-call | tf_op jit(solution)/shard_map/own_rows/pallas_call | solution.py:78
  9.9 2.2 %copy-done.6 = bf16[2048,1024]{1,0:T(8,128)(2,1)S(1)} copy-done((bf16[2048,1024]{1,0:T(8,128)(2,1)S(1)}, bf16[2048,1024]{1,0:T(8,128)(2,1)}, u32[]{:S(2)}) %copy-start.6) | copy-done | bytes 4194328
  12.1 1.6 copy-done.8
  13.6 7.9 %scores.1 = (bf16[2048,1024]{1,0:T(8,128)(2,1)S(1)}, bf16[1024,1024]{1,0:T(8,128)(2,1)S(1)}, f32[2048,1024]{1,0:T(8,128)S(1)}, bf16[2048,1024]{1,0:T(8,128)(2,1)...) custom-call(bf16[2048,1024]{1,0:T(8,128)(2,1)S(1)} %copy-done.6, bf16[1024,1024]{1,0:T(8,128)(2,1)S(1)} %copy-done.8), custom_call_target="tpu_custom_call" | custom-call | flops 4294967296 | bytes 23068672 | tf_op jit(solution)/shard_map/scores/pallas_call | solution.py:127
  21.6 3.0 %collective-permute-start = (f32[1,1024]{1,0:T(1,128)S(1)}, f32[1,1024]{1,0:T(1,128)S(1)}, u32[]{:S(2)}, u32[]{:S(2)}) collective-permute-start(f32[1,1024]{1,0:T(1,128)S(1)} %get-tuple-element.21.refs_0_), channel_id=1, source_target_pairs={{0,8},{8,0},{16,24},{24,16},{1,9},{9,1},{17,25},{25,17},{2,10},{10... | collective-permute-start | bytes 12296 | tf_op jit(solution)/shard_map/ppermute | solution.py:526
  26.3 2.0 collective-permute-done.1.refs_2_
  28.2 2.5 %collective-permute-done.2.refs_3_ = f32[1,1024]{1,0:T(1,128)S(1)} collective-permute-done((f32[1,1024]{1,0:T(1,128)S(1)}, f32[1,1024]{1,0:T(1,128)S(1)}, u32[]{:S(2)}, u32[]{:S(2)}) %collective-permute-start.2) | collective-permute-done | bytes 4128 | tf_op jit(solution)/shard_map/ppermute | solution.py:526
  33.4 1.6 collective-permute-start.4
  35.0 2.6 %collective-permute-start.5 = (f32[1,2048]{1,0:T(1,128)S(1)}, f32[1,2048]{1,0:T(1,128)S(1)}, u32[]{:S(2)}, u32[]{:S(2)}) collective-permute-start(f32[1,2048]{1,0:T(1,128)S(1)} %add.68.refs_0_), channel_id=1, source_target_pairs={{0,4},{2,6},{4,0},{6,2},{1,5},{3,7},{5,1},{7,3},{8,12},{10,14},{12... | collective-permute-start | bytes 24584 | tf_op jit(solution)/shard_map/ppermute | solution.py:526
  37.8 1.8 collective-permute-done.5.refs_2_
  39.7 3.5 %collective-permute-done.6.refs_3_ = f32[1,2048]{1,0:T(1,128)S(1)} collective-permute-done((f32[1,2048]{1,0:T(1,128)S(1)}, f32[1,2048]{1,0:T(1,128)S(1)}, u32[]{:S(2)}, u32[]{:S(2)}) %collective-permute-start.6) | collective-permute-done | bytes 8224 | tf_op jit(solution)/shard_map/ppermute | solution.py:526
  45.0 2.5 %collective-permute-start.9 = (f32[1,1024]{1,0:T(1,128)S(1)}, f32[1,1024]{1,0:T(1,128)S(1)}, u32[]{:S(2)}, u32[]{:S(2)}) collective-permute-start(f32[1,1024]{1,0:T(1,128)S(1)} %column_pass.2.refs_0_), channel_id=1, source_target_pairs={{0,24},{8,16},{16,8},{24,0},{1,25},{9,17},{17,9},{25,1},{2,26},{10... | collective-permute-start | bytes 12296 | tf_op jit(solution)/shard_map/ppermute | solution.py:526
  53.0 3.7 %collective-permute-start.13 = (f32[1,2048]{1,0:T(1,128)S(1)}, f32[1,2048]{1,0:T(1,128)S(1)}, u32[]{:S(2)}, u32[]{:S(2)}) collective-permute-start(f32[1,2048]{1,0:T(1,128)S(1)} %add.69.refs_0_), channel_id=1, source_target_pairs={{0,6},{2,4},{4,2},{6,0},{1,7},{3,5},{5,3},{7,1},{8,14},{10,12},{12... | collective-permute-start | bytes 24584 | tf_op jit(solution)/shard_map/ppermute | solution.py:526
  57.0 1.7 collective-permute-done.13.refs_3_
  64.7 2.5 %collective-permute-done.16.refs_3_ = f32[1,1024]{1,0:T(1,128)S(1)} collective-permute-done((f32[1,1024]{1,0:T(1,128)S(1)}, f32[1,1024]{1,0:T(1,128)S(1)}, u32[]{:S(2)}, u32[]{:S(2)}) %collective-permute-start.16) | collective-permute-done | bytes 4128 | tf_op jit(solution)/shard_map/ppermute | solution.py:526
  67.2 2.3 %copy-done.1 = bf16[2048,1024]{1,0:T(8,128)(2,1)S(1)} copy-done((bf16[2048,1024]{1,0:T(8,128)(2,1)S(1)}, bf16[2048,1024]{1,0:T(8,128)(2,1)}, u32[]{:S(2)}) %copy-start.1) | copy-done | bytes 4194328
  72.5 4.0 %collective-permute-start.19 = (f32[2,2048]{1,0:T(2,128)S(1)}, f32[2,2048]{1,0:T(2,128)S(1)}, u32[]{:S(2)}, u32[]{:S(2)}) collective-permute-start(f32[2,2048]{1,0:T(2,128)S(1)} %fusion.1), channel_id=1, source_target_pairs={{0,4},{2,6},{4,0},{6,2},{1,5},{3,7},{5,1},{7,3},{8,12},{10,14},{12... | collective-permute-start | bytes 49160 | tf_op jit(solution)/shard_map/ppermute | solution.py:526
  76.7 1.6 collective-permute-done.19
  78.3 4.0 %collective-permute-done.20 = f32[2,2048]{1,0:T(2,128)S(1)} collective-permute-done((f32[2,2048]{1,0:T(2,128)S(1)}, f32[2,2048]{1,0:T(2,128)S(1)}, u32[]{:S(2)}, u32[]{:S(2)}) %collective-permute-start.20) | collective-permute-done | bytes 16416 | tf_op jit(solution)/shard_map/ppermute | solution.py:526
  83.1 2.8 %collective-permute-start.23 = (f32[2048]{0:T(1024)S(1)}, f32[2048]{0:T(1024)S(1)}, u32[]{:S(2)}, u32[]{:S(2)}) collective-permute-start(f32[2048]{0:T(1024)S(1)} %bitcast.63), channel_id=1, source_target_pairs={{0,24},{8,16},{16,8},{24,0},{1,25},{9,17},{17,9},{25,1},{2,26},{10... | collective-permute-start | bytes 24584 | tf_op jit(solution)/shard_map/ppermute | solution.py:526
  87.8 10.1 %lookup.1 = f32[4096]{0:T(1024)S(1)} custom-call(s32[2048]{0:T(1024)S(1)} %bitcast.56, s32[2048]{0:T(1024)S(1)} %bitcast.55, f32[8192]{0:T(1024)S(1)} %pad_maximum_fusion.totals_ref), custom_call_target="tpu_custom_call" | custom-call | flops 1048576 | bytes 1048576 | tf_op jit(solution)/shard_map/lookup/pallas_call | solution.py:333
  97.9 6.1 %all-gather.2.cloned.1.call-done.refs_5_ = bf16[8192,8,128]{2,1,0:T(8,128)(2,1)} async-done(((bf16[512,8,128]{2,1,0:T(8,128)(2,1)}), bf16[8192,8,128]{2,1,0:T(8,128)(2,1)}) %all-gather.2.cloned.1.call-update) | async-done | bytes 16777232 | tf_op jit(solution)/shard_map/all_gather | solution.py:563
  104.1 25.6 %partner_scores.1 = (bf16[2048,1024]{1,0:T(8,128)(2,1)S(1)}, f32[1,128]{1,0:T(1,128)S(1)}) custom-call(s32[2048]{0:T(1024)S(1)} %bitcast.58, s32[2048]{0:T(1024)S(1)} %bitcast.57, f32[1,1024]{1,0:T(1,128)S(1)} %column_pass.3.refs_0_, f32[1,1024]{1,0:T(1,128)S(1)} %collective-permute-done.14.refs_1_, f32[1,1024]{1,0:T(1,128)S(1)} %collective-permute-done.15.refs_2_, ...), custom_call_target="tpu_custom_call" | custom-call | flops 8589934592 | bytes 33554432 | tf_op jit(solution)/shard_map/partner_scores/pallas_call | solution.py:292
  139.8 1.8 collective-permute-start.34
  143.8 6.3 %proto_gradient.1 = (f32[1024,256]{1,0:T(8,128)S(1)}, bf16[4,1040,256]{2,1,0:T(8,128)(2,1)S(1)}) custom-call(s32[1]{0:T(128)} %bitcast.6.index_ref, bf16[1,2,2,2,256,1024]{5,4,3,2,1,0:T(8,128)(2,1)S(1)} %bitcast.36, bf16[1,2,2,2,256,1024]{5,4,3,2,1,0:T(8,128)(2,1)S(1)} %bitcast.37, bf16[1,2,2,2,256,1024]{5,4,3,2,1,0:T(8,128)(2,1)S(1)} %bitcast.38, ...), custom_call_target="tpu_custom_call" | custom-call | flops 1048576 | bytes 1048576 | tf_op jit(solution)/shard_map/proto_gradient/pallas_call | solution.py:469
  156.1 8.8 %collective-permute-done.34 = bf16[1,256,1024]{2,1,0:T(8,128)(2,1)S(1)} collective-permute-done((bf16[1,256,1024]{2,1,0:T(8,128)(2,1)S(1)}, bf16[1,256,1024]{2,1,0:T(8,128)(2,1)S(1)}, u32[]{:S(2)}, u32[]{:S(2)}) %collective-permute-start.34) | collective-permute-done | bytes 524320 | tf_op jit(solution)/shard_map/ppermute | solution.py:526
  165.9 2.4 %collective-permute-start.37 = (bf16[1,256,1024]{2,1,0:T(8,128)(2,1)}, bf16[1,256,1024]{2,1,0:T(8,128)(2,1)}, u32[]{:S(2)}, u32[]{:S(2)}) collective-permute-start(bf16[1,256,1024]{2,1,0:T(8,128)(2,1)} %add_blocks.5), channel_id=1, source_target_pairs={{0,4},{2,6},{4,0},{6,2},{1,5},{3,7},{5,1},{7,3},{8,12},{10,14},{12... | collective-permute-start | bytes 1572872 | tf_op jit(solution)/shard_map/ppermute | solution.py:526
  168.3 2.2 %copy-done.3 = bf16[2048,1024]{1,0:T(8,128)(2,1)S(1)} copy-done((bf16[2048,1024]{1,0:T(8,128)(2,1)S(1)}, bf16[2048,1024]{1,0:T(8,128)(2,1)}, u32[]{:S(2)}) %copy-start.3) | copy-done | bytes 4194328
  172.7 18.8 %collective-permute-done.37 = bf16[1,256,1024]{2,1,0:T(8,128)(2,1)} collective-permute-done((bf16[1,256,1024]{2,1,0:T(8,128)(2,1)}, bf16[1,256,1024]{2,1,0:T(8,128)(2,1)}, u32[]{:S(2)}, u32[]{:S(2)}) %collective-permute-start.37) | collective-permute-done | bytes 524320 | tf_op jit(solution)/shard_map/ppermute | solution.py:526
  191.5 3.4 %embed_gradient.1 = f32[256,1024]{1,0:T(8,128)} custom-call(s32[1]{0:T(128)} %bitcast.20.index_ref, bf16[2048,1024]{1,0:T(8,128)(2,1)} %embeddings_ref.5, f32[256,1024]{1,0:T(8,128)} %bitcast.54, bf16[256,1024]{1,0:T(8,128)(2,1)} %bitcast.59, bf16[256,1024]{1,0:T(8,128)(2,1)} %bitcast.60, bf16[256,1024]{1,0:T(8,128)(2,1)} %bitcast.24.refs_3_), custom_call_target="tpu_custom_call" | custom-call | flops 2097152 | bytes 4194304 | tf_op jit(solution)/shard_map/embed_gradient/pallas_call | solution.py:506
  195.6 3.0 %collective-permute-start.32 = (f32[1,128]{1,0:T(1,128)S(1)}, f32[1,128]{1,0:T(1,128)S(1)}, u32[]{:S(2)}, u32[]{:S(2)}) collective-permute-start(f32[1,128]{1,0:T(1,128)S(1)} %bitcast_add_fusion), channel_id=1, source_target_pairs={{0,4},{2,6},{4,0},{6,2},{1,5},{3,7},{5,1},{7,3},{8,12},{10,14},{12... | collective-permute-start | bytes 1544 | tf_op jit(solution)/shard_map/ppermute | solution.py:526
  200.0 2.5 %convert_add_fusion = f32[1024,256]{1,0:T(8,128)} fusion(f32[1024,256]{1,0:T(8,128)S(1)} %get-tuple-element.34, bf16[1040,256]{1,0:T(8,128)(2,1)} %collective-permute-done.30, bf16[1040,256]{1,0:T(8,128)(2,1)} %collective-permute-done.29, bf16[1040,256]{1,0:T(8,128)(2,1)} %collective-permute-done.28), kind=kLoop, calls=%fused_computation | loop fusion | flops 1572864 | bytes 3670016 | tf_op jit(solution)/shard_map/add | solution.py:617
  (117 shorter events, 49.1 us)
Async XLA Ops:
  7.2 96.9 %all-gather.2.cloned.1.call-start = ((), (), s32[]{:S(2)}) async-start(), calls=%async_computation | async-start | bytes 17825792 | tf_op jit(solution)/shard_map/all_gather | solution.py:563
  21.6 4.7 %collective-permute-start = (f32[1,1024]{1,0:T(1,128)S(1)}, f32[1,1024]{1,0:T(1,128)S(1)}, u32[]{:S(2)}, u32[]{:S(2)}) collective-permute-start(f32[1,1024]{1,0:T(1,128)S(1)} %get-tuple-element.21.refs_0_), channel_id=1, source_target_pairs={{0,8},{8,0},{16,24},{24,16},{1,9},{9,1},{17,25},{25,17},{2,10},{10... | collective-permute-start | bytes 12296 | tf_op jit(solution)/shard_map/ppermute | solution.py:526
  24.6 3.6 %collective-permute-start.1 = (f32[1,1024]{1,0:T(1,128)S(1)}, f32[1,1024]{1,0:T(1,128)S(1)}, u32[]{:S(2)}, u32[]{:S(2)}) collective-permute-start(f32[1,1024]{1,0:T(1,128)S(1)} %get-tuple-element.21.refs_0_), channel_id=1, source_target_pairs={{0,16},{8,24},{16,0},{24,8},{1,17},{9,25},{17,1},{25,9},{2,18},{10... | collective-permute-start | bytes 12296 | tf_op jit(solution)/shard_map/ppermute | solution.py:526
  26.1 4.6 %collective-permute-start.2 = (f32[1,1024]{1,0:T(1,128)S(1)}, f32[1,1024]{1,0:T(1,128)S(1)}, u32[]{:S(2)}, u32[]{:S(2)}) collective-permute-start(f32[1,1024]{1,0:T(1,128)S(1)} %get-tuple-element.21.refs_0_), channel_id=1, source_target_pairs={{0,24},{8,16},{16,8},{24,0},{1,25},{9,17},{17,9},{25,1},{2,26},{10... | collective-permute-start | bytes 12296 | tf_op jit(solution)/shard_map/ppermute | solution.py:526
  33.4 4.5 %collective-permute-start.4 = (f32[1,2048]{1,0:T(1,128)S(1)}, f32[1,2048]{1,0:T(1,128)S(1)}, u32[]{:S(2)}, u32[]{:S(2)}) collective-permute-start(f32[1,2048]{1,0:T(1,128)S(1)} %add.68.refs_0_), channel_id=1, source_target_pairs={{0,2},{2,0},{4,6},{6,4},{1,3},{3,1},{5,7},{7,5},{8,10},{10,8},{12,... | collective-permute-start | bytes 24584 | tf_op jit(solution)/shard_map/ppermute | solution.py:526
  35.0 4.7 %collective-permute-start.5 = (f32[1,2048]{1,0:T(1,128)S(1)}, f32[1,2048]{1,0:T(1,128)S(1)}, u32[]{:S(2)}, u32[]{:S(2)}) collective-permute-start(f32[1,2048]{1,0:T(1,128)S(1)} %add.68.refs_0_), channel_id=1, source_target_pairs={{0,4},{2,6},{4,0},{6,2},{1,5},{3,7},{5,1},{7,3},{8,12},{10,14},{12... | collective-permute-start | bytes 24584 | tf_op jit(solution)/shard_map/ppermute | solution.py:526
  37.6 5.6 %collective-permute-start.6 = (f32[1,2048]{1,0:T(1,128)S(1)}, f32[1,2048]{1,0:T(1,128)S(1)}, u32[]{:S(2)}, u32[]{:S(2)}) collective-permute-start(f32[1,2048]{1,0:T(1,128)S(1)} %add.68.refs_0_), channel_id=1, source_target_pairs={{0,6},{2,4},{4,2},{6,0},{1,7},{3,5},{5,3},{7,1},{8,14},{10,12},{12... | collective-permute-start | bytes 24584 | tf_op jit(solution)/shard_map/ppermute | solution.py:526
  44.0 3.7 %collective-permute-start.7 = (f32[1,1024]{1,0:T(1,128)S(1)}, f32[1,1024]{1,0:T(1,128)S(1)}, u32[]{:S(2)}, u32[]{:S(2)}) collective-permute-start(f32[1,1024]{1,0:T(1,128)S(1)} %column_pass.2.refs_0_), channel_id=1, source_target_pairs={{0,8},{8,0},{16,24},{24,16},{1,9},{9,1},{17,25},{25,17},{2,10},{10... | collective-permute-start | bytes 12296 | tf_op jit(solution)/shard_map/ppermute | solution.py:526
  44.5 3.6 %collective-permute-start.8 = (f32[1,1024]{1,0:T(1,128)S(1)}, f32[1,1024]{1,0:T(1,128)S(1)}, u32[]{:S(2)}, u32[]{:S(2)}) collective-permute-start(f32[1,1024]{1,0:T(1,128)S(1)} %column_pass.2.refs_0_), channel_id=1, source_target_pairs={{0,16},{8,24},{16,0},{24,8},{1,17},{9,25},{17,1},{25,9},{2,18},{10... | collective-permute-start | bytes 12296 | tf_op jit(solution)/shard_map/ppermute | solution.py:526
  45.0 4.6 %collective-permute-start.9 = (f32[1,1024]{1,0:T(1,128)S(1)}, f32[1,1024]{1,0:T(1,128)S(1)}, u32[]{:S(2)}, u32[]{:S(2)}) collective-permute-start(f32[1,1024]{1,0:T(1,128)S(1)} %column_pass.2.refs_0_), channel_id=1, source_target_pairs={{0,24},{8,16},{16,8},{24,0},{1,25},{9,17},{17,9},{25,1},{2,26},{10... | collective-permute-start | bytes 12296 | tf_op jit(solution)/shard_map/ppermute | solution.py:526
  52.2 4.5 %collective-permute-start.11 = (f32[1,2048]{1,0:T(1,128)S(1)}, f32[1,2048]{1,0:T(1,128)S(1)}, u32[]{:S(2)}, u32[]{:S(2)}) collective-permute-start(f32[1,2048]{1,0:T(1,128)S(1)} %add.69.refs_0_), channel_id=1, source_target_pairs={{0,2},{2,0},{4,6},{6,4},{1,3},{3,1},{5,7},{7,5},{8,10},{10,8},{12,... | collective-permute-start | bytes 24584 | tf_op jit(solution)/shard_map/ppermute | solution.py:526
  52.3 4.7 %collective-permute-start.12 = (f32[1,2048]{1,0:T(1,128)S(1)}, f32[1,2048]{1,0:T(1,128)S(1)}, u32[]{:S(2)}, u32[]{:S(2)}) collective-permute-start(f32[1,2048]{1,0:T(1,128)S(1)} %add.69.refs_0_), channel_id=1, source_target_pairs={{0,4},{2,6},{4,0},{6,2},{1,5},{3,7},{5,1},{7,3},{8,12},{10,14},{12... | collective-permute-start | bytes 24584 | tf_op jit(solution)/shard_map/ppermute | solution.py:526
  53.0 5.8 %collective-permute-start.13 = (f32[1,2048]{1,0:T(1,128)S(1)}, f32[1,2048]{1,0:T(1,128)S(1)}, u32[]{:S(2)}, u32[]{:S(2)}) collective-permute-start(f32[1,2048]{1,0:T(1,128)S(1)} %add.69.refs_0_), channel_id=1, source_target_pairs={{0,6},{2,4},{4,2},{6,0},{1,7},{3,5},{5,3},{7,1},{8,14},{10,12},{12... | collective-permute-start | bytes 24584 | tf_op jit(solution)/shard_map/ppermute | solution.py:526
  59.6 3.8 %collective-permute-start.14 = (f32[1,1024]{1,0:T(1,128)S(1)}, f32[1,1024]{1,0:T(1,128)S(1)}, u32[]{:S(2)}, u32[]{:S(2)}) collective-permute-start(f32[1,1024]{1,0:T(1,128)S(1)} %column_pass.3.refs_0_), channel_id=1, source_target_pairs={{0,8},{8,0},{16,24},{24,16},{1,9},{9,1},{17,25},{25,17},{2,10},{10... | collective-permute-start | bytes 12296 | tf_op jit(solution)/shard_map/ppermute | solution.py:526
  62.6 4.6 %collective-permute-start.16 = (f32[1,1024]{1,0:T(1,128)S(1)}, f32[1,1024]{1,0:T(1,128)S(1)}, u32[]{:S(2)}, u32[]{:S(2)}) collective-permute-start(f32[1,1024]{1,0:T(1,128)S(1)} %column_pass.3.refs_0_), channel_id=1, source_target_pairs={{0,24},{8,16},{16,8},{24,0},{1,25},{9,17},{17,9},{25,1},{2,26},{10... | collective-permute-start | bytes 12296 | tf_op jit(solution)/shard_map/ppermute | solution.py:526
  72.2 4.5 %collective-permute-start.18 = (f32[2,2048]{1,0:T(2,128)S(1)}, f32[2,2048]{1,0:T(2,128)S(1)}, u32[]{:S(2)}, u32[]{:S(2)}) collective-permute-start(f32[2,2048]{1,0:T(2,128)S(1)} %fusion.1), channel_id=1, source_target_pairs={{0,2},{2,0},{4,6},{6,4},{1,3},{3,1},{5,7},{7,5},{8,10},{10,8},{12,... | collective-permute-start | bytes 49160 | tf_op jit(solution)/shard_map/ppermute | solution.py:526
  72.5 5.8 %collective-permute-start.19 = (f32[2,2048]{1,0:T(2,128)S(1)}, f32[2,2048]{1,0:T(2,128)S(1)}, u32[]{:S(2)}, u32[]{:S(2)}) collective-permute-start(f32[2,2048]{1,0:T(2,128)S(1)} %fusion.1), channel_id=1, source_target_pairs={{0,4},{2,6},{4,0},{6,2},{1,5},{3,7},{5,1},{7,3},{8,12},{10,14},{12... | collective-permute-start | bytes 49160 | tf_op jit(solution)/shard_map/ppermute | solution.py:526
  76.4 5.9 %collective-permute-start.20 = (f32[2,2048]{1,0:T(2,128)S(1)}, f32[2,2048]{1,0:T(2,128)S(1)}, u32[]{:S(2)}, u32[]{:S(2)}) collective-permute-start(f32[2,2048]{1,0:T(2,128)S(1)} %fusion.1), channel_id=1, source_target_pairs={{0,6},{2,4},{4,2},{6,0},{1,7},{3,5},{5,3},{7,1},{8,14},{10,12},{12... | collective-permute-start | bytes 49160 | tf_op jit(solution)/shard_map/ppermute | solution.py:526
  82.4 3.9 %collective-permute-start.21 = (f32[2048]{0:T(1024)S(1)}, f32[2048]{0:T(1024)S(1)}, u32[]{:S(2)}, u32[]{:S(2)}) collective-permute-start(f32[2048]{0:T(1024)S(1)} %bitcast.61), channel_id=1, source_target_pairs={{0,8},{8,0},{16,24},{24,16},{1,9},{9,1},{17,25},{25,17},{2,10},{10... | collective-permute-start | bytes 24584 | tf_op jit(solution)/shard_map/ppermute | solution.py:526
  82.6 3.7 %collective-permute-start.22 = (f32[2048]{0:T(1024)S(1)}, f32[2048]{0:T(1024)S(1)}, u32[]{:S(2)}, u32[]{:S(2)}) collective-permute-start(f32[2048]{0:T(1024)S(1)} %bitcast.62), channel_id=1, source_target_pairs={{0,16},{8,24},{16,0},{24,8},{1,17},{9,25},{17,1},{25,9},{2,18},{10... | collective-permute-start | bytes 24584 | tf_op jit(solution)/shard_map/ppermute | solution.py:526
  83.1 4.7 %collective-permute-start.23 = (f32[2048]{0:T(1024)S(1)}, f32[2048]{0:T(1024)S(1)}, u32[]{:S(2)}, u32[]{:S(2)}) collective-permute-start(f32[2048]{0:T(1024)S(1)} %bitcast.63), channel_id=1, source_target_pairs={{0,24},{8,16},{16,8},{24,0},{1,25},{9,17},{17,9},{25,1},{2,26},{10... | collective-permute-start | bytes 24584 | tf_op jit(solution)/shard_map/ppermute | solution.py:526
  137.6 5.3 %collective-permute-start.27 = (bf16[1,256,1024]{2,1,0:T(8,128)(2,1)S(1)}, bf16[1,256,1024]{2,1,0:T(8,128)(2,1)S(1)}, u32[]{:S(2)}, u32[]{:S(2)}) collective-permute-start(bf16[1,256,1024]{2,1,0:T(8,128)(2,1)S(1)} %gradients.12), channel_id=1, source_target_pairs={{0,1},{1,0},{2,3},{3,2},{4,5},{5,4},{6,7},{7,6},{8,9},{9,8},{10,11... | collective-permute-start | bytes 1572872 | tf_op jit(solution)/shard_map/ppermute | solution.py:526
  139.6 14.8 %collective-permute-start.36 = (bf16[1,256,1024]{2,1,0:T(8,128)(2,1)S(1)}, bf16[1,256,1024]{2,1,0:T(8,128)(2,1)S(1)}, u32[]{:S(2)}, u32[]{:S(2)}) collective-permute-start(bf16[1,256,1024]{2,1,0:T(8,128)(2,1)S(1)} %add_blocks.3), channel_id=1, source_target_pairs={{0,2},{2,0},{4,6},{6,4},{1,3},{3,1},{5,7},{7,5},{8,10},{10,8},{12,... | collective-permute-start | bytes 1572872 | tf_op jit(solution)/shard_map/ppermute | solution.py:526
  139.8 25.1 %collective-permute-start.34 = (bf16[1,256,1024]{2,1,0:T(8,128)(2,1)S(1)}, bf16[1,256,1024]{2,1,0:T(8,128)(2,1)S(1)}, u32[]{:S(2)}, u32[]{:S(2)}) collective-permute-start(bf16[1,256,1024]{2,1,0:T(8,128)(2,1)S(1)} %add_blocks.4), channel_id=1, source_target_pairs={{0,2},{2,0},{4,6},{6,4},{1,3},{3,1},{5,7},{7,5},{8,10},{10,8},{12,... | collective-permute-start | bytes 1572872 | tf_op jit(solution)/shard_map/ppermute | solution.py:526
  142.8 22.1 %collective-permute-start.35 = (bf16[1,256,1024]{2,1,0:T(8,128)(2,1)S(1)}, bf16[1,256,1024]{2,1,0:T(8,128)(2,1)S(1)}, u32[]{:S(2)}, u32[]{:S(2)}) collective-permute-start(bf16[1,256,1024]{2,1,0:T(8,128)(2,1)S(1)} %gradients.15), channel_id=1, source_target_pairs={{0,1},{1,0},{2,3},{3,2},{4,5},{5,4},{6,7},{7,6},{8,9},{9,8},{10,11... | collective-permute-start | bytes 1572872 | tf_op jit(solution)/shard_map/ppermute | solution.py:526
  151.3 43.5 %collective-permute-start.28 = (bf16[1040,256]{1,0:T(8,128)(2,1)}, bf16[1040,256]{1,0:T(8,128)(2,1)}, u32[]{:S(2)}, u32[]{:S(2)}) collective-permute-start(bf16[1040,256]{1,0:T(8,128)(2,1)} %get-tuple-element.39), channel_id=1, source_target_pairs={{0,24},{8,16},{16,8},{24,0},{1,25},{9,17},{17,9},{25,1},{2,26},{10... | collective-permute-start | bytes 1597448 | tf_op jit(solution)/shard_map/ppermute | solution.py:526
  151.5 43.3 %collective-permute-start.29 = (bf16[1040,256]{1,0:T(8,128)(2,1)}, bf16[1040,256]{1,0:T(8,128)(2,1)}, u32[]{:S(2)}, u32[]{:S(2)}) collective-permute-start(bf16[1040,256]{1,0:T(8,128)(2,1)} %get-tuple-element.41), channel_id=1, source_target_pairs={{0,16},{8,24},{16,0},{24,8},{1,17},{9,25},{17,1},{25,9},{2,18},{10... | collective-permute-start | bytes 1597448 | tf_op jit(solution)/shard_map/ppermute | solution.py:526
  154.3 40.5 %collective-permute-start.30 = (bf16[1040,256]{1,0:T(8,128)(2,1)}, bf16[1040,256]{1,0:T(8,128)(2,1)}, u32[]{:S(2)}, u32[]{:S(2)}) collective-permute-start(bf16[1040,256]{1,0:T(8,128)(2,1)} %get-tuple-element.40), channel_id=1, source_target_pairs={{0,8},{8,0},{16,24},{24,16},{1,9},{9,1},{17,25},{25,17},{2,10},{10... | collective-permute-start | bytes 1597448 | tf_op jit(solution)/shard_map/ppermute | solution.py:526
  165.9 25.6 %collective-permute-start.37 = (bf16[1,256,1024]{2,1,0:T(8,128)(2,1)}, bf16[1,256,1024]{2,1,0:T(8,128)(2,1)}, u32[]{:S(2)}, u32[]{:S(2)}) collective-permute-start(bf16[1,256,1024]{2,1,0:T(8,128)(2,1)} %add_blocks.5), channel_id=1, source_target_pairs={{0,4},{2,6},{4,0},{6,2},{1,5},{3,7},{5,1},{7,3},{8,12},{10,14},{12... | collective-permute-start | bytes 1572872 | tf_op jit(solution)/shard_map/ppermute | solution.py:526
  195.5 7.0 %collective-permute-start.31 = (f32[1,128]{1,0:T(1,128)S(1)}, f32[1,128]{1,0:T(1,128)S(1)}, u32[]{:S(2)}, u32[]{:S(2)}) collective-permute-start(f32[1,128]{1,0:T(1,128)S(1)} %bitcast_add_fusion), channel_id=1, source_target_pairs={{0,2},{2,0},{4,6},{6,4},{1,3},{3,1},{5,7},{7,5},{8,10},{10,8},{12,... | collective-permute-start | bytes 1544 | tf_op jit(solution)/shard_map/ppermute | solution.py:526
  195.6 6.9 %collective-permute-start.32 = (f32[1,128]{1,0:T(1,128)S(1)}, f32[1,128]{1,0:T(1,128)S(1)}, u32[]{:S(2)}, u32[]{:S(2)}) collective-permute-start(f32[1,128]{1,0:T(1,128)S(1)} %bitcast_add_fusion), channel_id=1, source_target_pairs={{0,4},{2,6},{4,0},{6,2},{1,5},{3,7},{5,1},{7,3},{8,12},{10,14},{12... | collective-permute-start | bytes 1544 | tf_op jit(solution)/shard_map/ppermute | solution.py:526
  198.6 5.3 %collective-permute-start.33 = (f32[1,128]{1,0:T(1,128)S(1)}, f32[1,128]{1,0:T(1,128)S(1)}, u32[]{:S(2)}, u32[]{:S(2)}) collective-permute-start(f32[1,128]{1,0:T(1,128)S(1)} %bitcast_add_fusion), channel_id=1, source_target_pairs={{0,6},{2,4},{4,2},{6,0},{1,7},{3,5},{5,3},{7,1},{8,14},{10,12},{12... | collective-permute-start | bytes 1544 | tf_op jit(solution)/shard_map/ppermute | solution.py:526
  (20 other events, 124.5 us)
Sparse Core Ops, SparseCore 0:
  10.2 93.8 all-gather.1
